TPU v7x, 512 devices: a whole 4x4x16 slice. The times are simulated.
512 devices in a mesh: lat: 16 (over z_hi, x, core), chan: 32 (over z_lo, y).
Axes of the slice: x: 4, y: 4, z: 16 (z_hi: 2, z_lo: 8; z = z_hi * 8 + z_lo), core: 2. Of those that a mesh axis runs over, the one named last changes fastest.
Arguments:
- block_input: bfloat16 [768, 128, 256], P('chan', 'lat'), may hold values from -6 to 6
- out_grad: bfloat16 [768, 128, 256], P('chan', 'lat'), may hold values from -6 to 6
- metric: float32 [128], P('lat'), may hold values from 1 to 4
- kernel: float32 [768, 49], P('chan'), may hold values from -0.875 to 0.875
- conv_bias: float32 [768], P('chan'), may hold values from -3 to 3
- ln_gain: float32 [768], replicated, may hold values from 0.1 to 1.9
- ln_bias: float32 [768], replicated, may hold values from -3 to 3
- w_in: bfloat16 [3072, 768], P('chan'), may hold values from -0.4375 to 0.4375
- b_in: float32 [3072], P('chan'), may hold values from -3 to 3
- w_out: bfloat16 [3072, 768], P('chan'), may hold values from -0.109375 to 0.109375
- b_out: float32 [768], P('chan'), may hold values from -3 to 3
- layer_scale: bfloat16 [768], replicated, may hold values from 0.5 to 2
Outputs:
- grad_input: float32 [768, 128, 256], P('chan', 'lat')
- grad_kernel: float32 [768, 49], P('chan')
- grad_conv_bias: float32 [768], P('chan')
- grad_ln_gain: float32 [768], P('chan')
- grad_ln_bias: float32 [768], P('chan')
- grad_w_in: float32 [3072, 768], P('chan')
- grad_b_in: float32 [3072], P('chan')
- grad_w_out: float32 [3072, 768], P('chan')
- grad_b_out: float32 [768], P('chan')
- grad_layer_scale: float32 [768], P('chan')
All inputs are finite; a program needn't handle non-finite values.
Results may differ from a plain program's by a relative error of at most 0.035.
Values may be sent and summed in bfloat16 or wider, within the bound.
No kernel may reach another device: no remote copies, remote signals or barrier semaphores. Data moves between devices by JAX's collectives and lax.ppermute only.
A program may use at most 64 MiB of HBM per device.

v0:
```python
import jax
import jax.numpy as jnp
from jax import lax
from jax.sharding import PartitionSpec as P


def extended_2(cells, sides, width):
    for axis, dim in sides:
        count = lax.axis_size(axis)
        ends = count - 1
        head = lax.slice_in_dim(cells, 0, width, axis=dim)
        tail = lax.slice_in_dim(cells, cells.shape[dim] - width, cells.shape[dim], axis=dim)
        cells = jnp.concatenate(
            [
                lax.ppermute(tail, axis, [(i, (i + 1) % count) for i in range(ends)]),
                cells,
                lax.ppermute(head, axis, [((i + 1) % count, i) for i in range(ends)]),
            ],
            axis=dim,
        )
    return cells


def gelu_exact(value):
    return jax.nn.gelu(value, approximate=False)


def per_device(
    block_input,
    out_grad,
    metric,
    kernel,
    conv_bias,
    ln_gain,
    ln_bias,
    w_in,
    b_in,
    w_out,
    b_out,
    layer_scale,
):
    cdev, rows, width = block_input.shape
    chans = ln_gain.shape[0]
    tokens = rows * width
    offset = lax.axis_index("chan") * cdev
    contract = (((1,), (1,)), ((), ()))
    gamma_f = layer_scale.astype(jnp.float32)
    gain_own = lax.dynamic_slice_in_dim(ln_gain, offset, cdev)
    bias_own = lax.dynamic_slice_in_dim(ln_bias, offset, cdev)
    gamma_own = lax.dynamic_slice_in_dim(gamma_f, offset, cdev)
    extended = extended_2(block_input, (("lat", 1),), 3)
    xpad = jnp.pad(extended.astype(jnp.float32), ((0, 0), (0, 0), (3, 3)))
    conv = jnp.zeros((cdev, rows, width), jnp.float32)
    for a in range(7):
        for b in range(7):
            conv = conv + kernel[:, a * 7 + b][:, None, None] * xpad[:, a : a + rows, b : b + width]
    h = (
        (conv_bias[:, None, None] + metric[None, :, None] * conv)
        .astype(jnp.bfloat16)
        .reshape(cdev, tokens)
    )
    hf = h.astype(jnp.float32)
    sums, squares = lax.psum((jnp.sum(hf, 0), jnp.sum(hf * hf, 0)), "chan")
    mean = sums / chans
    var = squares / chans - mean * mean
    rstd = 1.0 / jnp.sqrt(var + 1e-06)
    nhat = (hf - mean) * rstd
    n_own = (nhat * gain_own[:, None] + bias_own[:, None]).astype(jnp.bfloat16)
    n_full = lax.all_gather(n_own, "chan", axis=0, tiled=True)
    pre = jnp.dot(w_in, n_full, preferred_element_type=jnp.float32) + b_in[:, None]
    g, back = jax.vjp(gelu_exact, pre)
    g_b = g.astype(jnp.bfloat16)
    dy_rows = out_grad.reshape(cdev, tokens)
    piece = lax.all_gather(dy_rows, "chan", axis=0, tiled=True)
    scaled = (gamma_f[:, None] * piece.astype(jnp.float32)).astype(jnp.bfloat16)
    cols = w_out
    grad_g = jnp.dot(cols, scaled, preferred_element_type=jnp.float32)
    part = lax.dot_general(g_b, piece, contract, preferred_element_type=jnp.float32)
    grad_g, proj = (grad_g, part)
    dpre = back(grad_g)[0].astype(jnp.bfloat16)
    dw_in = lax.dot_general(dpre, n_full, contract, preferred_element_type=jnp.float32)
    db_in = jnp.sum(dpre.astype(jnp.float32), 1)
    cols = w_in
    dn = lax.psum_scatter(
        lax.dot_general(
            cols, dpre, (((0,), (0,)), ((), ())), preferred_element_type=jnp.float32
        ).astype(jnp.bfloat16),
        "chan",
        scatter_dimension=0,
        tiled=True,
    ).astype(jnp.float32)
    gam_part = jnp.sum(w_out.astype(jnp.float32) * proj, 0)
    dnhat = gain_own[:, None] * dn
    first, second, gam_all = lax.psum(
        (jnp.sum(dnhat, 0), jnp.sum(dnhat * nhat, 0), gam_part), "chan"
    )
    dh = rstd * (dnhat - first / chans - nhat * (second / chans))
    grad_ln_gain = jnp.sum(dn * nhat, 1)
    grad_ln_bias = jnp.sum(dn, 1)
    dh3 = dh.reshape(cdev, rows, width)
    grad_conv_bias = jnp.sum(dh3, (1, 2))
    dconv = metric[None, :, None] * dh3
    taps = []
    for a in range(7):
        for b in range(7):
            taps.append(jnp.sum(xpad[:, a : a + rows, b : b + width] * dconv, (1, 2)))
    grad_kernel = jnp.stack(taps, 1)
    fetched = extended_2(dconv, (("lat", 1),), 3)
    dpad = jnp.pad(fetched, ((0, 0), (0, 0), (3, 3)))
    spread = jnp.zeros((cdev, rows, width), jnp.float32)
    for a in range(7):
        for b in range(7):
            spread = (
                spread
                + kernel[:, a * 7 + b][:, None, None]
                * dpad[:, 6 - a : 6 - a + rows, 6 - b : 6 - b + width]
            )
    grad_input = out_grad.astype(jnp.float32) + spread
    dysum = jnp.sum(out_grad.astype(jnp.float32), (1, 2))
    grad_b_out = gamma_own * dysum
    grad_layer_scale = lax.dynamic_slice_in_dim(gam_all, offset, cdev) + b_out * dysum
    dw_out = proj * gamma_f[None, :]
    summed = lax.psum(
        (
            dw_in,
            dw_out,
            db_in,
            grad_kernel,
            grad_conv_bias,
            grad_ln_gain,
            grad_ln_bias,
            grad_b_out,
            grad_layer_scale,
        ),
        "lat",
    )
    return (
        grad_input,
        summed[3],
        summed[4],
        summed[5],
        summed[6],
        summed[0],
        summed[2],
        summed[1],
        summed[7],
        summed[8],
    )


def solution(mesh):
    return jax.shard_map(
        per_device,
        mesh=mesh,
        in_specs=(
            P("chan", "lat", None),
            P("chan", "lat", None),
            P("lat"),
            P("chan", None),
            P("chan"),
            P(),
            P(),
            P("chan", None),
            P("chan"),
            P("chan", None),
            P("chan"),
            P(),
        ),
        out_specs=(
            P("chan", "lat", None),
            P("chan", None),
            P("chan"),
            P("chan"),
            P("chan"),
            P("chan", None),
            P("chan"),
            P("chan", None),
            P("chan"),
            P("chan"),
        ),
        check_vma=False,
    )
```

profile of v0, /device:TPU:1, one launch (start us, length us, event | category | flops | bytes accessed | tf_op | source)
XLA Modules:
  0.0 1354.7 jit_solution(5100898651147134416)
XLA Ops:
  8.3 4.5 collective-permute-start
  12.8 5.6 collective-permute-start.1
  18.4 2.0 slice_reduce_fusion.48
  20.4 2.0 slice_reduce_fusion.47
  26.4 4.6 multiply_reduce_fusion.50
  31.0 205.9 %all-reduce.3 = (f32[2048]{0:T(1024)S(1)}, f32[2048]{0:T(1024)S(1)}) all-reduce(f32[2048]{0:T(1024)S(1)} %bitcast.169, f32[2048]{0:T(1024)S(1)} %bitcast.168), channel_id=1, replica_groups=mesh['lat'=16,'chan'=32] {'chan'}, use_global_device_ids=true, to_apply=%region_3.4 | all-reduce | flops 4096 | bytes 32768 | tf_op jit(solution)/shard_map/psum | solution.py:63
  238.5 235.9 %all-gather.3.cloned.1.call-done = bf16[768,2048]{1,0:T(8,128)(2,1)} async-done(((bf16[24,2048]{1,0:T(8,128)(2,1)}), bf16[768,2048]{1,0:T(8,128)(2,1)}) %all-gather.3.cloned.1.call-update) | async-done | bytes 3145744 | tf_op jit(solution)/shard_map/all_gather | solution.py:69
  474.5 2.5 convolution_add_fusion
  477.0 224.5 %all-gather.5.cloned.1.call-done = bf16[768,2048]{1,0:T(8,128)(2,1)} async-done(((bf16[24,2048]{1,0:T(8,128)(2,1)}), bf16[768,2048]{1,0:T(8,128)(2,1)}) %all-gather.5.cloned.1.call-update) | async-done | bytes 3145744 | tf_op jit(solution)/shard_map/all_gather | solution.py:74
  701.5 4.6 convert_reduce_fusion
  706.1 2.7 fusion.2
  708.7 4.8 copy.78
  713.8 3.9 fusion.100
  717.7 3.2 broadcast_multiply_fusion
  721.0 231.1 %reduce-scatter.4.cloned.1.call-done = bf16[24,2048]{1,0:T(8,128)(2,1)} async-done(((bf16[768,2048]{1,0:T(8,128)(2,1)}), bf16[24,2048]{1,0:T(8,128)(2,1)}) %reduce-scatter.4.cloned.1.call-update) | async-done | bytes 98320 | tf_op jit(solution)/shard_map/reduce_scatter | solution.py:84
  953.2 201.2 %all-reduce.2 = (f32[2048]{0:T(1024)S(1)}, f32[2048]{0:T(1024)S(1)}, f32[768]{0:T(1024)S(1)}) all-reduce(f32[2048]{0:T(1024)S(1)} %get-tuple-element.80, f32[2048]{0:T(1024)S(1)} %get-tuple-element.81, f32[768]{0:T(1024)S(1)} %get-tuple-element.153), channel_id=1, replica_groups=mesh['lat'=16,'chan'=32] {'chan'}, use_global_device_ids=true, to_apply=%region_8.9 | all-reduce | flops 4864 | bytes 38912 | tf_op jit(solution)/shard_map/psum | solution.py:94
  1155.6 1.8 multiply_reduce_fusion.1
  1157.5 1.9 multiply_reduce_fusion.2
  1159.4 52.4 %collective-permute-start.3 = (f32[24,3,256]{2,1,0:T(4,128)S(1)}, f32[24,3,256]{2,1,0:T(4,128)S(1)}, u32[]{:S(2)}, u32[]{:S(2)}) collective-permute-start(f32[24,3,256]{2,1,0:T(4,128)S(1)} %get-tuple-element.154), channel_id=1, source_target_pairs={{32,0},{64,32},{96,64},{128,96},{160,128},{192,160},{224,192},{256... | collective-permute-start | bytes 221192 | tf_op jit(solution)/shard_map/ppermute | solution.py:17
  1211.8 2.6 collective-permute-start.2
  1220.2 119.9 %all-reduce.4 = (f32[24,49]{1,0:T(8,128)}, f32[24]{0:T(128)}, f32[24]{0:T(128)}, f32[24]{0:T(128)}, f32[96]{0:T(128)}, /*index=5*/f32[24]{0:T(128)}, f32[24]{0:T(128)}) all-reduce(f32[24,49]{1,0:T(8,128)S(1)} %stack.199, f32[24]{0:T(128)S(1)} %get-tuple-element.148, ...), channel_id=1, replica_groups=mesh['lat'=16,'chan'=32] {'lat'}, use_global_device_ids=true, to_apply=%region_58.59 | all-reduce | flops 1392 | bytes 11136 | tf_op jit(solution)/shard_map/psum | solution.py:123
  1340.6 4.2 convert_add_fusion
  1344.8 1.7 copy.87
  1346.4 1.7 copy.88
  (100 shorter events, 15.5 us)
Async XLA Ops:
  7.2 467.3 %copy-start = (bf16[96,768]{1,0:T(8,128)(2,1)S(1)}, bf16[96,768]{1,0:T(8,128)(2,1)}, u32[]{:S(2)}) copy-start(bf16[96,768]{1,0:T(8,128)(2,1)} %param.19) | copy-start | bytes 442372
  7.2 230.6 %copy-start.1 = (bf16[24,8,256]{2,1,0:T(8,128)(2,1)S(1)}, bf16[24,8,256]{2,1,0:T(8,128)(2,1)}, u32[]{:S(2)}) copy-start(bf16[24,8,256]{2,1,0:T(8,128)(2,1)} %param.13) | copy-start | bytes 294916
  7.2 231.3 %copy-start.2 = (bf16[768]{0:T(1024)(128)(2,1)S(1)}, bf16[768]{0:T(1024)(128)(2,1)}, u32[]{:S(2)}) copy-start(bf16[768]{0:T(1024)(128)(2,1)} %param.23) | copy-start | bytes 4612
  7.2 467.2 %copy-start.4 = (f32[96]{0:T(128)S(1)}, f32[96]{0:T(128)}, u32[]{:S(2)}) copy-start(f32[96]{0:T(128)} %param.20) | copy-start | bytes 1156
  7.2 467.2 %all-gather.3.cloned.1.call-start = ((), (), s32[]{:S(2)}) async-start(), calls=%async_computation.1 | async-start | bytes 3244032 | tf_op jit(solution)/shard_map/all_gather | solution.py:69
  8.3 17.1 %collective-permute-start = (bf16[24,3,256]{2,1,0:T(4,128)(2,1)S(1)}, bf16[24,3,256]{2,1,0:T(4,128)(2,1)S(1)}, u32[]{:S(2)}, u32[]{:S(2)}) collective-permute-start(bf16[24,3,256]{2,1,0:T(4,128)(2,1)S(1)} %get-tuple-element.156), channel_id=1, source_target_pairs={{0,32},{32,64},{64,96},{96,128},{128,160},{160,192},{192,224},{224... | collective-permute-start | bytes 110600 | tf_op jit(solution)/shard_map/ppermute | solution.py:15
  12.8 12.5 collective-permute-start.1
  26.4 675.1 %copy-start.7 = (bf16[96,768]{1,0:T(8,128)(2,1)S(1)}, bf16[96,768]{1,0:T(8,128)(2,1)}, u32[]{:S(2)}) copy-start(bf16[96,768]{1,0:T(8,128)(2,1)} %param.21) | copy-start | bytes 442372
  237.7 463.7 %all-gather.5.cloned.1.call-start = ((), (), s32[]{:S(2)}) async-start(), calls=%async_computation.2 | async-start | bytes 3244032 | tf_op jit(solution)/shard_map/all_gather | solution.py:74
  238.5 713.6 %reduce-scatter.4.cloned.1.call-start = ((), (), s32[]{:S(2)}) async-start(), calls=%async_computation.3 | async-start | bytes 3244032 | tf_op jit(solution)/shard_map/reduce_scatter | solution.py:84
  713.5 631.2 %all-reduce.8.cloned.1.call-start = ((), (), s32[]{:S(2)}) async-start(), calls=%async_computation.4 | async-start | bytes 1179648 | tf_op jit(solution)/shard_map/psum | solution.py:123
  713.6 4.1 copy-start.6
  717.7 437.9 %copy-start.3 = (f32[8]{0:T(128)S(1)}, f32[8]{0:T(128)}, u32[]{:S(2)}) copy-start(f32[8]{0:T(128)} %param.14) | copy-start | bytes 100
  720.9 493.5 %copy-start.5 = (f32[24]{0:T(128)S(1)}, f32[24]{0:T(128)}, u32[]{:S(2)}) copy-start(f32[24]{0:T(128)} %param.22) | copy-start | bytes 292
  1159.4 180.8 %collective-permute-start.3 = (f32[24,3,256]{2,1,0:T(4,128)S(1)}, f32[24,3,256]{2,1,0:T(4,128)S(1)}, u32[]{:S(2)}, u32[]{:S(2)}) collective-permute-start(f32[24,3,256]{2,1,0:T(4,128)S(1)} %get-tuple-element.154), channel_id=1, source_target_pairs={{32,0},{64,32},{96,64},{128,96},{160,128},{192,160},{224,192},{256... | collective-permute-start | bytes 221192 | tf_op jit(solution)/shard_map/ppermute | solution.py:17
  1211.8 128.4 %collective-permute-start.2 = (f32[24,3,256]{2,1,0:T(4,128)S(1)}, f32[24,3,256]{2,1,0:T(4,128)S(1)}, u32[]{:S(2)}, u32[]{:S(2)}) collective-permute-start(f32[24,3,256]{2,1,0:T(4,128)S(1)} %get-tuple-element.155), channel_id=1, source_target_pairs={{0,32},{32,64},{64,96},{96,128},{128,160},{160,192},{192,224},{224... | collective-permute-start | bytes 221192 | tf_op jit(solution)/shard_map/ppermute | solution.py:15
Sparse Core Ops, SparseCore 0:
  237.8 236.5 all-gather.2
  477.1 224.3 all-gather.4
  713.6 238.4 reduce-scatter.3
  955.8 270.4 all-reduce.7
where the time goes:
time: 1370 us; the launch traced here: 1350 us
  waiting for transfers between devices  692 us (51%)
  blocking collectives  527 us (38%)
  starting transfers between devices  65.2 us (5%)
  local copies, waits for them, and re-layouts  21.3 us (2%)
  other arithmetic  18.5 us (1%)
  matrix products  16.9 us (1%)
  between operations  14 us (1%)
    all_gather x1, waiting for transfers between devices, per_device(): n_full = lax.all_gather(n_own, 'chan', axis=0, tiled=True)  236 us
    reduce_scatter x1, waiting for transfers between devices, per_device(): lax.psum_scatter(lax.dot_general(cols, dpre, (((0,), (0,)), ((), ())), pr...  231 us
    all_gather x1, waiting for transfers between devices, per_device(): piece = lax.all_gather(dy_rows, 'chan', axis=0, tiled=True)  224 us
    psum x1, blocking collectives, per_device(): sums, squares = lax.psum((jnp.sum(hf, 0), jnp.sum(hf * hf, 0)), 'chan')  206 us
    psum x1, blocking collectives, per_device(): lax.psum((jnp.sum(dnhat, 0), jnp.sum(dnhat * nhat, 0), gam_part), 'chan')  201 us
    psum x1, blocking collectives, per_device(): lax.psum((dw_in, dw_out, db_in, grad_kernel, grad_conv_bias, grad_ln_gain...  120 us
    ppermute x2, starting transfers between devices, extended_2(): lax.ppermute(head, axis, [((i + 1) % count, i) for i in range(ends)])  58 us
  transfers between devices with their start and end apart: 8, of which 3 were waited for; matrix products, arithmetic and copies ran while one was open for 3% of the time, Pallas kernels for 0%

commit v1 on v0

v1 whole, which is shorter than its diff:
```python
import jax
import jax.numpy as jnp
from jax import lax
from jax.sharding import Mesh, PartitionSpec as P

LAT = ("zh", "x", "c")
CHAN = ("zl", "y")
GROUP = 8
F32 = jnp.float32
BF = jnp.bfloat16


def extended(cells, width):
    count = lax.axis_size(LAT)
    ends = count - 1
    head = lax.slice_in_dim(cells, 0, width, axis=1)
    tail = lax.slice_in_dim(cells, cells.shape[1] - width, cells.shape[1], axis=1)
    return jnp.concatenate(
        [
            lax.ppermute(tail, LAT, [(i, i + 1) for i in range(ends)]),
            cells,
            lax.ppermute(head, LAT, [(i + 1, i) for i in range(ends)]),
        ],
        axis=1,
    )


def gelu_exact(value):
    return jax.nn.gelu(value, approximate=False)


def two_parts(value):
    high = lax.reduce_precision(value, 8, 7)
    return high.astype(BF), (value - high).astype(BF)


def per_device(
    block_input,
    out_grad,
    metric,
    kernel,
    conv_bias,
    ln_gain,
    ln_bias,
    w_in,
    b_in,
    w_out,
    b_out,
    layer_scale,
):
    cdev, rows, width = block_input.shape
    chans = ln_gain.shape[0]
    tokens = rows * width
    nz, ny = lax.axis_size("zl"), lax.axis_size("y")
    nchan = nz * ny
    hdev = w_in.shape[0]
    part = hdev // GROUP
    hid = part * nchan
    piece = tokens // nchan
    member = lax.axis_index(("x", "c"))
    owner = lax.axis_index(CHAN)
    gamma_f = layer_scale.astype(F32)
    gamma_own = lax.dynamic_slice_in_dim(gamma_f, owner * cdev, cdev)

    bias_high, bias_low = two_parts(lax.dynamic_slice_in_dim(b_in, member * part, part))
    bias_row = jnp.zeros((1, chans), BF)
    bias_row = bias_row.at[0, :part].set(bias_high).at[0, part : 2 * part].set(bias_low)
    mine = jnp.concatenate(
        [
            lax.dynamic_slice_in_dim(w_in, member * part, part),
            lax.dynamic_slice_in_dim(w_out, member * part, part),
            bias_row,
        ],
        0,
    )
    shards = lax.all_gather(mine, "y", axis=0)
    shards = lax.all_gather(shards, "zl", axis=1)
    wi = shards[:, :, :part].reshape(hid, chans)
    wo = shards[:, :, part : 2 * part].reshape(hid, chans)
    bias_rows = shards[:, :, 2 * part].astype(F32)
    bi = (bias_rows[..., :part] + bias_rows[..., part : 2 * part]).reshape(hid)

    xpad = jnp.pad(extended(block_input, 3).astype(F32), ((0, 0), (0, 0), (3, 3)))
    conv = jnp.zeros((cdev, rows, width), F32)
    for a in range(7):
        for b in range(7):
            conv = conv + kernel[:, a * 7 + b][:, None, None] * xpad[:, a : a + rows, b : b + width]
    h = (conv_bias[:, None, None] + metric[None, :, None] * conv).astype(BF)

    both = jnp.concatenate(
        [h.reshape(cdev, nchan, piece), out_grad.reshape(cdev, nchan, piece)], 2
    ).transpose(1, 0, 2)
    both = lax.all_to_all(both, CHAN, 0, 0, tiled=True).reshape(chans, 2 * piece).T
    hf = both[:piece].astype(F32)
    dy_piece = both[piece:]
    mean = jnp.sum(hf, 1, keepdims=True) / chans
    var = jnp.sum(hf * hf, 1, keepdims=True) / chans - mean * mean
    rstd = 1.0 / jnp.sqrt(var + 1e-06)
    nhat = (hf - mean) * rstd
    n_piece = (nhat * ln_gain + ln_bias).astype(BF)

    pair = jnp.concatenate([n_piece, dy_piece], 0)
    pair = lax.all_gather(pair, "x", axis=0)
    pair = lax.all_gather(pair, "c", axis=0)
    n = pair[:, :, :piece].reshape(GROUP * piece, chans)
    dy = pair[:, :, piece:].reshape(GROUP * piece, chans)

    over_last = (((1,), (1,)), ((), ()))
    over_first = (((0,), (0,)), ((), ()))
    pre = lax.dot_general(n, wi, over_last, preferred_element_type=F32) + bi
    g, back = jax.vjp(gelu_exact, pre)
    g_b = g.astype(BF)
    dmlp = (gamma_f * dy.astype(F32)).astype(BF)
    grad_g = lax.dot_general(dmlp, wo, over_last, preferred_element_type=F32)
    dpre = back(grad_g)[0].astype(BF)
    dn_part = jnp.dot(dpre, wi, preferred_element_type=F32).astype(BF)
    dw_in = lax.dot_general(dpre, n, over_first, preferred_element_type=F32)
    proj = lax.dot_general(g_b, dy, over_first, preferred_element_type=F32)
    db_in = jnp.sum(dpre.astype(F32), 0)
    gam_part = jnp.sum(wo.astype(F32) * proj, 0)
    dw_out = proj * gamma_f

    grid = (ny, nz, part)
    db_row = jnp.pad(db_in.astype(BF).reshape(grid)[:, :, None, :], ((0, 0), (0, 0), (0, 0), (0, chans - part)))
    dws = jnp.concatenate(
        [dw_in.astype(BF).reshape(grid + (chans,)), dw_out.astype(BF).reshape(grid + (chans,)), db_row], 2
    )
    dws = lax.psum_scatter(dws, "y", scatter_dimension=0, tiled=False)

    dn = lax.all_to_all(dn_part.reshape(GROUP, piece, chans), ("c", "x"), 0, 0, tiled=True)
    dn = jnp.sum(dn.astype(F32), 0)
    dnhat = ln_gain * dn
    s1 = jnp.sum(dnhat, 1, keepdims=True) / chans
    s2 = jnp.sum(dnhat * nhat, 1, keepdims=True) / chans
    dh = rstd * (dnhat - s1 - nhat * s2)
    extra = []
    for value in (jnp.sum(dn * nhat, 0), jnp.sum(dn, 0), gam_part):
        extra += list(two_parts(value))
    payload = jnp.concatenate([dh.astype(BF), jnp.stack(extra, 0)], 0)
    payload = payload.T.reshape(nchan, cdev, piece + 6)
    payload = lax.all_to_all(payload, CHAN, 0, 0, tiled=True)
    dh3 = payload[:, :, :piece].transpose(1, 0, 2).reshape(cdev, rows, width).astype(F32)
    sums = jnp.sum(payload[:, :, piece:].astype(F32), 0)
    sums = sums[:, 0::2] + sums[:, 1::2]

    dws = lax.all_to_all(dws, "zl", 0, 0, tiled=True)
    dws = jnp.sum(dws.astype(F32), 0)

    dconv = metric[None, :, None] * dh3
    taps = []
    for a in range(7):
        for b in range(7):
            taps.append(jnp.sum(xpad[:, a : a + rows, b : b + width] * dconv, (1, 2)))
    dpad = jnp.pad(extended(dconv.astype(BF), 3).astype(F32), ((0, 0), (0, 0), (3, 3)))
    spread = jnp.zeros((cdev, rows, width), F32)
    for a in range(7):
        for b in range(7):
            spread = (
                spread
                + kernel[:, a * 7 + b][:, None, None]
                * dpad[:, 6 - a : 6 - a + rows, 6 - b : 6 - b + width]
            )
    grad_input = out_grad.astype(F32) + spread
    dysum = jnp.sum(out_grad.astype(F32), (1, 2))

    small = jnp.concatenate(
        [jnp.stack(taps, 1), jnp.sum(dh3, (1, 2))[:, None], sums, dysum[:, None]], 1
    )
    n_small = small.size
    small_rows = -(-n_small // chans)
    small = jnp.pad(small.reshape(n_small), (0, small_rows * chans - n_small)).reshape(small_rows, chans)
    swap = [(0, 1), (1, 0)]
    high, low = two_parts(small)
    mine = jnp.concatenate([dws.astype(BF), high, low], 0)
    other = lax.ppermute(mine, "zh", swap).astype(F32)
    wrows = 2 * part + 1
    dws = dws + other[:wrows]
    small = small + other[wrows : wrows + small_rows] + other[wrows + small_rows :]
    high, low = two_parts(small)
    mine = jnp.concatenate([dws.astype(BF), high, low], 0)
    gathered = lax.all_gather(mine, "c", axis=0)
    gathered = lax.all_gather(gathered, "x", axis=0).reshape(GROUP, -1, chans).astype(F32)
    grad_w_in = gathered[:, :part].reshape(hdev, chans)
    grad_w_out = gathered[:, part : 2 * part].reshape(hdev, chans)
    grad_b_in = gathered[:, 2 * part, :part].reshape(hdev)
    small = jnp.sum(gathered[:, wrows : wrows + small_rows] + gathered[:, wrows + small_rows :], 0)
    small = small.reshape(-1)[:n_small].reshape(cdev, -1)
    taps_n = kernel.shape[1]
    dysum = small[:, taps_n + 4]
    return (
        grad_input,
        small[:, :taps_n],
        small[:, taps_n],
        small[:, taps_n + 1],
        small[:, taps_n + 2],
        grad_w_in,
        grad_b_in,
        grad_w_out,
        gamma_own * dysum,
        small[:, taps_n + 3] + b_out * dysum,
    )


def solution(mesh):
    split = Mesh(mesh.devices.reshape(2, 4, 2, 8, 4), ("zh", "x", "c", "zl", "y"))
    return jax.shard_map(
        per_device,
        mesh=split,
        in_specs=(
            P(CHAN, LAT, None),
            P(CHAN, LAT, None),
            P(LAT),
            P(CHAN, None),
            P(CHAN),
            P(),
            P(),
            P(CHAN, None),
            P(CHAN),
            P(CHAN, None),
            P(CHAN),
            P(),
        ),
        out_specs=(
            P(CHAN, LAT, None),
            P(CHAN, None),
            P(CHAN),
            P(CHAN),
            P(CHAN),
            P(CHAN, None),
            P(CHAN),
            P(CHAN, None),
            P(CHAN),
            P(CHAN),
        ),
        check_vma=False,
    )
```

time: 1370 us -> 268 us (0.20)
  waiting for transfers between devices: 692 us -> 68.6 us
  blocking collectives: 527 us -> 81.7 us
  starting transfers between devices: 65.2 us -> 45.1 us
    psum x3 -> x0, blocking collectives: 527 us -> none  [the longest x1 206 us: per_device(): sums, squares = lax.psum((jnp.sum(hf, 0), jnp.sum(hf * hf, 0)), 'chan')]
    all_gather x2, waiting for transfers between devices: 460 us -> 39.2 us  [the longest x1 21.3 us: per_device(): pair = lax.all_gather(pair, 'c', axis=0)]
    reduce_scatter x1, waiting for transfers between devices: 231 us -> 0.02 us  [per_device(): dws = lax.psum_scatter(dws, 'y', scatter_dimension=0, tiled=False)]
    all_gather x0 -> x4, blocking collectives: none -> 56.8 us  [the longest x1 21.7 us: per_device(): pair = lax.all_gather(pair, 'x', axis=0)]
    ppermute x4 -> x5, starting transfers between devices: 65.1 us -> 21.2 us  [the longest x2 8.38 us: extended(): lax.ppermute(tail, LAT, [(i, i + 1) for i in range(ends)])]
    all_to_all x0 -> x1, blocking collectives: none -> 24.9 us  [per_device(): lax.all_to_all(both, CHAN, 0, 0, tiled=True).reshape(chans, 2 * piece)]
    all_to_all x0 -> x3, starting transfers between devices: none -> 23.8 us  [the longest x1 12.3 us: per_device(): payload = lax.all_to_all(payload, CHAN, 0, 0, tiled=True)]
    all_to_all x0 -> x3, waiting for transfers between devices: none -> 21.9 us  [the longest x1 14 us: per_device(): payload = lax.all_to_all(payload, CHAN, 0, 0, tiled=True)]
  transfers between devices with their start and end apart: 8 -> 11, of which waited for: 3 -> 6; matrix products, arithmetic and copies ran while one was open for 3% -> 15% of each run, Pallas kernels for 0% -> 0%
where the time goes in v1:
time: 268 us; the launch traced here: 266 us
  blocking collectives  81.7 us (30%)
  waiting for transfers between devices  68.6 us (26%)
  starting transfers between devices  45.1 us (17%)
  other arithmetic  22.8 us (9%)
  local copies, waits for them, and re-layouts  22.5 us (8%)
  between operations  15.4 us (6%)
  matrix products  9.62 us (4%)
    all_to_all x1, blocking collectives, per_device(): lax.all_to_all(both, CHAN, 0, 0, tiled=True).reshape(chans, 2 * piece)  24.9 us
    all_gather x1, blocking collectives, per_device(): pair = lax.all_gather(pair, 'x', axis=0)  21.7 us
    all_gather x1, waiting for transfers between devices, per_device(): pair = lax.all_gather(pair, 'c', axis=0)  21.3 us
    all_gather x1, waiting for transfers between devices, per_device(): shards = lax.all_gather(shards, 'zl', axis=1)  17.9 us
    all_gather x1, blocking collectives, per_device(): lax.all_gather(gathered, 'x', axis=0).reshape(GROUP, -1, chans).astype(F32)  17.2 us
    all_to_all x1, waiting for transfers between devices, per_device(): payload = lax.all_to_all(payload, CHAN, 0, 0, tiled=True)  14 us
    all_to_all x1, starting transfers between devices, per_device(): payload = lax.all_to_all(payload, CHAN, 0, 0, tiled=True)  12.3 us
    all_gather x1, blocking collectives, per_device(): shards = lax.all_gather(mine, 'y', axis=0)  9.61 us
  transfers between devices with their start and end apart: 11, of which 6 were waited for; matrix products, arithmetic and copies ran while one was open for 15% of the time, Pallas kernels for 0%

profile of v1, /device:TPU:1, one launch (start us, length us, event | category | flops | bytes accessed | tf_op | source)
XLA Modules:
  0.0 265.7 jit_solution(3015278212150179185)
XLA Ops:
  8.3 4.5 %collective-permute-start = (bf16[24,3,256]{2,1,0:T(4,128)(2,1)S(1)}, bf16[24,3,256]{2,1,0:T(4,128)(2,1)S(1)}, u32[]{:S(2)}, u32[]{:S(2)}) collective-permute-start(bf16[24,3,256]{2,1,0:T(4,128)(2,1)S(1)} %get-tuple-element.160), channel_id=1, source_target_pairs={{0,32},{32,64},{64,96},{96,128},{128,160},{160,192},{192,224},{224... | collective-permute-start | bytes 110600 | tf_op jit(solution)/shard_map/ppermute | solution.py:20
  12.8 5.6 %collective-permute-start.1 = (bf16[24,3,256]{2,1,0:T(4,128)(2,1)S(1)}, bf16[24,3,256]{2,1,0:T(4,128)(2,1)S(1)}, u32[]{:S(2)}, u32[]{:S(2)}) collective-permute-start(bf16[24,3,256]{2,1,0:T(4,128)(2,1)S(1)} %get-tuple-element.161), channel_id=1, source_target_pairs={{32,0},{64,32},{96,64},{128,96},{160,128},{192,160},{224,192},{256... | collective-permute-start | bytes 110600 | tf_op jit(solution)/shard_map/ppermute | solution.py:22
  21.0 2.0 broadcast_select_fusion
  24.8 9.6 %all-gather.6 = bf16[4,25,768]{2,1,0:T(8,128)(2,1)S(1)} all-gather(bf16[1,25,768]{2,1,0:T(8,128)(2,1)S(1)} %maximum_bitcast_fusion.1), channel_id=4, replica_groups=mesh['zh'=2,'x'=4,'c'=2,'zl'=8,'y'=4] {'y'}, dimensions={0}, use_global_device_ids=true | all-gather | bytes 192000 | tf_op jit(solution)/shard_map/all_gather | solution.py:76
  35.3 2.0 slice_reduce_fusion.53
  38.8 3.9 %add_convert_fusion.1 = bf16[24,8,256]{2,1,0:T(8,128)(2,1)S(1)} fusion(f32[24,14,256]{2,1,0:T(8,128)S(1)} %maximum_convert_fusion, f32[24]{0:T(128)S(1)} %get-tuple-element.142, f32[24]{0:T(128)S(1)} %get-tuple-element.143, f32[24]{0:T(128)S(1)} %get-tuple-element.96, f32[24]{0:T(128)S(1)} %get-tuple-element.97, f32[24]{0:T(128)S(1)} %get-tuple-element.98, ...), kind=kLoop, calls=%fused_computation.286 | loop fusion | flops 4915200 | bytes 1893888 | tf_op jit(solution)/shard_map/convert_element_type | solution.py:88
  43.4 24.9 %all_to_all.20 = bf16[32,24,128]{2,1,0:T(8,128)(2,1)S(1)} all-to-all(bf16[32,24,128]{2,1,0:T(8,128)(2,1)S(1)} %copy.202), channel_id=1, replica_groups=mesh['zh'=2,'x'=4,'c'=2,'zl'=8,'y'=4] {'zl','y'}, dimensions={0} | all-to-all | bytes 393216 | tf_op jit(solution)/shard_map/all_to_all | solution.py:93
  68.7 21.7 %all-gather = bf16[512,768]{1,0:T(8,128)(2,1)} all-gather(bf16[128,768]{1,0:T(8,128)(2,1)S(1)} %pad_maximum_fusion), channel_id=2, replica_groups=mesh['zh'=2,'x'=4,'c'=2,'zl'=8,'y'=4] {'x'}, dimensions={0}, use_global_device_ids=true | all-gather | bytes 983040 | tf_op jit(solution)/shard_map/all_gather | solution.py:103
  90.5 17.9 %all-gather.13.cloned.1.call-done = bf16[4,200,768]{2,0,1:T(4,128)(2,1)} async-done(((bf16[4,25,768]{2,0,1:T(4,128)(2,1)}), bf16[4,200,768]{2,0,1:T(4,128)(2,1)}) %all-gather.13.cloned.1.call-update) | async-done | bytes 1228816 | tf_op jit(solution)/shard_map/all_gather | solution.py:77
  111.5 21.3 %all-gather.11.cloned.1.call-done = bf16[8,128,768]{2,1,0:T(8,128)(2,1)} async-done(((bf16[4,128,768]{2,1,0:T(8,128)(2,1)}), bf16[8,128,768]{2,1,0:T(8,128)(2,1)}) %all-gather.11.cloned.1.call-update) | async-done | bytes 1572880 | tf_op jit(solution)/shard_map/all_gather | solution.py:104
  135.6 3.2 %fusion.126 = (bf16[384]{0:T(512)(128)(2,1)S(1)}, bf16[512,384]{1,0:T(8,128)(2,1)}, f32[512,384]{1,0:T(8,128)}) fusion(f32[512,384]{1,0:T(8,128)S(1)} %convolution_add_fusion, bf16[512,768]{1,0:T(8,128)(2,1)S(1)} %bitcast.105, bf16[384,768]{1,0:T(8,128)(2,1)S(1)} %reshape.296), kind=kOutput, calls=%fused_computation.393 | convolution fusion | flops 316341888 | bytes 3343104 | tf_op jit(solution)/shard_map/dot_general | solution.py:114
  141.0 2.6 convolution_convert_fusion
  143.5 3.7 %all-to-all-start.1 = ((bf16[8,64,768]{2,1,0:T(8,128)(2,1)}), bf16[8,64,768]{2,1,0:T(8,128)(2,1)S(1)}, u32[]{:S(2)}, u32[]{:S(2)}) async-start(bf16[8,64,768]{2,1,0:T(8,128)(2,1)} %bitcast.14), calls=%async_computation.1 | async-start | bytes 1572864 | tf_op jit(solution)/shard_map/all_to_all | solution.py:130
  151.6 7.9 %all-to-all-done.1 = bf16[8,64,768]{2,1,0:T(8,128)(2,1)S(1)} async-done(((bf16[8,64,768]{2,1,0:T(8,128)(2,1)}), bf16[8,64,768]{2,1,0:T(8,128)(2,1)S(1)}, u32[]{:S(2)}, u32[]{:S(2)}) %all-to-all-start.1) | async-done | bytes 786464 | tf_op jit(solution)/shard_map/all_to_all | solution.py:130
  160.9 12.3 %all-to-all-start.2 = ((bf16[32,24,70]{2,1,0:T(8,128)(2,1)}), bf16[32,24,70]{2,1,0:T(8,128)(2,1)S(1)}, u32[]{:S(2)}, u32[]{:S(2)}) async-start(bf16[32,24,70]{2,1,0:T(8,128)(2,1)} %bitcast.17), calls=%async_computation.2 | async-start | bytes 393216 | tf_op jit(solution)/shard_map/all_to_all | solution.py:141
  173.6 14.0 %all-to-all-done.2 = bf16[32,24,70]{2,1,0:T(8,128)(2,1)S(1)} async-done(((bf16[32,24,70]{2,1,0:T(8,128)(2,1)}), bf16[32,24,70]{2,1,0:T(8,128)(2,1)S(1)}, u32[]{:S(2)}, u32[]{:S(2)}) %all-to-all-start.2) | async-done | bytes 107552 | tf_op jit(solution)/shard_map/all_to_all | solution.py:141
  189.8 7.8 %all-to-all-start.3 = ((bf16[8,25,768]{2,1,0:T(8,128)(2,1)}), bf16[8,25,768]{2,1,0:T(8,128)(2,1)S(1)}, u32[]{:S(2)}, u32[]{:S(2)}) async-start(bf16[8,25,768]{2,1,0:T(8,128)(2,1)} %bitcast.111), calls=%async_computation.4 | async-start | bytes 786432 | tf_op jit(solution)/shard_map/all_to_all | solution.py:146
  206.1 3.9 %collective-permute-start.2 = (bf16[24,3,256]{2,1,0:T(4,128)(2,1)S(1)}, bf16[24,3,256]{2,1,0:T(4,128)(2,1)S(1)}, u32[]{:S(2)}, u32[]{:S(2)}) collective-permute-start(bf16[24,3,256]{2,1,0:T(4,128)(2,1)S(1)} %get-tuple-element.158), channel_id=1, source_target_pairs={{0,32},{32,64},{64,96},{96,128},{128,160},{160,192},{192,224},{224... | collective-permute-start | bytes 110600 | tf_op jit(solution)/shard_map/ppermute | solution.py:20
  212.0 3.7 %collective-permute-done.3 = bf16[24,3,256]{2,1,0:T(4,128)(2,1)S(1)} collective-permute-done((bf16[24,3,256]{2,1,0:T(4,128)(2,1)S(1)}, bf16[24,3,256]{2,1,0:T(4,128)(2,1)S(1)}, u32[]{:S(2)}, u32[]{:S(2)}) %collective-permute-start.3) | collective-permute-done | bytes 36896 | tf_op jit(solution)/shard_map/ppermute | solution.py:22
  215.9 5.3 %collective-permute-start.4 = (bf16[29,768]{1,0:T(8,128)(2,1)S(1)}, bf16[29,768]{1,0:T(8,128)(2,1)S(1)}, u32[]{:S(2)}, u32[]{:S(2)}) collective-permute-start(bf16[29,768]{1,0:T(8,128)(2,1)S(1)} %pad_maximum_fusion.1), channel_id=1, source_target_pairs={{0,256},{256,0},{1,257},{257,1},{2,258},{258,2},{3,259},{259,3},{4... | collective-permute-start | bytes 133640 | tf_op jit(solution)/shard_map/ppermute | solution.py:175
  221.5 4.5 %convert_add_fusion = f32[24,8,256]{2,1,0:T(8,128)} fusion(bf16[24,8,256]{2,1,0:T(8,128)(2,1)S(1)} %copy-done.2, f32[24,14,256]{2,1,0:T(8,128)S(1)} %maximum_convert_fusion.1, f32[24]{0:T(128)S(1)} %copy-done.70, f32[24]{0:T(128)S(1)} %copy-done.72, f32[24]{0:T(128)S(1)} %get-tuple-element.96, f32[24]{0:T(128)S(1)} %get-tuple-element.97, ...), kind=kLoop, calls=%fused_computation.122 | loop fusion | flops 4866048 | bytes 2089472 | tf_op jit(solution)/shard_map/add | solution.py:163
  226.1 3.7 %collective-permute-done.4 = bf16[29,768]{1,0:T(8,128)(2,1)S(1)} collective-permute-done((bf16[29,768]{1,0:T(8,128)(2,1)S(1)}, bf16[29,768]{1,0:T(8,128)(2,1)S(1)}, u32[]{:S(2)}, u32[]{:S(2)}) %collective-permute-start.4) | collective-permute-done | bytes 44576 | tf_op jit(solution)/shard_map/ppermute | solution.py:175
  229.9 8.3 %all-gather.7 = bf16[2,29,768]{2,1,0:T(8,128)(2,1)S(1)} all-gather(bf16[1,29,768]{2,1,0:T(8,128)(2,1)S(1)} %maximum_bitcast_fusion.2), channel_id=6, replica_groups=mesh['zh'=2,'x'=4,'c'=2,'zl'=8,'y'=4] {'c'}, dimensions={0}, use_global_device_ids=true | all-gather | bytes 133632 | tf_op jit(solution)/shard_map/all_gather | solution.py:181
  238.2 17.2 %all-gather.5 = bf16[8,29,768]{2,1,0:T(8,128)(2,1)S(1)} all-gather(bf16[2,29,768]{2,1,0:T(8,128)(2,1)S(1)} %all-gather.7), channel_id=7, replica_groups=mesh['zh'=2,'x'=4,'c'=2,'zl'=8,'y'=4] {'x'}, dimensions={0}, use_global_device_ids=true | all-gather | bytes 445440 | tf_op jit(solution)/shard_map/all_gather | solution.py:182
  (307 shorter events, 38.8 us)
Async XLA Ops:
  7.2 31.5 %copy-start.8 = (bf16[24,8,256]{2,1,0:T(8,128)(2,1)S(1)}, bf16[24,8,256]{2,1,0:T(8,128)(2,1)}, u32[]{:S(2)}) copy-start(bf16[24,8,256]{2,1,0:T(8,128)(2,1)} %param.16) | copy-start | bytes 294916
  7.2 30.0 %copy-start = (f32[24,49]{1,0:T(8,128)S(1)}, f32[24,49]{1,0:T(8,128)}, u32[]{:S(2)}) copy-start(f32[24,49]{1,0:T(8,128)} %param.19) | copy-start | bytes 14116
  7.2 31.2 %copy-start.2 = (bf16[24,8,256]{2,1,0:T(8,128)(2,1)S(1)}, bf16[24,8,256]{2,1,0:T(8,128)(2,1)}, u32[]{:S(2)}) copy-start(bf16[24,8,256]{2,1,0:T(8,128)(2,1)} %param.17) | copy-start | bytes 294916
  7.2 31.5 %copy-start.10 = (f32[8]{0:T(128)S(1)}, f32[8]{0:T(128)}, u32[]{:S(2)}) copy-start(f32[8]{0:T(128)} %param.18) | copy-start | bytes 100
  7.2 31.5 %copy-start.76 = (f32[24]{0:T(128)S(1)}, f32[24]{0:T(128)}, u32[]{:S(2)}) copy-start(f32[24]{0:T(128)} %param.20) | copy-start | bytes 292
  7.2 101.1 %all-gather.13.cloned.1.call-start = ((), (), s32[]{:S(2)}) async-start(), calls=%async_computation.7 | async-start | bytes 1382400 | tf_op jit(solution)/shard_map/all_gather | solution.py:77
  8.3 30.3 %collective-permute-start = (bf16[24,3,256]{2,1,0:T(4,128)(2,1)S(1)}, bf16[24,3,256]{2,1,0:T(4,128)(2,1)S(1)}, u32[]{:S(2)}, u32[]{:S(2)}) collective-permute-start(bf16[24,3,256]{2,1,0:T(4,128)(2,1)S(1)} %get-tuple-element.160), channel_id=1, source_target_pairs={{0,32},{32,64},{64,96},{96,128},{128,160},{160,192},{192,224},{224... | collective-permute-start | bytes 110600 | tf_op jit(solution)/shard_map/ppermute | solution.py:20
  12.8 25.8 %collective-permute-start.1 = (bf16[24,3,256]{2,1,0:T(4,128)(2,1)S(1)}, bf16[24,3,256]{2,1,0:T(4,128)(2,1)S(1)}, u32[]{:S(2)}, u32[]{:S(2)}) collective-permute-start(bf16[24,3,256]{2,1,0:T(4,128)(2,1)S(1)} %get-tuple-element.161), channel_id=1, source_target_pairs={{32,0},{64,32},{96,64},{128,96},{160,128},{192,160},{224,192},{256... | collective-permute-start | bytes 110600 | tf_op jit(solution)/shard_map/ppermute | solution.py:22
  35.2 97.6 %all-gather.11.cloned.1.call-start = ((), (), s32[]{:S(2)}) async-start(), calls=%async_computation.6 | async-start | bytes 2359296 | tf_op jit(solution)/shard_map/all_gather | solution.py:104
  42.7 25.9 %copy-start.9 = (f32[768]{0:T(1024)S(1)}, f32[768]{0:T(1024)}, u32[]{:S(2)}) copy-start(f32[768]{0:T(1024)} %param.21) | copy-start | bytes 9220
  42.7 25.9 %copy-start.73 = (f32[768]{0:T(1024)S(1)}, f32[768]{0:T(1024)}, u32[]{:S(2)}) copy-start(f32[768]{0:T(1024)} %param.22) | copy-start | bytes 9220
  68.3 22.2 %copy-start.74 = (bf16[768]{0:T(1024)(128)(2,1)S(1)}, bf16[768]{0:T(1024)(128)(2,1)}, u32[]{:S(2)}) copy-start(bf16[768]{0:T(1024)(128)(2,1)} %param.27) | copy-start | bytes 4612
  143.5 15.9 %all-to-all-start.1 = ((bf16[8,64,768]{2,1,0:T(8,128)(2,1)}), bf16[8,64,768]{2,1,0:T(8,128)(2,1)S(1)}, u32[]{:S(2)}, u32[]{:S(2)}) async-start(bf16[8,64,768]{2,1,0:T(8,128)(2,1)} %bitcast.14), calls=%async_computation.1 | async-start | bytes 1572864 | tf_op jit(solution)/shard_map/all_to_all | solution.py:130
  147.2 42.6 %reduce-scatter.2.cloned.1.call-start = ((), (), s32[]{:S(2)}) async-start(), calls=%async_computation.5 | async-start | bytes 1966080 | tf_op jit(solution)/shard_map/reduce_scatter | solution.py:128
  160.9 26.7 %all-to-all-start.2 = ((bf16[32,24,70]{2,1,0:T(8,128)(2,1)}), bf16[32,24,70]{2,1,0:T(8,128)(2,1)S(1)}, u32[]{:S(2)}, u32[]{:S(2)}) async-start(bf16[32,24,70]{2,1,0:T(8,128)(2,1)} %bitcast.17), calls=%async_computation.2 | async-start | bytes 393216 | tf_op jit(solution)/shard_map/all_to_all | solution.py:141
  189.8 26.0 %all-to-all-start.3 = ((bf16[8,25,768]{2,1,0:T(8,128)(2,1)}), bf16[8,25,768]{2,1,0:T(8,128)(2,1)S(1)}, u32[]{:S(2)}, u32[]{:S(2)}) async-start(bf16[8,25,768]{2,1,0:T(8,128)(2,1)} %bitcast.111), calls=%async_computation.4 | async-start | bytes 786432 | tf_op jit(solution)/shard_map/all_to_all | solution.py:146
  201.6 19.7 %copy-start.12 = (f32[24]{0:T(128)S(1)}, f32[24]{0:T(128)}, u32[]{:S(2)}) copy-start(f32[24]{0:T(128)} %copy-done.11) | copy-start | bytes 292
  201.6 19.7 %copy-start.14 = (f32[24]{0:T(128)S(1)}, f32[24]{0:T(128)}, u32[]{:S(2)}) copy-start(f32[24]{0:T(128)} %copy-done.13) | copy-start | bytes 292
  201.6 19.7 %copy-start.16 = (f32[24]{0:T(128)S(1)}, f32[24]{0:T(128)}, u32[]{:S(2)}) copy-start(f32[24]{0:T(128)} %copy-done.15) | copy-start | bytes 292
  201.6 19.7 %copy-start.18 = (f32[24]{0:T(128)S(1)}, f32[24]{0:T(128)}, u32[]{:S(2)}) copy-start(f32[24]{0:T(128)} %copy-done.17) | copy-start | bytes 292
  201.6 19.7 %copy-start.20 = (f32[24]{0:T(128)S(1)}, f32[24]{0:T(128)}, u32[]{:S(2)}) copy-start(f32[24]{0:T(128)} %copy-done.19) | copy-start | bytes 292
  206.1 5.8 %collective-permute-start.2 = (bf16[24,3,256]{2,1,0:T(4,128)(2,1)S(1)}, bf16[24,3,256]{2,1,0:T(4,128)(2,1)S(1)}, u32[]{:S(2)}, u32[]{:S(2)}) collective-permute-start(bf16[24,3,256]{2,1,0:T(4,128)(2,1)S(1)} %get-tuple-element.158), channel_id=1, source_target_pairs={{0,32},{32,64},{64,96},{96,128},{128,160},{160,192},{192,224},{224... | collective-permute-start | bytes 110600 | tf_op jit(solution)/shard_map/ppermute | solution.py:20
  210.0 5.7 %collective-permute-start.3 = (bf16[24,3,256]{2,1,0:T(4,128)(2,1)S(1)}, bf16[24,3,256]{2,1,0:T(4,128)(2,1)S(1)}, u32[]{:S(2)}, u32[]{:S(2)}) collective-permute-start(bf16[24,3,256]{2,1,0:T(4,128)(2,1)S(1)} %get-tuple-element.159), channel_id=1, source_target_pairs={{32,0},{64,32},{96,64},{128,96},{160,128},{192,160},{224,192},{256... | collective-permute-start | bytes 110600 | tf_op jit(solution)/shard_map/ppermute | solution.py:22
  215.9 13.8 %collective-permute-start.4 = (bf16[29,768]{1,0:T(8,128)(2,1)S(1)}, bf16[29,768]{1,0:T(8,128)(2,1)S(1)}, u32[]{:S(2)}, u32[]{:S(2)}) collective-permute-start(bf16[29,768]{1,0:T(8,128)(2,1)S(1)} %pad_maximum_fusion.1), channel_id=1, source_target_pairs={{0,256},{256,0},{1,257},{257,1},{2,258},{258,2},{3,259},{259,3},{4... | collective-permute-start | bytes 133640 | tf_op jit(solution)/shard_map/ppermute | solution.py:175
  (64 other events, 689.5 us)
Sparse Core Ops, SparseCore 0:
  35.3 72.9 all-gather.12
  110.5 22.2 all-gather.10
  151.7 35.2 reduce-scatter.1

commit v2 on v1

--- a/solution.py
+++ b/solution.py
@@ -5,6 +5,7 @@
 
 LAT = ("zh", "x", "c")
 CHAN = ("zl", "y")
+SLOT = 16
 GROUP = 8
 F32 = jnp.float32
 BF = jnp.bfloat16
@@ -32,6 +33,70 @@
 def two_parts(value):
     high = lax.reduce_precision(value, 8, 7)
     return high.astype(BF), (value - high).astype(BF)
+
+
+def to_all(block, axis):
+    count = lax.axis_size(axis)
+    return lax.all_to_all(jnp.broadcast_to(block[None], (count,) + block.shape), axis, 0, 0, tiled=True)
+
+
+def exchange(blocks):
+    return lax.all_to_all(blocks, CHAN, 0, 0, tiled=True)
+
+
+def with_other_core(block):
+    return jnp.concatenate([block, lax.ppermute(block, "c", [(0, 1), (1, 0)])], 0)
+
+
+def pieces(cells):
+    half = cells.shape[0] // 2
+    return jnp.concatenate([cells[:half], cells[half:]], 2).transpose(1, 0, 2)
+
+
+def halves(owners, slot, per_owner):
+    shape = (owners * slot, owners * per_owner)
+    row = lax.broadcasted_iota(jnp.int32, shape, 0)
+    chan = lax.broadcasted_iota(jnp.int32, shape, 1)
+    half = per_owner // 2
+    inside = row % slot < half
+    first = (row // slot) * per_owner + row % slot
+    return [(inside & (chan == first + shift)).astype(BF) for shift in (0, half)]
+
+
+def flipped(block, bit):
+    return lax.ppermute(block, "zl", [(i, i ^ bit) for i in range(lax.axis_size("zl"))])
+
+
+def gather_chan(block):
+    parts = block[None]
+    for bit in (4, 2, 1):
+        parts = jnp.concatenate([parts, flipped(parts, bit)], 0)
+    count = lax.axis_size("y")
+    ahead = [lax.ppermute(parts, "y", [((i + k) % count, i) for i in range(count)]) for k in range(1, count)]
+    return jnp.concatenate([parts] + ahead, 0)
+
+
+def scatter_chan(blocks):
+    count = lax.axis_size("y")
+    parts = blocks.reshape((count, -1) + blocks.shape[1:])
+    total = parts[0].astype(F32)
+    for k in range(1, count):
+        total = total + lax.ppermute(parts[k], "y", [(i, (i + k) % count) for i in range(count)]).astype(F32)
+    for bit in (1, 2, 4):
+        keep = total.shape[0] // 2
+        total = total[:keep] + flipped(total[keep:].astype(BF), bit).astype(F32)
+    return total[0]
+
+
+def channels_last(blocks, picks):
+    flat = blocks.reshape(-1, blocks.shape[2])
+    piece = flat.shape[1] // 2
+    over_first = (((0,), (0,)), ((), ()))
+    parts = [
+        lax.dot_general(flat[:, i * piece : (i + 1) * piece], pick, over_first, preferred_element_type=F32)
+        for i, pick in enumerate(picks)
+    ]
+    return (parts[0] + parts[1]).astype(BF)
 
 
 def per_device(
@@ -62,9 +127,8 @@
     gamma_f = layer_scale.astype(F32)
     gamma_own = lax.dynamic_slice_in_dim(gamma_f, owner * cdev, cdev)
 
-    bias_high, bias_low = two_parts(lax.dynamic_slice_in_dim(b_in, member * part, part))
-    bias_row = jnp.zeros((1, chans), BF)
-    bias_row = bias_row.at[0, :part].set(bias_high).at[0, part : 2 * part].set(bias_low)
+    bias_parts = two_parts(lax.dynamic_slice_in_dim(b_in, member * part, part))
+    bias_row = jnp.concatenate(bias_parts + (jnp.zeros((chans - 2 * part,), BF),))[None]
     mine = jnp.concatenate(
         [
             lax.dynamic_slice_in_dim(w_in, member * part, part),
@@ -73,12 +137,11 @@
         ],
         0,
     )
-    shards = lax.all_gather(mine, "y", axis=0)
-    shards = lax.all_gather(shards, "zl", axis=1)
-    wi = shards[:, :, :part].reshape(hid, chans)
-    wo = shards[:, :, part : 2 * part].reshape(hid, chans)
-    bias_rows = shards[:, :, 2 * part].astype(F32)
-    bi = (bias_rows[..., :part] + bias_rows[..., part : 2 * part]).reshape(hid)
+    shards = gather_chan(mine)
+    wi = shards[:, :part].reshape(hid, chans)
+    wo = shards[:, part : 2 * part].reshape(hid, chans)
+    bias_rows = shards[:, 2 * part].astype(F32)
+    bi = (bias_rows[:, :part] + bias_rows[:, part : 2 * part]).reshape(hid)
 
     xpad = jnp.pad(extended(block_input, 3).astype(F32), ((0, 0), (0, 0), (3, 3)))
     conv = jnp.zeros((cdev, rows, width), F32)
@@ -88,22 +151,20 @@
     h = (conv_bias[:, None, None] + metric[None, :, None] * conv).astype(BF)
 
     both = jnp.concatenate(
-        [h.reshape(cdev, nchan, piece), out_grad.reshape(cdev, nchan, piece)], 2
-    ).transpose(1, 0, 2)
-    both = lax.all_to_all(both, CHAN, 0, 0, tiled=True).reshape(chans, 2 * piece).T
-    hf = both[:piece].astype(F32)
-    dy_piece = both[piece:]
+        [pieces(h.reshape(cdev, nchan, piece)), pieces(out_grad.reshape(cdev, nchan, piece))], 1
+    )
+    both = exchange(both)
+    hf = channels_last(both[:, : cdev // 2], halves(nchan, cdev // 2, cdev)).astype(F32)
+    dy_piece = channels_last(both[:, cdev // 2 :], halves(nchan, cdev // 2, cdev))
     mean = jnp.sum(hf, 1, keepdims=True) / chans
     var = jnp.sum(hf * hf, 1, keepdims=True) / chans - mean * mean
     rstd = 1.0 / jnp.sqrt(var + 1e-06)
     nhat = (hf - mean) * rstd
     n_piece = (nhat * ln_gain + ln_bias).astype(BF)
 
-    pair = jnp.concatenate([n_piece, dy_piece], 0)
-    pair = lax.all_gather(pair, "x", axis=0)
-    pair = lax.all_gather(pair, "c", axis=0)
-    n = pair[:, :, :piece].reshape(GROUP * piece, chans)
-    dy = pair[:, :, piece:].reshape(GROUP * piece, chans)
+    pair = with_other_core(to_all(jnp.concatenate([n_piece, dy_piece], 0), "x"))
+    n = pair[:, :piece].reshape(GROUP * piece, chans)
+    dy = pair[:, piece:].reshape(GROUP * piece, chans)
 
     over_last = (((1,), (1,)), ((), ()))
     over_first = (((0,), (0,)), ((), ()))
@@ -113,19 +174,21 @@
     dmlp = (gamma_f * dy.astype(F32)).astype(BF)
     grad_g = lax.dot_general(dmlp, wo, over_last, preferred_element_type=F32)
     dpre = back(grad_g)[0].astype(BF)
-    dn_part = jnp.dot(dpre, wi, preferred_element_type=F32).astype(BF)
+    turned = jnp.roll(dpre, dpre.shape[0] // 2, 0)
+    ordered = jnp.where(lax.axis_index("c") == 0, dpre, turned)
+    dn_part = jnp.dot(ordered, wi, preferred_element_type=F32).astype(BF)
     dw_in = lax.dot_general(dpre, n, over_first, preferred_element_type=F32)
     proj = lax.dot_general(g_b, dy, over_first, preferred_element_type=F32)
     db_in = jnp.sum(dpre.astype(F32), 0)
     gam_part = jnp.sum(wo.astype(F32) * proj, 0)
     dw_out = proj * gamma_f
 
-    grid = (ny, nz, part)
-    db_row = jnp.pad(db_in.astype(BF).reshape(grid)[:, :, None, :], ((0, 0), (0, 0), (0, 0), (0, chans - part)))
-    dws = jnp.concatenate(
-        [dw_in.astype(BF).reshape(grid + (chans,)), dw_out.astype(BF).reshape(grid + (chans,)), db_row], 2
-    )
-    dws = lax.psum_scatter(dws, "y", scatter_dimension=0, tiled=False)
+    db_row = jnp.pad(db_in.astype(BF).reshape(nchan, 1, part), ((0, 0), (0, 0), (0, chans - part)))
+    dws = scatter_chan(
+        jnp.concatenate(
+            [dw_in.astype(BF).reshape(nchan, part, chans), dw_out.astype(BF).reshape(nchan, part, chans), db_row], 1
+        )
+    )
 
     dn = lax.all_to_all(dn_part.reshape(GROUP, piece, chans), ("c", "x"), 0, 0, tiled=True)
     dn = jnp.sum(dn.astype(F32), 0)
@@ -133,18 +196,18 @@
     s1 = jnp.sum(dnhat, 1, keepdims=True) / chans
     s2 = jnp.sum(dnhat * nhat, 1, keepdims=True) / chans
     dh = rstd * (dnhat - s1 - nhat * s2)
-    extra = []
-    for value in (jnp.sum(dn * nhat, 0), jnp.sum(dn, 0), gam_part):
-        extra += list(two_parts(value))
-    payload = jnp.concatenate([dh.astype(BF), jnp.stack(extra, 0)], 0)
-    payload = payload.T.reshape(nchan, cdev, piece + 6)
-    payload = lax.all_to_all(payload, CHAN, 0, 0, tiled=True)
-    dh3 = payload[:, :, :piece].transpose(1, 0, 2).reshape(cdev, rows, width).astype(F32)
-    sums = jnp.sum(payload[:, :, piece:].astype(F32), 0)
-    sums = sums[:, 0::2] + sums[:, 1::2]
-
-    dws = lax.all_to_all(dws, "zl", 0, 0, tiled=True)
-    dws = jnp.sum(dws.astype(F32), 0)
+    extra = jnp.stack([jnp.sum(dn * nhat, 0), jnp.sum(dn, 0), gam_part], 0)
+    extra = extra.reshape(3, nchan, cdev).transpose(1, 0, 2).reshape(nchan, 3 * cdev)
+    extra = jnp.stack(two_parts(jnp.pad(extra, ((0, 0), (0, 2 * piece - 3 * cdev)))), 1)
+    picks = halves(nchan, SLOT, cdev)
+    payload = jnp.concatenate(
+        [lax.dot_general(pick, dh.astype(BF), over_last, preferred_element_type=F32) for pick in picks], 1
+    ).astype(BF).reshape(nchan, SLOT, 2 * piece)
+    half = cdev // 2
+    payload = exchange(jnp.concatenate([payload[:, :half], extra, payload[:, half + 2 :]], 1))
+    dh3 = jnp.concatenate([payload[:, :half, :piece], payload[:, :half, piece:]], 1)
+    dh3 = dh3.transpose(1, 0, 2).reshape(cdev, rows, width).astype(F32)
+    sums = jnp.sum(payload[:, half : half + 2].astype(F32), (0, 1))[: 3 * cdev].reshape(3, cdev).T
 
     dconv = metric[None, :, None] * dh3
     taps = []
@@ -178,8 +241,7 @@
     small = small + other[wrows : wrows + small_rows] + other[wrows + small_rows :]
     high, low = two_parts(small)
     mine = jnp.concatenate([dws.astype(BF), high, low], 0)
-    gathered = lax.all_gather(mine, "c", axis=0)
-    gathered = lax.all_gather(gathered, "x", axis=0).reshape(GROUP, -1, chans).astype(F32)
+    gathered = to_all(mine, ("x", "c")).astype(F32)
     grad_w_in = gathered[:, :part].reshape(hdev, chans)
     grad_w_out = gathered[:, part : 2 * part].reshape(hdev, chans)
     grad_b_in = gathered[:, 2 * part, :part].reshape(hdev)

time: 268 us -> 244 us (0.910)
  starting transfers between devices: 45.1 us -> 130 us
  blocking collectives: 81.7 us -> 0 us
  waiting for transfers between devices: 68.6 us -> 41.7 us
  between operations: 15.4 us -> 3.05 us
  local copies, waits for them, and re-layouts: 22.5 us -> 30 us
  matrix products: 9.62 us -> 13.3 us
    all_gather x4 -> x0, blocking collectives: 56.8 us -> none  [the longest x1 21.7 us: per_device(): pair = lax.all_gather(pair, 'x', axis=0)]
    ppermute x0 -> x13, starting transfers between devices: none -> 49.2 us  [the longest x6 26.9 us: flipped(): lax.ppermute(block, 'zl', [(i, i ^ bit) for i in range(lax.axis_size('zl'...]
    all_gather x2 -> x0, waiting for transfers between devices: 39.2 us -> none  [the longest x1 21.3 us: per_device(): pair = lax.all_gather(pair, 'c', axis=0)]
    ppermute x0 -> x13, waiting for transfers between devices: none -> 38 us  [the longest x6 21.5 us: flipped(): lax.ppermute(block, 'zl', [(i, i ^ bit) for i in range(lax.axis_size('zl'...]
    all_to_all x1 -> x0, blocking collectives: 24.9 us -> none  [per_device(): lax.all_to_all(both, CHAN, 0, 0, tiled=True).reshape(chans, 2 * piece)]
    all_to_all x2 -> x4, starting transfers between devices: 20.1 us -> 40.8 us  [the longest x2 20.6 us: to_all(): lax.all_to_all(jnp.broadcast_to(block[None], (count,) + block.shape), axi...]
    all_to_all x2 -> x4, waiting for transfers between devices: 14 us -> 2.37 us  [the longest x2 2.36 us: to_all(): lax.all_to_all(jnp.broadcast_to(block[None], (count,) + block.shape), axi...]
    ppermute x1, starting transfers between devices: 5.28 us -> 14.5 us  [per_device(): other = lax.ppermute(mine, 'zh', swap).astype(F32)]
  transfers between devices with their start and end apart: 11 -> 23, of which waited for: 6 -> 10; matrix products, arithmetic and copies ran while one was open for 15% -> 16% of each run, Pallas kernels for 0% -> 0%
where the time goes in v2:
time: 244 us; the launch traced here: 242 us
  starting transfers between devices  130 us (53%)
  waiting for transfers between devices  41.7 us (17%)
  local copies, waits for them, and re-layouts  30 us (12%)
  other arithmetic  23.7 us (10%)
  matrix products  13.3 us (5%)
  between operations  3.05 us (1%)
    ppermute x6, starting transfers between devices, flipped(): lax.ppermute(block, 'zl', [(i, i ^ bit) for i in range(lax.axis_size('zl'...  26.9 us
    ppermute x6, waiting for transfers between devices, flipped(): lax.ppermute(block, 'zl', [(i, i ^ bit) for i in range(lax.axis_size('zl'...  21.5 us
    all_to_all x2, starting transfers between devices, to_all(): lax.all_to_all(jnp.broadcast_to(block[None], (count,) + block.shape), axi...  20.6 us
    all_to_all x2, starting transfers between devices, exchange(): return lax.all_to_all(blocks, CHAN, 0, 0, tiled=True)  20.2 us
    ppermute x1, starting transfers between devices, per_device(): other = lax.ppermute(mine, 'zh', swap).astype(F32)  14.5 us
    ppermute x2, starting transfers between devices, extended(): lax.ppermute(tail, LAT, [(i, i + 1) for i in range(ends)])  13 us
    ppermute x3, starting transfers between devices, gather_chan(): lax.ppermute(parts, 'y', [((i + k) % count, i) for i in range(count)])  10.6 us
    ppermute x3, waiting for transfers between devices, gather_chan(): lax.ppermute(parts, 'y', [((i + k) % count, i) for i in range(count)])  8.53 us
  transfers between devices with their start and end apart: 23, of which 10 were waited for; matrix products, arithmetic and copies ran while one was open for 16% of the time, Pallas kernels for 0%

profile of v2, /device:TPU:1, one launch (start us, length us, event | category | flops | bytes accessed | tf_op | source)
XLA Modules:
  0.0 241.8 jit_solution(3594968075755254626)
XLA Ops:
  1.7 4.5 %collective-permute-start = (bf16[24,3,256]{2,1,0:T(4,128)(2,1)S(1)}, bf16[24,3,256]{2,1,0:T(4,128)(2,1)S(1)}, u32[]{:S(2)}, u32[]{:S(2)}) collective-permute-start(bf16[24,3,256]{2,1,0:T(4,128)(2,1)S(1)} %get-tuple-element.149), channel_id=1, source_target_pairs={{0,32},{32,64},{64,96},{96,128},{128,160},{160,192},{192,224},{224... | collective-permute-start | bytes 110600 | tf_op jit(solution)/shard_map/ppermute | solution.py:21
  6.2 5.6 %collective-permute-start.1 = (bf16[24,3,256]{2,1,0:T(4,128)(2,1)S(1)}, bf16[24,3,256]{2,1,0:T(4,128)(2,1)S(1)}, u32[]{:S(2)}, u32[]{:S(2)}) collective-permute-start(bf16[24,3,256]{2,1,0:T(4,128)(2,1)S(1)} %get-tuple-element.150), channel_id=1, source_target_pairs={{32,0},{64,32},{96,64},{128,96},{160,128},{192,160},{224,192},{256... | collective-permute-start | bytes 110600 | tf_op jit(solution)/shard_map/ppermute | solution.py:23
  13.5 5.2 %collective-permute-start.3 = (bf16[1,25,768]{2,1,0:T(8,128)(2,1)S(1)}, bf16[1,25,768]{2,1,0:T(8,128)(2,1)S(1)}, u32[]{:S(2)}, u32[]{:S(2)}) collective-permute-start(bf16[1,25,768]{2,1,0:T(8,128)(2,1)S(1)} %get-tuple-element.126), channel_id=1, source_target_pairs={{0,16},{4,20},{8,24},{12,28},{16,0},{20,4},{24,8},{28,12},{1,17},{... | collective-permute-start | bytes 115208 | tf_op jit(solution)/shard_map/ppermute | solution.py:67
  26.3 4.8 %add_convert_fusion.2 = bf16[24,8,256]{2,1,0:T(8,128)(2,1)S(1)} fusion(f32[24,14,256]{2,1,0:T(8,128)S(1)} %maximum_convert_fusion, f32[24]{0:T(128)S(1)} %get-tuple-element.118, f32[24]{0:T(128)S(1)} %get-tuple-element.119, f32[24]{0:T(128)S(1)} %get-tuple-element.72, f32[24]{0:T(128)S(1)} %get-tuple-element.73, f32[24]{0:T(128)S(1)} %get-tuple-element.74, ...), kind=kLoop, calls=%fused_computation.326 | loop fusion | flops 4915200 | bytes 1889728 | tf_op jit(solution)/shard_map/convert_element_type | solution.py:151
  32.8 8.6 %all-to-all-start = ((bf16[32,24,128]{2,1,0:T(8,128)(2,1)}), bf16[32,24,128]{2,1,0:T(8,128)(2,1)S(1)}, u32[]{:S(2)}, u32[]{:S(2)}) async-start(bf16[32,24,128]{2,1,0:T(8,128)(2,1)} %pad_maximum_fusion.1), calls=%async_computation | async-start | bytes 393216 | tf_op jit(solution)/shard_map/all_to_all | solution.py:44
  42.0 4.0 %collective-permute-start.4 = (bf16[2,25,768]{2,1,0:T(8,128)(2,1)S(1)}, bf16[2,25,768]{2,1,0:T(8,128)(2,1)S(1)}, u32[]{:S(2)}, u32[]{:S(2)}) collective-permute-start(bf16[2,25,768]{2,1,0:T(8,128)(2,1)S(1)} %pad_maximum_fusion.5), channel_id=1, source_target_pairs={{0,8},{4,12},{8,0},{12,4},{16,24},{20,28},{24,16},{28,20},{1,9},{5... | collective-permute-start | bytes 230408 | tf_op jit(solution)/shard_map/ppermute | solution.py:67
  46.1 7.0 %collective-permute-done.4 = bf16[2,25,768]{2,1,0:T(8,128)(2,1)S(1)} collective-permute-done((bf16[2,25,768]{2,1,0:T(8,128)(2,1)S(1)}, bf16[2,25,768]{2,1,0:T(8,128)(2,1)S(1)}, u32[]{:S(2)}, u32[]{:S(2)}) %collective-permute-start.4) | collective-permute-done | bytes 76832 | tf_op jit(solution)/shard_map/ppermute | solution.py:67
  53.1 4.0 %collective-permute-start.5 = (bf16[4,25,768]{2,1,0:T(8,128)(2,1)S(1)}, bf16[4,25,768]{2,1,0:T(8,128)(2,1)S(1)}, u32[]{:S(2)}, u32[]{:S(2)}) collective-permute-start(bf16[4,25,768]{2,1,0:T(8,128)(2,1)S(1)} %pad_maximum_fusion.3), channel_id=1, source_target_pairs={{0,4},{4,0},{8,12},{12,8},{16,20},{20,16},{24,28},{28,24},{1,5},{5... | collective-permute-start | bytes 460808 | tf_op jit(solution)/shard_map/ppermute | solution.py:67
  57.2 5.1 %collective-permute-done.5 = bf16[4,25,768]{2,1,0:T(8,128)(2,1)S(1)} collective-permute-done((bf16[4,25,768]{2,1,0:T(8,128)(2,1)S(1)}, bf16[4,25,768]{2,1,0:T(8,128)(2,1)S(1)}, u32[]{:S(2)}, u32[]{:S(2)}) %collective-permute-start.5) | collective-permute-done | bytes 153632 | tf_op jit(solution)/shard_map/ppermute | solution.py:67
  62.3 5.1 %collective-permute-start.7 = (bf16[8,25,768]{2,1,0:T(8,128)(2,1)S(1)}, bf16[8,25,768]{2,1,0:T(8,128)(2,1)}, u32[]{:S(2)}, u32[]{:S(2)}) collective-permute-start(bf16[8,25,768]{2,1,0:T(8,128)(2,1)S(1)} %pad_maximum_fusion), channel_id=1, source_target_pairs={{2,0},{3,1},{0,2},{1,3},{6,4},{7,5},{4,6},{5,7},{10,8},{11,9},{8,1... | collective-permute-start | bytes 921608 | tf_op jit(solution)/shard_map/ppermute | solution.py:75
  73.9 5.4 %all-to-all-start.1 = ((bf16[4,128,768]{2,1,0:T(8,128)(2,1)}), bf16[4,128,768]{2,1,0:T(8,128)(2,1)S(1)}, u32[]{:S(2)}, u32[]{:S(2)}) async-start(bf16[4,128,768]{2,1,0:T(8,128)(2,1)} %broadcast_in_dim.14), calls=%async_computation.1 | async-start | bytes 1572864 | tf_op jit(solution)/shard_map/all_to_all | solution.py:40
  87.6 5.2 %collective-permute-done.8 = bf16[8,25,768]{2,1,0:T(8,128)(2,1)S(1)} collective-permute-done((bf16[8,25,768]{2,1,0:T(8,128)(2,1)S(1)}, bf16[8,25,768]{2,1,0:T(8,128)(2,1)S(1)}, u32[]{:S(2)}, u32[]{:S(2)}) %collective-permute-start.8) | collective-permute-done | bytes 307232 | tf_op jit(solution)/shard_map/ppermute | solution.py:75
  113.6 4.6 %collective-permute-start.13 = (bf16[8,25,768]{2,1,0:T(8,128)(2,1)S(1)}, bf16[8,25,768]{2,1,0:T(8,128)(2,1)}, u32[]{:S(2)}, u32[]{:S(2)}) collective-permute-start(bf16[8,25,768]{2,1,0:T(8,128)(2,1)S(1)} %get-tuple-element.128), channel_id=1, source_target_pairs={{0,3},{1,0},{2,1},{3,2},{4,7},{5,4},{6,5},{7,6},{8,11},{9,8},{10,9... | collective-permute-start | bytes 921608 | tf_op jit(solution)/shard_map/ppermute | solution.py:84
  121.7 5.1 %all-to-all-start.2 = ((bf16[8,64,768]{2,1,0:T(8,128)(2,1)}), bf16[8,64,768]{2,1,0:T(8,128)(2,1)S(1)}, u32[]{:S(2)}, u32[]{:S(2)}) async-start(bf16[8,64,768]{2,1,0:T(8,128)(2,1)} %bitcast.5), calls=%async_computation.2 | async-start | bytes 1572864 | tf_op jit(solution)/shard_map/all_to_all | solution.py:193
  126.8 7.5 %collective-permute-done.11 = bf16[8,25,768]{2,1,0:T(8,128)(2,1)} collective-permute-done((bf16[8,25,768]{2,1,0:T(8,128)(2,1)}, bf16[8,25,768]{2,1,0:T(8,128)(2,1)}, u32[]{:S(2)}, u32[]{:S(2)}) %collective-permute-start.11) | collective-permute-done | bytes 307232 | tf_op jit(solution)/shard_map/ppermute | solution.py:84
  136.2 3.4 %collective-permute-start.14 = (bf16[4,25,768]{2,1,0:T(8,128)(2,1)S(1)}, bf16[4,25,768]{2,1,0:T(8,128)(2,1)S(1)}, u32[]{:S(2)}, u32[]{:S(2)}) collective-permute-start(bf16[4,25,768]{2,1,0:T(8,128)(2,1)S(1)} %slice.1771), channel_id=1, source_target_pairs={{0,4},{4,0},{8,12},{12,8},{16,20},{20,16},{24,28},{28,24},{1,5},{5... | collective-permute-start | bytes 460808 | tf_op jit(solution)/shard_map/ppermute | solution.py:67
  139.7 3.7 %collective-permute-done.14 = bf16[4,25,768]{2,1,0:T(8,128)(2,1)S(1)} collective-permute-done((bf16[4,25,768]{2,1,0:T(8,128)(2,1)S(1)}, bf16[4,25,768]{2,1,0:T(8,128)(2,1)S(1)}, u32[]{:S(2)}, u32[]{:S(2)}) %collective-permute-start.14) | collective-permute-done | bytes 153632 | tf_op jit(solution)/shard_map/ppermute | solution.py:67
  150.8 11.6 %all-to-all-start.3 = ((bf16[32,16,128]{2,1,0:T(8,128)(2,1)}), bf16[32,16,128]{2,1,0:T(8,128)(2,1)S(1)}, u32[]{:S(2)}, u32[]{:S(2)}) async-start(bf16[32,16,128]{2,1,0:T(8,128)(2,1)} %fusion.141), calls=%async_computation.3 | async-start | bytes 262144 | tf_op jit(solution)/shard_map/all_to_all | solution.py:44
  162.5 7.3 %collective-permute-start.16 = (bf16[1,25,768]{2,1,0:T(8,128)(2,1)S(1)}, bf16[1,25,768]{2,1,0:T(8,128)(2,1)S(1)}, u32[]{:S(2)}, u32[]{:S(2)}) collective-permute-start(bf16[1,25,768]{2,1,0:T(8,128)(2,1)S(1)} %slice.1773), channel_id=1, source_target_pairs={{0,16},{4,20},{8,24},{12,28},{16,0},{20,4},{24,8},{28,12},{1,17},{... | collective-permute-start | bytes 115208 | tf_op jit(solution)/shard_map/ppermute | solution.py:67
  170.1 5.8 %collective-permute-done.16 = bf16[1,25,768]{2,1,0:T(8,128)(2,1)S(1)} collective-permute-done((bf16[1,25,768]{2,1,0:T(8,128)(2,1)S(1)}, bf16[1,25,768]{2,1,0:T(8,128)(2,1)S(1)}, u32[]{:S(2)}, u32[]{:S(2)}) %collective-permute-start.16) | collective-permute-done | bytes 38432 | tf_op jit(solution)/shard_map/ppermute | solution.py:67
  186.8 8.5 %collective-permute-start.9 = (bf16[24,3,256]{2,1,0:T(4,128)(2,1)S(1)}, bf16[24,3,256]{2,1,0:T(4,128)(2,1)S(1)}, u32[]{:S(2)}, u32[]{:S(2)}) collective-permute-start(bf16[24,3,256]{2,1,0:T(4,128)(2,1)S(1)} %get-tuple-element.145), channel_id=1, source_target_pairs={{0,32},{32,64},{64,96},{96,128},{128,160},{160,192},{192,224},{224... | collective-permute-start | bytes 110600 | tf_op jit(solution)/shard_map/ppermute | solution.py:21
  197.2 14.5 %collective-permute-start.17 = (bf16[29,768]{1,0:T(8,128)(2,1)S(1)}, bf16[29,768]{1,0:T(8,128)(2,1)S(1)}, u32[]{:S(2)}, u32[]{:S(2)}) collective-permute-start(bf16[29,768]{1,0:T(8,128)(2,1)S(1)} %pad_maximum_fusion.6), channel_id=1, source_target_pairs={{0,256},{256,0},{1,257},{257,1},{2,258},{258,2},{3,259},{259,3},{4... | collective-permute-start | bytes 133640 | tf_op jit(solution)/shard_map/ppermute | solution.py:238
  214.0 15.2 %all-to-all-start.4 = ((bf16[8,29,768]{2,1,0:T(8,128)(2,1)}), bf16[8,29,768]{2,1,0:T(8,128)(2,1)S(1)}, u32[]{:S(2)}, u32[]{:S(2)}) async-start(bf16[8,29,768]{2,1,0:T(8,128)(2,1)} %broadcast_in_dim.20), calls=%async_computation.4 | async-start | bytes 786432 | tf_op jit(solution)/shard_map/all_to_all | solution.py:40
  229.6 5.4 %convert_add_fusion.1 = f32[24,8,256]{2,1,0:T(8,128)} fusion(bf16[24,8,256]{2,1,0:T(8,128)(2,1)S(1)} %copy-done.3, f32[24,14,256]{2,1,0:T(8,128)S(1)} %maximum_convert_fusion.1, f32[24]{0:T(128)S(1)} %copy-done.40, f32[24]{0:T(128)S(1)} %copy-done.42, f32[24]{0:T(128)S(1)} %copy-done.46, f32[24]{0:T(128)S(1)} %copy-done.48, f32[24]{0:T(128)S(1)} %copy-done.50, ...), kind=kLoop, calls=%fused_computation.165 | loop fusion | flops 4866048 | bytes 2085312 | tf_op jit(solution)/shard_map/add | solution.py:226
  (421 shorter events, 81.9 us)
Async XLA Ops:
  1.7 24.4 %collective-permute-start = (bf16[24,3,256]{2,1,0:T(4,128)(2,1)S(1)}, bf16[24,3,256]{2,1,0:T(4,128)(2,1)S(1)}, u32[]{:S(2)}, u32[]{:S(2)}) collective-permute-start(bf16[24,3,256]{2,1,0:T(4,128)(2,1)S(1)} %get-tuple-element.149), channel_id=1, source_target_pairs={{0,32},{32,64},{64,96},{96,128},{128,160},{160,192},{192,224},{224... | collective-permute-start | bytes 110600 | tf_op jit(solution)/shard_map/ppermute | solution.py:21
  6.2 19.9 %collective-permute-start.1 = (bf16[24,3,256]{2,1,0:T(4,128)(2,1)S(1)}, bf16[24,3,256]{2,1,0:T(4,128)(2,1)S(1)}, u32[]{:S(2)}, u32[]{:S(2)}) collective-permute-start(bf16[24,3,256]{2,1,0:T(4,128)(2,1)S(1)} %get-tuple-element.150), channel_id=1, source_target_pairs={{32,0},{64,32},{96,64},{128,96},{160,128},{192,160},{224,192},{256... | collective-permute-start | bytes 110600 | tf_op jit(solution)/shard_map/ppermute | solution.py:23
  13.5 28.5 %collective-permute-start.3 = (bf16[1,25,768]{2,1,0:T(8,128)(2,1)S(1)}, bf16[1,25,768]{2,1,0:T(8,128)(2,1)S(1)}, u32[]{:S(2)}, u32[]{:S(2)}) collective-permute-start(bf16[1,25,768]{2,1,0:T(8,128)(2,1)S(1)} %get-tuple-element.126), channel_id=1, source_target_pairs={{0,16},{4,20},{8,24},{12,28},{16,0},{20,4},{24,8},{28,12},{1,17},{... | collective-permute-start | bytes 115208 | tf_op jit(solution)/shard_map/ppermute | solution.py:67
  32.8 37.3 %all-to-all-start = ((bf16[32,24,128]{2,1,0:T(8,128)(2,1)}), bf16[32,24,128]{2,1,0:T(8,128)(2,1)S(1)}, u32[]{:S(2)}, u32[]{:S(2)}) async-start(bf16[32,24,128]{2,1,0:T(8,128)(2,1)} %pad_maximum_fusion.1), calls=%async_computation | async-start | bytes 393216 | tf_op jit(solution)/shard_map/all_to_all | solution.py:44
  42.0 11.0 %collective-permute-start.4 = (bf16[2,25,768]{2,1,0:T(8,128)(2,1)S(1)}, bf16[2,25,768]{2,1,0:T(8,128)(2,1)S(1)}, u32[]{:S(2)}, u32[]{:S(2)}) collective-permute-start(bf16[2,25,768]{2,1,0:T(8,128)(2,1)S(1)} %pad_maximum_fusion.5), channel_id=1, source_target_pairs={{0,8},{4,12},{8,0},{12,4},{16,24},{20,28},{24,16},{28,20},{1,9},{5... | collective-permute-start | bytes 230408 | tf_op jit(solution)/shard_map/ppermute | solution.py:67
  53.1 9.2 %collective-permute-start.5 = (bf16[4,25,768]{2,1,0:T(8,128)(2,1)S(1)}, bf16[4,25,768]{2,1,0:T(8,128)(2,1)S(1)}, u32[]{:S(2)}, u32[]{:S(2)}) collective-permute-start(bf16[4,25,768]{2,1,0:T(8,128)(2,1)S(1)} %pad_maximum_fusion.3), channel_id=1, source_target_pairs={{0,4},{4,0},{8,12},{12,8},{16,20},{20,16},{24,28},{28,24},{1,5},{5... | collective-permute-start | bytes 460808 | tf_op jit(solution)/shard_map/ppermute | solution.py:67
  57.1 49.7 %copy-start.11 = (f32[768]{0:T(1024)}, f32[768]{0:T(1024)S(1)}, u32[]{:S(2)}) copy-start(f32[768]{0:T(1024)S(1)} %convert_element_type.178) | copy-start | bytes 9220
  62.3 24.2 %collective-permute-start.7 = (bf16[8,25,768]{2,1,0:T(8,128)(2,1)S(1)}, bf16[8,25,768]{2,1,0:T(8,128)(2,1)}, u32[]{:S(2)}, u32[]{:S(2)}) collective-permute-start(bf16[8,25,768]{2,1,0:T(8,128)(2,1)S(1)} %pad_maximum_fusion), channel_id=1, source_target_pairs={{2,0},{3,1},{0,2},{1,3},{6,4},{7,5},{4,6},{5,7},{10,8},{11,9},{8,1... | collective-permute-start | bytes 921608 | tf_op jit(solution)/shard_map/ppermute | solution.py:75
  67.4 18.1 %collective-permute-start.6 = (bf16[8,25,768]{2,1,0:T(8,128)(2,1)S(1)}, bf16[8,25,768]{2,1,0:T(8,128)(2,1)}, u32[]{:S(2)}, u32[]{:S(2)}) collective-permute-start(bf16[8,25,768]{2,1,0:T(8,128)(2,1)S(1)} %pad_maximum_fusion), channel_id=1, source_target_pairs={{1,0},{2,1},{3,2},{0,3},{5,4},{6,5},{7,6},{4,7},{9,8},{10,9},{11,1... | collective-permute-start | bytes 921608 | tf_op jit(solution)/shard_map/ppermute | solution.py:75
  73.9 18.9 %all-to-all-start.1 = ((bf16[4,128,768]{2,1,0:T(8,128)(2,1)}), bf16[4,128,768]{2,1,0:T(8,128)(2,1)S(1)}, u32[]{:S(2)}, u32[]{:S(2)}) async-start(bf16[4,128,768]{2,1,0:T(8,128)(2,1)} %broadcast_in_dim.14), calls=%async_computation.1 | async-start | bytes 1572864 | tf_op jit(solution)/shard_map/all_to_all | solution.py:40
  79.3 13.5 %collective-permute-start.8 = (bf16[8,25,768]{2,1,0:T(8,128)(2,1)S(1)}, bf16[8,25,768]{2,1,0:T(8,128)(2,1)S(1)}, u32[]{:S(2)}, u32[]{:S(2)}) collective-permute-start(bf16[8,25,768]{2,1,0:T(8,128)(2,1)S(1)} %pad_maximum_fusion), channel_id=1, source_target_pairs={{3,0},{0,1},{1,2},{2,3},{7,4},{4,5},{5,6},{6,7},{11,8},{8,9},{9,10... | collective-permute-start | bytes 921608 | tf_op jit(solution)/shard_map/ppermute | solution.py:75
  92.9 6.4 %collective-permute-start.2 = (bf16[4,128,768]{2,1,0:T(8,128)(2,1)S(1)}, bf16[4,128,768]{2,1,0:T(8,128)(2,1)}, u32[]{:S(2)}, u32[]{:S(2)}) collective-permute-start(bf16[4,128,768]{2,1,0:T(8,128)(2,1)S(1)} %all-to-all-done.1), channel_id=1, source_target_pairs={{0,32},{32,0},{1,33},{33,1},{2,34},{34,2},{3,35},{35,3},{4,36},{36... | collective-permute-start | bytes 2359304 | tf_op jit(solution)/shard_map/ppermute | solution.py:48
  111.7 22.6 %collective-permute-start.11 = (bf16[8,25,768]{2,1,0:T(8,128)(2,1)}, bf16[8,25,768]{2,1,0:T(8,128)(2,1)}, u32[]{:S(2)}, u32[]{:S(2)}) collective-permute-start(bf16[8,25,768]{2,1,0:T(8,128)(2,1)} %get-tuple-element.127), channel_id=1, source_target_pairs={{0,1},{1,2},{2,3},{3,0},{4,5},{5,6},{6,7},{7,4},{8,9},{9,10},{10,1... | collective-permute-start | bytes 921608 | tf_op jit(solution)/shard_map/ppermute | solution.py:84
  113.6 21.1 %collective-permute-start.13 = (bf16[8,25,768]{2,1,0:T(8,128)(2,1)S(1)}, bf16[8,25,768]{2,1,0:T(8,128)(2,1)}, u32[]{:S(2)}, u32[]{:S(2)}) collective-permute-start(bf16[8,25,768]{2,1,0:T(8,128)(2,1)S(1)} %get-tuple-element.128), channel_id=1, source_target_pairs={{0,3},{1,0},{2,1},{3,2},{4,7},{5,4},{6,5},{7,6},{8,11},{9,8},{10,9... | collective-permute-start | bytes 921608 | tf_op jit(solution)/shard_map/ppermute | solution.py:84
  118.2 16.5 %collective-permute-start.12 = (bf16[8,25,768]{2,1,0:T(8,128)(2,1)S(1)}, bf16[8,25,768]{2,1,0:T(8,128)(2,1)}, u32[]{:S(2)}, u32[]{:S(2)}) collective-permute-start(bf16[8,25,768]{2,1,0:T(8,128)(2,1)S(1)} %get-tuple-element.129), channel_id=1, source_target_pairs={{0,2},{1,3},{2,0},{3,1},{4,6},{5,7},{6,4},{7,5},{8,10},{9,11},{10,... | collective-permute-start | bytes 921608 | tf_op jit(solution)/shard_map/ppermute | solution.py:84
  121.7 24.9 %all-to-all-start.2 = ((bf16[8,64,768]{2,1,0:T(8,128)(2,1)}), bf16[8,64,768]{2,1,0:T(8,128)(2,1)S(1)}, u32[]{:S(2)}, u32[]{:S(2)}) async-start(bf16[8,64,768]{2,1,0:T(8,128)(2,1)} %bitcast.5), calls=%async_computation.2 | async-start | bytes 1572864 | tf_op jit(solution)/shard_map/all_to_all | solution.py:193
  136.2 7.2 %collective-permute-start.14 = (bf16[4,25,768]{2,1,0:T(8,128)(2,1)S(1)}, bf16[4,25,768]{2,1,0:T(8,128)(2,1)S(1)}, u32[]{:S(2)}, u32[]{:S(2)}) collective-permute-start(bf16[4,25,768]{2,1,0:T(8,128)(2,1)S(1)} %slice.1771), channel_id=1, source_target_pairs={{0,4},{4,0},{8,12},{12,8},{16,20},{20,16},{24,28},{28,24},{1,5},{5... | collective-permute-start | bytes 460808 | tf_op jit(solution)/shard_map/ppermute | solution.py:67
  143.4 19.0 %collective-permute-start.15 = (bf16[2,25,768]{2,1,0:T(8,128)(2,1)S(1)}, bf16[2,25,768]{2,1,0:T(8,128)(2,1)S(1)}, u32[]{:S(2)}, u32[]{:S(2)}) collective-permute-start(bf16[2,25,768]{2,1,0:T(8,128)(2,1)S(1)} %slice.1772), channel_id=1, source_target_pairs={{0,8},{4,12},{8,0},{12,4},{16,24},{20,28},{24,16},{28,20},{1,9},{5... | collective-permute-start | bytes 230408 | tf_op jit(solution)/shard_map/ppermute | solution.py:67
  150.8 25.1 %all-to-all-start.3 = ((bf16[32,16,128]{2,1,0:T(8,128)(2,1)}), bf16[32,16,128]{2,1,0:T(8,128)(2,1)S(1)}, u32[]{:S(2)}, u32[]{:S(2)}) async-start(bf16[32,16,128]{2,1,0:T(8,128)(2,1)} %fusion.141), calls=%async_computation.3 | async-start | bytes 262144 | tf_op jit(solution)/shard_map/all_to_all | solution.py:44
  162.5 13.4 %collective-permute-start.16 = (bf16[1,25,768]{2,1,0:T(8,128)(2,1)S(1)}, bf16[1,25,768]{2,1,0:T(8,128)(2,1)S(1)}, u32[]{:S(2)}, u32[]{:S(2)}) collective-permute-start(bf16[1,25,768]{2,1,0:T(8,128)(2,1)S(1)} %slice.1773), channel_id=1, source_target_pairs={{0,16},{4,20},{8,24},{12,28},{16,0},{20,4},{24,8},{28,12},{1,17},{... | collective-permute-start | bytes 115208 | tf_op jit(solution)/shard_map/ppermute | solution.py:67
  186.8 24.9 %collective-permute-start.9 = (bf16[24,3,256]{2,1,0:T(4,128)(2,1)S(1)}, bf16[24,3,256]{2,1,0:T(4,128)(2,1)S(1)}, u32[]{:S(2)}, u32[]{:S(2)}) collective-permute-start(bf16[24,3,256]{2,1,0:T(4,128)(2,1)S(1)} %get-tuple-element.145), channel_id=1, source_target_pairs={{0,32},{32,64},{64,96},{96,128},{128,160},{160,192},{192,224},{224... | collective-permute-start | bytes 110600 | tf_op jit(solution)/shard_map/ppermute | solution.py:21
  195.3 16.4 %collective-permute-start.10 = (bf16[24,3,256]{2,1,0:T(4,128)(2,1)S(1)}, bf16[24,3,256]{2,1,0:T(4,128)(2,1)S(1)}, u32[]{:S(2)}, u32[]{:S(2)}) collective-permute-start(bf16[24,3,256]{2,1,0:T(4,128)(2,1)S(1)} %get-tuple-element.146), channel_id=1, source_target_pairs={{32,0},{64,32},{96,64},{128,96},{160,128},{192,160},{224,192},{256... | collective-permute-start | bytes 110600 | tf_op jit(solution)/shard_map/ppermute | solution.py:23
  197.2 15.9 %collective-permute-start.17 = (bf16[29,768]{1,0:T(8,128)(2,1)S(1)}, bf16[29,768]{1,0:T(8,128)(2,1)S(1)}, u32[]{:S(2)}, u32[]{:S(2)}) collective-permute-start(bf16[29,768]{1,0:T(8,128)(2,1)S(1)} %pad_maximum_fusion.6), channel_id=1, source_target_pairs={{0,256},{256,0},{1,257},{257,1},{2,258},{258,2},{3,259},{259,3},{4... | collective-permute-start | bytes 133640 | tf_op jit(solution)/shard_map/ppermute | solution.py:238
  214.0 23.3 %all-to-all-start.4 = ((bf16[8,29,768]{2,1,0:T(8,128)(2,1)}), bf16[8,29,768]{2,1,0:T(8,128)(2,1)S(1)}, u32[]{:S(2)}, u32[]{:S(2)}) async-start(bf16[8,29,768]{2,1,0:T(8,128)(2,1)} %broadcast_in_dim.20), calls=%async_computation.4 | async-start | bytes 786432 | tf_op jit(solution)/shard_map/all_to_all | solution.py:40
  (104 other events, 2288.0 us)

commit v3 on v1

v3 whole, which is shorter than its diff:
```python
import jax
import jax.numpy as jnp
from jax import lax
from jax.experimental import pallas as pl
from jax.experimental.pallas import tpu as pltpu
from jax.sharding import Mesh, PartitionSpec as P

LAT = ("zh", "x", "c")
CHAN = ("zl", "y")
GROUP = 8
F32 = jnp.float32
BF = jnp.bfloat16
EXT = 16
VMEM_BYTES = 48 * 1024 * 1024
SIDE = 128


def vmem():
    return pl.BlockSpec(memory_space=pltpu.VMEM)


def smem():
    return pl.BlockSpec(memory_space=pltpu.SMEM)


def call(body, out_shape, in_specs, scratch=()):
    many = isinstance(out_shape, (list, tuple))
    return pl.pallas_call(
        body,
        out_shape=out_shape,
        in_specs=in_specs,
        out_specs=[vmem()] * len(out_shape) if many else vmem(),
        scratch_shapes=list(scratch),
        compiler_params=pltpu.CompilerParams(vmem_limit_bytes=VMEM_BYTES),
    )


def fill_rows(x_ref, up_ref, down_ref, ext):
    rows = x_ref.shape[1]
    ext[:, :3, :] = up_ref[...].astype(F32)
    ext[:, 3 : 3 + rows, :] = x_ref[...].astype(F32)
    ext[:, 3 + rows : 6 + rows, :] = down_ref[...].astype(F32)


def fill_shifts(cells, shifted):
    width = cells.shape[1]
    lane = lax.broadcasted_iota(jnp.int32, cells.shape, 1)
    for b in range(7):
        move = b - 3
        if move == 0:
            shifted[b] = cells
        else:
            turned = pltpu.roll(cells, (-move) % width, 1)
            inside = lane < width - move if move > 0 else lane >= -move
            shifted[b] = jnp.where(inside, turned, 0.0)


def stencil(taps_ref, c, shifted, rows, flip):
    total = None
    for a in range(7):
        for b in range(7):
            tap = a * 7 + b
            term = taps_ref[c, 48 - tap if flip else tap] * shifted[b, a : a + rows, :]
            total = term if total is None else total + term
    return total


def forward_body(taps_ref, bias_ref, x_ref, up_ref, down_ref, metric_ref, dy_ref, out_ref, ext, shifted, h_rows, dy_rows):
    cdev, rows, width = x_ref.shape
    fill_rows(x_ref, up_ref, down_ref, ext)
    dy_rows[...] = dy_ref[...].astype(F32)
    metric = jnp.broadcast_to(metric_ref[...], (rows, width))

    def channel(c, carry):
        fill_shifts(ext[c], shifted)
        h_rows[c] = bias_ref[c] + metric * stencil(taps_ref, c, shifted, rows, False)
        return carry

    lax.fori_loop(0, cdev, channel, 0)
    low = lax.broadcasted_iota(jnp.int32, (cdev, 128), 1) < 64
    for r in range(rows):
        h_row, dy_row = h_rows[:, r, :], dy_rows[:, r, :]
        for t in range(width // 128):
            h_tile, dy_tile = h_row[:, t * 128 : t * 128 + 128], dy_row[:, t * 128 : t * 128 + 128]
            at = (r * width + t * 128) // 64
            out_ref[at] = jnp.where(low, h_tile, pltpu.roll(dy_tile, 64, 1)).astype(BF)
            out_ref[at + 1] = jnp.where(low, pltpu.roll(h_tile, 64, 1), dy_tile).astype(BF)


def forward(taps, bias, x, up, down, metric, dy):
    cdev, rows, width = x.shape
    return call(
        forward_body,
        jax.ShapeDtypeStruct((rows * width // 64, cdev, 128), BF),
        [smem(), smem()] + [vmem()] * 5,
        [
            pltpu.VMEM((cdev, EXT, width), F32),
            pltpu.VMEM((7, EXT, width), F32),
            pltpu.VMEM((cdev, rows, width), F32),
            pltpu.VMEM((cdev, rows, width), F32),
        ],
    )(taps, bias, x, up, down, metric[:, None], dy)


def norm_body(recv_ref, gain_ref, bias_ref, pair_ref, nhat_ref, rstd_ref):
    chans, lanes = recv_ref.shape
    piece = lanes // 2
    both = recv_ref[...].astype(F32).T
    h = both[:piece]
    mean = jnp.sum(h, 1, keepdims=True) / chans
    var = jnp.sum(h * h, 1, keepdims=True) / chans - mean * mean
    rstd = 1.0 / jnp.sqrt(var + 1e-06)
    nhat = (h - mean) * rstd
    nhat_ref[...] = nhat
    rstd_ref[...] = jnp.broadcast_to(rstd, rstd_ref.shape)
    n = (nhat * gain_ref[...] + bias_ref[...]).astype(BF)
    dy = both[piece:].astype(BF)
    for k in range(pair_ref.shape[0]):
        pair_ref[k, :piece] = n
        pair_ref[k, piece:] = dy


def norm(recv, gain, bias, copies):
    chans, lanes = recv.shape
    return call(
        norm_body,
        [
            jax.ShapeDtypeStruct((copies, lanes, chans), BF),
            jax.ShapeDtypeStruct((lanes // 2, chans), F32),
            jax.ShapeDtypeStruct((lanes // 2, 128), F32),
        ],
        [vmem()] * 3,
    )(recv, gain[None], bias[None])


def norm_back_body(recv_ref, nhat_ref, rstd_ref, gain_ref, gam_ref, out_ref, flat):
    piece, chans = nhat_ref.shape
    dn = recv_ref[0].astype(F32)
    for k in range(1, recv_ref.shape[0]):
        dn = dn + recv_ref[k].astype(F32)
    nhat = nhat_ref[...]
    dnhat = dn * gain_ref[...]
    s1 = jnp.sum(dnhat, 1, keepdims=True) / chans
    s2 = jnp.sum(dnhat * nhat, 1, keepdims=True) / chans
    dh = rstd_ref[:, :1] * (dnhat - s1 - nhat * s2)
    flat[:piece] = dh
    flat[piece:] = jnp.zeros((flat.shape[0] - piece, chans), F32)
    sums = (jnp.sum(dn * nhat, 0, keepdims=True), jnp.sum(dn, 0, keepdims=True), gam_ref[...])
    for k, value in enumerate(sums):
        high = value.astype(BF).astype(F32)
        flat[piece + 2 * k : piece + 2 * k + 1] = high
        flat[piece + 2 * k + 1 : piece + 2 * k + 2] = value - high
    blocks = flat[...].T.reshape(out_ref.shape[0], 24, 128)
    one, two, three = blocks[:, :8], blocks[:, 8:16], blocks[:, 16:]
    lane = lax.broadcasted_iota(jnp.int32, one.shape, 2)
    out_ref[:, :8] = jnp.where(lane < 64, one, pltpu.roll(three, 64, 2)).astype(BF)
    last = jnp.where(lane < 72, one, jnp.where(lane < 80, pltpu.roll(two, 8, 2), pltpu.roll(three, 16, 2)))
    out_ref[:, 8:] = jnp.where(lane < 64, two, last).astype(BF)


def norm_back(recv, nhat, rstd, gain, gam, owners):
    piece, chans = nhat.shape
    return call(
        norm_back_body,
        jax.ShapeDtypeStruct((owners, 16, 128), BF),
        [vmem()] * 5,
        [pltpu.VMEM((128, chans), F32)],
    )(recv, nhat, rstd, gain[None], gam[None])


def taps_body(recv_ref, x_ref, up_ref, down_ref, metric_ref, dy_ref, dconv_ref, ends_ref, sums_ref, extra_ref, ext, shifted, dh_rows, prods):
    cdev, rows, width = x_ref.shape
    fill_rows(x_ref, up_ref, down_ref, ext)
    low16 = lax.broadcasted_iota(jnp.int32, (16, 128), 1) < 64
    low8 = lax.broadcasted_iota(jnp.int32, (8, 128), 1) < 64
    extra = jnp.zeros((8, 128), F32)
    for r in range(rows):
        for t in range(width // 128):
            at = (r * width + t * 128) // 64
            first, second = recv_ref[at].astype(F32), recv_ref[at + 1].astype(F32)
            lanes = slice(t * 128, t * 128 + 128)
            dh_rows[:16, r, lanes] = jnp.where(low16, first, pltpu.roll(second, 64, 1))
            dh_rows[16:, r, lanes] = jnp.where(low8, pltpu.roll(first[:8], 64, 1), second[:8])
            extra = extra + first[8:] + second[8:]
    for g in range(3):
        extra_ref[8 * g : 8 * g + 8] = pltpu.roll(extra, 64 - 8 * g, 1)
    metric = jnp.broadcast_to(metric_ref[...], (rows, width))

    def channel(c, carry):
        fill_shifts(ext[c], shifted)
        dh = dh_rows[c]
        dconv = metric * dh
        dconv_ref[c] = dconv
        ends_ref[0, c] = dconv[:3].astype(BF)
        ends_ref[1, c] = dconv[rows - 3 :].astype(BF)
        for a in range(7):
            for b in range(7):
                product = shifted[b, a : a + rows, :] * dconv
                prods[(a * 7 + b) * 8 : (a * 7 + b) * 8 + 8, :] = product[:, :128] + product[:, 128:]
        dy = dy_ref[c].astype(F32)
        prods[392:400, :] = dh[:, :128] + dh[:, 128:]
        prods[400:408, :] = dy[:, :128] + dy[:, 128:]
        total = prods[pl.ds(0, 56, 8), :]
        for i in range(1, 8):
            total = total + prods[pl.ds(i, 56, 8), :]
        sums_ref[c] = total
        return carry

    prods[408:, :] = jnp.zeros((prods.shape[0] - 408, 128), F32)
    lax.fori_loop(0, cdev, channel, 0)


def tap_sums(recv, x, up, down, metric, dy):
    cdev, rows, width = x.shape
    return call(
        taps_body,
        [
            jax.ShapeDtypeStruct((cdev, rows, width), F32),
            jax.ShapeDtypeStruct((2, cdev, 3, width), BF),
            jax.ShapeDtypeStruct((cdev, 56, 128), F32),
            jax.ShapeDtypeStruct((cdev, 128), F32),
        ],
        [vmem()] * 6,
        [
            pltpu.VMEM((cdev, EXT, width), F32),
            pltpu.VMEM((7, EXT, width), F32),
            pltpu.VMEM((cdev, rows, width), F32),
            pltpu.VMEM((448, 128), F32),
        ],
    )(recv, x, up, down, metric[:, None], dy)


def spread_body(taps_ref, x_ref, up_ref, down_ref, dy_ref, out_ref, ext, shifted):
    cdev, rows, width = x_ref.shape
    fill_rows(x_ref, up_ref, down_ref, ext)

    def channel(c, carry):
        fill_shifts(ext[c], shifted)
        out_ref[c] = dy_ref[c].astype(F32) + stencil(taps_ref, c, shifted, rows, True)
        return carry

    lax.fori_loop(0, cdev, channel, 0)


def spread_back(taps, dconv, up, down, dy):
    cdev, rows, width = dconv.shape
    return call(
        spread_body,
        jax.ShapeDtypeStruct((cdev, rows, width), F32),
        [smem()] + [vmem()] * 4,
        [pltpu.VMEM((cdev, EXT, width), F32), pltpu.VMEM((7, EXT, width), F32)],
    )(taps, dconv, up, down, dy)


def gelu_exact(value):
    return jax.nn.gelu(value, approximate=False)


def two_parts(value):
    high = lax.reduce_precision(value, 8, 7)
    return high.astype(BF), (value - high).astype(BF)


def to_all(block, axis):
    count = lax.axis_size(axis)
    return lax.all_to_all(jnp.broadcast_to(block[None], (count,) + block.shape), axis, 0, 0, tiled=True)


def exchange(blocks):
    return lax.all_to_all(blocks, CHAN, 0, 0, tiled=True)


def halos(first, last):
    ends = lax.axis_size(LAT) - 1
    up = lax.ppermute(last, LAT, [(i, i + 1) for i in range(ends)])
    down = lax.ppermute(first, LAT, [(i + 1, i) for i in range(ends)])
    return up, down


def with_other_core(block):
    return jnp.concatenate([block, lax.ppermute(block, "c", [(0, 1), (1, 0)])], 0)


def from_ring(block):
    count = lax.axis_size("y")
    ahead = [lax.ppermute(block, "y", [((i + k) % count, i) for i in range(count)]) for k in range(1, count)]
    return jnp.stack([block] + ahead, 0)


def to_ring(blocks):
    count = lax.axis_size("y")
    total = blocks[0].astype(F32)
    for k in range(1, count):
        total = total + lax.ppermute(blocks[k], "y", [(i, (i + k) % count) for i in range(count)]).astype(F32)
    return total


def per_device(
    block_input,
    out_grad,
    metric,
    kernel,
    conv_bias,
    ln_gain,
    ln_bias,
    w_in,
    b_in,
    w_out,
    b_out,
    layer_scale,
):
    cdev, rows, width = block_input.shape
    chans = ln_gain.shape[0]
    tokens = rows * width
    nz, ny = lax.axis_size("zl"), lax.axis_size("y")
    nchan = nz * ny
    hdev = w_in.shape[0]
    part = hdev // GROUP
    hid = part * nchan
    piece = tokens // nchan
    member = lax.axis_index(("x", "c"))
    owner = lax.axis_index(CHAN)
    gamma_f = layer_scale.astype(F32)
    gamma_own = lax.dynamic_slice_in_dim(gamma_f, owner * cdev, cdev)

    side = jnp.pad(jnp.stack(two_parts(lax.dynamic_slice_in_dim(b_in, member * part, part)), 1), ((0, part), (0, SIDE - 2)))
    mine = jnp.concatenate(
        [lax.dynamic_slice_in_dim(w_in, member * part, part), lax.dynamic_slice_in_dim(w_out, member * part, part)], 0
    )
    shards = to_all(jnp.concatenate([mine, side], 1), "zl")

    up, down = halos(block_input[:, :3], block_input[:, rows - 3 :])
    blocks = forward(kernel, conv_bias, block_input, up, down, metric, out_grad)
    blocks, shards = lax.optimization_barrier((blocks, shards))

    shards = from_ring(shards).reshape(nchan, 2 * part, chans + SIDE)
    wi = shards[:, :part, :chans].reshape(hid, chans)
    wo = shards[:, part:, :chans].reshape(hid, chans)
    bi = jnp.sum(shards[:, :part, chans : chans + 2].astype(F32), 2).reshape(hid)

    recv = exchange(blocks).reshape(chans, 2 * piece)
    pair, nhat, rstd = norm(recv, ln_gain, ln_bias, GROUP // 2)
    pair = with_other_core(lax.all_to_all(pair, "x", 0, 0, tiled=True))
    n = pair[:, :piece].reshape(GROUP * piece, chans)
    dy = pair[:, piece:].reshape(GROUP * piece, chans)

    over_last = (((1,), (1,)), ((), ()))
    over_first = (((0,), (0,)), ((), ()))
    pre = lax.dot_general(n, wi, over_last, preferred_element_type=F32) + bi
    g, back = jax.vjp(gelu_exact, pre)
    g_b = g.astype(BF)
    dmlp = (gamma_f * dy.astype(F32)).astype(BF)
    grad_g = lax.dot_general(dmlp, wo, over_last, preferred_element_type=F32)
    dpre = back(grad_g)[0].astype(BF)
    turned = jnp.roll(dpre, dpre.shape[0] // 2, 0)
    ordered = jnp.where(lax.axis_index("c") == 0, dpre, turned)
    dn = jnp.dot(ordered, wi, preferred_element_type=F32).astype(BF)
    dn = lax.all_to_all(dn.reshape(GROUP, piece, chans), ("c", "x"), 0, 0, tiled=True)
    dw_in = lax.dot_general(dpre, n, over_first, preferred_element_type=F32)
    proj = lax.dot_general(g_b, dy, over_first, preferred_element_type=F32)
    db_in = jnp.sum(dpre.astype(F32), 0)
    gam_part = jnp.sum(wo.astype(F32) * proj, 0)
    dw_out = proj * gamma_f

    side = jnp.broadcast_to(db_in.astype(BF).reshape(nchan, part, 1), (nchan, part, SIDE))
    dws = jnp.concatenate(
        [
            jnp.concatenate([dw_in.astype(BF).reshape(nchan, part, chans), side], 2),
            jnp.pad(dw_out.astype(BF).reshape(nchan, part, chans), ((0, 0), (0, 0), (0, SIDE))),
        ],
        1,
    )
    dws = to_ring(dws.reshape(ny, nz, 2 * part, chans + SIDE)).astype(BF)
    dws = lax.all_to_all(dws, "zl", 0, 0, tiled=True)
    dws = jnp.sum(dws.astype(F32), 0)

    payload = exchange(norm_back(dn, nhat, rstd, ln_gain, gam_part, nchan))
    dconv, ends, taps, extra = tap_sums(payload, block_input, up, down, metric, out_grad)
    dup, ddown = halos(ends[0], ends[1])
    grad_input = spread_back(kernel, dconv, dup, ddown, out_grad)

    small = jnp.concatenate([jnp.sum(taps, 2), extra[:, :8]], 1)
    mine = jnp.concatenate([dws.astype(BF)] + list(two_parts(small)), 1)
    other = lax.ppermute(mine, "zh", [(0, 1), (1, 0)]).astype(F32)
    wide = chans + SIDE
    count = small.shape[1]
    dws = dws + other[:, :wide]
    small = small + other[:, wide : wide + count] + other[:, wide + count :]
    mine = jnp.concatenate([dws.astype(BF)] + list(two_parts(small)), 1)
    gathered = to_all(mine, ("x", "c")).astype(F32)
    grad_w_in = gathered[:, :part, :chans].reshape(hdev, chans)
    grad_w_out = gathered[:, part:, :chans].reshape(hdev, chans)
    grad_b_in = gathered[:, :part, chans].reshape(hdev)
    small = jnp.sum(gathered[:, :, wide : wide + count] + gathered[:, :, wide + count :], 0)
    n_taps = kernel.shape[1]
    dysum = small[:, n_taps + 1]
    rest = small[:, count - 8 :]
    return (
        grad_input,
        small[:, :n_taps],
        small[:, n_taps],
        rest[:, 0] + rest[:, 1],
        rest[:, 2] + rest[:, 3],
        grad_w_in,
        grad_b_in,
        grad_w_out,
        gamma_own * dysum,
        rest[:, 4] + rest[:, 5] + b_out * dysum,
    )


def solution(mesh):
    split = Mesh(mesh.devices.reshape(2, 4, 2, 8, 4), ("zh", "x", "c", "zl", "y"))
    return jax.shard_map(
        per_device,
        mesh=split,
        in_specs=(
            P(CHAN, LAT, None),
            P(CHAN, LAT, None),
            P(LAT),
            P(CHAN, None),
            P(CHAN),
            P(),
            P(),
            P(CHAN, None),
            P(CHAN),
            P(CHAN, None),
            P(CHAN),
            P(),
        ),
        out_specs=(
            P(CHAN, LAT, None),
            P(CHAN, None),
            P(CHAN),
            P(CHAN),
            P(CHAN),
            P(CHAN, None),
            P(CHAN),
            P(CHAN, None),
            P(CHAN),
            P(CHAN),
        ),
        check_vma=False,
    )
```

time: 268 us -> 219 us (0.82)
  the two profiles are of different devices: /device:TPU:1 before, /device:TPU:288 now
where the time goes in v3:
time: 219 us; the launch traced here: 218 us
  waiting for transfers between devices  85.5 us (39%)
  starting transfers between devices  83.3 us (38%)
  Pallas kernels  18 us (8%)
  local copies, waits for them, and re-layouts  13.4 us (6%)
  matrix products  8.46 us (4%)
  other arithmetic  8.04 us (4%)
    ppermute x2, waiting for transfers between devices, halos(): up = lax.ppermute(last, LAT, [(i, i + 1) for i in range(ends)])  28.6 us
    all_to_all x2, starting transfers between devices, exchange(): return lax.all_to_all(blocks, CHAN, 0, 0, tiled=True)  20.9 us
    all_to_all x2, waiting for transfers between devices, exchange(): return lax.all_to_all(blocks, CHAN, 0, 0, tiled=True)  19.4 us
    all_to_all x1, waiting for transfers between devices, per_device(): dws = lax.all_to_all(dws, 'zl', 0, 0, tiled=True)  14.3 us
    ppermute x1, waiting for transfers between devices, per_device(): other = lax.ppermute(mine, 'zh', [(0, 1), (1, 0)]).astype(F32)  13.7 us
    ppermute x2, starting transfers between devices, halos(): down = lax.ppermute(first, LAT, [(i + 1, i) for i in range(ends)])  11.3 us
    all_to_all x2, starting transfers between devices, to_all(): lax.all_to_all(jnp.broadcast_to(block[None], (count,) + block.shape), axi...  10.4 us
    ppermute x3, starting transfers between devices, to_ring(): lax.ppermute(blocks[k], 'y', [(i, (i + k) % count) for i in range(count)])  9.86 us
  transfers between devices with their start and end apart: 19, of which 9 were waited for; matrix products, arithmetic and copies ran while one was open for 5% of the time, Pallas kernels for 8%

profile of v3, /device:TPU:288, one launch (start us, length us, event | category | flops | bytes accessed | tf_op | source)
XLA Modules:
  0.0 218.0 jit_solution(5339853868828986933)
XLA Ops:
  3.3 6.0 %all-to-all-start = ((bf16[8,24,896]{2,1,0:T(8,128)(2,1)}), bf16[8,24,896]{2,1,0:T(8,128)(2,1)S(1)}, u32[]{:S(2)}, u32[]{:S(2)}) async-start(bf16[8,24,896]{2,1,0:T(8,128)(2,1)} %broadcast_in_dim.17), calls=%async_computation | async-start | bytes 688128 | tf_op jit(solution)/shard_map/all_to_all | solution.py:266
  9.3 7.4 %collective-permute-start.1 = (bf16[24,3,256]{2,1,0:T(4,128)(2,1)S(1)}, bf16[24,3,256]{2,1,0:T(4,128)(2,1)S(1)}, u32[]{:S(2)}, u32[]{:S(2)}) collective-permute-start(bf16[24,3,256]{2,1,0:T(4,128)(2,1)S(1)} %get-tuple-element.55), channel_id=1, source_target_pairs={{32,0},{64,32},{96,64},{128,96},{160,128},{192,160},{224,192},{256... | collective-permute-start | bytes 110600 | tf_op jit(solution)/shard_map/ppermute | solution.py:276
  18.8 14.2 %collective-permute-done.up_ref = bf16[24,3,256]{2,1,0:T(4,128)(2,1)S(1)} collective-permute-done((bf16[24,3,256]{2,1,0:T(4,128)(2,1)S(1)}, bf16[24,3,256]{2,1,0:T(4,128)(2,1)S(1)}, u32[]{:S(2)}, u32[]{:S(2)}) %collective-permute-start) | collective-permute-done | bytes 36896 | tf_op jit(solution)/shard_map/ppermute | solution.py:275
  33.0 5.8 %shard_map.195 = bf16[32,24,128]{2,1,0:T(8,128)(2,1)} custom-call(f32[24,49]{1,0:T(8,128)S(1)} %copy-done.2, f32[24]{0:T(128)S(1)} %copy-done.3, bf16[24,8,256]{2,1,0:T(8,128)(2,1)S(1)} %copy-done.1, bf16[24,3,256]{2,1,0:T(4,128)(2,1)S(1)} %collective-permute-done.up_ref, bf16[24,3,256]{2,1,0:T(4,128)(2,1)S(1)} %collective-permute-done.1.down_ref, ...), custom_call_target="tpu_custom_call" | custom-call | tf_op jit(solution)/shard_map/pallas_call | solution.py:92
  38.8 13.1 %all-to-all-start.1 = ((bf16[32,24,128]{2,1,0:T(8,128)(2,1)}), bf16[32,24,128]{2,1,0:T(8,128)(2,1)S(1)}, u32[]{:S(2)}, u32[]{:S(2)}) async-start(bf16[32,24,128]{2,1,0:T(8,128)(2,1)} %shard_map.195), calls=%async_computation.1 | async-start | bytes 393216 | tf_op jit(solution)/shard_map/all_to_all | solution.py:270
  52.0 12.6 %all-to-all-done.1 = bf16[32,24,128]{2,1,0:T(8,128)(2,1)S(1)} async-done(((bf16[32,24,128]{2,1,0:T(8,128)(2,1)}), bf16[32,24,128]{2,1,0:T(8,128)(2,1)S(1)}, u32[]{:S(2)}, u32[]{:S(2)}) %all-to-all-start.1) | async-done | bytes 196640 | tf_op jit(solution)/shard_map/all_to_all | solution.py:270
  65.7 3.5 %all-to-all-start.2 = ((bf16[4,128,768]{2,1,0:T(8,128)(2,1)}), bf16[4,128,768]{2,1,0:T(8,128)(2,1)S(1)}, u32[]{:S(2)}, u32[]{:S(2)}) async-start(bf16[4,128,768]{2,1,0:T(8,128)(2,1)} %get-tuple-element.20), calls=%async_computation.2 | async-start | bytes 1572864 | tf_op jit(solution)/shard_map/all_to_all | solution.py:343
  71.4 4.4 %collective-permute-start.4 = (bf16[8,24,896]{2,1,0:T(8,128)(2,1)S(1)}, bf16[8,24,896]{2,1,0:T(8,128)(2,1)S(1)}, u32[]{:S(2)}, u32[]{:S(2)}) collective-permute-start(bf16[8,24,896]{2,1,0:T(8,128)(2,1)S(1)} %all-to-all-done), channel_id=1, source_target_pairs={{2,0},{3,1},{0,2},{1,3},{6,4},{7,5},{4,6},{5,7},{10,8},{11,9},{8,1... | collective-permute-start | bytes 1032200 | tf_op jit(solution)/shard_map/ppermute | solution.py:286
  75.8 3.0 %collective-permute-start.3 = (bf16[8,24,896]{2,1,0:T(8,128)(2,1)S(1)}, bf16[8,24,896]{2,1,0:T(8,128)(2,1)S(1)}, u32[]{:S(2)}, u32[]{:S(2)}) collective-permute-start(bf16[8,24,896]{2,1,0:T(8,128)(2,1)S(1)} %all-to-all-done), channel_id=1, source_target_pairs={{1,0},{2,1},{3,2},{0,3},{5,4},{6,5},{7,6},{4,7},{9,8},{10,9},{11,1... | collective-permute-start | bytes 1032200 | tf_op jit(solution)/shard_map/ppermute | solution.py:286
  93.4 3.2 %fusion.27 = (bf16[384]{0:T(512)(128)(2,1)S(1)}, bf16[512,384]{1,0:T(8,128)(2,1)}, f32[512,384]{1,0:T(8,128)}) fusion(f32[512,384]{1,0:T(8,128)S(1)} %convolution_add_fusion, bf16[512,768]{1,0:T(8,128)(2,1)S(1)} %bitcast.36, bf16[384,768]{1,0:T(8,128)(2,1)S(1)} %reshape.81), kind=kOutput, calls=%fused_computation.79 | convolution fusion | flops 316341888 | bytes 3343104 | tf_op jit(solution)/shard_map/dot_general | solution.py:353
  101.1 4.9 %all-to-all-start.3 = ((bf16[8,64,768]{2,1,0:T(8,128)(2,1)}), bf16[8,64,768]{2,1,0:T(8,128)(2,1)S(1)}, u32[]{:S(2)}, u32[]{:S(2)}) async-start(bf16[8,64,768]{2,1,0:T(8,128)(2,1)} %bitcast.11), calls=%async_computation.3 | async-start | bytes 1572864 | tf_op jit(solution)/shard_map/all_to_all | solution.py:358
  113.7 4.6 %collective-permute-start.10 = (bf16[8,24,896]{2,1,0:T(8,128)(2,1)}, bf16[8,24,896]{2,1,0:T(8,128)(2,1)S(1)}, u32[]{:S(2)}, u32[]{:S(2)}) collective-permute-start(bf16[8,24,896]{2,1,0:T(8,128)(2,1)} %get-tuple-element.41), channel_id=1, source_target_pairs={{0,3},{1,0},{2,1},{3,2},{4,7},{5,4},{6,5},{7,6},{8,11},{9,8},{10,9... | collective-permute-start | bytes 1032200 | tf_op jit(solution)/shard_map/ppermute | solution.py:294
  118.3 2.8 %collective-permute-start.9 = (bf16[8,24,896]{2,1,0:T(8,128)(2,1)}, bf16[8,24,896]{2,1,0:T(8,128)(2,1)}, u32[]{:S(2)}, u32[]{:S(2)}) collective-permute-start(bf16[8,24,896]{2,1,0:T(8,128)(2,1)} %get-tuple-element.42), channel_id=1, source_target_pairs={{0,2},{1,3},{2,0},{3,1},{4,6},{5,7},{6,4},{7,5},{8,10},{9,11},{10,... | collective-permute-start | bytes 1032200 | tf_op jit(solution)/shard_map/ppermute | solution.py:294
  122.3 7.8 %all-to-all-start.4 = ((bf16[32,16,128]{2,1,0:T(8,128)(2,1)}), bf16[32,16,128]{2,1,0:T(8,128)(2,1)S(1)}, u32[]{:S(2)}, u32[]{:S(2)}) async-start(bf16[32,16,128]{2,1,0:T(8,128)(2,1)} %shard_map.197), calls=%async_computation.4 | async-start | bytes 262144 | tf_op jit(solution)/shard_map/all_to_all | solution.py:270
  130.1 4.2 %collective-permute-done.10 = bf16[8,24,896]{2,1,0:T(8,128)(2,1)S(1)} collective-permute-done((bf16[8,24,896]{2,1,0:T(8,128)(2,1)}, bf16[8,24,896]{2,1,0:T(8,128)(2,1)S(1)}, u32[]{:S(2)}, u32[]{:S(2)}) %collective-permute-start.10) | collective-permute-done | bytes 344096 | tf_op jit(solution)/shard_map/ppermute | solution.py:294
  136.2 6.8 %all-to-all-done.4.recv_ref = bf16[32,16,128]{2,1,0:T(8,128)(2,1)S(1)} async-done(((bf16[32,16,128]{2,1,0:T(8,128)(2,1)}), bf16[32,16,128]{2,1,0:T(8,128)(2,1)S(1)}, u32[]{:S(2)}, u32[]{:S(2)}) %all-to-all-start.4) | async-done | bytes 131104 | tf_op jit(solution)/shard_map/all_to_all | solution.py:270
  143.0 5.2 %all-to-all-start.5 = ((bf16[8,24,896]{2,1,0:T(8,128)(2,1)}), bf16[8,24,896]{2,1,0:T(8,128)(2,1)S(1)}, u32[]{:S(2)}, u32[]{:S(2)}) async-start(bf16[8,24,896]{2,1,0:T(8,128)(2,1)} %add_convert_fusion.1), calls=%async_computation.5 | async-start | bytes 688128 | tf_op jit(solution)/shard_map/all_to_all | solution.py:374
  148.2 4.3 %shard_map.198 = (f32[24,8,256]{2,1,0:T(8,128)S(1)}, bf16[2,24,3,256]{3,2,1,0:T(4,128)(2,1)S(1)}, f32[24,56,128]{2,1,0:T(8,128)S(1)}, f32[24,128]{1,0:T(8,128)S(1)}) custom-call(bf16[32,16,128]{2,1,0:T(8,128)(2,1)S(1)} %all-to-all-done.4.recv_ref, bf16[24,8,256]{2,1,0:T(8,128)(2,1)S(1)} %copy-done.1, bf16[24,3,256]{2,1,0:T(4,128)(2,1)S(1)} %collective-permute-done.up_ref, ...), custom_call_target="tpu_custom_call" | custom-call | tf_op jit(solution)/shard_map/pallas_call | solution.py:215
  152.9 14.3 %all-to-all-done.5 = bf16[8,24,896]{2,1,0:T(8,128)(2,1)S(1)} async-done(((bf16[8,24,896]{2,1,0:T(8,128)(2,1)}), bf16[8,24,896]{2,1,0:T(8,128)(2,1)S(1)}, u32[]{:S(2)}, u32[]{:S(2)}) %all-to-all-start.5) | async-done | bytes 344096 | tf_op jit(solution)/shard_map/all_to_all | solution.py:374
  169.3 13.7 %collective-permute-done.11 = bf16[24,1024]{1,0:T(8,128)(2,1)S(1)} collective-permute-done((bf16[24,1024]{1,0:T(8,128)(2,1)S(1)}, bf16[24,1024]{1,0:T(8,128)(2,1)S(1)}, u32[]{:S(2)}, u32[]{:S(2)}) %collective-permute-start.11) | collective-permute-done | bytes 49184 | tf_op jit(solution)/shard_map/ppermute | solution.py:384
  184.0 4.4 %all-to-all-start.6 = ((bf16[8,24,1024]{2,1,0:T(8,128)(2,1)}), bf16[8,24,1024]{2,1,0:T(8,128)(2,1)S(1)}, u32[]{:S(2)}, u32[]{:S(2)}) async-start(bf16[8,24,1024]{2,1,0:T(8,128)(2,1)} %broadcast_in_dim.42), calls=%async_computation.6 | async-start | bytes 786432 | tf_op jit(solution)/shard_map/all_to_all | solution.py:266
  188.4 3.9 %collective-permute-start.7 = (bf16[24,3,256]{2,1,0:T(4,128)(2,1)S(1)}, bf16[24,3,256]{2,1,0:T(4,128)(2,1)S(1)}, u32[]{:S(2)}, u32[]{:S(2)}) collective-permute-start(bf16[24,3,256]{2,1,0:T(4,128)(2,1)S(1)} %get-tuple-element.53), channel_id=1, source_target_pairs={{32,0},{64,32},{96,64},{128,96},{160,128},{192,160},{224,192},{256... | collective-permute-start | bytes 110600 | tf_op jit(solution)/shard_map/ppermute | solution.py:276
  194.3 14.4 %collective-permute-done.6.up_ref = bf16[24,3,256]{2,1,0:T(4,128)(2,1)S(1)} collective-permute-done((bf16[24,3,256]{2,1,0:T(4,128)(2,1)S(1)}, bf16[24,3,256]{2,1,0:T(4,128)(2,1)S(1)}, u32[]{:S(2)}, u32[]{:S(2)}) %collective-permute-start.6) | collective-permute-done | bytes 36896 | tf_op jit(solution)/shard_map/ppermute | solution.py:275
  208.7 5.6 %shard_map.199 = f32[24,8,256]{2,1,0:T(8,128)} custom-call(f32[24,49]{1,0:T(8,128)S(1)} %copy-done.2, f32[24,8,256]{2,1,0:T(8,128)S(1)} %get-tuple-element.24.x_ref, bf16[24,3,256]{2,1,0:T(4,128)(2,1)S(1)} %collective-permute-done.6.up_ref, bf16[24,3,256]{2,1,0:T(4,128)(2,1)S(1)} %collective-permute-done.7.down_ref, bf16[24,8,256]{2,1,0:T(8,128)(2,1)S(1)} %copy-done), custom_call_target="tpu_custom_call" | custom-call | tf_op jit(solution)/shard_map/pallas_call | solution.py:247
  (109 shorter events, 46.5 us)
Async XLA Ops:
  0.7 32.3 %copy-start = (bf16[24,8,256]{2,1,0:T(8,128)(2,1)S(1)}, bf16[24,8,256]{2,1,0:T(8,128)(2,1)}, u32[]{:S(2)}) copy-start(bf16[24,8,256]{2,1,0:T(8,128)(2,1)} %dy_ref.5) | copy-start | bytes 294916
  0.7 32.3 %copy-start.2 = (f32[24,49]{1,0:T(8,128)S(1)}, f32[24,49]{1,0:T(8,128)}, u32[]{:S(2)}) copy-start(f32[24,49]{1,0:T(8,128)} %taps_ref.3) | copy-start | bytes 14116
  0.7 51.2 %copy-start.12 = (f32[768]{0:T(1024)S(1)}, f32[768]{0:T(1024)}, u32[]{:S(2)}) copy-start(f32[768]{0:T(1024)} %param.17) | copy-start | bytes 9220
  0.7 51.2 %copy-start.13 = (f32[768]{0:T(1024)S(1)}, f32[768]{0:T(1024)}, u32[]{:S(2)}) copy-start(f32[768]{0:T(1024)} %param.18) | copy-start | bytes 9220
  3.3 35.6 %all-to-all-start = ((bf16[8,24,896]{2,1,0:T(8,128)(2,1)}), bf16[8,24,896]{2,1,0:T(8,128)(2,1)S(1)}, u32[]{:S(2)}, u32[]{:S(2)}) async-start(bf16[8,24,896]{2,1,0:T(8,128)(2,1)} %broadcast_in_dim.17), calls=%async_computation | async-start | bytes 688128 | tf_op jit(solution)/shard_map/all_to_all | solution.py:266
  9.3 71.4 %copy-start.14 = (bf16[768]{0:T(1024)(128)(2,1)S(1)}, bf16[768]{0:T(1024)(128)(2,1)}, u32[]{:S(2)}) copy-start(bf16[768]{0:T(1024)(128)(2,1)} %param.23) | copy-start | bytes 4612
  9.3 9.4 %collective-permute-start.1 = (bf16[24,3,256]{2,1,0:T(4,128)(2,1)S(1)}, bf16[24,3,256]{2,1,0:T(4,128)(2,1)S(1)}, u32[]{:S(2)}, u32[]{:S(2)}) collective-permute-start(bf16[24,3,256]{2,1,0:T(4,128)(2,1)S(1)} %get-tuple-element.55), channel_id=1, source_target_pairs={{32,0},{64,32},{96,64},{128,96},{160,128},{192,160},{224,192},{256... | collective-permute-start | bytes 110600 | tf_op jit(solution)/shard_map/ppermute | solution.py:276
  16.7 16.2 %collective-permute-start = (bf16[24,3,256]{2,1,0:T(4,128)(2,1)S(1)}, bf16[24,3,256]{2,1,0:T(4,128)(2,1)S(1)}, u32[]{:S(2)}, u32[]{:S(2)}) collective-permute-start(bf16[24,3,256]{2,1,0:T(4,128)(2,1)S(1)} %get-tuple-element.56), channel_id=1, source_target_pairs={{0,32},{32,64},{64,96},{96,128},{128,160},{160,192},{192,224},{224... | collective-permute-start | bytes 110600 | tf_op jit(solution)/shard_map/ppermute | solution.py:275
  38.8 25.8 %all-to-all-start.1 = ((bf16[32,24,128]{2,1,0:T(8,128)(2,1)}), bf16[32,24,128]{2,1,0:T(8,128)(2,1)S(1)}, u32[]{:S(2)}, u32[]{:S(2)}) async-start(bf16[32,24,128]{2,1,0:T(8,128)(2,1)} %shard_map.195), calls=%async_computation.1 | async-start | bytes 393216 | tf_op jit(solution)/shard_map/all_to_all | solution.py:270
  65.7 13.1 %all-to-all-start.2 = ((bf16[4,128,768]{2,1,0:T(8,128)(2,1)}), bf16[4,128,768]{2,1,0:T(8,128)(2,1)S(1)}, u32[]{:S(2)}, u32[]{:S(2)}) async-start(bf16[4,128,768]{2,1,0:T(8,128)(2,1)} %get-tuple-element.20), calls=%async_computation.2 | async-start | bytes 1572864 | tf_op jit(solution)/shard_map/all_to_all | solution.py:343
  69.2 14.0 %collective-permute-start.5 = (bf16[8,24,896]{2,1,0:T(8,128)(2,1)S(1)}, bf16[8,24,896]{2,1,0:T(8,128)(2,1)S(1)}, u32[]{:S(2)}, u32[]{:S(2)}) collective-permute-start(bf16[8,24,896]{2,1,0:T(8,128)(2,1)S(1)} %all-to-all-done), channel_id=1, source_target_pairs={{3,0},{0,1},{1,2},{2,3},{7,4},{4,5},{5,6},{6,7},{11,8},{8,9},{9,10... | collective-permute-start | bytes 1032200 | tf_op jit(solution)/shard_map/ppermute | solution.py:286
  71.4 11.9 %collective-permute-start.4 = (bf16[8,24,896]{2,1,0:T(8,128)(2,1)S(1)}, bf16[8,24,896]{2,1,0:T(8,128)(2,1)S(1)}, u32[]{:S(2)}, u32[]{:S(2)}) collective-permute-start(bf16[8,24,896]{2,1,0:T(8,128)(2,1)S(1)} %all-to-all-done), channel_id=1, source_target_pairs={{2,0},{3,1},{0,2},{1,3},{6,4},{7,5},{4,6},{5,7},{10,8},{11,9},{8,1... | collective-permute-start | bytes 1032200 | tf_op jit(solution)/shard_map/ppermute | solution.py:286
  75.8 10.3 %collective-permute-start.3 = (bf16[8,24,896]{2,1,0:T(8,128)(2,1)S(1)}, bf16[8,24,896]{2,1,0:T(8,128)(2,1)S(1)}, u32[]{:S(2)}, u32[]{:S(2)}) collective-permute-start(bf16[8,24,896]{2,1,0:T(8,128)(2,1)S(1)} %all-to-all-done), channel_id=1, source_target_pairs={{1,0},{2,1},{3,2},{0,3},{5,4},{6,5},{7,6},{4,7},{9,8},{10,9},{11,1... | collective-permute-start | bytes 1032200 | tf_op jit(solution)/shard_map/ppermute | solution.py:286
  78.8 12.2 %collective-permute-start.2 = (bf16[4,128,768]{2,1,0:T(8,128)(2,1)S(1)}, bf16[4,128,768]{2,1,0:T(8,128)(2,1)}, u32[]{:S(2)}, u32[]{:S(2)}) collective-permute-start(bf16[4,128,768]{2,1,0:T(8,128)(2,1)S(1)} %all-to-all-done.2), channel_id=1, source_target_pairs={{0,32},{32,0},{1,33},{33,1},{2,34},{34,2},{3,35},{35,3},{4,36},{36... | collective-permute-start | bytes 2359304 | tf_op jit(solution)/shard_map/ppermute | solution.py:281
  101.1 20.0 %all-to-all-start.3 = ((bf16[8,64,768]{2,1,0:T(8,128)(2,1)}), bf16[8,64,768]{2,1,0:T(8,128)(2,1)S(1)}, u32[]{:S(2)}, u32[]{:S(2)}) async-start(bf16[8,64,768]{2,1,0:T(8,128)(2,1)} %bitcast.11), calls=%async_computation.3 | async-start | bytes 1572864 | tf_op jit(solution)/shard_map/all_to_all | solution.py:358
  111.2 18.9 %collective-permute-start.8 = (bf16[8,24,896]{2,1,0:T(8,128)(2,1)}, bf16[8,24,896]{2,1,0:T(8,128)(2,1)S(1)}, u32[]{:S(2)}, u32[]{:S(2)}) collective-permute-start(bf16[8,24,896]{2,1,0:T(8,128)(2,1)} %get-tuple-element.40), channel_id=1, source_target_pairs={{0,1},{1,2},{2,3},{3,0},{4,5},{5,6},{6,7},{7,4},{8,9},{9,10},{10,1... | collective-permute-start | bytes 1032200 | tf_op jit(solution)/shard_map/ppermute | solution.py:294
  113.7 20.6 %collective-permute-start.10 = (bf16[8,24,896]{2,1,0:T(8,128)(2,1)}, bf16[8,24,896]{2,1,0:T(8,128)(2,1)S(1)}, u32[]{:S(2)}, u32[]{:S(2)}) collective-permute-start(bf16[8,24,896]{2,1,0:T(8,128)(2,1)} %get-tuple-element.41), channel_id=1, source_target_pairs={{0,3},{1,0},{2,1},{3,2},{4,7},{5,4},{6,5},{7,6},{8,11},{9,8},{10,9... | collective-permute-start | bytes 1032200 | tf_op jit(solution)/shard_map/ppermute | solution.py:294
  118.3 16.0 %collective-permute-start.9 = (bf16[8,24,896]{2,1,0:T(8,128)(2,1)}, bf16[8,24,896]{2,1,0:T(8,128)(2,1)}, u32[]{:S(2)}, u32[]{:S(2)}) collective-permute-start(bf16[8,24,896]{2,1,0:T(8,128)(2,1)} %get-tuple-element.42), channel_id=1, source_target_pairs={{0,2},{1,3},{2,0},{3,1},{4,6},{5,7},{6,4},{7,5},{8,10},{9,11},{10,... | collective-permute-start | bytes 1032200 | tf_op jit(solution)/shard_map/ppermute | solution.py:294
  122.3 20.7 %all-to-all-start.4 = ((bf16[32,16,128]{2,1,0:T(8,128)(2,1)}), bf16[32,16,128]{2,1,0:T(8,128)(2,1)S(1)}, u32[]{:S(2)}, u32[]{:S(2)}) async-start(bf16[32,16,128]{2,1,0:T(8,128)(2,1)} %shard_map.197), calls=%async_computation.4 | async-start | bytes 262144 | tf_op jit(solution)/shard_map/all_to_all | solution.py:270
  143.0 24.2 %all-to-all-start.5 = ((bf16[8,24,896]{2,1,0:T(8,128)(2,1)}), bf16[8,24,896]{2,1,0:T(8,128)(2,1)S(1)}, u32[]{:S(2)}, u32[]{:S(2)}) async-start(bf16[8,24,896]{2,1,0:T(8,128)(2,1)} %add_convert_fusion.1), calls=%async_computation.5 | async-start | bytes 688128 | tf_op jit(solution)/shard_map/all_to_all | solution.py:374
  167.4 15.7 %collective-permute-start.11 = (bf16[24,1024]{1,0:T(8,128)(2,1)S(1)}, bf16[24,1024]{1,0:T(8,128)(2,1)S(1)}, u32[]{:S(2)}, u32[]{:S(2)}) collective-permute-start(bf16[24,1024]{1,0:T(8,128)(2,1)S(1)} %pad_maximum_fusion.1), channel_id=1, source_target_pairs={{0,256},{256,0},{1,257},{257,1},{2,258},{258,2},{3,259},{259,3},{4... | collective-permute-start | bytes 147464 | tf_op jit(solution)/shard_map/ppermute | solution.py:384
  184.0 30.2 %all-to-all-start.6 = ((bf16[8,24,1024]{2,1,0:T(8,128)(2,1)}), bf16[8,24,1024]{2,1,0:T(8,128)(2,1)S(1)}, u32[]{:S(2)}, u32[]{:S(2)}) async-start(bf16[8,24,1024]{2,1,0:T(8,128)(2,1)} %broadcast_in_dim.42), calls=%async_computation.6 | async-start | bytes 786432 | tf_op jit(solution)/shard_map/all_to_all | solution.py:266
  188.4 5.9 %collective-permute-start.7 = (bf16[24,3,256]{2,1,0:T(4,128)(2,1)S(1)}, bf16[24,3,256]{2,1,0:T(4,128)(2,1)S(1)}, u32[]{:S(2)}, u32[]{:S(2)}) collective-permute-start(bf16[24,3,256]{2,1,0:T(4,128)(2,1)S(1)} %get-tuple-element.53), channel_id=1, source_target_pairs={{32,0},{64,32},{96,64},{128,96},{160,128},{192,160},{224,192},{256... | collective-permute-start | bytes 110600 | tf_op jit(solution)/shard_map/ppermute | solution.py:276
  192.4 16.3 %collective-permute-start.6 = (bf16[24,3,256]{2,1,0:T(4,128)(2,1)S(1)}, bf16[24,3,256]{2,1,0:T(4,128)(2,1)S(1)}, u32[]{:S(2)}, u32[]{:S(2)}) collective-permute-start(bf16[24,3,256]{2,1,0:T(4,128)(2,1)S(1)} %get-tuple-element.54), channel_id=1, source_target_pairs={{0,32},{32,64},{64,96},{96,128},{128,160},{160,192},{192,224},{224... | collective-permute-start | bytes 110600 | tf_op jit(solution)/shard_map/ppermute | solution.py:275
  (12 other events, 76.6 us)

commit v4 on v3

--- a/solution.py
+++ b/solution.py
@@ -1,3 +1,5 @@
+import functools
+
 import jax
 import jax.numpy as jnp
 from jax import lax
@@ -252,8 +254,108 @@
     )(taps, dconv, up, down, dy)
 
 
-def gelu_exact(value):
-    return jax.nn.gelu(value, approximate=False)
+def picks(blocks, part):
+    shape = (blocks * 2 * part, blocks * part)
+    row = lax.broadcasted_iota(jnp.int32, shape, 0)
+    place = lax.broadcasted_iota(jnp.int32, shape, 1)
+    block = jnp.floor((row.astype(F32) + 0.5) * (0.5 / part)).astype(jnp.int32)
+    inside = row - block * 2 * part
+    first = (inside < part) & (place == block * part + inside)
+    second = (inside >= part) & (place == block * part + inside - part)
+    return [jnp.where(m, 1.0, 0.0).astype(BF) for m in (first, second)]
+
+
+def dot(a, b, a_dim, b_dim):
+    return lax.dot_general(a, b, (((a_dim,), (b_dim,)), ((), ())), preferred_element_type=F32)
+
+
+def weights_body(part, own_ref, one_ref, two_ref, three_ref, wi_ref, wo_ref, bi_ref, rows):
+    blocks = 0
+    for ref in (own_ref, one_ref, two_ref, three_ref):
+        for k in range(ref.shape[0]):
+            at = blocks * 2 * part
+            rows[at : at + 2 * part] = ref[k].astype(F32)
+            blocks += 1
+    chans = wi_ref.shape[1]
+    flat = rows[...].astype(BF)
+    first, second = picks(blocks, part)
+    wi_ref[...] = dot(first, flat[:, :chans], 0, 0).astype(BF)
+    wo_ref[...] = dot(second, flat[:, :chans], 0, 0).astype(BF)
+    both = dot(flat[:, chans:], first, 0, 0)
+    bi_ref[...] = both[:1] + both[1:2]
+
+
+def weights(parts, part, chans):
+    blocks = sum(p.shape[0] for p in parts)
+    return call(
+        functools.partial(weights_body, part),
+        [
+            jax.ShapeDtypeStruct((blocks * part, chans), BF),
+            jax.ShapeDtypeStruct((blocks * part, chans), BF),
+            jax.ShapeDtypeStruct((1, blocks * part), F32),
+        ],
+        [vmem()] * 4,
+        [pltpu.VMEM((blocks * 2 * part, parts[0].shape[2]), F32)],
+    )(*parts)
+
+
+def mlp_body(core_ref, own_ref, other_ref, wi_ref, wo_ref, bi_ref, gamma_ref, dn_ref, n_ref, dy_ref, g_ref, dpre_ref):
+    members, lanes, _ = own_ref.shape
+    piece = lanes // 2
+    for at, ref in ((0, own_ref), (members, other_ref)):
+        for k in range(members):
+            n_ref[(at + k) * piece : (at + k + 1) * piece] = ref[k, :piece]
+            dy_ref[(at + k) * piece : (at + k + 1) * piece] = ref[k, piece:]
+    pre = dot(n_ref[...], wi_ref[...], 1, 1) + bi_ref[...]
+    cdf = 0.5 + 0.5 * lax.erf(pre * (0.5**0.5))
+    g_ref[...] = (pre * cdf).astype(BF)
+    slope = cdf + pre * (jnp.exp(-0.5 * pre * pre) * (0.5 / 3.141592653589793) ** 0.5)
+    dmlp = (gamma_ref[...] * dy_ref[...].astype(F32)).astype(BF)
+    dpre = (slope * dot(dmlp, wo_ref[...], 1, 1)).astype(BF)
+    dpre_ref[...] = dpre
+    dn = dot(dpre, wi_ref[...], 1, 0).astype(BF)
+    core = core_ref[0]
+    for k in range(members):
+        dn_ref[core * members + k] = dn[k * piece : (k + 1) * piece]
+        dn_ref[(1 - core) * members + k] = dn[(members + k) * piece : (members + k + 1) * piece]
+
+
+def mlp(core, own, other, wi, wo, bi, gamma):
+    members, lanes, chans = own.shape
+    toks, hid = members * lanes, wi.shape[0]
+    return call(
+        mlp_body,
+        [
+            jax.ShapeDtypeStruct((2 * members, lanes // 2, chans), BF),
+            jax.ShapeDtypeStruct((toks, chans), BF),
+            jax.ShapeDtypeStruct((toks, chans), BF),
+            jax.ShapeDtypeStruct((toks, hid), BF),
+            jax.ShapeDtypeStruct((toks, hid), BF),
+        ],
+        [smem()] + [vmem()] * 6,
+    )(core, own, other, wi, wo, bi, gamma[None])
+
+
+def grads_body(part, n_ref, dy_ref, g_ref, dpre_ref, wo_ref, gamma_ref, out_ref, gam_ref):
+    toks, chans = n_ref.shape
+    hid = g_ref.shape[1]
+    first, second = picks(hid // part, part)
+    dw_in = dot(dpre_ref[...], n_ref[...], 0, 0).astype(BF)
+    proj = dot(g_ref[...], dy_ref[...], 0, 0)
+    gam_ref[...] = jnp.sum(wo_ref[...].astype(F32) * proj, 0, keepdims=True)
+    dw_out = (proj * gamma_ref[...]).astype(BF)
+    out_ref[:, :chans] = (dot(first, dw_in, 1, 0) + dot(second, dw_out, 1, 0)).astype(BF)
+    ones = jnp.ones((toks, out_ref.shape[1] - chans), BF)
+    out_ref[:, chans:] = dot(first, dot(dpre_ref[...], ones, 0, 0).astype(BF), 1, 0).astype(BF)
+
+
+def grads(part, side, n, dy, g, dpre, wo, gamma):
+    toks, chans = n.shape
+    return call(
+        functools.partial(grads_body, part),
+        [jax.ShapeDtypeStruct((2 * g.shape[1], chans + side), BF), jax.ShapeDtypeStruct((1, chans), F32)],
+        [vmem()] * 6,
+    )(n, dy, g, dpre, wo, gamma[None])
 
 
 def two_parts(value):
@@ -271,20 +373,20 @@
 
 
 def halos(first, last):
-    ends = lax.axis_size(LAT) - 1
-    up = lax.ppermute(last, LAT, [(i, i + 1) for i in range(ends)])
-    down = lax.ppermute(first, LAT, [(i + 1, i) for i in range(ends)])
-    return up, down
-
-
-def with_other_core(block):
-    return jnp.concatenate([block, lax.ppermute(block, "c", [(0, 1), (1, 0)])], 0)
+    count = lax.axis_size(LAT)
+    place = lax.axis_index(LAT)
+    even = place % 2 == 0
+    pairs = [(i, i + 1) for i in range(0, count, 2)]
+    within = lax.ppermute(jnp.where(even, last, first), LAT, pairs + [(j, i) for i, j in pairs])
+    pairs = [(i, i + 1) for i in range(1, count - 1, 2)]
+    across = lax.ppermute(jnp.where(even, first, last), LAT, pairs + [(j, i) for i, j in pairs])
+    return jnp.where(even, across, within), jnp.where(even, within, across)
 
 
 def from_ring(block):
     count = lax.axis_size("y")
     ahead = [lax.ppermute(block, "y", [((i + k) % count, i) for i in range(count)]) for k in range(1, count)]
-    return jnp.stack([block] + ahead, 0)
+    return [block] + ahead
 
 
 def to_ring(blocks):
@@ -316,7 +418,6 @@
     nchan = nz * ny
     hdev = w_in.shape[0]
     part = hdev // GROUP
-    hid = part * nchan
     piece = tokens // nchan
     member = lax.axis_index(("x", "c"))
     owner = lax.axis_index(CHAN)
@@ -333,51 +434,27 @@
     blocks = forward(kernel, conv_bias, block_input, up, down, metric, out_grad)
     blocks, shards = lax.optimization_barrier((blocks, shards))
 
-    shards = from_ring(shards).reshape(nchan, 2 * part, chans + SIDE)
-    wi = shards[:, :part, :chans].reshape(hid, chans)
-    wo = shards[:, part:, :chans].reshape(hid, chans)
-    bi = jnp.sum(shards[:, :part, chans : chans + 2].astype(F32), 2).reshape(hid)
-
-    recv = exchange(blocks).reshape(chans, 2 * piece)
+    recv = exchange(blocks)
+    wi, wo, bi = weights(from_ring(shards), part, chans)
+
+    recv, wi, wo, bi = lax.optimization_barrier((recv, wi, wo, bi))
+    recv = recv.reshape(chans, 2 * piece)
     pair, nhat, rstd = norm(recv, ln_gain, ln_bias, GROUP // 2)
-    pair = with_other_core(lax.all_to_all(pair, "x", 0, 0, tiled=True))
-    n = pair[:, :piece].reshape(GROUP * piece, chans)
-    dy = pair[:, piece:].reshape(GROUP * piece, chans)
-
-    over_last = (((1,), (1,)), ((), ()))
-    over_first = (((0,), (0,)), ((), ()))
-    pre = lax.dot_general(n, wi, over_last, preferred_element_type=F32) + bi
-    g, back = jax.vjp(gelu_exact, pre)
-    g_b = g.astype(BF)
-    dmlp = (gamma_f * dy.astype(F32)).astype(BF)
-    grad_g = lax.dot_general(dmlp, wo, over_last, preferred_element_type=F32)
-    dpre = back(grad_g)[0].astype(BF)
-    turned = jnp.roll(dpre, dpre.shape[0] // 2, 0)
-    ordered = jnp.where(lax.axis_index("c") == 0, dpre, turned)
-    dn = jnp.dot(ordered, wi, preferred_element_type=F32).astype(BF)
-    dn = lax.all_to_all(dn.reshape(GROUP, piece, chans), ("c", "x"), 0, 0, tiled=True)
-    dw_in = lax.dot_general(dpre, n, over_first, preferred_element_type=F32)
-    proj = lax.dot_general(g_b, dy, over_first, preferred_element_type=F32)
-    db_in = jnp.sum(dpre.astype(F32), 0)
-    gam_part = jnp.sum(wo.astype(F32) * proj, 0)
-    dw_out = proj * gamma_f
-
-    side = jnp.broadcast_to(db_in.astype(BF).reshape(nchan, part, 1), (nchan, part, SIDE))
-    dws = jnp.concatenate(
-        [
-            jnp.concatenate([dw_in.astype(BF).reshape(nchan, part, chans), side], 2),
-            jnp.pad(dw_out.astype(BF).reshape(nchan, part, chans), ((0, 0), (0, 0), (0, SIDE))),
-        ],
-        1,
-    )
+    pair = lax.all_to_all(pair, "x", 0, 0, tiled=True)
+    other = lax.ppermute(pair, "c", [(0, 1), (1, 0)])
+
+    core = lax.axis_index("c").astype(jnp.int32)[None]
+    dn, n, dy, g, dpre = mlp(core, pair, other, wi, wo, bi, gamma_f)
+    dn = lax.all_to_all(dn, ("c", "x"), 0, 0, tiled=True)
+
+    dws, gam_part = grads(part, SIDE, n, dy, g, dpre, wo, gamma_f)
     dws = to_ring(dws.reshape(ny, nz, 2 * part, chans + SIDE)).astype(BF)
     dws = lax.all_to_all(dws, "zl", 0, 0, tiled=True)
     dws = jnp.sum(dws.astype(F32), 0)
 
-    payload = exchange(norm_back(dn, nhat, rstd, ln_gain, gam_part, nchan))
+    payload = exchange(norm_back(dn, nhat, rstd, ln_gain, gam_part[0], nchan))
     dconv, ends, taps, extra = tap_sums(payload, block_input, up, down, metric, out_grad)
     dup, ddown = halos(ends[0], ends[1])
-    grad_input = spread_back(kernel, dconv, dup, ddown, out_grad)
 
     small = jnp.concatenate([jnp.sum(taps, 2), extra[:, :8]], 1)
     mine = jnp.concatenate([dws.astype(BF)] + list(two_parts(small)), 1)
@@ -387,6 +464,8 @@
     dws = dws + other[:, :wide]
     small = small + other[:, wide : wide + count] + other[:, wide + count :]
     mine = jnp.concatenate([dws.astype(BF)] + list(two_parts(small)), 1)
+    mine, dup, ddown = lax.optimization_barrier((mine, dup, ddown))
+    grad_input = spread_back(kernel, dconv, dup, ddown, out_grad)
     gathered = to_all(mine, ("x", "c")).astype(F32)
     grad_w_in = gathered[:, :part, :chans].reshape(hdev, chans)
     grad_w_out = gathered[:, part:, :chans].reshape(hdev, chans)

time: 219 us -> 202 us (0.922)
  the two profiles are of different devices: /device:TPU:288 before, /device:TPU:1 now
where the time goes in v4:
time: 202 us; the launch traced here: 201 us
  starting transfers between devices  95.3 us (47%)
  waiting for transfers between devices  48 us (24%)
  Pallas kernels  23.6 us (12%)
  blocking collectives  18.8 us (9%)
  local copies, waits for them, and re-layouts  10.2 us (5%)
  other arithmetic  4.11 us (2%)
    all_to_all x2, starting transfers between devices, to_all(): lax.all_to_all(jnp.broadcast_to(block[None], (count,) + block.shape), axi...  23.9 us
    all_to_all x2, starting transfers between devices, exchange(): return lax.all_to_all(blocks, CHAN, 0, 0, tiled=True)  23.2 us
    all_to_all x1, blocking collectives, per_device(): pair = lax.all_to_all(pair, 'x', 0, 0, tiled=True)  18.8 us
    ppermute x3, waiting for transfers between devices, from_ring(): lax.ppermute(block, 'y', [((i + k) % count, i) for i in range(count)])  16.8 us
    all_to_all x2, waiting for transfers between devices, exchange(): return lax.all_to_all(blocks, CHAN, 0, 0, tiled=True)  9.9 us
    ppermute x3, starting transfers between devices, from_ring(): lax.ppermute(block, 'y', [((i + k) % count, i) for i in range(count)])  9.32 us
    ppermute x2, starting transfers between devices, halos(): lax.ppermute(jnp.where(even, first, last), LAT, pairs + [(j, i) for i, j...  8.71 us
    ppermute x3, starting transfers between devices, to_ring(): lax.ppermute(blocks[k], 'y', [(i, (i + k) % count) for i in range(count)])  8.41 us
  transfers between devices with their start and end apart: 18, of which 11 were waited for; matrix products, arithmetic and copies ran while one was open for 1% of the time, Pallas kernels for 10%

profile of v4, /device:TPU:1, one launch (start us, length us, event | category | flops | bytes accessed | tf_op | source)
XLA Modules:
  0.0 201.1 jit_solution(8848200145043682001)
XLA Ops:
  3.3 13.1 %all-to-all-start = ((bf16[8,24,896]{2,1,0:T(8,128)(2,1)}), bf16[8,24,896]{2,1,0:T(8,128)(2,1)S(1)}, u32[]{:S(2)}, u32[]{:S(2)}) async-start(bf16[8,24,896]{2,1,0:T(8,128)(2,1)} %broadcast_in_dim.32), calls=%async_computation | async-start | bytes 688128 | tf_op jit(solution)/shard_map/all_to_all | solution.py:368
  16.4 4.0 %collective-permute-start = (bf16[24,3,256]{2,1,0:T(4,128)(2,1)S(1)}, bf16[24,3,256]{2,1,0:T(4,128)(2,1)S(1)}, u32[]{:S(2)}, u32[]{:S(2)}) collective-permute-start(bf16[24,3,256]{2,1,0:T(4,128)(2,1)S(1)} %get-tuple-element.84), channel_id=1, source_target_pairs={{32,64},{96,128},{160,192},{224,256},{288,320},{352,384},{416,448}... | collective-permute-start | bytes 110600 | tf_op jit(solution)/shard_map/ppermute | solution.py:382
  23.6 5.8 %shard_map.195 = bf16[32,24,128]{2,1,0:T(8,128)(2,1)} custom-call(f32[24,49]{1,0:T(8,128)S(1)} %copy-done.8, f32[24]{0:T(128)S(1)} %copy-done.9, bf16[24,8,256]{2,1,0:T(8,128)(2,1)S(1)} %copy-done.1, bf16[24,3,256]{2,1,0:T(4,128)(2,1)S(1)} %get-tuple-element.82.up_ref, bf16[24,3,256]{2,1,0:T(4,128)(2,1)S(1)} %get-tuple-element.81.down_ref, ...), custom_call_target="tpu_custom_call" | custom-call | tf_op jit(solution)/shard_map/pallas_call | solution.py:94
  29.4 3.1 %all-to-all-done.own_ref = bf16[8,24,896]{2,1,0:T(8,128)(2,1)S(1)} async-done(((bf16[8,24,896]{2,1,0:T(8,128)(2,1)}), bf16[8,24,896]{2,1,0:T(8,128)(2,1)S(1)}, u32[]{:S(2)}, u32[]{:S(2)}) %all-to-all-start) | async-done | bytes 344096 | tf_op jit(solution)/shard_map/all_to_all | solution.py:368
  32.5 11.6 %all-to-all-start.1 = ((bf16[32,24,128]{2,1,0:T(8,128)(2,1)}), bf16[32,24,128]{2,1,0:T(8,128)(2,1)S(1)}, u32[]{:S(2)}, u32[]{:S(2)}) async-start(bf16[32,24,128]{2,1,0:T(8,128)(2,1)} %shard_map.195), calls=%async_computation.1 | async-start | bytes 393216 | tf_op jit(solution)/shard_map/all_to_all | solution.py:372
  44.1 4.3 %collective-permute-start.2 = (bf16[8,24,896]{2,1,0:T(8,128)(2,1)S(1)}, bf16[8,24,896]{2,1,0:T(8,128)(2,1)S(1)}, u32[]{:S(2)}, u32[]{:S(2)}) collective-permute-start(bf16[8,24,896]{2,1,0:T(8,128)(2,1)S(1)} %all-to-all-done.own_ref), channel_id=1, source_target_pairs={{1,0},{2,1},{3,2},{0,3},{5,4},{6,5},{7,6},{4,7},{9,8},{10,9},{11,1... | collective-permute-start | bytes 1032200 | tf_op jit(solution)/shard_map/ppermute | solution.py:388
  50.9 2.5 %collective-permute-start.4 = (bf16[8,24,896]{2,1,0:T(8,128)(2,1)S(1)}, bf16[8,24,896]{2,1,0:T(8,128)(2,1)S(1)}, u32[]{:S(2)}, u32[]{:S(2)}) collective-permute-start(bf16[8,24,896]{2,1,0:T(8,128)(2,1)S(1)} %all-to-all-done.own_ref), channel_id=1, source_target_pairs={{3,0},{0,1},{1,2},{2,3},{7,4},{4,5},{5,6},{6,7},{11,8},{8,9},{9,10... | collective-permute-start | bytes 1032200 | tf_op jit(solution)/shard_map/ppermute | solution.py:388
  55.7 5.2 %collective-permute-done.3.two_ref = bf16[8,24,896]{2,1,0:T(8,128)(2,1)S(1)} collective-permute-done((bf16[8,24,896]{2,1,0:T(8,128)(2,1)S(1)}, bf16[8,24,896]{2,1,0:T(8,128)(2,1)S(1)}, u32[]{:S(2)}, u32[]{:S(2)}) %collective-permute-start.3) | collective-permute-done | bytes 344096 | tf_op jit(solution)/shard_map/ppermute | solution.py:388
  60.9 9.4 %collective-permute-done.4.three_ref = bf16[8,24,896]{2,1,0:T(8,128)(2,1)S(1)} collective-permute-done((bf16[8,24,896]{2,1,0:T(8,128)(2,1)S(1)}, bf16[8,24,896]{2,1,0:T(8,128)(2,1)S(1)}, u32[]{:S(2)}, u32[]{:S(2)}) %collective-permute-start.4) | collective-permute-done | bytes 344096 | tf_op jit(solution)/shard_map/ppermute | solution.py:388
  72.7 18.8 %all_to_all.35.own_ref = bf16[4,128,768]{2,1,0:T(8,128)(2,1)S(1)} all-to-all(bf16[4,128,768]{2,1,0:T(8,128)(2,1)S(1)} %get-tuple-element.42), channel_id=1, replica_groups=mesh['zh'=2,'x'=4,'c'=2,'zl'=8,'y'=4] {'x'}, dimensions={0} | all-to-all | bytes 1572864 | tf_op jit(solution)/shard_map/all_to_all | solution.py:443
  99.7 3.6 %all-to-all-start.3 = ((bf16[8,64,768]{2,1,0:T(8,128)(2,1)}), bf16[8,64,768]{2,1,0:T(8,128)(2,1)S(1)}, u32[]{:S(2)}, u32[]{:S(2)}) async-start(bf16[8,64,768]{2,1,0:T(8,128)(2,1)} %get-tuple-element.46), calls=%async_computation.3 | async-start | bytes 1572864 | tf_op jit(solution)/shard_map/all_to_all | solution.py:448
  105.3 2.6 %shard_map.199 = (bf16[768,896]{1,0:T(8,128)(2,1)S(1)}, f32[1,768]{1,0:T(1,128)S(1)}) custom-call(bf16[512,768]{1,0:T(8,128)(2,1)S(1)} %get-tuple-element.49.n_ref, bf16[512,768]{1,0:T(8,128)(2,1)S(1)} %get-tuple-element.50.dy_ref, bf16[512,384]{1,0:T(8,128)(2,1)S(1)} %copy-done.5, bf16[512,384]{1,0:T(8,128)(2,1)S(1)} %copy-done.7, ...), custom_call_target="tpu_custom_call" | custom-call | tf_op jit(solution)/shard_map/pallas_call | solution.py:354
  113.1 4.3 %collective-permute-start.8 = (bf16[8,24,896]{2,1,0:T(8,128)(2,1)S(1)}, bf16[8,24,896]{2,1,0:T(8,128)(2,1)S(1)}, u32[]{:S(2)}, u32[]{:S(2)}) collective-permute-start(bf16[8,24,896]{2,1,0:T(8,128)(2,1)S(1)} %bitcast.22), channel_id=1, source_target_pairs={{0,3},{1,0},{2,1},{3,2},{4,7},{5,4},{6,5},{7,6},{8,11},{9,8},{10,9... | collective-permute-start | bytes 1032200 | tf_op jit(solution)/shard_map/ppermute | solution.py:396
  118.5 11.6 %all-to-all-start.4 = ((bf16[32,16,128]{2,1,0:T(8,128)(2,1)}), bf16[32,16,128]{2,1,0:T(8,128)(2,1)S(1)}, u32[]{:S(2)}, u32[]{:S(2)}) async-start(bf16[32,16,128]{2,1,0:T(8,128)(2,1)} %shard_map.200), calls=%async_computation.4 | async-start | bytes 262144 | tf_op jit(solution)/shard_map/all_to_all | solution.py:372
  132.4 9.9 %all-to-all-done.4.recv_ref = bf16[32,16,128]{2,1,0:T(8,128)(2,1)S(1)} async-done(((bf16[32,16,128]{2,1,0:T(8,128)(2,1)}), bf16[32,16,128]{2,1,0:T(8,128)(2,1)S(1)}, u32[]{:S(2)}, u32[]{:S(2)}) %all-to-all-start.4) | async-done | bytes 131104 | tf_op jit(solution)/shard_map/all_to_all | solution.py:372
  142.3 5.3 %all-to-all-start.5 = ((bf16[8,24,896]{2,1,0:T(8,128)(2,1)}), bf16[8,24,896]{2,1,0:T(8,128)(2,1)S(1)}, u32[]{:S(2)}, u32[]{:S(2)}) async-start(bf16[8,24,896]{2,1,0:T(8,128)(2,1)} %fusion.2), calls=%async_computation.5 | async-start | bytes 688128 | tf_op jit(solution)/shard_map/all_to_all | solution.py:452
  147.6 4.3 %shard_map.201 = (f32[24,8,256]{2,1,0:T(8,128)S(1)}, bf16[2,24,3,256]{3,2,1,0:T(4,128)(2,1)S(1)}, f32[24,56,128]{2,1,0:T(8,128)S(1)}, f32[24,128]{1,0:T(8,128)S(1)}) custom-call(bf16[32,16,128]{2,1,0:T(8,128)(2,1)S(1)} %all-to-all-done.4.recv_ref, bf16[24,8,256]{2,1,0:T(8,128)(2,1)S(1)} %copy-done.1, bf16[24,3,256]{2,1,0:T(4,128)(2,1)S(1)} %get-tuple-element.82.up_ref, ...), custom_call_target="tpu_custom_call" | custom-call | tf_op jit(solution)/shard_map/pallas_call | solution.py:217
  151.9 4.7 %collective-permute-start.10 = (bf16[24,3,256]{2,1,0:T(4,128)(2,1)S(1)}, bf16[24,3,256]{2,1,0:T(4,128)(2,1)S(1)}, u32[]{:S(2)}, u32[]{:S(2)}) collective-permute-start(bf16[24,3,256]{2,1,0:T(4,128)(2,1)S(1)} %get-tuple-element.80), channel_id=1, source_target_pairs={{32,64},{96,128},{160,192},{224,256},{288,320},{352,384},{416,448}... | collective-permute-start | bytes 110600 | tf_op jit(solution)/shard_map/ppermute | solution.py:382
  159.0 4.7 %all-to-all-done.5 = bf16[8,24,896]{2,1,0:T(8,128)(2,1)S(1)} async-done(((bf16[8,24,896]{2,1,0:T(8,128)(2,1)}), bf16[8,24,896]{2,1,0:T(8,128)(2,1)S(1)}, u32[]{:S(2)}, u32[]{:S(2)}) %all-to-all-start.5) | async-done | bytes 344096 | tf_op jit(solution)/shard_map/all_to_all | solution.py:452
  163.8 7.2 %collective-permute-start.9 = (bf16[24,1024]{1,0:T(8,128)(2,1)S(1)}, bf16[24,1024]{1,0:T(8,128)(2,1)S(1)}, u32[]{:S(2)}, u32[]{:S(2)}) collective-permute-start(bf16[24,1024]{1,0:T(8,128)(2,1)S(1)} %pad_maximum_fusion), channel_id=1, source_target_pairs={{0,256},{256,0},{1,257},{257,1},{2,258},{258,2},{3,259},{259,3},{4... | collective-permute-start | bytes 147464 | tf_op jit(solution)/shard_map/ppermute | solution.py:461
  171.1 6.4 %collective-permute-done.9 = bf16[24,1024]{1,0:T(8,128)(2,1)S(1)} collective-permute-done((bf16[24,1024]{1,0:T(8,128)(2,1)S(1)}, bf16[24,1024]{1,0:T(8,128)(2,1)S(1)}, u32[]{:S(2)}, u32[]{:S(2)}) %collective-permute-start.9) | collective-permute-done | bytes 49184 | tf_op jit(solution)/shard_map/ppermute | solution.py:461
  178.4 10.8 %all-to-all-start.6 = ((bf16[8,24,1024]{2,1,0:T(8,128)(2,1)}), bf16[8,24,1024]{2,1,0:T(8,128)(2,1)S(1)}, u32[]{:S(2)}, u32[]{:S(2)}) async-start(bf16[8,24,1024]{2,1,0:T(8,128)(2,1)} %broadcast_in_dim.36), calls=%async_computation.6 | async-start | bytes 786432 | tf_op jit(solution)/shard_map/all_to_all | solution.py:368
  189.2 5.6 %shard_map.202 = f32[24,8,256]{2,1,0:T(8,128)} custom-call(f32[24,49]{1,0:T(8,128)S(1)} %copy-done.8, f32[24,8,256]{2,1,0:T(8,128)S(1)} %get-tuple-element.54.x_ref, bf16[24,3,256]{2,1,0:T(4,128)(2,1)S(1)} %get-tuple-element.59.up_ref, bf16[24,3,256]{2,1,0:T(4,128)(2,1)S(1)} %get-tuple-element.60.down_ref, bf16[24,8,256]{2,1,0:T(8,128)(2,1)S(1)} %copy-done), custom_call_target="tpu_custom_call" | custom-call | tf_op jit(solution)/shard_map/pallas_call | solution.py:249
  194.8 2.5 %all-to-all-done.6 = bf16[8,24,1024]{2,1,0:T(8,128)(2,1)S(1)} async-done(((bf16[8,24,1024]{2,1,0:T(8,128)(2,1)}), bf16[8,24,1024]{2,1,0:T(8,128)(2,1)S(1)}, u32[]{:S(2)}, u32[]{:S(2)}) %all-to-all-start.6) | async-done | bytes 393248 | tf_op jit(solution)/shard_map/all_to_all | solution.py:368
  (90 shorter events, 38.7 us)
Async XLA Ops:
  0.7 22.9 %copy-start = (bf16[24,8,256]{2,1,0:T(8,128)(2,1)S(1)}, bf16[24,8,256]{2,1,0:T(8,128)(2,1)}, u32[]{:S(2)}) copy-start(bf16[24,8,256]{2,1,0:T(8,128)(2,1)} %dy_ref.5) | copy-start | bytes 294916
  0.7 22.9 %copy-start.8 = (f32[24,49]{1,0:T(8,128)S(1)}, f32[24,49]{1,0:T(8,128)}, u32[]{:S(2)}) copy-start(f32[24,49]{1,0:T(8,128)} %taps_ref.3) | copy-start | bytes 14116
  0.7 52.7 %copy-start.12 = (f32[768]{0:T(1024)S(1)}, f32[768]{0:T(1024)}, u32[]{:S(2)}) copy-start(f32[768]{0:T(1024)} %param.17) | copy-start | bytes 9220
  0.7 52.8 %copy-start.13 = (f32[768]{0:T(1024)S(1)}, f32[768]{0:T(1024)}, u32[]{:S(2)}) copy-start(f32[768]{0:T(1024)} %param.18) | copy-start | bytes 9220
  3.3 29.2 %all-to-all-start = ((bf16[8,24,896]{2,1,0:T(8,128)(2,1)}), bf16[8,24,896]{2,1,0:T(8,128)(2,1)S(1)}, u32[]{:S(2)}, u32[]{:S(2)}) async-start(bf16[8,24,896]{2,1,0:T(8,128)(2,1)} %broadcast_in_dim.32), calls=%async_computation | async-start | bytes 688128 | tf_op jit(solution)/shard_map/all_to_all | solution.py:368
  16.4 6.0 %collective-permute-start = (bf16[24,3,256]{2,1,0:T(4,128)(2,1)S(1)}, bf16[24,3,256]{2,1,0:T(4,128)(2,1)S(1)}, u32[]{:S(2)}, u32[]{:S(2)}) collective-permute-start(bf16[24,3,256]{2,1,0:T(4,128)(2,1)S(1)} %get-tuple-element.84), channel_id=1, source_target_pairs={{32,64},{96,128},{160,192},{224,256},{288,320},{352,384},{416,448}... | collective-permute-start | bytes 110600 | tf_op jit(solution)/shard_map/ppermute | solution.py:382
  20.4 3.1 %collective-permute-start.1 = (bf16[24,3,256]{2,1,0:T(4,128)(2,1)S(1)}, bf16[24,3,256]{2,1,0:T(4,128)(2,1)S(1)}, u32[]{:S(2)}, u32[]{:S(2)}) collective-permute-start(bf16[24,3,256]{2,1,0:T(4,128)(2,1)S(1)} %get-tuple-element.83), channel_id=1, source_target_pairs={{0,32},{64,96},{128,160},{192,224},{256,288},{320,352},{384,416},{... | collective-permute-start | bytes 110600 | tf_op jit(solution)/shard_map/ppermute | solution.py:380
  32.5 40.0 %all-to-all-start.1 = ((bf16[32,24,128]{2,1,0:T(8,128)(2,1)}), bf16[32,24,128]{2,1,0:T(8,128)(2,1)S(1)}, u32[]{:S(2)}, u32[]{:S(2)}) async-start(bf16[32,24,128]{2,1,0:T(8,128)(2,1)} %shard_map.195), calls=%async_computation.1 | async-start | bytes 393216 | tf_op jit(solution)/shard_map/all_to_all | solution.py:372
  44.1 11.6 %collective-permute-start.2 = (bf16[8,24,896]{2,1,0:T(8,128)(2,1)S(1)}, bf16[8,24,896]{2,1,0:T(8,128)(2,1)S(1)}, u32[]{:S(2)}, u32[]{:S(2)}) collective-permute-start(bf16[8,24,896]{2,1,0:T(8,128)(2,1)S(1)} %all-to-all-done.own_ref), channel_id=1, source_target_pairs={{1,0},{2,1},{3,2},{0,3},{5,4},{6,5},{7,6},{4,7},{9,8},{10,9},{11,1... | collective-permute-start | bytes 1032200 | tf_op jit(solution)/shard_map/ppermute | solution.py:388
  48.5 12.4 %collective-permute-start.3 = (bf16[8,24,896]{2,1,0:T(8,128)(2,1)S(1)}, bf16[8,24,896]{2,1,0:T(8,128)(2,1)S(1)}, u32[]{:S(2)}, u32[]{:S(2)}) collective-permute-start(bf16[8,24,896]{2,1,0:T(8,128)(2,1)S(1)} %all-to-all-done.own_ref), channel_id=1, source_target_pairs={{2,0},{3,1},{0,2},{1,3},{6,4},{7,5},{4,6},{5,7},{10,8},{11,9},{8,1... | collective-permute-start | bytes 1032200 | tf_op jit(solution)/shard_map/ppermute | solution.py:388
  50.9 19.3 %collective-permute-start.4 = (bf16[8,24,896]{2,1,0:T(8,128)(2,1)S(1)}, bf16[8,24,896]{2,1,0:T(8,128)(2,1)S(1)}, u32[]{:S(2)}, u32[]{:S(2)}) collective-permute-start(bf16[8,24,896]{2,1,0:T(8,128)(2,1)S(1)} %all-to-all-done.own_ref), channel_id=1, source_target_pairs={{3,0},{0,1},{1,2},{2,3},{7,4},{4,5},{5,6},{6,7},{11,8},{8,9},{9,10... | collective-permute-start | bytes 1032200 | tf_op jit(solution)/shard_map/ppermute | solution.py:388
  53.5 40.0 %copy-start.11 = (bf16[768]{0:T(1024)(128)(2,1)S(1)}, bf16[768]{0:T(1024)(128)(2,1)}, u32[]{:S(2)}) copy-start(bf16[768]{0:T(1024)(128)(2,1)} %param.23) | copy-start | bytes 4612
  72.5 23.3 %copy-start.3 = (bf16[384,768]{1,0:T(8,128)(2,1)S(1)}, bf16[384,768]{1,0:T(8,128)(2,1)}, u32[]{:S(2)}) copy-start(bf16[384,768]{1,0:T(8,128)(2,1)} %copy-done.2) | copy-start | bytes 1769476
  91.5 4.2 %collective-permute-start.5 = (bf16[4,128,768]{2,1,0:T(8,128)(2,1)S(1)}, bf16[4,128,768]{2,1,0:T(8,128)(2,1)S(1)}, u32[]{:S(2)}, u32[]{:S(2)}) collective-permute-start(bf16[4,128,768]{2,1,0:T(8,128)(2,1)S(1)} %all_to_all.35.own_ref), channel_id=1, source_target_pairs={{0,32},{32,0},{1,33},{33,1},{2,34},{34,2},{3,35},{35,3},{4,36},{36... | collective-permute-start | bytes 2359304 | tf_op jit(solution)/shard_map/ppermute | solution.py:444
  99.7 17.7 %all-to-all-start.3 = ((bf16[8,64,768]{2,1,0:T(8,128)(2,1)}), bf16[8,64,768]{2,1,0:T(8,128)(2,1)S(1)}, u32[]{:S(2)}, u32[]{:S(2)}) async-start(bf16[8,64,768]{2,1,0:T(8,128)(2,1)} %get-tuple-element.46), calls=%async_computation.3 | async-start | bytes 1572864 | tf_op jit(solution)/shard_map/all_to_all | solution.py:448
  108.9 21.2 %collective-permute-start.6 = (bf16[8,24,896]{2,1,0:T(8,128)(2,1)}, bf16[8,24,896]{2,1,0:T(8,128)(2,1)S(1)}, u32[]{:S(2)}, u32[]{:S(2)}) collective-permute-start(bf16[8,24,896]{2,1,0:T(8,128)(2,1)} %bitcast.6), channel_id=1, source_target_pairs={{0,1},{1,2},{2,3},{3,0},{4,5},{5,6},{6,7},{7,4},{8,9},{9,10},{10,1... | collective-permute-start | bytes 1032200 | tf_op jit(solution)/shard_map/ppermute | solution.py:396
  110.9 19.3 %collective-permute-start.7 = (bf16[8,24,896]{2,1,0:T(8,128)(2,1)}, bf16[8,24,896]{2,1,0:T(8,128)(2,1)S(1)}, u32[]{:S(2)}, u32[]{:S(2)}) collective-permute-start(bf16[8,24,896]{2,1,0:T(8,128)(2,1)} %bitcast.7), channel_id=1, source_target_pairs={{0,2},{1,3},{2,0},{3,1},{4,6},{5,7},{6,4},{7,5},{8,10},{9,11},{10,... | collective-permute-start | bytes 1032200 | tf_op jit(solution)/shard_map/ppermute | solution.py:396
  113.1 18.4 %collective-permute-start.8 = (bf16[8,24,896]{2,1,0:T(8,128)(2,1)S(1)}, bf16[8,24,896]{2,1,0:T(8,128)(2,1)S(1)}, u32[]{:S(2)}, u32[]{:S(2)}) collective-permute-start(bf16[8,24,896]{2,1,0:T(8,128)(2,1)S(1)} %bitcast.22), channel_id=1, source_target_pairs={{0,3},{1,0},{2,1},{3,2},{4,7},{5,4},{6,5},{7,6},{8,11},{9,8},{10,9... | collective-permute-start | bytes 1032200 | tf_op jit(solution)/shard_map/ppermute | solution.py:396
  118.5 23.7 %all-to-all-start.4 = ((bf16[32,16,128]{2,1,0:T(8,128)(2,1)}), bf16[32,16,128]{2,1,0:T(8,128)(2,1)S(1)}, u32[]{:S(2)}, u32[]{:S(2)}) async-start(bf16[32,16,128]{2,1,0:T(8,128)(2,1)} %shard_map.200), calls=%async_computation.4 | async-start | bytes 262144 | tf_op jit(solution)/shard_map/all_to_all | solution.py:372
  142.3 21.4 %all-to-all-start.5 = ((bf16[8,24,896]{2,1,0:T(8,128)(2,1)}), bf16[8,24,896]{2,1,0:T(8,128)(2,1)S(1)}, u32[]{:S(2)}, u32[]{:S(2)}) async-start(bf16[8,24,896]{2,1,0:T(8,128)(2,1)} %fusion.2), calls=%async_computation.5 | async-start | bytes 688128 | tf_op jit(solution)/shard_map/all_to_all | solution.py:452
  151.9 19.0 %collective-permute-start.10 = (bf16[24,3,256]{2,1,0:T(4,128)(2,1)S(1)}, bf16[24,3,256]{2,1,0:T(4,128)(2,1)S(1)}, u32[]{:S(2)}, u32[]{:S(2)}) collective-permute-start(bf16[24,3,256]{2,1,0:T(4,128)(2,1)S(1)} %get-tuple-element.80), channel_id=1, source_target_pairs={{32,64},{96,128},{160,192},{224,256},{288,320},{352,384},{416,448}... | collective-permute-start | bytes 110600 | tf_op jit(solution)/shard_map/ppermute | solution.py:382
  156.7 14.3 %collective-permute-start.11 = (bf16[24,3,256]{2,1,0:T(4,128)(2,1)S(1)}, bf16[24,3,256]{2,1,0:T(4,128)(2,1)S(1)}, u32[]{:S(2)}, u32[]{:S(2)}) collective-permute-start(bf16[24,3,256]{2,1,0:T(4,128)(2,1)S(1)} %get-tuple-element.79), channel_id=1, source_target_pairs={{0,32},{64,96},{128,160},{192,224},{256,288},{320,352},{384,416},{... | collective-permute-start | bytes 110600 | tf_op jit(solution)/shard_map/ppermute | solution.py:380
  163.8 13.6 %collective-permute-start.9 = (bf16[24,1024]{1,0:T(8,128)(2,1)S(1)}, bf16[24,1024]{1,0:T(8,128)(2,1)S(1)}, u32[]{:S(2)}, u32[]{:S(2)}) collective-permute-start(bf16[24,1024]{1,0:T(8,128)(2,1)S(1)} %pad_maximum_fusion), channel_id=1, source_target_pairs={{0,256},{256,0},{1,257},{257,1},{2,258},{258,2},{3,259},{259,3},{4... | collective-permute-start | bytes 147464 | tf_op jit(solution)/shard_map/ppermute | solution.py:461
  178.4 18.9 %all-to-all-start.6 = ((bf16[8,24,1024]{2,1,0:T(8,128)(2,1)}), bf16[8,24,1024]{2,1,0:T(8,128)(2,1)S(1)}, u32[]{:S(2)}, u32[]{:S(2)}) async-start(bf16[8,24,1024]{2,1,0:T(8,128)(2,1)} %broadcast_in_dim.36), calls=%async_computation.6 | async-start | bytes 786432 | tf_op jit(solution)/shard_map/all_to_all | solution.py:368
  (10 other events, 69.2 us)

commit v5 on v4

--- a/solution.py
+++ b/solution.py
@@ -13,7 +13,7 @@
 F32 = jnp.float32
 BF = jnp.bfloat16
 EXT = 16
-VMEM_BYTES = 48 * 1024 * 1024
+VMEM_BYTES = 20 * 1024 * 1024
 SIDE = 128
 
 
@@ -44,38 +44,40 @@
     ext[:, 3 + rows : 6 + rows, :] = down_ref[...].astype(F32)
 
 
-def fill_shifts(cells, shifted):
+def row_shifts(ext, c, rows):
+    return [ext[c, a : a + rows, :] for a in range(7)]
+
+
+def along(cells, move):
     width = cells.shape[1]
+    if move == 0:
+        return cells
     lane = lax.broadcasted_iota(jnp.int32, cells.shape, 1)
+    inside = lane < width - move if move > 0 else lane >= -move
+    return jnp.where(inside, pltpu.roll(cells, (-move) % width, 1), 0.0)
+
+
+def stencil(taps_ref, c, shifts, flip):
+    total = None
     for b in range(7):
-        move = b - 3
-        if move == 0:
-            shifted[b] = cells
-        else:
-            turned = pltpu.roll(cells, (-move) % width, 1)
-            inside = lane < width - move if move > 0 else lane >= -move
-            shifted[b] = jnp.where(inside, turned, 0.0)
-
-
-def stencil(taps_ref, c, shifted, rows, flip):
-    total = None
-    for a in range(7):
-        for b in range(7):
+        column = None
+        for a in range(7):
             tap = a * 7 + b
-            term = taps_ref[c, 48 - tap if flip else tap] * shifted[b, a : a + rows, :]
-            total = term if total is None else total + term
+            term = taps_ref[c, 48 - tap if flip else tap] * shifts[a]
+            column = term if column is None else column + term
+        column = along(column, b - 3)
+        total = column if total is None else total + column
     return total
 
 
-def forward_body(taps_ref, bias_ref, x_ref, up_ref, down_ref, metric_ref, dy_ref, out_ref, ext, shifted, h_rows, dy_rows):
+def forward_body(taps_ref, bias_ref, x_ref, up_ref, down_ref, metric_ref, dy_ref, out_ref, ext, h_rows, dy_rows):
     cdev, rows, width = x_ref.shape
     fill_rows(x_ref, up_ref, down_ref, ext)
     dy_rows[...] = dy_ref[...].astype(F32)
     metric = jnp.broadcast_to(metric_ref[...], (rows, width))
 
     def channel(c, carry):
-        fill_shifts(ext[c], shifted)
-        h_rows[c] = bias_ref[c] + metric * stencil(taps_ref, c, shifted, rows, False)
+        h_rows[c] = bias_ref[c] + metric * stencil(taps_ref, c, row_shifts(ext, c, rows), False)
         return carry
 
     lax.fori_loop(0, cdev, channel, 0)
@@ -97,7 +99,6 @@
         [smem(), smem()] + [vmem()] * 5,
         [
             pltpu.VMEM((cdev, EXT, width), F32),
-            pltpu.VMEM((7, EXT, width), F32),
             pltpu.VMEM((cdev, rows, width), F32),
             pltpu.VMEM((cdev, rows, width), F32),
         ],
@@ -135,7 +136,7 @@
     )(recv, gain[None], bias[None])
 
 
-def norm_back_body(recv_ref, nhat_ref, rstd_ref, gain_ref, gam_ref, out_ref, flat):
+def norm_back_body(recv_ref, nhat_ref, rstd_ref, gain_ref, gam_ref, db_ref, out_ref, flat):
     piece, chans = nhat_ref.shape
     dn = recv_ref[0].astype(F32)
     for k in range(1, recv_ref.shape[0]):
@@ -147,7 +148,7 @@
     dh = rstd_ref[:, :1] * (dnhat - s1 - nhat * s2)
     flat[:piece] = dh
     flat[piece:] = jnp.zeros((flat.shape[0] - piece, chans), F32)
-    sums = (jnp.sum(dn * nhat, 0, keepdims=True), jnp.sum(dn, 0, keepdims=True), gam_ref[...])
+    sums = (jnp.sum(dn * nhat, 0, keepdims=True), jnp.sum(dn, 0, keepdims=True), gam_ref[...], db_ref[...])
     for k, value in enumerate(sums):
         high = value.astype(BF).astype(F32)
         flat[piece + 2 * k : piece + 2 * k + 1] = high
@@ -160,17 +161,17 @@
     out_ref[:, 8:] = jnp.where(lane < 64, two, last).astype(BF)
 
 
-def norm_back(recv, nhat, rstd, gain, gam, owners):
+def norm_back(recv, nhat, rstd, gain, gam, db, owners):
     piece, chans = nhat.shape
     return call(
         norm_back_body,
         jax.ShapeDtypeStruct((owners, 16, 128), BF),
-        [vmem()] * 5,
+        [vmem()] * 6,
         [pltpu.VMEM((128, chans), F32)],
-    )(recv, nhat, rstd, gain[None], gam[None])
-
-
-def taps_body(recv_ref, x_ref, up_ref, down_ref, metric_ref, dy_ref, dconv_ref, ends_ref, sums_ref, extra_ref, ext, shifted, dh_rows, prods):
+    )(recv, nhat, rstd, gain[None], gam, db)
+
+
+def taps_body(recv_ref, x_ref, up_ref, down_ref, metric_ref, dy_ref, dconv_ref, ends_ref, sums_ref, extra_ref, ext, dh_rows, prods):
     cdev, rows, width = x_ref.shape
     fill_rows(x_ref, up_ref, down_ref, ext)
     low16 = lax.broadcasted_iota(jnp.int32, (16, 128), 1) < 64
@@ -189,15 +190,16 @@
     metric = jnp.broadcast_to(metric_ref[...], (rows, width))
 
     def channel(c, carry):
-        fill_shifts(ext[c], shifted)
         dh = dh_rows[c]
         dconv = metric * dh
         dconv_ref[c] = dconv
         ends_ref[0, c] = dconv[:3].astype(BF)
         ends_ref[1, c] = dconv[rows - 3 :].astype(BF)
-        for a in range(7):
-            for b in range(7):
-                product = shifted[b, a : a + rows, :] * dconv
+        shifts = row_shifts(ext, c, rows)
+        for b in range(7):
+            moved = along(dconv, 3 - b)
+            for a in range(7):
+                product = shifts[a] * moved
                 prods[(a * 7 + b) * 8 : (a * 7 + b) * 8 + 8, :] = product[:, :128] + product[:, 128:]
         dy = dy_ref[c].astype(F32)
         prods[392:400, :] = dh[:, :128] + dh[:, 128:]
@@ -225,20 +227,18 @@
         [vmem()] * 6,
         [
             pltpu.VMEM((cdev, EXT, width), F32),
-            pltpu.VMEM((7, EXT, width), F32),
             pltpu.VMEM((cdev, rows, width), F32),
             pltpu.VMEM((448, 128), F32),
         ],
     )(recv, x, up, down, metric[:, None], dy)
 
 
-def spread_body(taps_ref, x_ref, up_ref, down_ref, dy_ref, out_ref, ext, shifted):
+def spread_body(taps_ref, x_ref, up_ref, down_ref, dy_ref, out_ref, ext):
     cdev, rows, width = x_ref.shape
     fill_rows(x_ref, up_ref, down_ref, ext)
 
     def channel(c, carry):
-        fill_shifts(ext[c], shifted)
-        out_ref[c] = dy_ref[c].astype(F32) + stencil(taps_ref, c, shifted, rows, True)
+        out_ref[c] = dy_ref[c].astype(F32) + stencil(taps_ref, c, row_shifts(ext, c, rows), True)
         return carry
 
     lax.fori_loop(0, cdev, channel, 0)
@@ -250,7 +250,7 @@
         spread_body,
         jax.ShapeDtypeStruct((cdev, rows, width), F32),
         [smem()] + [vmem()] * 4,
-        [pltpu.VMEM((cdev, EXT, width), F32), pltpu.VMEM((7, EXT, width), F32)],
+        [pltpu.VMEM((cdev, EXT, width), F32)],
     )(taps, dconv, up, down, dy)
 
 
@@ -336,26 +336,93 @@
     )(core, own, other, wi, wo, bi, gamma[None])
 
 
-def grads_body(part, n_ref, dy_ref, g_ref, dpre_ref, wo_ref, gamma_ref, out_ref, gam_ref):
-    toks, chans = n_ref.shape
+def grads_body(part, ny, y_ref, n_ref, dy_ref, g_ref, dpre_ref, wo_ref, gamma_ref, out_ref, gam_ref, db_ref):
+    toks = n_ref.shape[0]
     hid = g_ref.shape[1]
     first, second = picks(hid // part, part)
     dw_in = dot(dpre_ref[...], n_ref[...], 0, 0).astype(BF)
     proj = dot(g_ref[...], dy_ref[...], 0, 0)
     gam_ref[...] = jnp.sum(wo_ref[...].astype(F32) * proj, 0, keepdims=True)
     dw_out = (proj * gamma_ref[...]).astype(BF)
-    out_ref[:, :chans] = (dot(first, dw_in, 1, 0) + dot(second, dw_out, 1, 0)).astype(BF)
-    ones = jnp.ones((toks, out_ref.shape[1] - chans), BF)
-    out_ref[:, chans:] = dot(first, dot(dpre_ref[...], ones, 0, 0).astype(BF), 1, 0).astype(BF)
-
-
-def grads(part, side, n, dy, g, dpre, wo, gamma):
+    out_ref[...] = (dot(first, dw_in, 1, 0) + dot(second, dw_out, 1, 0)).astype(BF)
+    nz = hid // part // ny
+    lane = lax.broadcasted_iota(jnp.int32, (db_ref.shape[1], hid), 0)
+    place = lax.broadcasted_iota(jnp.int32, (1, hid), 1)
+    block = jnp.floor((place.astype(F32) + 0.5) * (1.0 / part)).astype(jnp.int32)
+    ring = jnp.floor((block.astype(F32) + 0.5) * (1.0 / nz)).astype(jnp.int32)
+    ahead = ring + y_ref[0]
+    owner = (block - ring * nz) * ny + jnp.where(ahead >= ny, ahead - ny, ahead)
+    spot = jnp.where(lane == owner * 2 * part + place - block * part, 1.0, 0.0).astype(BF)
+    db = dot(jnp.ones((16, toks), BF), dpre_ref[...], 1, 0).astype(BF)
+    db_ref[...] = dot(db, spot, 1, 1)[:1]
+
+
+def grads(part, ny, y, n, dy, g, dpre, wo, gamma):
     toks, chans = n.shape
     return call(
-        functools.partial(grads_body, part),
-        [jax.ShapeDtypeStruct((2 * g.shape[1], chans + side), BF), jax.ShapeDtypeStruct((1, chans), F32)],
-        [vmem()] * 6,
-    )(n, dy, g, dpre, wo, gamma[None])
+        functools.partial(grads_body, part, ny),
+        [
+            jax.ShapeDtypeStruct((2 * g.shape[1], chans), BF),
+            jax.ShapeDtypeStruct((1, chans), F32),
+            jax.ShapeDtypeStruct((1, 2 * g.shape[1]), F32),
+        ],
+        [smem()] + [vmem()] * 6,
+    )(y, n, dy, g, dpre, wo, gamma[None])
+
+
+def slices_body(part, member_ref, w_in_ref, w_out_ref, b_ref, out_ref):
+    hdev, chans = w_in_ref.shape
+    row = lax.broadcasted_iota(jnp.int32, (2 * part, hdev), 0)
+    place = lax.broadcasted_iota(jnp.int32, (2 * part, hdev), 1)
+    start = member_ref[0] * part
+    first = jnp.where((row < part) & (place == start + row), 1.0, 0.0).astype(BF)
+    second = jnp.where((row >= part) & (place == start + row - part), 1.0, 0.0).astype(BF)
+    rows = (dot(first, w_in_ref[...], 1, 0) + dot(second, w_out_ref[...], 1, 0)).astype(BF)
+    bias = jnp.broadcast_to(b_ref[...], (SIDE, hdev))
+    high = bias.astype(BF)
+    low = (bias - high.astype(F32)).astype(BF)
+    line = lax.broadcasted_iota(jnp.int32, (SIDE, hdev), 0)
+    high = jnp.where(line == 0, high.astype(F32), jnp.where(line == 1, low.astype(F32), 0.0)).astype(BF)
+    side = dot(first, high, 1, 1).astype(BF)
+    for k in range(out_ref.shape[0]):
+        out_ref[k, :, :chans] = rows
+        out_ref[k, :, chans:] = side
+
+
+def slices(part, copies, member, w_in, w_out, b_in):
+    return call(
+        functools.partial(slices_body, part),
+        jax.ShapeDtypeStruct((copies, 2 * part, w_in.shape[1] + SIDE), BF),
+        [smem()] + [vmem()] * 3,
+    )(member, w_in, w_out, b_in[None])
+
+
+def results_body(part, gathered_ref, dw_in_ref, dw_out_ref, side_ref, total_ref):
+    chans = dw_in_ref.shape[1]
+    total = None
+    for k in range(gathered_ref.shape[0]):
+        block = gathered_ref[k].astype(F32)
+        dw_in_ref[k * part : (k + 1) * part] = block[:part, :chans]
+        dw_out_ref[k * part : (k + 1) * part] = block[part:, :chans]
+        side = block[:, chans:]
+        side = side + pltpu.roll(side, 64, 1)
+        side_ref[k] = side
+        total = side if total is None else total + side
+    total_ref[...] = total
+
+
+def results(part, gathered, chans):
+    members, rows, lanes = gathered.shape
+    return call(
+        functools.partial(results_body, part),
+        [
+            jax.ShapeDtypeStruct((members * part, chans), F32),
+            jax.ShapeDtypeStruct((members * part, chans), F32),
+            jax.ShapeDtypeStruct((members, rows, lanes - chans), F32),
+            jax.ShapeDtypeStruct((rows, lanes - chans), F32),
+        ],
+        [vmem()],
+    )(gathered)
 
 
 def two_parts(value):
@@ -419,16 +486,12 @@
     hdev = w_in.shape[0]
     part = hdev // GROUP
     piece = tokens // nchan
-    member = lax.axis_index(("x", "c"))
     owner = lax.axis_index(CHAN)
     gamma_f = layer_scale.astype(F32)
     gamma_own = lax.dynamic_slice_in_dim(gamma_f, owner * cdev, cdev)
 
-    side = jnp.pad(jnp.stack(two_parts(lax.dynamic_slice_in_dim(b_in, member * part, part)), 1), ((0, part), (0, SIDE - 2)))
-    mine = jnp.concatenate(
-        [lax.dynamic_slice_in_dim(w_in, member * part, part), lax.dynamic_slice_in_dim(w_out, member * part, part)], 0
-    )
-    shards = to_all(jnp.concatenate([mine, side], 1), "zl")
+    member = lax.axis_index(("x", "c")).astype(jnp.int32)[None]
+    shards = lax.all_to_all(slices(part, nz, member, w_in, w_out, b_in), "zl", 0, 0, tiled=True)
 
     up, down = halos(block_input[:, :3], block_input[:, rows - 3 :])
     blocks = forward(kernel, conv_bias, block_input, up, down, metric, out_grad)
@@ -437,7 +500,6 @@
     recv = exchange(blocks)
     wi, wo, bi = weights(from_ring(shards), part, chans)
 
-    recv, wi, wo, bi = lax.optimization_barrier((recv, wi, wo, bi))
     recv = recv.reshape(chans, 2 * piece)
     pair, nhat, rstd = norm(recv, ln_gain, ln_bias, GROUP // 2)
     pair = lax.all_to_all(pair, "x", 0, 0, tiled=True)
@@ -447,33 +509,28 @@
     dn, n, dy, g, dpre = mlp(core, pair, other, wi, wo, bi, gamma_f)
     dn = lax.all_to_all(dn, ("c", "x"), 0, 0, tiled=True)
 
-    dws, gam_part = grads(part, SIDE, n, dy, g, dpre, wo, gamma_f)
-    dws = to_ring(dws.reshape(ny, nz, 2 * part, chans + SIDE)).astype(BF)
+    dws, gam_part, db_part = grads(part, ny, lax.axis_index("y").astype(jnp.int32)[None], n, dy, g, dpre, wo, gamma_f)
+    dws = to_ring(dws.reshape(ny, nz, 2 * part, chans)).astype(BF)
     dws = lax.all_to_all(dws, "zl", 0, 0, tiled=True)
     dws = jnp.sum(dws.astype(F32), 0)
 
-    payload = exchange(norm_back(dn, nhat, rstd, ln_gain, gam_part[0], nchan))
+    payload = exchange(norm_back(dn, nhat, rstd, ln_gain, gam_part, db_part, nchan))
     dconv, ends, taps, extra = tap_sums(payload, block_input, up, down, metric, out_grad)
     dup, ddown = halos(ends[0], ends[1])
 
     small = jnp.concatenate([jnp.sum(taps, 2), extra[:, :8]], 1)
     mine = jnp.concatenate([dws.astype(BF)] + list(two_parts(small)), 1)
     other = lax.ppermute(mine, "zh", [(0, 1), (1, 0)]).astype(F32)
-    wide = chans + SIDE
     count = small.shape[1]
-    dws = dws + other[:, :wide]
-    small = small + other[:, wide : wide + count] + other[:, wide + count :]
+    dws = dws + other[:, :chans]
+    small = small + other[:, chans : chans + count] + other[:, chans + count :]
     mine = jnp.concatenate([dws.astype(BF)] + list(two_parts(small)), 1)
     mine, dup, ddown = lax.optimization_barrier((mine, dup, ddown))
     grad_input = spread_back(kernel, dconv, dup, ddown, out_grad)
-    gathered = to_all(mine, ("x", "c")).astype(F32)
-    grad_w_in = gathered[:, :part, :chans].reshape(hdev, chans)
-    grad_w_out = gathered[:, part:, :chans].reshape(hdev, chans)
-    grad_b_in = gathered[:, :part, chans].reshape(hdev)
-    small = jnp.sum(gathered[:, :, wide : wide + count] + gathered[:, :, wide + count :], 0)
+    grad_w_in, grad_w_out, side, small = results(part, to_all(mine, ("x", "c")), chans)
     n_taps = kernel.shape[1]
     dysum = small[:, n_taps + 1]
-    rest = small[:, count - 8 :]
+    rest = small[:, count - 8 : count]
     return (
         grad_input,
         small[:, :n_taps],
@@ -481,7 +538,7 @@
         rest[:, 0] + rest[:, 1],
         rest[:, 2] + rest[:, 3],
         grad_w_in,
-        grad_b_in,
+        (side[:, :part, count - 2] + side[:, :part, count - 1]).reshape(hdev),
         grad_w_out,
         gamma_own * dysum,
         rest[:, 4] + rest[:, 5] + b_out * dysum,

time: 202 us -> 204 us (level)
  blocking collectives: 18.8 us -> 21.5 us
  local copies, waits for them, and re-layouts: 10.2 us -> 7.56 us
  waiting for transfers between devices: 48 us -> 50.3 us
    all_to_all x0 -> x1, starting transfers between devices: none -> 13.1 us  [per_device(): lax.all_to_all(slices(part, nz, member, w_in, w_out, b_in), 'zl', 0, 0, t...]
    all_to_all x2 -> x1, starting transfers between devices: 23.9 us -> 12.3 us  [to_all(): lax.all_to_all(jnp.broadcast_to(block[None], (count,) + block.shape), axi...]
    all_to_all x2, waiting for transfers between devices: 9.9 us -> 19.4 us  [exchange(): return lax.all_to_all(blocks, CHAN, 0, 0, tiled=True)]
    all_to_all x2, starting transfers between devices: 23.2 us -> 17.5 us  [exchange(): return lax.all_to_all(blocks, CHAN, 0, 0, tiled=True)]
    all_to_all x0 -> x1, waiting for transfers between devices: none -> 3.79 us  [per_device(): lax.all_to_all(slices(part, nz, member, w_in, w_out, b_in), 'zl', 0, 0, t...]
    ppermute x1, waiting for transfers between devices: 6.37 us -> 2.78 us  [per_device(): other = lax.ppermute(mine, 'zh', [(0, 1), (1, 0)]).astype(F32)]
    ppermute x1, starting transfers between devices: 7.16 us -> 10.7 us  [per_device(): other = lax.ppermute(mine, 'zh', [(0, 1), (1, 0)]).astype(F32)]
    all_to_all x1, waiting for transfers between devices: 4.71 us -> 1.17 us  [per_device(): dws = lax.all_to_all(dws, 'zl', 0, 0, tiled=True)]
  transfers between devices with their start and end apart: 18 -> 18, of which waited for: 11 -> 12; matrix products, arithmetic and copies ran while one was open for 1% -> 1% of each run, Pallas kernels for 10% -> 9%
where the time goes in v5:
time: 204 us; the launch traced here: 203 us
  starting transfers between devices  94.3 us (46%)
  waiting for transfers between devices  50.3 us (25%)
  Pallas kernels  23.2 us (11%)
  blocking collectives  21.5 us (11%)
  local copies, waits for them, and re-layouts  7.56 us (4%)
  other arithmetic  5.18 us (3%)
    all_to_all x1, blocking collectives, per_device(): pair = lax.all_to_all(pair, 'x', 0, 0, tiled=True)  21.5 us
    all_to_all x2, waiting for transfers between devices, exchange(): return lax.all_to_all(blocks, CHAN, 0, 0, tiled=True)  19.4 us
    all_to_all x2, starting transfers between devices, exchange(): return lax.all_to_all(blocks, CHAN, 0, 0, tiled=True)  17.5 us
    ppermute x3, waiting for transfers between devices, from_ring(): lax.ppermute(block, 'y', [((i + k) % count, i) for i in range(count)])  15.5 us
    all_to_all x1, starting transfers between devices, per_device(): lax.all_to_all(slices(part, nz, member, w_in, w_out, b_in), 'zl', 0, 0, t...  13.1 us
    all_to_all x1, starting transfers between devices, to_all(): lax.all_to_all(jnp.broadcast_to(block[None], (count,) + block.shape), axi...  12.3 us
    ppermute x1, starting transfers between devices, per_device(): other = lax.ppermute(mine, 'zh', [(0, 1), (1, 0)]).astype(F32)  10.7 us
    ppermute x3, starting transfers between devices, to_ring(): lax.ppermute(blocks[k], 'y', [(i, (i + k) % count) for i in range(count)])  9.18 us
  transfers between devices with their start and end apart: 18, of which 12 were waited for; matrix products, arithmetic and copies ran while one was open for 1% of the time, Pallas kernels for 9%

profile of v5, /device:TPU:1, one launch (start us, length us, event | category | flops | bytes accessed | tf_op | source)
XLA Modules:
  0.0 203.1 jit_solution(3582680225857575279)
XLA Ops:
  4.1 13.1 %all-to-all-start = ((bf16[8,24,896]{2,1,0:T(8,128)(2,1)}), bf16[8,24,896]{2,1,0:T(8,128)(2,1)S(1)}, u32[]{:S(2)}, u32[]{:S(2)}) async-start(bf16[8,24,896]{2,1,0:T(8,128)(2,1)} %shard_map.196), calls=%async_computation | async-start | bytes 688128 | tf_op jit(solution)/shard_map/all_to_all | solution.py:494
  17.3 4.0 %collective-permute-start = (bf16[24,3,256]{2,1,0:T(4,128)(2,1)S(1)}, bf16[24,3,256]{2,1,0:T(4,128)(2,1)S(1)}, u32[]{:S(2)}, u32[]{:S(2)}) collective-permute-start(bf16[24,3,256]{2,1,0:T(4,128)(2,1)S(1)} %get-tuple-element.84), channel_id=1, source_target_pairs={{32,64},{96,128},{160,192},{224,256},{288,320},{352,384},{416,448}... | collective-permute-start | bytes 110600 | tf_op jit(solution)/shard_map/ppermute | solution.py:449
  24.4 5.1 %shard_map.195 = bf16[32,24,128]{2,1,0:T(8,128)(2,1)} custom-call(f32[24,49]{1,0:T(8,128)S(1)} %copy-done.8, f32[24]{0:T(128)S(1)} %copy-done.10, bf16[24,8,256]{2,1,0:T(8,128)(2,1)S(1)} %copy-done.1, bf16[24,3,256]{2,1,0:T(4,128)(2,1)S(1)} %get-tuple-element.82.up_ref, bf16[24,3,256]{2,1,0:T(4,128)(2,1)S(1)} %get-tuple-element.81.down_ref, ...), custom_call_target="tpu_custom_call" | custom-call | tf_op jit(solution)/shard_map/pallas_call | solution.py:96
  29.6 3.8 %all-to-all-done.own_ref = bf16[8,24,896]{2,1,0:T(8,128)(2,1)S(1)} async-done(((bf16[8,24,896]{2,1,0:T(8,128)(2,1)}), bf16[8,24,896]{2,1,0:T(8,128)(2,1)S(1)}, u32[]{:S(2)}, u32[]{:S(2)}) %all-to-all-start) | async-done | bytes 344096 | tf_op jit(solution)/shard_map/all_to_all | solution.py:494
  33.4 11.6 %all-to-all-start.1 = ((bf16[32,24,128]{2,1,0:T(8,128)(2,1)}), bf16[32,24,128]{2,1,0:T(8,128)(2,1)S(1)}, u32[]{:S(2)}, u32[]{:S(2)}) async-start(bf16[32,24,128]{2,1,0:T(8,128)(2,1)} %shard_map.195), calls=%async_computation.1 | async-start | bytes 393216 | tf_op jit(solution)/shard_map/all_to_all | solution.py:439
  45.0 13.2 %all-to-all-done.1 = bf16[32,24,128]{2,1,0:T(8,128)(2,1)S(1)} async-done(((bf16[32,24,128]{2,1,0:T(8,128)(2,1)}), bf16[32,24,128]{2,1,0:T(8,128)(2,1)S(1)}, u32[]{:S(2)}, u32[]{:S(2)}) %all-to-all-start.1) | async-done | bytes 196640 | tf_op jit(solution)/shard_map/all_to_all | solution.py:439
  58.5 21.5 %all_to_all.35.own_ref = bf16[4,128,768]{2,1,0:T(8,128)(2,1)S(1)} all-to-all(bf16[4,128,768]{2,1,0:T(8,128)(2,1)S(1)} %get-tuple-element.38), channel_id=1, replica_groups=mesh['zh'=2,'x'=4,'c'=2,'zl'=8,'y'=4] {'x'}, dimensions={0} | all-to-all | bytes 1572864 | tf_op jit(solution)/shard_map/all_to_all | solution.py:505
  82.0 2.6 %collective-permute-start.3 = (bf16[8,24,896]{2,1,0:T(8,128)(2,1)S(1)}, bf16[8,24,896]{2,1,0:T(8,128)(2,1)S(1)}, u32[]{:S(2)}, u32[]{:S(2)}) collective-permute-start(bf16[8,24,896]{2,1,0:T(8,128)(2,1)S(1)} %all-to-all-done.own_ref), channel_id=1, source_target_pairs={{1,0},{2,1},{3,2},{0,3},{5,4},{6,5},{7,6},{4,7},{9,8},{10,9},{11,1... | collective-permute-start | bytes 1032200 | tf_op jit(solution)/shard_map/ppermute | solution.py:455
  84.6 3.3 %collective-permute-start.4 = (bf16[8,24,896]{2,1,0:T(8,128)(2,1)S(1)}, bf16[8,24,896]{2,1,0:T(8,128)(2,1)S(1)}, u32[]{:S(2)}, u32[]{:S(2)}) collective-permute-start(bf16[8,24,896]{2,1,0:T(8,128)(2,1)S(1)} %all-to-all-done.own_ref), channel_id=1, source_target_pairs={{2,0},{3,1},{0,2},{1,3},{6,4},{7,5},{4,6},{5,7},{10,8},{11,9},{8,1... | collective-permute-start | bytes 1032200 | tf_op jit(solution)/shard_map/ppermute | solution.py:455
  89.9 3.1 %collective-permute-done.3.one_ref = bf16[8,24,896]{2,1,0:T(8,128)(2,1)S(1)} collective-permute-done((bf16[8,24,896]{2,1,0:T(8,128)(2,1)S(1)}, bf16[8,24,896]{2,1,0:T(8,128)(2,1)S(1)}, u32[]{:S(2)}, u32[]{:S(2)}) %collective-permute-start.3) | collective-permute-done | bytes 344096 | tf_op jit(solution)/shard_map/ppermute | solution.py:455
  93.0 3.9 %collective-permute-done.4.two_ref = bf16[8,24,896]{2,1,0:T(8,128)(2,1)S(1)} collective-permute-done((bf16[8,24,896]{2,1,0:T(8,128)(2,1)S(1)}, bf16[8,24,896]{2,1,0:T(8,128)(2,1)S(1)}, u32[]{:S(2)}, u32[]{:S(2)}) %collective-permute-start.4) | collective-permute-done | bytes 344096 | tf_op jit(solution)/shard_map/ppermute | solution.py:455
  96.8 8.5 %collective-permute-done.5.three_ref = bf16[8,24,896]{2,1,0:T(8,128)(2,1)S(1)} collective-permute-done((bf16[8,24,896]{2,1,0:T(8,128)(2,1)S(1)}, bf16[8,24,896]{2,1,0:T(8,128)(2,1)S(1)}, u32[]{:S(2)}, u32[]{:S(2)}) %collective-permute-start.5) | collective-permute-done | bytes 344096 | tf_op jit(solution)/shard_map/ppermute | solution.py:455
  110.7 4.0 %all-to-all-start.3 = ((bf16[8,64,768]{2,1,0:T(8,128)(2,1)}), bf16[8,64,768]{2,1,0:T(8,128)(2,1)S(1)}, u32[]{:S(2)}, u32[]{:S(2)}) async-start(bf16[8,64,768]{2,1,0:T(8,128)(2,1)} %get-tuple-element.43), calls=%async_computation.3 | async-start | bytes 1572864 | tf_op jit(solution)/shard_map/all_to_all | solution.py:510
  121.1 3.4 %collective-permute-start.7 = (bf16[8,24,768]{2,1,0:T(8,128)(2,1)S(1)}, bf16[8,24,768]{2,1,0:T(8,128)(2,1)S(1)}, u32[]{:S(2)}, u32[]{:S(2)}) collective-permute-start(bf16[8,24,768]{2,1,0:T(8,128)(2,1)S(1)} %bitcast.23), channel_id=1, source_target_pairs={{0,2},{1,3},{2,0},{3,1},{4,6},{5,7},{6,4},{7,5},{8,10},{9,11},{10,... | collective-permute-start | bytes 884744 | tf_op jit(solution)/shard_map/ppermute | solution.py:463
  124.5 3.8 %collective-permute-start.8 = (bf16[8,24,768]{2,1,0:T(8,128)(2,1)S(1)}, bf16[8,24,768]{2,1,0:T(8,128)(2,1)}, u32[]{:S(2)}, u32[]{:S(2)}) collective-permute-start(bf16[8,24,768]{2,1,0:T(8,128)(2,1)S(1)} %bitcast.22), channel_id=1, source_target_pairs={{0,3},{1,0},{2,1},{3,2},{4,7},{5,4},{6,5},{7,6},{8,11},{9,8},{10,9... | collective-permute-start | bytes 884744 | tf_op jit(solution)/shard_map/ppermute | solution.py:463
  129.5 5.9 %all-to-all-start.4 = ((bf16[32,16,128]{2,1,0:T(8,128)(2,1)}), bf16[32,16,128]{2,1,0:T(8,128)(2,1)S(1)}, u32[]{:S(2)}, u32[]{:S(2)}) async-start(bf16[32,16,128]{2,1,0:T(8,128)(2,1)} %shard_map.201), calls=%async_computation.4 | async-start | bytes 262144 | tf_op jit(solution)/shard_map/all_to_all | solution.py:439
  141.4 6.1 %all-to-all-done.4.recv_ref = bf16[32,16,128]{2,1,0:T(8,128)(2,1)S(1)} async-done(((bf16[32,16,128]{2,1,0:T(8,128)(2,1)}), bf16[32,16,128]{2,1,0:T(8,128)(2,1)S(1)}, u32[]{:S(2)}, u32[]{:S(2)}) %all-to-all-start.4) | async-done | bytes 131104 | tf_op jit(solution)/shard_map/all_to_all | solution.py:439
  147.5 5.3 %all-to-all-start.5 = ((bf16[8,24,768]{2,1,0:T(8,128)(2,1)}), bf16[8,24,768]{2,1,0:T(8,128)(2,1)S(1)}, u32[]{:S(2)}, u32[]{:S(2)}) async-start(bf16[8,24,768]{2,1,0:T(8,128)(2,1)} %fusion.2), calls=%async_computation.5 | async-start | bytes 589824 | tf_op jit(solution)/shard_map/all_to_all | solution.py:514
  152.8 3.9 %shard_map.202 = (f32[24,8,256]{2,1,0:T(8,128)S(1)}, bf16[2,24,3,256]{3,2,1,0:T(4,128)(2,1)S(1)}, f32[24,56,128]{2,1,0:T(8,128)S(1)}, f32[24,128]{1,0:T(8,128)S(1)}) custom-call(bf16[32,16,128]{2,1,0:T(8,128)(2,1)S(1)} %all-to-all-done.4.recv_ref, bf16[24,8,256]{2,1,0:T(8,128)(2,1)S(1)} %copy-done.1, bf16[24,3,256]{2,1,0:T(4,128)(2,1)S(1)} %get-tuple-element.82.up_ref, ...), custom_call_target="tpu_custom_call" | custom-call | tf_op jit(solution)/shard_map/pallas_call | solution.py:219
  156.8 4.7 %collective-permute-start.10 = (bf16[24,3,256]{2,1,0:T(4,128)(2,1)S(1)}, bf16[24,3,256]{2,1,0:T(4,128)(2,1)S(1)}, u32[]{:S(2)}, u32[]{:S(2)}) collective-permute-start(bf16[24,3,256]{2,1,0:T(4,128)(2,1)S(1)} %get-tuple-element.78), channel_id=1, source_target_pairs={{32,64},{96,128},{160,192},{224,256},{288,320},{352,384},{416,448}... | collective-permute-start | bytes 110600 | tf_op jit(solution)/shard_map/ppermute | solution.py:449
  165.1 10.7 %collective-permute-start.9 = (bf16[24,896]{1,0:T(8,128)(2,1)S(1)}, bf16[24,896]{1,0:T(8,128)(2,1)S(1)}, u32[]{:S(2)}, u32[]{:S(2)}) collective-permute-start(bf16[24,896]{1,0:T(8,128)(2,1)S(1)} %pad_maximum_fusion), channel_id=1, source_target_pairs={{0,256},{256,0},{1,257},{257,1},{2,258},{258,2},{3,259},{259,3},{4... | collective-permute-start | bytes 129032 | tf_op jit(solution)/shard_map/ppermute | solution.py:523
  175.9 2.8 %collective-permute-done.9 = bf16[24,896]{1,0:T(8,128)(2,1)S(1)} collective-permute-done((bf16[24,896]{1,0:T(8,128)(2,1)S(1)}, bf16[24,896]{1,0:T(8,128)(2,1)S(1)}, u32[]{:S(2)}, u32[]{:S(2)}) %collective-permute-start.9) | collective-permute-done | bytes 43040 | tf_op jit(solution)/shard_map/ppermute | solution.py:523
  179.6 12.3 %all-to-all-start.6 = ((bf16[8,24,896]{2,1,0:T(8,128)(2,1)}), bf16[8,24,896]{2,1,0:T(8,128)(2,1)S(1)}, u32[]{:S(2)}, u32[]{:S(2)}) async-start(bf16[8,24,896]{2,1,0:T(8,128)(2,1)} %broadcast_in_dim.41), calls=%async_computation.6 | async-start | bytes 688128 | tf_op jit(solution)/shard_map/all_to_all | solution.py:435
  191.9 4.9 %shard_map.203 = f32[24,8,256]{2,1,0:T(8,128)} custom-call(f32[24,49]{1,0:T(8,128)S(1)} %copy-done.8, f32[24,8,256]{2,1,0:T(8,128)S(1)} %get-tuple-element.52.x_ref, bf16[24,3,256]{2,1,0:T(4,128)(2,1)S(1)} %get-tuple-element.57.up_ref, bf16[24,3,256]{2,1,0:T(4,128)(2,1)S(1)} %get-tuple-element.58.down_ref, bf16[24,8,256]{2,1,0:T(8,128)(2,1)S(1)} %copy-done), custom_call_target="tpu_custom_call" | custom-call | tf_op jit(solution)/shard_map/pallas_call | solution.py:249
  (81 shorter events, 40.6 us)
Async XLA Ops:
  0.7 23.8 %copy-start = (bf16[24,8,256]{2,1,0:T(8,128)(2,1)S(1)}, bf16[24,8,256]{2,1,0:T(8,128)(2,1)}, u32[]{:S(2)}) copy-start(bf16[24,8,256]{2,1,0:T(8,128)(2,1)} %dy_ref.5) | copy-start | bytes 294916
  3.2 21.2 %copy-start.10 = (f32[24]{0:T(128)S(1)}, f32[24]{0:T(128)}, u32[]{:S(2)}) copy-start(f32[24]{0:T(128)} %bias_ref.1) | copy-start | bytes 292
  3.2 41.8 %copy-start.12 = (f32[768]{0:T(1024)S(1)}, f32[768]{0:T(1024)}, u32[]{:S(2)}) copy-start(f32[768]{0:T(1024)} %param.17) | copy-start | bytes 9220
  3.2 41.8 %copy-start.13 = (f32[768]{0:T(1024)S(1)}, f32[768]{0:T(1024)}, u32[]{:S(2)}) copy-start(f32[768]{0:T(1024)} %param.18) | copy-start | bytes 9220
  4.1 29.2 %all-to-all-start = ((bf16[8,24,896]{2,1,0:T(8,128)(2,1)}), bf16[8,24,896]{2,1,0:T(8,128)(2,1)S(1)}, u32[]{:S(2)}, u32[]{:S(2)}) async-start(bf16[8,24,896]{2,1,0:T(8,128)(2,1)} %shard_map.196), calls=%async_computation | async-start | bytes 688128 | tf_op jit(solution)/shard_map/all_to_all | solution.py:494
  17.3 6.0 %collective-permute-start = (bf16[24,3,256]{2,1,0:T(4,128)(2,1)S(1)}, bf16[24,3,256]{2,1,0:T(4,128)(2,1)S(1)}, u32[]{:S(2)}, u32[]{:S(2)}) collective-permute-start(bf16[24,3,256]{2,1,0:T(4,128)(2,1)S(1)} %get-tuple-element.84), channel_id=1, source_target_pairs={{32,64},{96,128},{160,192},{224,256},{288,320},{352,384},{416,448}... | collective-permute-start | bytes 110600 | tf_op jit(solution)/shard_map/ppermute | solution.py:449
  21.2 3.1 %collective-permute-start.1 = (bf16[24,3,256]{2,1,0:T(4,128)(2,1)S(1)}, bf16[24,3,256]{2,1,0:T(4,128)(2,1)S(1)}, u32[]{:S(2)}, u32[]{:S(2)}) collective-permute-start(bf16[24,3,256]{2,1,0:T(4,128)(2,1)S(1)} %get-tuple-element.83), channel_id=1, source_target_pairs={{0,32},{64,96},{128,160},{192,224},{256,288},{320,352},{384,416},{... | collective-permute-start | bytes 110600 | tf_op jit(solution)/shard_map/ppermute | solution.py:447
  29.6 60.3 %copy-start.11 = (bf16[768]{0:T(1024)(128)(2,1)S(1)}, bf16[768]{0:T(1024)(128)(2,1)}, u32[]{:S(2)}) copy-start(bf16[768]{0:T(1024)(128)(2,1)} %param.23) | copy-start | bytes 4612
  33.4 24.9 %all-to-all-start.1 = ((bf16[32,24,128]{2,1,0:T(8,128)(2,1)}), bf16[32,24,128]{2,1,0:T(8,128)(2,1)S(1)}, u32[]{:S(2)}, u32[]{:S(2)}) async-start(bf16[32,24,128]{2,1,0:T(8,128)(2,1)} %shard_map.195), calls=%async_computation.1 | async-start | bytes 393216 | tf_op jit(solution)/shard_map/all_to_all | solution.py:439
  80.0 26.6 %collective-permute-start.2 = (bf16[4,128,768]{2,1,0:T(8,128)(2,1)S(1)}, bf16[4,128,768]{2,1,0:T(8,128)(2,1)S(1)}, u32[]{:S(2)}, u32[]{:S(2)}) collective-permute-start(bf16[4,128,768]{2,1,0:T(8,128)(2,1)S(1)} %all_to_all.35.own_ref), channel_id=1, source_target_pairs={{0,32},{32,0},{1,33},{33,1},{2,34},{34,2},{3,35},{35,3},{4,36},{36... | collective-permute-start | bytes 2359304 | tf_op jit(solution)/shard_map/ppermute | solution.py:506
  82.0 11.0 %collective-permute-start.3 = (bf16[8,24,896]{2,1,0:T(8,128)(2,1)S(1)}, bf16[8,24,896]{2,1,0:T(8,128)(2,1)S(1)}, u32[]{:S(2)}, u32[]{:S(2)}) collective-permute-start(bf16[8,24,896]{2,1,0:T(8,128)(2,1)S(1)} %all-to-all-done.own_ref), channel_id=1, source_target_pairs={{1,0},{2,1},{3,2},{0,3},{5,4},{6,5},{7,6},{4,7},{9,8},{10,9},{11,1... | collective-permute-start | bytes 1032200 | tf_op jit(solution)/shard_map/ppermute | solution.py:455
  84.6 12.2 %collective-permute-start.4 = (bf16[8,24,896]{2,1,0:T(8,128)(2,1)S(1)}, bf16[8,24,896]{2,1,0:T(8,128)(2,1)S(1)}, u32[]{:S(2)}, u32[]{:S(2)}) collective-permute-start(bf16[8,24,896]{2,1,0:T(8,128)(2,1)S(1)} %all-to-all-done.own_ref), channel_id=1, source_target_pairs={{2,0},{3,1},{0,2},{1,3},{6,4},{7,5},{4,6},{5,7},{10,8},{11,9},{8,1... | collective-permute-start | bytes 1032200 | tf_op jit(solution)/shard_map/ppermute | solution.py:455
  87.9 17.5 %collective-permute-start.5 = (bf16[8,24,896]{2,1,0:T(8,128)(2,1)S(1)}, bf16[8,24,896]{2,1,0:T(8,128)(2,1)S(1)}, u32[]{:S(2)}, u32[]{:S(2)}) collective-permute-start(bf16[8,24,896]{2,1,0:T(8,128)(2,1)S(1)} %all-to-all-done.own_ref), channel_id=1, source_target_pairs={{3,0},{0,1},{1,2},{2,3},{7,4},{4,5},{5,6},{6,7},{11,8},{8,9},{9,10... | collective-permute-start | bytes 1032200 | tf_op jit(solution)/shard_map/ppermute | solution.py:455
  110.7 17.7 %all-to-all-start.3 = ((bf16[8,64,768]{2,1,0:T(8,128)(2,1)}), bf16[8,64,768]{2,1,0:T(8,128)(2,1)S(1)}, u32[]{:S(2)}, u32[]{:S(2)}) async-start(bf16[8,64,768]{2,1,0:T(8,128)(2,1)} %get-tuple-element.43), calls=%async_computation.3 | async-start | bytes 1572864 | tf_op jit(solution)/shard_map/all_to_all | solution.py:510
  119.2 18.0 %collective-permute-start.6 = (bf16[8,24,768]{2,1,0:T(8,128)(2,1)S(1)}, bf16[8,24,768]{2,1,0:T(8,128)(2,1)S(1)}, u32[]{:S(2)}, u32[]{:S(2)}) collective-permute-start(bf16[8,24,768]{2,1,0:T(8,128)(2,1)S(1)} %bitcast.24), channel_id=1, source_target_pairs={{0,1},{1,2},{2,3},{3,0},{4,5},{5,6},{6,7},{7,4},{8,9},{9,10},{10,1... | collective-permute-start | bytes 884744 | tf_op jit(solution)/shard_map/ppermute | solution.py:463
  121.1 16.1 %collective-permute-start.7 = (bf16[8,24,768]{2,1,0:T(8,128)(2,1)S(1)}, bf16[8,24,768]{2,1,0:T(8,128)(2,1)S(1)}, u32[]{:S(2)}, u32[]{:S(2)}) collective-permute-start(bf16[8,24,768]{2,1,0:T(8,128)(2,1)S(1)} %bitcast.23), channel_id=1, source_target_pairs={{0,2},{1,3},{2,0},{3,1},{4,6},{5,7},{6,4},{7,5},{8,10},{9,11},{10,... | collective-permute-start | bytes 884744 | tf_op jit(solution)/shard_map/ppermute | solution.py:463
  124.5 15.1 %collective-permute-start.8 = (bf16[8,24,768]{2,1,0:T(8,128)(2,1)S(1)}, bf16[8,24,768]{2,1,0:T(8,128)(2,1)}, u32[]{:S(2)}, u32[]{:S(2)}) collective-permute-start(bf16[8,24,768]{2,1,0:T(8,128)(2,1)S(1)} %bitcast.22), channel_id=1, source_target_pairs={{0,3},{1,0},{2,1},{3,2},{4,7},{5,4},{6,5},{7,6},{8,11},{9,8},{10,9... | collective-permute-start | bytes 884744 | tf_op jit(solution)/shard_map/ppermute | solution.py:463
  129.5 18.0 %all-to-all-start.4 = ((bf16[32,16,128]{2,1,0:T(8,128)(2,1)}), bf16[32,16,128]{2,1,0:T(8,128)(2,1)S(1)}, u32[]{:S(2)}, u32[]{:S(2)}) async-start(bf16[32,16,128]{2,1,0:T(8,128)(2,1)} %shard_map.201), calls=%async_computation.4 | async-start | bytes 262144 | tf_op jit(solution)/shard_map/all_to_all | solution.py:439
  147.5 17.4 %all-to-all-start.5 = ((bf16[8,24,768]{2,1,0:T(8,128)(2,1)}), bf16[8,24,768]{2,1,0:T(8,128)(2,1)S(1)}, u32[]{:S(2)}, u32[]{:S(2)}) async-start(bf16[8,24,768]{2,1,0:T(8,128)(2,1)} %fusion.2), calls=%async_computation.5 | async-start | bytes 589824 | tf_op jit(solution)/shard_map/all_to_all | solution.py:514
  156.8 19.0 %collective-permute-start.10 = (bf16[24,3,256]{2,1,0:T(4,128)(2,1)S(1)}, bf16[24,3,256]{2,1,0:T(4,128)(2,1)S(1)}, u32[]{:S(2)}, u32[]{:S(2)}) collective-permute-start(bf16[24,3,256]{2,1,0:T(4,128)(2,1)S(1)} %get-tuple-element.78), channel_id=1, source_target_pairs={{32,64},{96,128},{160,192},{224,256},{288,320},{352,384},{416,448}... | collective-permute-start | bytes 110600 | tf_op jit(solution)/shard_map/ppermute | solution.py:449
  161.5 14.3 %collective-permute-start.11 = (bf16[24,3,256]{2,1,0:T(4,128)(2,1)S(1)}, bf16[24,3,256]{2,1,0:T(4,128)(2,1)S(1)}, u32[]{:S(2)}, u32[]{:S(2)}) collective-permute-start(bf16[24,3,256]{2,1,0:T(4,128)(2,1)S(1)} %get-tuple-element.77), channel_id=1, source_target_pairs={{0,32},{64,96},{128,160},{192,224},{256,288},{320,352},{384,416},{... | collective-permute-start | bytes 110600 | tf_op jit(solution)/shard_map/ppermute | solution.py:447
  165.1 13.6 %collective-permute-start.9 = (bf16[24,896]{1,0:T(8,128)(2,1)S(1)}, bf16[24,896]{1,0:T(8,128)(2,1)S(1)}, u32[]{:S(2)}, u32[]{:S(2)}) collective-permute-start(bf16[24,896]{1,0:T(8,128)(2,1)S(1)} %pad_maximum_fusion), channel_id=1, source_target_pairs={{0,256},{256,0},{1,257},{257,1},{2,258},{258,2},{3,259},{259,3},{4... | collective-permute-start | bytes 129032 | tf_op jit(solution)/shard_map/ppermute | solution.py:523
  178.8 23.8 %copy-start.15 = (f32[24]{0:T(128)S(1)}, f32[24]{0:T(128)}, u32[]{:S(2)}) copy-start(f32[24]{0:T(128)} %param.22) | copy-start | bytes 292
  179.6 19.6 %all-to-all-start.6 = ((bf16[8,24,896]{2,1,0:T(8,128)(2,1)}), bf16[8,24,896]{2,1,0:T(8,128)(2,1)S(1)}, u32[]{:S(2)}, u32[]{:S(2)}) async-start(bf16[8,24,896]{2,1,0:T(8,128)(2,1)} %broadcast_in_dim.41), calls=%async_computation.6 | async-start | bytes 688128 | tf_op jit(solution)/shard_map/all_to_all | solution.py:435
  (10 other events, 63.8 us)

commit v6 on v5

--- a/solution.py
+++ b/solution.py
@@ -80,7 +80,7 @@
         h_rows[c] = bias_ref[c] + metric * stencil(taps_ref, c, row_shifts(ext, c, rows), False)
         return carry
 
-    lax.fori_loop(0, cdev, channel, 0)
+    lax.fori_loop(0, cdev, channel, 0, unroll=4)
     low = lax.broadcasted_iota(jnp.int32, (cdev, 128), 1) < 64
     for r in range(rows):
         h_row, dy_row = h_rows[:, r, :], dy_rows[:, r, :]
@@ -211,7 +211,7 @@
         return carry
 
     prods[408:, :] = jnp.zeros((prods.shape[0] - 408, 128), F32)
-    lax.fori_loop(0, cdev, channel, 0)
+    lax.fori_loop(0, cdev, channel, 0, unroll=4)
 
 
 def tap_sums(recv, x, up, down, metric, dy):
@@ -241,7 +241,7 @@
         out_ref[c] = dy_ref[c].astype(F32) + stencil(taps_ref, c, row_shifts(ext, c, rows), True)
         return carry
 
-    lax.fori_loop(0, cdev, channel, 0)
+    lax.fori_loop(0, cdev, channel, 0, unroll=4)
 
 
 def spread_back(taps, dconv, up, down, dy):
@@ -269,9 +269,9 @@
     return lax.dot_general(a, b, (((a_dim,), (b_dim,)), ((), ())), preferred_element_type=F32)
 
 
-def weights_body(part, own_ref, one_ref, two_ref, three_ref, wi_ref, wo_ref, bi_ref, rows):
+def weights_body(part, own_ref, one_ref, low_ref, high_ref, last_ref, wi_ref, wo_ref, bi_ref, rows):
     blocks = 0
-    for ref in (own_ref, one_ref, two_ref, three_ref):
+    for ref in (own_ref, one_ref, low_ref, high_ref, last_ref):
         for k in range(ref.shape[0]):
             at = blocks * 2 * part
             rows[at : at + 2 * part] = ref[k].astype(F32)
@@ -294,7 +294,7 @@
             jax.ShapeDtypeStruct((blocks * part, chans), BF),
             jax.ShapeDtypeStruct((1, blocks * part), F32),
         ],
-        [vmem()] * 4,
+        [vmem()] * len(parts),
         [pltpu.VMEM((blocks * 2 * part, parts[0].shape[2]), F32)],
     )(*parts)
 
@@ -397,7 +397,7 @@
     )(member, w_in, w_out, b_in[None])
 
 
-def results_body(part, gathered_ref, dw_in_ref, dw_out_ref, side_ref, total_ref):
+def results_body(part, n_taps, gathered_ref, gamma_ref, b_out_ref, dw_in_ref, dw_out_ref, taps_ref, db_ref, rest_ref):
     chans = dw_in_ref.shape[1]
     total = None
     for k in range(gathered_ref.shape[0]):
@@ -406,23 +406,32 @@
         dw_out_ref[k * part : (k + 1) * part] = block[part:, :chans]
         side = block[:, chans:]
         side = side + pltpu.roll(side, 64, 1)
-        side_ref[k] = side
+        line = side.T
+        db_ref[k : k + 1] = (line[62:63] + line[63:64])[:, :part]
         total = side if total is None else total + side
-    total_ref[...] = total
-
-
-def results(part, gathered, chans):
-    members, rows, lanes = gathered.shape
-    return call(
-        functools.partial(results_body, part),
+    taps_ref[...] = total[:, :n_taps]
+    lines = total.T
+    dysum = lines[n_taps + 1 : n_taps + 2]
+    rest_ref[0:1] = lines[n_taps : n_taps + 1]
+    rest_ref[1:2] = lines[56:57] + lines[57:58]
+    rest_ref[2:3] = lines[58:59] + lines[59:60]
+    rest_ref[3:4] = gamma_ref[...] * dysum
+    rest_ref[4:5] = lines[60:61] + lines[61:62] + b_out_ref[...] * dysum
+
+
+def results(part, n_taps, gathered, chans, gamma, b_out):
+    members, rows, _ = gathered.shape
+    return call(
+        functools.partial(results_body, part, n_taps),
         [
             jax.ShapeDtypeStruct((members * part, chans), F32),
             jax.ShapeDtypeStruct((members * part, chans), F32),
-            jax.ShapeDtypeStruct((members, rows, lanes - chans), F32),
-            jax.ShapeDtypeStruct((rows, lanes - chans), F32),
-        ],
-        [vmem()],
-    )(gathered)
+            jax.ShapeDtypeStruct((rows, n_taps), F32),
+            jax.ShapeDtypeStruct((members, part), F32),
+            jax.ShapeDtypeStruct((5, rows), F32),
+        ],
+        [vmem()] * 3,
+    )(gathered, gamma[None], b_out[None])
 
 
 def two_parts(value):
@@ -450,10 +459,9 @@
     return jnp.where(even, across, within), jnp.where(even, within, across)
 
 
-def from_ring(block):
+def along_ring(block, ahead):
     count = lax.axis_size("y")
-    ahead = [lax.ppermute(block, "y", [((i + k) % count, i) for i in range(count)]) for k in range(1, count)]
-    return [block] + ahead
+    return lax.ppermute(block, "y", [((i + ahead) % count, i) for i in range(count)])
 
 
 def to_ring(blocks):
@@ -498,11 +506,14 @@
     blocks, shards = lax.optimization_barrier((blocks, shards))
 
     recv = exchange(blocks)
-    wi, wo, bi = weights(from_ring(shards), part, chans)
-
-    recv = recv.reshape(chans, 2 * piece)
-    pair, nhat, rstd = norm(recv, ln_gain, ln_bias, GROUP // 2)
+    one, last = along_ring(shards, 1), along_ring(shards, -1)
+    recv, one, last = lax.optimization_barrier((recv, one, last))
+
+    pair, nhat, rstd = norm(recv.reshape(chans, 2 * piece), ln_gain, ln_bias, GROUP // 2)
     pair = lax.all_to_all(pair, "x", 0, 0, tiled=True)
+    low, high = along_ring(one[: nz // 2], 1), along_ring(last[nz // 2 :], -1)
+    pair, low, high = lax.optimization_barrier((pair, low, high))
+    wi, wo, bi = weights([shards, one, low, high, last], part, chans)
     other = lax.ppermute(pair, "c", [(0, 1), (1, 0)])
 
     core = lax.axis_index("c").astype(jnp.int32)[None]
@@ -527,21 +538,20 @@
     mine = jnp.concatenate([dws.astype(BF)] + list(two_parts(small)), 1)
     mine, dup, ddown = lax.optimization_barrier((mine, dup, ddown))
     grad_input = spread_back(kernel, dconv, dup, ddown, out_grad)
-    grad_w_in, grad_w_out, side, small = results(part, to_all(mine, ("x", "c")), chans)
-    n_taps = kernel.shape[1]
-    dysum = small[:, n_taps + 1]
-    rest = small[:, count - 8 : count]
+    grad_w_in, grad_w_out, grad_kernel, db, rest = results(
+        part, kernel.shape[1], to_all(mine, ("x", "c")), chans, gamma_own, b_out
+    )
     return (
         grad_input,
-        small[:, :n_taps],
-        small[:, n_taps],
-        rest[:, 0] + rest[:, 1],
-        rest[:, 2] + rest[:, 3],
+        grad_kernel,
+        rest[0],
+        rest[1],
+        rest[2],
         grad_w_in,
-        (side[:, :part, count - 2] + side[:, :part, count - 1]).reshape(hdev),
+        db.reshape(hdev),
         grad_w_out,
-        gamma_own * dysum,
-        rest[:, 4] + rest[:, 5] + b_out * dysum,
+        rest[3],
+        rest[4],
     )
 
 

time: 204 us -> 189 us (0.926)
  blocking collectives: 21.5 us -> 0 us
  starting transfers between devices: 94.3 us -> 115 us
  waiting for transfers between devices: 50.3 us -> 40 us
  other arithmetic: 5.18 us -> 1.72 us
  Pallas kernels: 23.2 us -> 20.4 us
    all_to_all x1 -> x0, blocking collectives: 21.5 us -> none  [per_device(): pair = lax.all_to_all(pair, 'x', 0, 0, tiled=True)]
    all_to_all x0 -> x1, starting transfers between devices: none -> 10.9 us  [per_device(): pair = lax.all_to_all(pair, 'x', 0, 0, tiled=True)]
    all_to_all x2, waiting for transfers between devices: 19.4 us -> 11.2 us  [exchange(): return lax.all_to_all(blocks, CHAN, 0, 0, tiled=True)]
    all_to_all x2, starting transfers between devices: 17.5 us -> 23 us  [exchange(): return lax.all_to_all(blocks, CHAN, 0, 0, tiled=True)]
    ppermute x3, waiting for transfers between devices: 4.15 us -> 0.01 us  [to_ring(): lax.ppermute(blocks[k], 'y', [(i, (i + k) % count) for i in range(count)])]
    ppermute x3 -> x4, starting transfers between devices: 7.87 us -> 11.6 us  [along_ring(): lax.ppermute(block, 'y', [((i + ahead) % count, i) for i in range(count)])]
    add x3 -> x0, other arithmetic: 2.52 us -> none  [the longest x2 2.34 us: per_device(): rest[:, 4] + rest[:, 5] + b_out * dysum]
    ppermute x3 -> x4, waiting for transfers between devices: 15.5 us -> 13.7 us  [along_ring(): lax.ppermute(block, 'y', [((i + ahead) % count, i) for i in range(count)])]
  transfers between devices with their start and end apart: 18 -> 20, of which waited for: 12 -> 11; matrix products, arithmetic and copies ran while one was open for 1% -> 1% of each run, Pallas kernels for 9% -> 8%
where the time goes in v6:
time: 189 us; the launch traced here: 188 us
  starting transfers between devices  115 us (61%)
  waiting for transfers between devices  40 us (21%)
  Pallas kernels  20.4 us (11%)
  local copies, waits for them, and re-layouts  9.54 us (5%)
    all_to_all x2, starting transfers between devices, exchange(): return lax.all_to_all(blocks, CHAN, 0, 0, tiled=True)  23 us
    ppermute x4, waiting for transfers between devices, along_ring(): lax.ppermute(block, 'y', [((i + ahead) % count, i) for i in range(count)])  13.7 us
    all_to_all x1, starting transfers between devices, per_device(): lax.all_to_all(slices(part, nz, member, w_in, w_out, b_in), 'zl', 0, 0, t...  13.1 us
    all_to_all x1, starting transfers between devices, to_all(): lax.all_to_all(jnp.broadcast_to(block[None], (count,) + block.shape), axi...  12.1 us
    ppermute x4, starting transfers between devices, along_ring(): lax.ppermute(block, 'y', [((i + ahead) % count, i) for i in range(count)])  11.6 us
    all_to_all x2, waiting for transfers between devices, exchange(): return lax.all_to_all(blocks, CHAN, 0, 0, tiled=True)  11.2 us
    ppermute x1, starting transfers between devices, per_device(): other = lax.ppermute(mine, 'zh', [(0, 1), (1, 0)]).astype(F32)  11.2 us
    all_to_all x1, starting transfers between devices, per_device(): pair = lax.all_to_all(pair, 'x', 0, 0, tiled=True)  10.9 us
  transfers between devices with their start and end apart: 20, of which 11 were waited for; matrix products, arithmetic and copies ran while one was open for 1% of the time, Pallas kernels for 8%

profile of v6, /device:TPU:1, one launch (start us, length us, event | category | flops | bytes accessed | tf_op | source)
XLA Modules:
  0.0 187.7 jit_solution(13867674884896504311)
XLA Ops:
  4.1 13.1 %all-to-all-start = ((bf16[8,24,896]{2,1,0:T(8,128)(2,1)}), bf16[8,24,896]{2,1,0:T(8,128)(2,1)S(1)}, u32[]{:S(2)}, u32[]{:S(2)}) async-start(bf16[8,24,896]{2,1,0:T(8,128)(2,1)} %shard_map.196), calls=%async_computation | async-start | bytes 688128 | tf_op jit(solution)/shard_map/all_to_all | solution.py:502
  17.3 4.0 %collective-permute-start = (bf16[24,3,256]{2,1,0:T(4,128)(2,1)S(1)}, bf16[24,3,256]{2,1,0:T(4,128)(2,1)S(1)}, u32[]{:S(2)}, u32[]{:S(2)}) collective-permute-start(bf16[24,3,256]{2,1,0:T(4,128)(2,1)S(1)} %get-tuple-element.93), channel_id=1, source_target_pairs={{32,64},{96,128},{160,192},{224,256},{288,320},{352,384},{416,448}... | collective-permute-start | bytes 110600 | tf_op jit(solution)/shard_map/ppermute | solution.py:458
  24.5 3.7 %shard_map.195 = bf16[32,24,128]{2,1,0:T(8,128)(2,1)} custom-call(f32[24,49]{1,0:T(8,128)S(1)} %copy-done.12, f32[24]{0:T(128)S(1)} %copy-done.20, bf16[24,8,256]{2,1,0:T(8,128)(2,1)S(1)} %copy-done.1, bf16[24,3,256]{2,1,0:T(4,128)(2,1)S(1)} %get-tuple-element.91.up_ref, bf16[24,3,256]{2,1,0:T(4,128)(2,1)S(1)} %get-tuple-element.90.down_ref, ...), custom_call_target="tpu_custom_call" | custom-call | tf_op jit(solution)/shard_map/pallas_call | solution.py:96
  28.8 4.6 %all-to-all-done.own_ref = bf16[8,24,896]{2,1,0:T(8,128)(2,1)S(1)} async-done(((bf16[8,24,896]{2,1,0:T(8,128)(2,1)}), bf16[8,24,896]{2,1,0:T(8,128)(2,1)S(1)}, u32[]{:S(2)}, u32[]{:S(2)}) %all-to-all-start) | async-done | bytes 344096 | tf_op jit(solution)/shard_map/all_to_all | solution.py:502
  33.4 11.6 %all-to-all-start.1 = ((bf16[32,24,128]{2,1,0:T(8,128)(2,1)}), bf16[32,24,128]{2,1,0:T(8,128)(2,1)S(1)}, u32[]{:S(2)}, u32[]{:S(2)}) async-start(bf16[32,24,128]{2,1,0:T(8,128)(2,1)} %shard_map.195), calls=%async_computation.1 | async-start | bytes 393216 | tf_op jit(solution)/shard_map/all_to_all | solution.py:448
  45.0 4.3 %collective-permute-start.2 = (bf16[8,24,896]{2,1,0:T(8,128)(2,1)S(1)}, bf16[8,24,896]{2,1,0:T(8,128)(2,1)S(1)}, u32[]{:S(2)}, u32[]{:S(2)}) collective-permute-start(bf16[8,24,896]{2,1,0:T(8,128)(2,1)S(1)} %all-to-all-done.own_ref), channel_id=1, source_target_pairs={{1,0},{2,1},{3,2},{0,3},{5,4},{6,5},{7,6},{4,7},{9,8},{10,9},{11,1... | collective-permute-start | bytes 1032200 | tf_op jit(solution)/shard_map/ppermute | solution.py:464
  51.3 5.3 %collective-permute-done.2.one_ref = bf16[8,24,896]{2,1,0:T(8,128)(2,1)S(1)} collective-permute-done((bf16[8,24,896]{2,1,0:T(8,128)(2,1)S(1)}, bf16[8,24,896]{2,1,0:T(8,128)(2,1)S(1)}, u32[]{:S(2)}, u32[]{:S(2)}) %collective-permute-start.2) | collective-permute-done | bytes 344096 | tf_op jit(solution)/shard_map/ppermute | solution.py:464
  56.6 4.5 %collective-permute-done.3.last_ref = bf16[8,24,896]{2,1,0:T(8,128)(2,1)S(1)} collective-permute-done((bf16[8,24,896]{2,1,0:T(8,128)(2,1)S(1)}, bf16[8,24,896]{2,1,0:T(8,128)(2,1)S(1)}, u32[]{:S(2)}, u32[]{:S(2)}) %collective-permute-start.3) | collective-permute-done | bytes 344096 | tf_op jit(solution)/shard_map/ppermute | solution.py:464
  62.9 10.9 %all-to-all-start.2 = ((bf16[4,128,768]{2,1,0:T(8,128)(2,1)}), bf16[4,128,768]{2,1,0:T(8,128)(2,1)S(1)}, u32[]{:S(2)}, u32[]{:S(2)}) async-start(bf16[4,128,768]{2,1,0:T(8,128)(2,1)} %get-tuple-element.47), calls=%async_computation.2 | async-start | bytes 1572864 | tf_op jit(solution)/shard_map/all_to_all | solution.py:513
  75.8 3.4 %collective-permute-start.5 = (bf16[4,24,896]{2,1,0:T(8,128)(2,1)S(1)}, bf16[4,24,896]{2,1,0:T(8,128)(2,1)S(1)}, u32[]{:S(2)}, u32[]{:S(2)}) collective-permute-start(bf16[4,24,896]{2,1,0:T(8,128)(2,1)S(1)} %slice.64), channel_id=1, source_target_pairs={{3,0},{0,1},{1,2},{2,3},{7,4},{4,5},{5,6},{6,7},{11,8},{8,9},{9,10... | collective-permute-start | bytes 516104 | tf_op jit(solution)/shard_map/ppermute | solution.py:464
  80.2 3.0 %collective-permute-done.5.high_ref = bf16[4,24,896]{2,1,0:T(8,128)(2,1)S(1)} collective-permute-done((bf16[4,24,896]{2,1,0:T(8,128)(2,1)S(1)}, bf16[4,24,896]{2,1,0:T(8,128)(2,1)S(1)}, u32[]{:S(2)}, u32[]{:S(2)}) %collective-permute-start.5) | collective-permute-done | bytes 172064 | tf_op jit(solution)/shard_map/ppermute | solution.py:464
  87.4 2.5 %shard_map.199 = (bf16[8,64,768]{2,1,0:T(8,128)(2,1)}, bf16[512,768]{1,0:T(8,128)(2,1)S(1)}, bf16[512,768]{1,0:T(8,128)(2,1)S(1)}, bf16[512,384]{1,0:T(8,128)(2,1)S(1)}, bf16[512,384]{1,0:T(8,128)(2,1)S(1)}) custom-call(s32[1]{0:T(128)} %bitcast.core_ref, bf16[4,128,768]{2,1,0:T(8,128)(2,1)S(1)} %all-to-all-done.2.own_ref, ...), custom_call_target="tpu_custom_call" | custom-call | tf_op jit(solution)/shard_map/pallas_call | solution.py:326
  91.4 4.8 %all-to-all-start.3 = ((bf16[8,64,768]{2,1,0:T(8,128)(2,1)}), bf16[8,64,768]{2,1,0:T(8,128)(2,1)S(1)}, u32[]{:S(2)}, u32[]{:S(2)}) async-start(bf16[8,64,768]{2,1,0:T(8,128)(2,1)} %get-tuple-element.56), calls=%async_computation.3 | async-start | bytes 1572864 | tf_op jit(solution)/shard_map/all_to_all | solution.py:521
  98.2 2.5 %shard_map.200 = (bf16[768,768]{1,0:T(8,128)(2,1)S(1)}, f32[1,768]{1,0:T(1,128)S(1)}, f32[1,768]{1,0:T(1,128)S(1)}) custom-call(s32[1]{0:T(128)} %bitcast.5.y_ref, bf16[512,768]{1,0:T(8,128)(2,1)S(1)} %get-tuple-element.59.n_ref, bf16[512,768]{1,0:T(8,128)(2,1)S(1)} %get-tuple-element.60.dy_ref, bf16[512,384]{1,0:T(8,128)(2,1)S(1)} %copy-done.5, ...), custom_call_target="tpu_custom_call" | custom-call | tf_op jit(solution)/shard_map/pallas_call | solution.py:362
  105.3 3.9 %collective-permute-start.9 = (bf16[8,24,768]{2,1,0:T(8,128)(2,1)S(1)}, bf16[8,24,768]{2,1,0:T(8,128)(2,1)S(1)}, u32[]{:S(2)}, u32[]{:S(2)}) collective-permute-start(bf16[8,24,768]{2,1,0:T(8,128)(2,1)S(1)} %bitcast.34), channel_id=1, source_target_pairs={{0,3},{1,0},{2,1},{3,2},{4,7},{5,4},{6,5},{7,6},{8,11},{9,8},{10,9... | collective-permute-start | bytes 884744 | tf_op jit(solution)/shard_map/ppermute | solution.py:471
  110.4 11.4 %all-to-all-start.4 = ((bf16[32,16,128]{2,1,0:T(8,128)(2,1)}), bf16[32,16,128]{2,1,0:T(8,128)(2,1)S(1)}, u32[]{:S(2)}, u32[]{:S(2)}) async-start(bf16[32,16,128]{2,1,0:T(8,128)(2,1)} %shard_map.201), calls=%async_computation.4 | async-start | bytes 262144 | tf_op jit(solution)/shard_map/all_to_all | solution.py:448
  122.7 11.2 %all-to-all-done.4.recv_ref = bf16[32,16,128]{2,1,0:T(8,128)(2,1)S(1)} async-done(((bf16[32,16,128]{2,1,0:T(8,128)(2,1)}), bf16[32,16,128]{2,1,0:T(8,128)(2,1)S(1)}, u32[]{:S(2)}, u32[]{:S(2)}) %all-to-all-start.4) | async-done | bytes 131104 | tf_op jit(solution)/shard_map/all_to_all | solution.py:448
  133.9 5.3 %all-to-all-start.5 = ((bf16[8,24,768]{2,1,0:T(8,128)(2,1)}), bf16[8,24,768]{2,1,0:T(8,128)(2,1)S(1)}, u32[]{:S(2)}, u32[]{:S(2)}) async-start(bf16[8,24,768]{2,1,0:T(8,128)(2,1)} %fusion.2), calls=%async_computation.5 | async-start | bytes 589824 | tf_op jit(solution)/shard_map/all_to_all | solution.py:525
  139.2 2.7 %shard_map.202 = (f32[24,8,256]{2,1,0:T(8,128)S(1)}, bf16[2,24,3,256]{3,2,1,0:T(4,128)(2,1)S(1)}, f32[24,56,128]{2,1,0:T(8,128)S(1)}, f32[24,128]{1,0:T(8,128)S(1)}) custom-call(bf16[32,16,128]{2,1,0:T(8,128)(2,1)S(1)} %all-to-all-done.4.recv_ref, bf16[24,8,256]{2,1,0:T(8,128)(2,1)S(1)} %copy-done.1, bf16[24,3,256]{2,1,0:T(4,128)(2,1)S(1)} %copy-done.3, ...), custom_call_target="tpu_custom_call" | custom-call | tf_op jit(solution)/shard_map/pallas_call | solution.py:219
  142.0 4.8 %collective-permute-start.11 = (bf16[24,3,256]{2,1,0:T(4,128)(2,1)S(1)}, bf16[24,3,256]{2,1,0:T(4,128)(2,1)S(1)}, u32[]{:S(2)}, u32[]{:S(2)}) collective-permute-start(bf16[24,3,256]{2,1,0:T(4,128)(2,1)S(1)} %get-tuple-element.87), channel_id=1, source_target_pairs={{32,64},{96,128},{160,192},{224,256},{288,320},{352,384},{416,448}... | collective-permute-start | bytes 110600 | tf_op jit(solution)/shard_map/ppermute | solution.py:458
  151.5 11.2 %collective-permute-start.10 = (bf16[24,896]{1,0:T(8,128)(2,1)S(1)}, bf16[24,896]{1,0:T(8,128)(2,1)S(1)}, u32[]{:S(2)}, u32[]{:S(2)}) collective-permute-start(bf16[24,896]{1,0:T(8,128)(2,1)S(1)} %pad_maximum_fusion), channel_id=1, source_target_pairs={{0,256},{256,0},{1,257},{257,1},{2,258},{258,2},{3,259},{259,3},{4... | collective-permute-start | bytes 129032 | tf_op jit(solution)/shard_map/ppermute | solution.py:534
  166.1 12.1 %all-to-all-start.6 = ((bf16[8,24,896]{2,1,0:T(8,128)(2,1)}), bf16[8,24,896]{2,1,0:T(8,128)(2,1)S(1)}, u32[]{:S(2)}, u32[]{:S(2)}) async-start(bf16[8,24,896]{2,1,0:T(8,128)(2,1)} %broadcast_in_dim.47), calls=%async_computation.6 | async-start | bytes 688128 | tf_op jit(solution)/shard_map/all_to_all | solution.py:444
  178.4 3.5 %shard_map.203 = f32[24,8,256]{2,1,0:T(8,128)} custom-call(f32[24,49]{1,0:T(8,128)S(1)} %copy-done.12, f32[24,8,256]{2,1,0:T(8,128)S(1)} %get-tuple-element.65.x_ref, bf16[24,3,256]{2,1,0:T(4,128)(2,1)S(1)} %get-tuple-element.70.up_ref, bf16[24,3,256]{2,1,0:T(4,128)(2,1)S(1)} %get-tuple-element.71.down_ref, bf16[24,8,256]{2,1,0:T(8,128)(2,1)S(1)} %copy-done), custom_call_target="tpu_custom_call" | custom-call | tf_op jit(solution)/shard_map/pallas_call | solution.py:249
  181.9 3.7 %all-to-all-done.6.gathered_ref = bf16[8,24,896]{2,1,0:T(8,128)(2,1)S(1)} async-done(((bf16[8,24,896]{2,1,0:T(8,128)(2,1)}), bf16[8,24,896]{2,1,0:T(8,128)(2,1)S(1)}, u32[]{:S(2)}, u32[]{:S(2)}) %all-to-all-start.6) | async-done | bytes 344096 | tf_op jit(solution)/shard_map/all_to_all | solution.py:444
  (107 shorter events, 38.8 us)
Async XLA Ops:
  3.2 48.1 %copy-start.24 = (f32[768]{0:T(1024)S(1)}, f32[768]{0:T(1024)}, u32[]{:S(2)}) copy-start(f32[768]{0:T(1024)} %param.17) | copy-start | bytes 9220
  3.2 48.1 %copy-start.25 = (f32[768]{0:T(1024)S(1)}, f32[768]{0:T(1024)}, u32[]{:S(2)}) copy-start(f32[768]{0:T(1024)} %param.18) | copy-start | bytes 9220
  4.1 29.2 %all-to-all-start = ((bf16[8,24,896]{2,1,0:T(8,128)(2,1)}), bf16[8,24,896]{2,1,0:T(8,128)(2,1)S(1)}, u32[]{:S(2)}, u32[]{:S(2)}) async-start(bf16[8,24,896]{2,1,0:T(8,128)(2,1)} %shard_map.196), calls=%async_computation | async-start | bytes 688128 | tf_op jit(solution)/shard_map/all_to_all | solution.py:502
  17.3 6.0 %collective-permute-start = (bf16[24,3,256]{2,1,0:T(4,128)(2,1)S(1)}, bf16[24,3,256]{2,1,0:T(4,128)(2,1)S(1)}, u32[]{:S(2)}, u32[]{:S(2)}) collective-permute-start(bf16[24,3,256]{2,1,0:T(4,128)(2,1)S(1)} %get-tuple-element.93), channel_id=1, source_target_pairs={{32,64},{96,128},{160,192},{224,256},{288,320},{352,384},{416,448}... | collective-permute-start | bytes 110600 | tf_op jit(solution)/shard_map/ppermute | solution.py:458
  21.3 3.1 %collective-permute-start.1 = (bf16[24,3,256]{2,1,0:T(4,128)(2,1)S(1)}, bf16[24,3,256]{2,1,0:T(4,128)(2,1)S(1)}, u32[]{:S(2)}, u32[]{:S(2)}) collective-permute-start(bf16[24,3,256]{2,1,0:T(4,128)(2,1)S(1)} %get-tuple-element.92), channel_id=1, source_target_pairs={{0,32},{64,96},{128,160},{192,224},{256,288},{320,352},{384,416},{... | collective-permute-start | bytes 110600 | tf_op jit(solution)/shard_map/ppermute | solution.py:456
  33.4 27.7 %all-to-all-start.1 = ((bf16[32,24,128]{2,1,0:T(8,128)(2,1)}), bf16[32,24,128]{2,1,0:T(8,128)(2,1)S(1)}, u32[]{:S(2)}, u32[]{:S(2)}) async-start(bf16[32,24,128]{2,1,0:T(8,128)(2,1)} %shard_map.195), calls=%async_computation.1 | async-start | bytes 393216 | tf_op jit(solution)/shard_map/all_to_all | solution.py:448
  45.0 11.6 %collective-permute-start.2 = (bf16[8,24,896]{2,1,0:T(8,128)(2,1)S(1)}, bf16[8,24,896]{2,1,0:T(8,128)(2,1)S(1)}, u32[]{:S(2)}, u32[]{:S(2)}) collective-permute-start(bf16[8,24,896]{2,1,0:T(8,128)(2,1)S(1)} %all-to-all-done.own_ref), channel_id=1, source_target_pairs={{1,0},{2,1},{3,2},{0,3},{5,4},{6,5},{7,6},{4,7},{9,8},{10,9},{11,1... | collective-permute-start | bytes 1032200 | tf_op jit(solution)/shard_map/ppermute | solution.py:464
  49.3 11.7 %collective-permute-start.3 = (bf16[8,24,896]{2,1,0:T(8,128)(2,1)S(1)}, bf16[8,24,896]{2,1,0:T(8,128)(2,1)S(1)}, u32[]{:S(2)}, u32[]{:S(2)}) collective-permute-start(bf16[8,24,896]{2,1,0:T(8,128)(2,1)S(1)} %all-to-all-done.own_ref), channel_id=1, source_target_pairs={{3,0},{0,1},{1,2},{2,3},{7,4},{4,5},{5,6},{6,7},{11,8},{8,9},{9,10... | collective-permute-start | bytes 1032200 | tf_op jit(solution)/shard_map/ppermute | solution.py:464
  62.9 20.3 %all-to-all-start.2 = ((bf16[4,128,768]{2,1,0:T(8,128)(2,1)}), bf16[4,128,768]{2,1,0:T(8,128)(2,1)S(1)}, u32[]{:S(2)}, u32[]{:S(2)}) async-start(bf16[4,128,768]{2,1,0:T(8,128)(2,1)} %get-tuple-element.47), calls=%async_computation.2 | async-start | bytes 1572864 | tf_op jit(solution)/shard_map/all_to_all | solution.py:513
  73.9 6.3 %collective-permute-start.4 = (bf16[4,24,896]{2,1,0:T(8,128)(2,1)S(1)}, bf16[4,24,896]{2,1,0:T(8,128)(2,1)S(1)}, u32[]{:S(2)}, u32[]{:S(2)}) collective-permute-start(bf16[4,24,896]{2,1,0:T(8,128)(2,1)S(1)} %slice.63), channel_id=1, source_target_pairs={{1,0},{2,1},{3,2},{0,3},{5,4},{6,5},{7,6},{4,7},{9,8},{10,9},{11,1... | collective-permute-start | bytes 516104 | tf_op jit(solution)/shard_map/ppermute | solution.py:464
  75.8 7.4 %collective-permute-start.5 = (bf16[4,24,896]{2,1,0:T(8,128)(2,1)S(1)}, bf16[4,24,896]{2,1,0:T(8,128)(2,1)S(1)}, u32[]{:S(2)}, u32[]{:S(2)}) collective-permute-start(bf16[4,24,896]{2,1,0:T(8,128)(2,1)S(1)} %slice.64), channel_id=1, source_target_pairs={{3,0},{0,1},{1,2},{2,3},{7,4},{4,5},{5,6},{6,7},{11,8},{8,9},{9,10... | collective-permute-start | bytes 516104 | tf_op jit(solution)/shard_map/ppermute | solution.py:464
  83.2 4.2 %collective-permute-start.6 = (bf16[4,128,768]{2,1,0:T(8,128)(2,1)S(1)}, bf16[4,128,768]{2,1,0:T(8,128)(2,1)S(1)}, u32[]{:S(2)}, u32[]{:S(2)}) collective-permute-start(bf16[4,128,768]{2,1,0:T(8,128)(2,1)S(1)} %all-to-all-done.2.own_ref), channel_id=1, source_target_pairs={{0,32},{32,0},{1,33},{33,1},{2,34},{34,2},{3,35},{35,3},{4,36},{36... | collective-permute-start | bytes 2359304 | tf_op jit(solution)/shard_map/ppermute | solution.py:517
  91.4 17.8 %all-to-all-start.3 = ((bf16[8,64,768]{2,1,0:T(8,128)(2,1)}), bf16[8,64,768]{2,1,0:T(8,128)(2,1)S(1)}, u32[]{:S(2)}, u32[]{:S(2)}) async-start(bf16[8,64,768]{2,1,0:T(8,128)(2,1)} %get-tuple-element.56), calls=%async_computation.3 | async-start | bytes 1572864 | tf_op jit(solution)/shard_map/all_to_all | solution.py:521
  100.7 21.1 %collective-permute-start.7 = (bf16[8,24,768]{2,1,0:T(8,128)(2,1)S(1)}, bf16[8,24,768]{2,1,0:T(8,128)(2,1)S(1)}, u32[]{:S(2)}, u32[]{:S(2)}) collective-permute-start(bf16[8,24,768]{2,1,0:T(8,128)(2,1)S(1)} %bitcast.36), channel_id=1, source_target_pairs={{0,1},{1,2},{2,3},{3,0},{4,5},{5,6},{6,7},{7,4},{8,9},{9,10},{10,1... | collective-permute-start | bytes 884744 | tf_op jit(solution)/shard_map/ppermute | solution.py:471
  102.9 18.9 %collective-permute-start.8 = (bf16[8,24,768]{2,1,0:T(8,128)(2,1)S(1)}, bf16[8,24,768]{2,1,0:T(8,128)(2,1)S(1)}, u32[]{:S(2)}, u32[]{:S(2)}) collective-permute-start(bf16[8,24,768]{2,1,0:T(8,128)(2,1)S(1)} %bitcast.35), channel_id=1, source_target_pairs={{0,2},{1,3},{2,0},{3,1},{4,6},{5,7},{6,4},{7,5},{8,10},{9,11},{10,... | collective-permute-start | bytes 884744 | tf_op jit(solution)/shard_map/ppermute | solution.py:471
  105.3 16.5 %collective-permute-start.9 = (bf16[8,24,768]{2,1,0:T(8,128)(2,1)S(1)}, bf16[8,24,768]{2,1,0:T(8,128)(2,1)S(1)}, u32[]{:S(2)}, u32[]{:S(2)}) collective-permute-start(bf16[8,24,768]{2,1,0:T(8,128)(2,1)S(1)} %bitcast.34), channel_id=1, source_target_pairs={{0,3},{1,0},{2,1},{3,2},{4,7},{5,4},{6,5},{7,6},{8,11},{9,8},{10,9... | collective-permute-start | bytes 884744 | tf_op jit(solution)/shard_map/ppermute | solution.py:471
  110.4 23.5 %all-to-all-start.4 = ((bf16[32,16,128]{2,1,0:T(8,128)(2,1)}), bf16[32,16,128]{2,1,0:T(8,128)(2,1)S(1)}, u32[]{:S(2)}, u32[]{:S(2)}) async-start(bf16[32,16,128]{2,1,0:T(8,128)(2,1)} %shard_map.201), calls=%async_computation.4 | async-start | bytes 262144 | tf_op jit(solution)/shard_map/all_to_all | solution.py:448
  133.9 17.4 %all-to-all-start.5 = ((bf16[8,24,768]{2,1,0:T(8,128)(2,1)}), bf16[8,24,768]{2,1,0:T(8,128)(2,1)S(1)}, u32[]{:S(2)}, u32[]{:S(2)}) async-start(bf16[8,24,768]{2,1,0:T(8,128)(2,1)} %fusion.2), calls=%async_computation.5 | async-start | bytes 589824 | tf_op jit(solution)/shard_map/all_to_all | solution.py:525
  142.0 20.7 %collective-permute-start.11 = (bf16[24,3,256]{2,1,0:T(4,128)(2,1)S(1)}, bf16[24,3,256]{2,1,0:T(4,128)(2,1)S(1)}, u32[]{:S(2)}, u32[]{:S(2)}) collective-permute-start(bf16[24,3,256]{2,1,0:T(4,128)(2,1)S(1)} %get-tuple-element.87), channel_id=1, source_target_pairs={{32,64},{96,128},{160,192},{224,256},{288,320},{352,384},{416,448}... | collective-permute-start | bytes 110600 | tf_op jit(solution)/shard_map/ppermute | solution.py:458
  146.8 15.9 %collective-permute-start.12 = (bf16[24,3,256]{2,1,0:T(4,128)(2,1)S(1)}, bf16[24,3,256]{2,1,0:T(4,128)(2,1)S(1)}, u32[]{:S(2)}, u32[]{:S(2)}) collective-permute-start(bf16[24,3,256]{2,1,0:T(4,128)(2,1)S(1)} %get-tuple-element.86), channel_id=1, source_target_pairs={{0,32},{64,96},{128,160},{192,224},{256,288},{320,352},{384,416},{... | collective-permute-start | bytes 110600 | tf_op jit(solution)/shard_map/ppermute | solution.py:456
  148.9 29.4 %copy-start.23 = (bf16[768]{0:T(1024)(128)(2,1)S(1)}, bf16[768]{0:T(1024)(128)(2,1)}, u32[]{:S(2)}) copy-start(bf16[768]{0:T(1024)(128)(2,1)} %param.23) | copy-start | bytes 4612
  151.5 34.1 %copy-start.21 = (f32[24]{0:T(128)S(1)}, f32[24]{0:T(128)}, u32[]{:S(2)}) copy-start(f32[24]{0:T(128)} %param.22) | copy-start | bytes 292
  151.5 13.7 %collective-permute-start.10 = (bf16[24,896]{1,0:T(8,128)(2,1)S(1)}, bf16[24,896]{1,0:T(8,128)(2,1)S(1)}, u32[]{:S(2)}, u32[]{:S(2)}) collective-permute-start(bf16[24,896]{1,0:T(8,128)(2,1)S(1)} %pad_maximum_fusion), channel_id=1, source_target_pairs={{0,256},{256,0},{1,257},{257,1},{2,258},{258,2},{3,259},{259,3},{4... | collective-permute-start | bytes 129032 | tf_op jit(solution)/shard_map/ppermute | solution.py:534
  166.1 19.4 %all-to-all-start.6 = ((bf16[8,24,896]{2,1,0:T(8,128)(2,1)}), bf16[8,24,896]{2,1,0:T(8,128)(2,1)S(1)}, u32[]{:S(2)}, u32[]{:S(2)}) async-start(bf16[8,24,896]{2,1,0:T(8,128)(2,1)} %broadcast_in_dim.47), calls=%async_computation.6 | async-start | bytes 688128 | tf_op jit(solution)/shard_map/all_to_all | solution.py:444
  (23 other events, 229.9 us)

commit v7 on v6

--- a/solution.py
+++ b/solution.py
@@ -8,7 +8,8 @@
 from jax.sharding import Mesh, PartitionSpec as P
 
 LAT = ("zh", "x", "c")
-CHAN = ("zl", "y")
+ZLO = ("zq", "zp")
+CHAN = ("zq", "zp", "y")
 GROUP = 8
 F32 = jnp.float32
 BF = jnp.bfloat16
@@ -80,7 +81,7 @@
         h_rows[c] = bias_ref[c] + metric * stencil(taps_ref, c, row_shifts(ext, c, rows), False)
         return carry
 
-    lax.fori_loop(0, cdev, channel, 0, unroll=4)
+    lax.fori_loop(0, cdev, channel, 0, unroll=8)
     low = lax.broadcasted_iota(jnp.int32, (cdev, 128), 1) < 64
     for r in range(rows):
         h_row, dy_row = h_rows[:, r, :], dy_rows[:, r, :]
@@ -211,7 +212,7 @@
         return carry
 
     prods[408:, :] = jnp.zeros((prods.shape[0] - 408, 128), F32)
-    lax.fori_loop(0, cdev, channel, 0, unroll=4)
+    lax.fori_loop(0, cdev, channel, 0, unroll=8)
 
 
 def tap_sums(recv, x, up, down, metric, dy):
@@ -241,7 +242,7 @@
         out_ref[c] = dy_ref[c].astype(F32) + stencil(taps_ref, c, row_shifts(ext, c, rows), True)
         return carry
 
-    lax.fori_loop(0, cdev, channel, 0, unroll=4)
+    lax.fori_loop(0, cdev, channel, 0, unroll=8)
 
 
 def spread_back(taps, dconv, up, down, dy):
@@ -299,7 +300,7 @@
     )(*parts)
 
 
-def mlp_body(core_ref, own_ref, other_ref, wi_ref, wo_ref, bi_ref, gamma_ref, dn_ref, n_ref, dy_ref, g_ref, dpre_ref):
+def mlp_body(core_ref, own_ref, other_ref, wi_ref, wo_ref, bi_ref, gamma_ref, dn_ref, n_ref, dy_ref, acts_ref):
     members, lanes, _ = own_ref.shape
     piece = lanes // 2
     for at, ref in ((0, own_ref), (members, other_ref)):
@@ -308,11 +309,12 @@
             dy_ref[(at + k) * piece : (at + k + 1) * piece] = ref[k, piece:]
     pre = dot(n_ref[...], wi_ref[...], 1, 1) + bi_ref[...]
     cdf = 0.5 + 0.5 * lax.erf(pre * (0.5**0.5))
-    g_ref[...] = (pre * cdf).astype(BF)
+    hid = pre.shape[1]
+    acts_ref[:, :hid] = (pre * cdf).astype(BF)
     slope = cdf + pre * (jnp.exp(-0.5 * pre * pre) * (0.5 / 3.141592653589793) ** 0.5)
     dmlp = (gamma_ref[...] * dy_ref[...].astype(F32)).astype(BF)
     dpre = (slope * dot(dmlp, wo_ref[...], 1, 1)).astype(BF)
-    dpre_ref[...] = dpre
+    acts_ref[:, hid:] = dpre
     dn = dot(dpre, wi_ref[...], 1, 0).astype(BF)
     core = core_ref[0]
     for k in range(members):
@@ -329,19 +331,19 @@
             jax.ShapeDtypeStruct((2 * members, lanes // 2, chans), BF),
             jax.ShapeDtypeStruct((toks, chans), BF),
             jax.ShapeDtypeStruct((toks, chans), BF),
-            jax.ShapeDtypeStruct((toks, hid), BF),
-            jax.ShapeDtypeStruct((toks, hid), BF),
+            jax.ShapeDtypeStruct((toks, 2 * hid), BF),
         ],
         [smem()] + [vmem()] * 6,
     )(core, own, other, wi, wo, bi, gamma[None])
 
 
-def grads_body(part, ny, y_ref, n_ref, dy_ref, g_ref, dpre_ref, wo_ref, gamma_ref, out_ref, gam_ref, db_ref):
+def grads_body(part, ny, y_ref, n_ref, dy_ref, acts_ref, wo_ref, gamma_ref, out_ref, gam_ref, db_ref):
     toks = n_ref.shape[0]
-    hid = g_ref.shape[1]
+    hid = acts_ref.shape[1] // 2
     first, second = picks(hid // part, part)
-    dw_in = dot(dpre_ref[...], n_ref[...], 0, 0).astype(BF)
-    proj = dot(g_ref[...], dy_ref[...], 0, 0)
+    dpre = acts_ref[:, hid:]
+    dw_in = dot(dpre, n_ref[...], 0, 0).astype(BF)
+    proj = dot(acts_ref[:, :hid], dy_ref[...], 0, 0)
     gam_ref[...] = jnp.sum(wo_ref[...].astype(F32) * proj, 0, keepdims=True)
     dw_out = (proj * gamma_ref[...]).astype(BF)
     out_ref[...] = (dot(first, dw_in, 1, 0) + dot(second, dw_out, 1, 0)).astype(BF)
@@ -353,24 +355,31 @@
     ahead = ring + y_ref[0]
     owner = (block - ring * nz) * ny + jnp.where(ahead >= ny, ahead - ny, ahead)
     spot = jnp.where(lane == owner * 2 * part + place - block * part, 1.0, 0.0).astype(BF)
-    db = dot(jnp.ones((16, toks), BF), dpre_ref[...], 1, 0).astype(BF)
+    db = dot(jnp.ones((16, toks), BF), dpre, 1, 0).astype(BF)
     db_ref[...] = dot(db, spot, 1, 1)[:1]
 
 
-def grads(part, ny, y, n, dy, g, dpre, wo, gamma):
-    toks, chans = n.shape
+def grads(part, ny, y, n, dy, acts, wo, gamma):
+    chans = n.shape[1]
+    hid = acts.shape[1] // 2
     return call(
         functools.partial(grads_body, part, ny),
         [
-            jax.ShapeDtypeStruct((2 * g.shape[1], chans), BF),
+            jax.ShapeDtypeStruct((2 * hid, chans), BF),
             jax.ShapeDtypeStruct((1, chans), F32),
-            jax.ShapeDtypeStruct((1, 2 * g.shape[1]), F32),
-        ],
-        [smem()] + [vmem()] * 6,
-    )(y, n, dy, g, dpre, wo, gamma[None])
-
-
-def slices_body(part, member_ref, w_in_ref, w_out_ref, b_ref, out_ref):
+            jax.ShapeDtypeStruct((1, 2 * hid), F32),
+        ],
+        [smem()] + [vmem()] * 5,
+    )(y, n, dy, acts, wo, gamma[None])
+
+
+def slices_body(part, member_ref, w_in_hbm, w_out_hbm, b_hbm, out_ref, w_in_ref, w_out_ref, b_ref, sems):
+    pairs = ((w_in_hbm, w_in_ref), (w_out_hbm, w_out_ref), (b_hbm, b_ref))
+    copies = [pltpu.make_async_copy(src, dst, sems.at[i]) for i, (src, dst) in enumerate(pairs)]
+    for copy in copies:
+        copy.start()
+    for copy in copies:
+        copy.wait()
     hdev, chans = w_in_ref.shape
     row = lax.broadcasted_iota(jnp.int32, (2 * part, hdev), 0)
     place = lax.broadcasted_iota(jnp.int32, (2 * part, hdev), 1)
@@ -393,7 +402,13 @@
     return call(
         functools.partial(slices_body, part),
         jax.ShapeDtypeStruct((copies, 2 * part, w_in.shape[1] + SIDE), BF),
-        [smem()] + [vmem()] * 3,
+        [smem()] + [pl.BlockSpec(memory_space=pl.ANY)] * 3,
+        [
+            pltpu.VMEM(w_in.shape, BF),
+            pltpu.VMEM(w_out.shape, BF),
+            pltpu.VMEM((1,) + b_in.shape, F32),
+            pltpu.SemaphoreType.DMA((3,)),
+        ],
     )(member, w_in, w_out, b_in[None])
 
 
@@ -434,6 +449,14 @@
     )(gathered, gamma[None], b_out[None])
 
 
+def to_neighbour(blocks):
+    sides = blocks.reshape((blocks.shape[0] // 2, 2) + blocks.shape[1:])
+    mine = lax.axis_index("zp")
+    kept = lax.dynamic_index_in_dim(sides, mine, 1, keepdims=False)
+    sent = lax.dynamic_index_in_dim(sides, 1 - mine, 1, keepdims=False).astype(BF)
+    return kept + lax.ppermute(sent, "zp", [(0, 1), (1, 0)]).astype(F32)
+
+
 def two_parts(value):
     high = lax.reduce_precision(value, 8, 7)
     return high.astype(BF), (value - high).astype(BF)
@@ -489,7 +512,7 @@
     cdev, rows, width = block_input.shape
     chans = ln_gain.shape[0]
     tokens = rows * width
-    nz, ny = lax.axis_size("zl"), lax.axis_size("y")
+    nz, ny = lax.axis_size(ZLO), lax.axis_size("y")
     nchan = nz * ny
     hdev = w_in.shape[0]
     part = hdev // GROUP
@@ -499,7 +522,7 @@
     gamma_own = lax.dynamic_slice_in_dim(gamma_f, owner * cdev, cdev)
 
     member = lax.axis_index(("x", "c")).astype(jnp.int32)[None]
-    shards = lax.all_to_all(slices(part, nz, member, w_in, w_out, b_in), "zl", 0, 0, tiled=True)
+    shards = lax.all_to_all(slices(part, nz, member, w_in, w_out, b_in), ZLO, 0, 0, tiled=True)
 
     up, down = halos(block_input[:, :3], block_input[:, rows - 3 :])
     blocks = forward(kernel, conv_bias, block_input, up, down, metric, out_grad)
@@ -517,12 +540,13 @@
     other = lax.ppermute(pair, "c", [(0, 1), (1, 0)])
 
     core = lax.axis_index("c").astype(jnp.int32)[None]
-    dn, n, dy, g, dpre = mlp(core, pair, other, wi, wo, bi, gamma_f)
+    dn, n, dy, acts = mlp(core, pair, other, wi, wo, bi, gamma_f)
     dn = lax.all_to_all(dn, ("c", "x"), 0, 0, tiled=True)
 
-    dws, gam_part, db_part = grads(part, ny, lax.axis_index("y").astype(jnp.int32)[None], n, dy, g, dpre, wo, gamma_f)
-    dws = to_ring(dws.reshape(ny, nz, 2 * part, chans)).astype(BF)
-    dws = lax.all_to_all(dws, "zl", 0, 0, tiled=True)
+    dws, gam_part, db_part = grads(part, ny, lax.axis_index("y").astype(jnp.int32)[None], n, dy, acts, wo, gamma_f)
+    dws = to_ring(dws.reshape(ny, nz, 2 * part, chans))
+    dws = to_neighbour(dws).astype(BF)
+    dws = lax.all_to_all(dws, "zq", 0, 0, tiled=True)
     dws = jnp.sum(dws.astype(F32), 0)
 
     payload = exchange(norm_back(dn, nhat, rstd, ln_gain, gam_part, db_part, nchan))
@@ -556,7 +580,7 @@
 
 
 def solution(mesh):
-    split = Mesh(mesh.devices.reshape(2, 4, 2, 8, 4), ("zh", "x", "c", "zl", "y"))
+    split = Mesh(mesh.devices.reshape(2, 4, 2, 4, 2, 4), ("zh", "x", "c", "zq", "zp", "y"))
     return jax.shard_map(
         per_device,
         mesh=split,

time: 189 us -> 209 us (1.11)
  waiting for transfers between devices: 40 us -> 57.5 us
  starting transfers between devices: 115 us -> 122 us
  local copies, waits for them, and re-layouts: 9.54 us -> 4.73 us
    ppermute x3, waiting for transfers between devices: 0.01 us -> 6.83 us  [to_ring(): lax.ppermute(blocks[k], 'y', [(i, (i + k) % count) for i in range(count)])]
    all_to_all x2, waiting for transfers between devices: 6.89 us -> 12.9 us  [the longest x1 7.64 us: per_device(): dws = lax.all_to_all(dws, 'zq', 0, 0, tiled=True)]
    unnamed x54 -> x24, local copies, waits for them, and re-layouts: 7.37 us -> 2.54 us
    ppermute x0 -> x1, starting transfers between devices: none -> 2.96 us  [to_neighbour(): return kept + lax.ppermute(sent, 'zp', [(0, 1), (1, 0)]).astype(F32)]
    ppermute x0 -> x1, waiting for transfers between devices: none -> 2.92 us  [to_neighbour(): return kept + lax.ppermute(sent, 'zp', [(0, 1), (1, 0)]).astype(F32)]
    all_to_all x2, starting transfers between devices: 18.4 us -> 20.6 us  [the longest x1 13.1 us: per_device(): lax.all_to_all(slices(part, nz, member, w_in, w_out, b_in), ZLO, 0, 0, ti...]
  transfers between devices with their start and end apart: 20 -> 21, of which waited for: 11 -> 15; matrix products, arithmetic and copies ran while one was open for 1% -> 1% of each run, Pallas kernels for 8% -> 5%
where the time goes in v7:
time: 209 us; the launch traced here: 207 us
  starting transfers between devices  122 us (58%)
  waiting for transfers between devices  57.5 us (28%)
  Pallas kernels  20.4 us (10%)
  local copies, waits for them, and re-layouts  4.73 us (2%)
    all_to_all x2, starting transfers between devices, exchange(): return lax.all_to_all(blocks, CHAN, 0, 0, tiled=True)  23.6 us
    ppermute x4, waiting for transfers between devices, along_ring(): lax.ppermute(block, 'y', [((i + ahead) % count, i) for i in range(count)])  13.8 us
    all_to_all x1, starting transfers between devices, per_device(): lax.all_to_all(slices(part, nz, member, w_in, w_out, b_in), ZLO, 0, 0, ti...  13.1 us
    all_to_all x1, starting transfers between devices, to_all(): lax.all_to_all(jnp.broadcast_to(block[None], (count,) + block.shape), axi...  12.8 us
    all_to_all x2, waiting for transfers between devices, exchange(): return lax.all_to_all(blocks, CHAN, 0, 0, tiled=True)  12.1 us
    ppermute x4, starting transfers between devices, along_ring(): lax.ppermute(block, 'y', [((i + ahead) % count, i) for i in range(count)])  11.6 us
    ppermute x1, starting transfers between devices, per_device(): other = lax.ppermute(mine, 'zh', [(0, 1), (1, 0)]).astype(F32)  11 us
    ppermute x2, starting transfers between devices, halos(): lax.ppermute(jnp.where(even, first, last), LAT, pairs + [(j, i) for i, j...  10.2 us
  transfers between devices with their start and end apart: 21, of which 15 were waited for; matrix products, arithmetic and copies ran while one was open for 1% of the time, Pallas kernels for 5%

profile of v7, /device:TPU:1, one launch (start us, length us, event | category | flops | bytes accessed | tf_op | source)
XLA Modules:
  0.0 207.4 jit_solution(10656136836683843964)
XLA Ops:
  4.5 13.1 %all-to-all-start = ((bf16[8,24,896]{2,1,0:T(8,128)(2,1)}), bf16[8,24,896]{2,1,0:T(8,128)(2,1)S(1)}, u32[]{:S(2)}, u32[]{:S(2)}) async-start(bf16[8,24,896]{2,1,0:T(8,128)(2,1)} %shard_map.196), calls=%async_computation | async-start | bytes 688128 | tf_op jit(solution)/shard_map/all_to_all | solution.py:525
  17.7 4.0 %collective-permute-start = (bf16[24,3,256]{2,1,0:T(4,128)(2,1)S(1)}, bf16[24,3,256]{2,1,0:T(4,128)(2,1)S(1)}, u32[]{:S(2)}, u32[]{:S(2)}) collective-permute-start(bf16[24,3,256]{2,1,0:T(4,128)(2,1)S(1)} %get-tuple-element.91), channel_id=1, source_target_pairs={{32,64},{96,128},{160,192},{224,256},{288,320},{352,384},{416,448}... | collective-permute-start | bytes 110600 | tf_op jit(solution)/shard_map/ppermute | solution.py:481
  24.9 3.6 %shard_map.195 = bf16[32,24,128]{2,1,0:T(8,128)(2,1)} custom-call(f32[24,49]{1,0:T(8,128)S(1)} %copy-done.4, f32[24]{0:T(128)S(1)} %copy-done.6, bf16[24,8,256]{2,1,0:T(8,128)(2,1)S(1)} %copy-done.1, bf16[24,3,256]{2,1,0:T(4,128)(2,1)S(1)} %get-tuple-element.89.up_ref, bf16[24,3,256]{2,1,0:T(4,128)(2,1)S(1)} %get-tuple-element.88.down_ref, ...), custom_call_target="tpu_custom_call" | custom-call | tf_op jit(solution)/shard_map/pallas_call | solution.py:97
  28.5 5.3 %all-to-all-done.own_ref = bf16[8,24,896]{2,1,0:T(8,128)(2,1)S(1)} async-done(((bf16[8,24,896]{2,1,0:T(8,128)(2,1)}), bf16[8,24,896]{2,1,0:T(8,128)(2,1)S(1)}, u32[]{:S(2)}, u32[]{:S(2)}) %all-to-all-start) | async-done | bytes 344096 | tf_op jit(solution)/shard_map/all_to_all | solution.py:525
  33.8 11.6 %all-to-all-start.1 = ((bf16[32,24,128]{2,1,0:T(8,128)(2,1)}), bf16[32,24,128]{2,1,0:T(8,128)(2,1)S(1)}, u32[]{:S(2)}, u32[]{:S(2)}) async-start(bf16[32,24,128]{2,1,0:T(8,128)(2,1)} %shard_map.195), calls=%async_computation.1 | async-start | bytes 393216 | tf_op jit(solution)/shard_map/all_to_all | solution.py:471
  45.4 4.3 %collective-permute-start.2 = (bf16[8,24,896]{2,1,0:T(8,128)(2,1)S(1)}, bf16[8,24,896]{2,1,0:T(8,128)(2,1)S(1)}, u32[]{:S(2)}, u32[]{:S(2)}) collective-permute-start(bf16[8,24,896]{2,1,0:T(8,128)(2,1)S(1)} %all-to-all-done.own_ref), channel_id=1, source_target_pairs={{1,0},{2,1},{3,2},{0,3},{5,4},{6,5},{7,6},{4,7},{9,8},{10,9},{11,1... | collective-permute-start | bytes 1032200 | tf_op jit(solution)/shard_map/ppermute | solution.py:487
  51.7 5.3 %collective-permute-done.2.one_ref = bf16[8,24,896]{2,1,0:T(8,128)(2,1)S(1)} collective-permute-done((bf16[8,24,896]{2,1,0:T(8,128)(2,1)S(1)}, bf16[8,24,896]{2,1,0:T(8,128)(2,1)S(1)}, u32[]{:S(2)}, u32[]{:S(2)}) %collective-permute-start.2) | collective-permute-done | bytes 344096 | tf_op jit(solution)/shard_map/ppermute | solution.py:487
  57.0 4.5 %collective-permute-done.3.last_ref = bf16[8,24,896]{2,1,0:T(8,128)(2,1)S(1)} collective-permute-done((bf16[8,24,896]{2,1,0:T(8,128)(2,1)S(1)}, bf16[8,24,896]{2,1,0:T(8,128)(2,1)S(1)}, u32[]{:S(2)}, u32[]{:S(2)}) %collective-permute-start.3) | collective-permute-done | bytes 344096 | tf_op jit(solution)/shard_map/ppermute | solution.py:487
  62.7 10.2 %all-to-all-start.2 = ((bf16[4,128,768]{2,1,0:T(8,128)(2,1)}), bf16[4,128,768]{2,1,0:T(8,128)(2,1)S(1)}, u32[]{:S(2)}, u32[]{:S(2)}) async-start(bf16[4,128,768]{2,1,0:T(8,128)(2,1)} %get-tuple-element.46), calls=%async_computation.2 | async-start | bytes 1572864 | tf_op jit(solution)/shard_map/all_to_all | solution.py:536
  74.8 3.4 %collective-permute-start.5 = (bf16[4,24,896]{2,1,0:T(8,128)(2,1)S(1)}, bf16[4,24,896]{2,1,0:T(8,128)(2,1)S(1)}, u32[]{:S(2)}, u32[]{:S(2)}) collective-permute-start(bf16[4,24,896]{2,1,0:T(8,128)(2,1)S(1)} %slice.64), channel_id=1, source_target_pairs={{3,0},{0,1},{1,2},{2,3},{7,4},{4,5},{5,6},{6,7},{11,8},{8,9},{9,10... | collective-permute-start | bytes 516104 | tf_op jit(solution)/shard_map/ppermute | solution.py:487
  96.6 3.8 %collective-permute-start.9 = (bf16[8,24,768]{2,1,0:T(8,128)(2,1)S(1)}, bf16[8,24,768]{2,1,0:T(8,128)(2,1)S(1)}, u32[]{:S(2)}, u32[]{:S(2)}) collective-permute-start(bf16[8,24,768]{2,1,0:T(8,128)(2,1)S(1)} %bitcast.43), channel_id=1, source_target_pairs={{0,3},{1,0},{2,1},{3,2},{4,7},{5,4},{6,5},{7,6},{8,11},{9,8},{10,9... | collective-permute-start | bytes 884744 | tf_op jit(solution)/shard_map/ppermute | solution.py:494
  100.5 4.8 %all-to-all-start.3 = ((bf16[8,64,768]{2,1,0:T(8,128)(2,1)}), bf16[8,64,768]{2,1,0:T(8,128)(2,1)S(1)}, u32[]{:S(2)}, u32[]{:S(2)}) async-start(bf16[8,64,768]{2,1,0:T(8,128)(2,1)} %get-tuple-element.55), calls=%async_computation.3 | async-start | bytes 1572864 | tf_op jit(solution)/shard_map/all_to_all | solution.py:544
  105.3 4.6 %collective-permute-done.7 = bf16[8,24,768]{2,1,0:T(8,128)(2,1)S(1)} collective-permute-done((bf16[8,24,768]{2,1,0:T(8,128)(2,1)S(1)}, bf16[8,24,768]{2,1,0:T(8,128)(2,1)S(1)}, u32[]{:S(2)}, u32[]{:S(2)}) %collective-permute-start.7) | collective-permute-done | bytes 294944 | tf_op jit(solution)/shard_map/ppermute | solution.py:494
  112.3 3.0 %collective-permute-start.10 = (bf16[4,24,768]{2,1,0:T(8,128)(2,1)S(1)}, bf16[4,24,768]{2,1,0:T(8,128)(2,1)S(1)}, u32[]{:S(2)}, u32[]{:S(2)}) collective-permute-start(bf16[4,24,768]{2,1,0:T(8,128)(2,1)S(1)} %fusion.3), channel_id=1, source_target_pairs={{0,4},{4,0},{1,5},{5,1},{2,6},{6,2},{3,7},{7,3},{8,12},{12,8},{9,1... | collective-permute-start | bytes 442376 | tf_op jit(solution)/shard_map/ppermute | solution.py:457
  115.3 2.9 %collective-permute-done.10 = bf16[4,24,768]{2,1,0:T(8,128)(2,1)S(1)} collective-permute-done((bf16[4,24,768]{2,1,0:T(8,128)(2,1)S(1)}, bf16[4,24,768]{2,1,0:T(8,128)(2,1)S(1)}, u32[]{:S(2)}, u32[]{:S(2)}) %collective-permute-start.10) | collective-permute-done | bytes 147488 | tf_op jit(solution)/shard_map/ppermute | solution.py:457
  118.9 7.5 %all-to-all-start.5 = ((bf16[4,24,768]{2,1,0:T(8,128)(2,1)}), bf16[4,24,768]{2,1,0:T(8,128)(2,1)S(1)}, u32[]{:S(2)}, u32[]{:S(2)}) async-start(bf16[4,24,768]{2,1,0:T(8,128)(2,1)} %fusion.2), calls=%async_computation.5 | async-start | bytes 294912 | tf_op jit(solution)/shard_map/all_to_all | solution.py:549
  127.6 7.6 %all-to-all-done.5 = bf16[4,24,768]{2,1,0:T(8,128)(2,1)S(1)} async-done(((bf16[4,24,768]{2,1,0:T(8,128)(2,1)}), bf16[4,24,768]{2,1,0:T(8,128)(2,1)S(1)}, u32[]{:S(2)}, u32[]{:S(2)}) %all-to-all-start.5) | async-done | bytes 147488 | tf_op jit(solution)/shard_map/all_to_all | solution.py:549
  135.2 12.1 %all-to-all-start.4 = ((bf16[32,16,128]{2,1,0:T(8,128)(2,1)}), bf16[32,16,128]{2,1,0:T(8,128)(2,1)S(1)}, u32[]{:S(2)}, u32[]{:S(2)}) async-start(bf16[32,16,128]{2,1,0:T(8,128)(2,1)} %shard_map.201), calls=%async_computation.4 | async-start | bytes 262144 | tf_op jit(solution)/shard_map/all_to_all | solution.py:471
  147.3 12.1 %all-to-all-done.4.recv_ref = bf16[32,16,128]{2,1,0:T(8,128)(2,1)S(1)} async-done(((bf16[32,16,128]{2,1,0:T(8,128)(2,1)}), bf16[32,16,128]{2,1,0:T(8,128)(2,1)S(1)}, u32[]{:S(2)}, u32[]{:S(2)}) %all-to-all-start.4) | async-done | bytes 131104 | tf_op jit(solution)/shard_map/all_to_all | solution.py:471
  161.9 6.3 %collective-permute-start.12 = (bf16[24,3,256]{2,1,0:T(4,128)(2,1)S(1)}, bf16[24,3,256]{2,1,0:T(4,128)(2,1)S(1)}, u32[]{:S(2)}, u32[]{:S(2)}) collective-permute-start(bf16[24,3,256]{2,1,0:T(4,128)(2,1)S(1)} %get-tuple-element.85), channel_id=1, source_target_pairs={{32,64},{96,128},{160,192},{224,256},{288,320},{352,384},{416,448}... | collective-permute-start | bytes 110600 | tf_op jit(solution)/shard_map/ppermute | solution.py:481
  170.6 11.0 %collective-permute-start.11 = (bf16[24,896]{1,0:T(8,128)(2,1)S(1)}, bf16[24,896]{1,0:T(8,128)(2,1)S(1)}, u32[]{:S(2)}, u32[]{:S(2)}) collective-permute-start(bf16[24,896]{1,0:T(8,128)(2,1)S(1)} %pad_maximum_fusion), channel_id=1, source_target_pairs={{0,256},{256,0},{1,257},{257,1},{2,258},{258,2},{3,259},{259,3},{4... | collective-permute-start | bytes 129032 | tf_op jit(solution)/shard_map/ppermute | solution.py:558
  185.1 12.8 %all-to-all-start.6 = ((bf16[8,24,896]{2,1,0:T(8,128)(2,1)}), bf16[8,24,896]{2,1,0:T(8,128)(2,1)S(1)}, u32[]{:S(2)}, u32[]{:S(2)}) async-start(bf16[8,24,896]{2,1,0:T(8,128)(2,1)} %broadcast_in_dim.47), calls=%async_computation.6 | async-start | bytes 688128 | tf_op jit(solution)/shard_map/all_to_all | solution.py:467
  198.0 3.4 %shard_map.203 = f32[24,8,256]{2,1,0:T(8,128)} custom-call(f32[24,49]{1,0:T(8,128)S(1)} %copy-done.4, f32[24,8,256]{2,1,0:T(8,128)S(1)} %get-tuple-element.63.x_ref, bf16[24,3,256]{2,1,0:T(4,128)(2,1)S(1)} %get-tuple-element.68.up_ref, bf16[24,3,256]{2,1,0:T(4,128)(2,1)S(1)} %get-tuple-element.69.down_ref, bf16[24,8,256]{2,1,0:T(8,128)(2,1)S(1)} %copy-done), custom_call_target="tpu_custom_call" | custom-call | tf_op jit(solution)/shard_map/pallas_call | solution.py:250
  201.4 3.8 %all-to-all-done.6.gathered_ref = bf16[8,24,896]{2,1,0:T(8,128)(2,1)S(1)} async-done(((bf16[8,24,896]{2,1,0:T(8,128)(2,1)}), bf16[8,24,896]{2,1,0:T(8,128)(2,1)S(1)}, u32[]{:S(2)}, u32[]{:S(2)}) %all-to-all-start.6) | async-done | bytes 344096 | tf_op jit(solution)/shard_map/all_to_all | solution.py:467
  (81 shorter events, 45.3 us)
Async XLA Ops:
  3.2 48.5 %copy-start.9 = (f32[768]{0:T(1024)S(1)}, f32[768]{0:T(1024)}, u32[]{:S(2)}) copy-start(f32[768]{0:T(1024)} %param.17) | copy-start | bytes 9220
  3.2 48.5 %copy-start.10 = (f32[768]{0:T(1024)S(1)}, f32[768]{0:T(1024)}, u32[]{:S(2)}) copy-start(f32[768]{0:T(1024)} %param.18) | copy-start | bytes 9220
  4.5 29.3 %all-to-all-start = ((bf16[8,24,896]{2,1,0:T(8,128)(2,1)}), bf16[8,24,896]{2,1,0:T(8,128)(2,1)S(1)}, u32[]{:S(2)}, u32[]{:S(2)}) async-start(bf16[8,24,896]{2,1,0:T(8,128)(2,1)} %shard_map.196), calls=%async_computation | async-start | bytes 688128 | tf_op jit(solution)/shard_map/all_to_all | solution.py:525
  17.7 6.0 %collective-permute-start = (bf16[24,3,256]{2,1,0:T(4,128)(2,1)S(1)}, bf16[24,3,256]{2,1,0:T(4,128)(2,1)S(1)}, u32[]{:S(2)}, u32[]{:S(2)}) collective-permute-start(bf16[24,3,256]{2,1,0:T(4,128)(2,1)S(1)} %get-tuple-element.91), channel_id=1, source_target_pairs={{32,64},{96,128},{160,192},{224,256},{288,320},{352,384},{416,448}... | collective-permute-start | bytes 110600 | tf_op jit(solution)/shard_map/ppermute | solution.py:481
  21.7 3.1 %collective-permute-start.1 = (bf16[24,3,256]{2,1,0:T(4,128)(2,1)S(1)}, bf16[24,3,256]{2,1,0:T(4,128)(2,1)S(1)}, u32[]{:S(2)}, u32[]{:S(2)}) collective-permute-start(bf16[24,3,256]{2,1,0:T(4,128)(2,1)S(1)} %get-tuple-element.90), channel_id=1, source_target_pairs={{0,32},{64,96},{128,160},{192,224},{256,288},{320,352},{384,416},{... | collective-permute-start | bytes 110600 | tf_op jit(solution)/shard_map/ppermute | solution.py:479
  33.8 27.7 %all-to-all-start.1 = ((bf16[32,24,128]{2,1,0:T(8,128)(2,1)}), bf16[32,24,128]{2,1,0:T(8,128)(2,1)S(1)}, u32[]{:S(2)}, u32[]{:S(2)}) async-start(bf16[32,24,128]{2,1,0:T(8,128)(2,1)} %shard_map.195), calls=%async_computation.1 | async-start | bytes 393216 | tf_op jit(solution)/shard_map/all_to_all | solution.py:471
  45.4 11.6 %collective-permute-start.2 = (bf16[8,24,896]{2,1,0:T(8,128)(2,1)S(1)}, bf16[8,24,896]{2,1,0:T(8,128)(2,1)S(1)}, u32[]{:S(2)}, u32[]{:S(2)}) collective-permute-start(bf16[8,24,896]{2,1,0:T(8,128)(2,1)S(1)} %all-to-all-done.own_ref), channel_id=1, source_target_pairs={{1,0},{2,1},{3,2},{0,3},{5,4},{6,5},{7,6},{4,7},{9,8},{10,9},{11,1... | collective-permute-start | bytes 1032200 | tf_op jit(solution)/shard_map/ppermute | solution.py:487
  49.8 11.7 %collective-permute-start.3 = (bf16[8,24,896]{2,1,0:T(8,128)(2,1)S(1)}, bf16[8,24,896]{2,1,0:T(8,128)(2,1)S(1)}, u32[]{:S(2)}, u32[]{:S(2)}) collective-permute-start(bf16[8,24,896]{2,1,0:T(8,128)(2,1)S(1)} %all-to-all-done.own_ref), channel_id=1, source_target_pairs={{3,0},{0,1},{1,2},{2,3},{7,4},{4,5},{5,6},{6,7},{11,8},{8,9},{9,10... | collective-permute-start | bytes 1032200 | tf_op jit(solution)/shard_map/ppermute | solution.py:487
  62.7 20.2 %all-to-all-start.2 = ((bf16[4,128,768]{2,1,0:T(8,128)(2,1)}), bf16[4,128,768]{2,1,0:T(8,128)(2,1)S(1)}, u32[]{:S(2)}, u32[]{:S(2)}) async-start(bf16[4,128,768]{2,1,0:T(8,128)(2,1)} %get-tuple-element.46), calls=%async_computation.2 | async-start | bytes 1572864 | tf_op jit(solution)/shard_map/all_to_all | solution.py:536
  72.9 6.4 %collective-permute-start.4 = (bf16[4,24,896]{2,1,0:T(8,128)(2,1)S(1)}, bf16[4,24,896]{2,1,0:T(8,128)(2,1)S(1)}, u32[]{:S(2)}, u32[]{:S(2)}) collective-permute-start(bf16[4,24,896]{2,1,0:T(8,128)(2,1)S(1)} %slice.63), channel_id=1, source_target_pairs={{1,0},{2,1},{3,2},{0,3},{5,4},{6,5},{7,6},{4,7},{9,8},{10,9},{11,1... | collective-permute-start | bytes 516104 | tf_op jit(solution)/shard_map/ppermute | solution.py:487
  74.8 7.4 %collective-permute-start.5 = (bf16[4,24,896]{2,1,0:T(8,128)(2,1)S(1)}, bf16[4,24,896]{2,1,0:T(8,128)(2,1)S(1)}, u32[]{:S(2)}, u32[]{:S(2)}) collective-permute-start(bf16[4,24,896]{2,1,0:T(8,128)(2,1)S(1)} %slice.64), channel_id=1, source_target_pairs={{3,0},{0,1},{1,2},{2,3},{7,4},{4,5},{5,6},{6,7},{11,8},{8,9},{9,10... | collective-permute-start | bytes 516104 | tf_op jit(solution)/shard_map/ppermute | solution.py:487
  82.9 4.2 %collective-permute-start.6 = (bf16[4,128,768]{2,1,0:T(8,128)(2,1)S(1)}, bf16[4,128,768]{2,1,0:T(8,128)(2,1)S(1)}, u32[]{:S(2)}, u32[]{:S(2)}) collective-permute-start(bf16[4,128,768]{2,1,0:T(8,128)(2,1)S(1)} %all-to-all-done.2.own_ref), channel_id=1, source_target_pairs={{0,32},{32,0},{1,33},{33,1},{2,34},{34,2},{3,35},{35,3},{4,36},{36... | collective-permute-start | bytes 2359304 | tf_op jit(solution)/shard_map/ppermute | solution.py:540
  92.0 17.9 %collective-permute-start.7 = (bf16[8,24,768]{2,1,0:T(8,128)(2,1)S(1)}, bf16[8,24,768]{2,1,0:T(8,128)(2,1)S(1)}, u32[]{:S(2)}, u32[]{:S(2)}) collective-permute-start(bf16[8,24,768]{2,1,0:T(8,128)(2,1)S(1)} %bitcast.45), channel_id=1, source_target_pairs={{0,1},{1,2},{2,3},{3,0},{4,5},{5,6},{6,7},{7,4},{8,9},{9,10},{10,1... | collective-permute-start | bytes 884744 | tf_op jit(solution)/shard_map/ppermute | solution.py:494
  94.0 16.0 %collective-permute-start.8 = (bf16[8,24,768]{2,1,0:T(8,128)(2,1)S(1)}, bf16[8,24,768]{2,1,0:T(8,128)(2,1)S(1)}, u32[]{:S(2)}, u32[]{:S(2)}) collective-permute-start(bf16[8,24,768]{2,1,0:T(8,128)(2,1)S(1)} %bitcast.44), channel_id=1, source_target_pairs={{0,2},{1,3},{2,0},{3,1},{4,6},{5,7},{6,4},{7,5},{8,10},{9,11},{10,... | collective-permute-start | bytes 884744 | tf_op jit(solution)/shard_map/ppermute | solution.py:494
  96.6 15.5 %collective-permute-start.9 = (bf16[8,24,768]{2,1,0:T(8,128)(2,1)S(1)}, bf16[8,24,768]{2,1,0:T(8,128)(2,1)S(1)}, u32[]{:S(2)}, u32[]{:S(2)}) collective-permute-start(bf16[8,24,768]{2,1,0:T(8,128)(2,1)S(1)} %bitcast.43), channel_id=1, source_target_pairs={{0,3},{1,0},{2,1},{3,2},{4,7},{5,4},{6,5},{7,6},{8,11},{9,8},{10,9... | collective-permute-start | bytes 884744 | tf_op jit(solution)/shard_map/ppermute | solution.py:494
  100.5 18.4 %all-to-all-start.3 = ((bf16[8,64,768]{2,1,0:T(8,128)(2,1)}), bf16[8,64,768]{2,1,0:T(8,128)(2,1)S(1)}, u32[]{:S(2)}, u32[]{:S(2)}) async-start(bf16[8,64,768]{2,1,0:T(8,128)(2,1)} %get-tuple-element.55), calls=%async_computation.3 | async-start | bytes 1572864 | tf_op jit(solution)/shard_map/all_to_all | solution.py:544
  112.3 5.9 %collective-permute-start.10 = (bf16[4,24,768]{2,1,0:T(8,128)(2,1)S(1)}, bf16[4,24,768]{2,1,0:T(8,128)(2,1)S(1)}, u32[]{:S(2)}, u32[]{:S(2)}) collective-permute-start(bf16[4,24,768]{2,1,0:T(8,128)(2,1)S(1)} %fusion.3), channel_id=1, source_target_pairs={{0,4},{4,0},{1,5},{5,1},{2,6},{6,2},{3,7},{7,3},{8,12},{12,8},{9,1... | collective-permute-start | bytes 442376 | tf_op jit(solution)/shard_map/ppermute | solution.py:457
  118.9 16.3 %all-to-all-start.5 = ((bf16[4,24,768]{2,1,0:T(8,128)(2,1)}), bf16[4,24,768]{2,1,0:T(8,128)(2,1)S(1)}, u32[]{:S(2)}, u32[]{:S(2)}) async-start(bf16[4,24,768]{2,1,0:T(8,128)(2,1)} %fusion.2), calls=%async_computation.5 | async-start | bytes 294912 | tf_op jit(solution)/shard_map/all_to_all | solution.py:549
  135.2 24.2 %all-to-all-start.4 = ((bf16[32,16,128]{2,1,0:T(8,128)(2,1)}), bf16[32,16,128]{2,1,0:T(8,128)(2,1)S(1)}, u32[]{:S(2)}, u32[]{:S(2)}) async-start(bf16[32,16,128]{2,1,0:T(8,128)(2,1)} %shard_map.201), calls=%async_computation.4 | async-start | bytes 262144 | tf_op jit(solution)/shard_map/all_to_all | solution.py:471
  161.9 19.6 %collective-permute-start.12 = (bf16[24,3,256]{2,1,0:T(4,128)(2,1)S(1)}, bf16[24,3,256]{2,1,0:T(4,128)(2,1)S(1)}, u32[]{:S(2)}, u32[]{:S(2)}) collective-permute-start(bf16[24,3,256]{2,1,0:T(4,128)(2,1)S(1)} %get-tuple-element.85), channel_id=1, source_target_pairs={{32,64},{96,128},{160,192},{224,256},{288,320},{352,384},{416,448}... | collective-permute-start | bytes 110600 | tf_op jit(solution)/shard_map/ppermute | solution.py:481
  168.2 13.3 %collective-permute-start.13 = (bf16[24,3,256]{2,1,0:T(4,128)(2,1)S(1)}, bf16[24,3,256]{2,1,0:T(4,128)(2,1)S(1)}, u32[]{:S(2)}, u32[]{:S(2)}) collective-permute-start(bf16[24,3,256]{2,1,0:T(4,128)(2,1)S(1)} %get-tuple-element.84), channel_id=1, source_target_pairs={{0,32},{64,96},{128,160},{192,224},{256,288},{320,352},{384,416},{... | collective-permute-start | bytes 110600 | tf_op jit(solution)/shard_map/ppermute | solution.py:479
  170.6 34.7 %copy-start.7 = (f32[24]{0:T(128)S(1)}, f32[24]{0:T(128)}, u32[]{:S(2)}) copy-start(f32[24]{0:T(128)} %param.22) | copy-start | bytes 292
  170.6 13.6 %collective-permute-start.11 = (bf16[24,896]{1,0:T(8,128)(2,1)S(1)}, bf16[24,896]{1,0:T(8,128)(2,1)S(1)}, u32[]{:S(2)}, u32[]{:S(2)}) collective-permute-start(bf16[24,896]{1,0:T(8,128)(2,1)S(1)} %pad_maximum_fusion), channel_id=1, source_target_pairs={{0,256},{256,0},{1,257},{257,1},{2,258},{258,2},{3,259},{259,3},{4... | collective-permute-start | bytes 129032 | tf_op jit(solution)/shard_map/ppermute | solution.py:558
  185.1 20.1 %all-to-all-start.6 = ((bf16[8,24,896]{2,1,0:T(8,128)(2,1)}), bf16[8,24,896]{2,1,0:T(8,128)(2,1)S(1)}, u32[]{:S(2)}, u32[]{:S(2)}) async-start(bf16[8,24,896]{2,1,0:T(8,128)(2,1)} %broadcast_in_dim.47), calls=%async_computation.6 | async-start | bytes 688128 | tf_op jit(solution)/shard_map/all_to_all | solution.py:467
  (9 other events, 129.6 us)

commit v8 on v7

--- a/solution.py
+++ b/solution.py
@@ -74,19 +74,22 @@
 def forward_body(taps_ref, bias_ref, x_ref, up_ref, down_ref, metric_ref, dy_ref, out_ref, ext, h_rows, dy_rows):
     cdev, rows, width = x_ref.shape
     fill_rows(x_ref, up_ref, down_ref, ext)
-    dy_rows[...] = dy_ref[...].astype(F32)
+    dy_flat = dy_ref[...].astype(F32).reshape(cdev * rows, width)
+    for t in range(width // 128):
+        dy_rows[t] = dy_flat[:, t * 128 : t * 128 + 128]
     metric = jnp.broadcast_to(metric_ref[...], (rows, width))
 
     def channel(c, carry):
-        h_rows[c] = bias_ref[c] + metric * stencil(taps_ref, c, row_shifts(ext, c, rows), False)
+        h = bias_ref[c] + metric * stencil(taps_ref, c, row_shifts(ext, c, rows), False)
+        for t in range(width // 128):
+            h_rows[t, pl.ds(pl.multiple_of(c * rows, rows), rows), :] = h[:, t * 128 : t * 128 + 128]
         return carry
 
     lax.fori_loop(0, cdev, channel, 0, unroll=8)
     low = lax.broadcasted_iota(jnp.int32, (cdev, 128), 1) < 64
     for r in range(rows):
-        h_row, dy_row = h_rows[:, r, :], dy_rows[:, r, :]
         for t in range(width // 128):
-            h_tile, dy_tile = h_row[:, t * 128 : t * 128 + 128], dy_row[:, t * 128 : t * 128 + 128]
+            h_tile, dy_tile = h_rows[t, pl.ds(r, cdev, rows), :], dy_rows[t, pl.ds(r, cdev, rows), :]
             at = (r * width + t * 128) // 64
             out_ref[at] = jnp.where(low, h_tile, pltpu.roll(dy_tile, 64, 1)).astype(BF)
             out_ref[at + 1] = jnp.where(low, pltpu.roll(h_tile, 64, 1), dy_tile).astype(BF)
@@ -100,8 +103,8 @@
         [smem(), smem()] + [vmem()] * 5,
         [
             pltpu.VMEM((cdev, EXT, width), F32),
-            pltpu.VMEM((cdev, rows, width), F32),
-            pltpu.VMEM((cdev, rows, width), F32),
+            pltpu.VMEM((width // 128, cdev * rows, 128), F32),
+            pltpu.VMEM((width // 128, cdev * rows, 128), F32),
         ],
     )(taps, bias, x, up, down, metric[:, None], dy)
 
@@ -182,16 +185,16 @@
         for t in range(width // 128):
             at = (r * width + t * 128) // 64
             first, second = recv_ref[at].astype(F32), recv_ref[at + 1].astype(F32)
-            lanes = slice(t * 128, t * 128 + 128)
-            dh_rows[:16, r, lanes] = jnp.where(low16, first, pltpu.roll(second, 64, 1))
-            dh_rows[16:, r, lanes] = jnp.where(low8, pltpu.roll(first[:8], 64, 1), second[:8])
+            dh_rows[t, pl.ds(r, 16, rows), :] = jnp.where(low16, first, pltpu.roll(second, 64, 1))
+            dh_rows[t, pl.ds(16 * rows + r, 8, rows), :] = jnp.where(low8, pltpu.roll(first[:8], 64, 1), second[:8])
             extra = extra + first[8:] + second[8:]
     for g in range(3):
         extra_ref[8 * g : 8 * g + 8] = pltpu.roll(extra, 64 - 8 * g, 1)
     metric = jnp.broadcast_to(metric_ref[...], (rows, width))
 
     def channel(c, carry):
-        dh = dh_rows[c]
+        here = pl.ds(pl.multiple_of(c * rows, rows), rows)
+        dh = jnp.concatenate([dh_rows[t, here, :] for t in range(width // 128)], 1)
         dconv = metric * dh
         dconv_ref[c] = dconv
         ends_ref[0, c] = dconv[:3].astype(BF)
@@ -228,7 +231,7 @@
         [vmem()] * 6,
         [
             pltpu.VMEM((cdev, EXT, width), F32),
-            pltpu.VMEM((cdev, rows, width), F32),
+            pltpu.VMEM((width // 128, cdev * rows, 128), F32),
             pltpu.VMEM((448, 128), F32),
         ],
     )(recv, x, up, down, metric[:, None], dy)
@@ -337,7 +340,7 @@
     )(core, own, other, wi, wo, bi, gamma[None])
 
 
-def grads_body(part, ny, y_ref, n_ref, dy_ref, acts_ref, wo_ref, gamma_ref, out_ref, gam_ref, db_ref):
+def grads_body(part, ny, place_ref, n_ref, dy_ref, acts_ref, wo_ref, gamma_ref, out_ref, gam_ref, db_ref):
     toks = n_ref.shape[0]
     hid = acts_ref.shape[1] // 2
     first, second = picks(hid // part, part)
@@ -352,14 +355,18 @@
     place = lax.broadcasted_iota(jnp.int32, (1, hid), 1)
     block = jnp.floor((place.astype(F32) + 0.5) * (1.0 / part)).astype(jnp.int32)
     ring = jnp.floor((block.astype(F32) + 0.5) * (1.0 / nz)).astype(jnp.int32)
-    ahead = ring + y_ref[0]
-    owner = (block - ring * nz) * ny + jnp.where(ahead >= ny, ahead - ny, ahead)
+    ahead = ring + place_ref[0]
+    along_z = block - ring * nz
+    far = along_z >= nz // 2
+    zq = jnp.where(far, along_z - nz // 2, along_z)
+    zp = jnp.where(far, 1 - place_ref[1], place_ref[1])
+    owner = (zq * 2 + zp) * ny + jnp.where(ahead >= ny, ahead - ny, ahead)
     spot = jnp.where(lane == owner * 2 * part + place - block * part, 1.0, 0.0).astype(BF)
     db = dot(jnp.ones((16, toks), BF), dpre, 1, 0).astype(BF)
     db_ref[...] = dot(db, spot, 1, 1)[:1]
 
 
-def grads(part, ny, y, n, dy, acts, wo, gamma):
+def grads(part, ny, place, n, dy, acts, wo, gamma):
     chans = n.shape[1]
     hid = acts.shape[1] // 2
     return call(
@@ -370,16 +377,10 @@
             jax.ShapeDtypeStruct((1, 2 * hid), F32),
         ],
         [smem()] + [vmem()] * 5,
-    )(y, n, dy, acts, wo, gamma[None])
-
-
-def slices_body(part, member_ref, w_in_hbm, w_out_hbm, b_hbm, out_ref, w_in_ref, w_out_ref, b_ref, sems):
-    pairs = ((w_in_hbm, w_in_ref), (w_out_hbm, w_out_ref), (b_hbm, b_ref))
-    copies = [pltpu.make_async_copy(src, dst, sems.at[i]) for i, (src, dst) in enumerate(pairs)]
-    for copy in copies:
-        copy.start()
-    for copy in copies:
-        copy.wait()
+    )(place, n, dy, acts, wo, gamma[None])
+
+
+def slices_body(part, member_ref, w_in_ref, w_out_ref, b_ref, out_ref):
     hdev, chans = w_in_ref.shape
     row = lax.broadcasted_iota(jnp.int32, (2 * part, hdev), 0)
     place = lax.broadcasted_iota(jnp.int32, (2 * part, hdev), 1)
@@ -402,13 +403,7 @@
     return call(
         functools.partial(slices_body, part),
         jax.ShapeDtypeStruct((copies, 2 * part, w_in.shape[1] + SIDE), BF),
-        [smem()] + [pl.BlockSpec(memory_space=pl.ANY)] * 3,
-        [
-            pltpu.VMEM(w_in.shape, BF),
-            pltpu.VMEM(w_out.shape, BF),
-            pltpu.VMEM((1,) + b_in.shape, F32),
-            pltpu.SemaphoreType.DMA((3,)),
-        ],
+        [smem()] + [vmem()] * 3,
     )(member, w_in, w_out, b_in[None])
 
 
@@ -450,11 +445,8 @@
 
 
 def to_neighbour(blocks):
-    sides = blocks.reshape((blocks.shape[0] // 2, 2) + blocks.shape[1:])
-    mine = lax.axis_index("zp")
-    kept = lax.dynamic_index_in_dim(sides, mine, 1, keepdims=False)
-    sent = lax.dynamic_index_in_dim(sides, 1 - mine, 1, keepdims=False).astype(BF)
-    return kept + lax.ppermute(sent, "zp", [(0, 1), (1, 0)]).astype(F32)
+    half = blocks.shape[0] // 2
+    return blocks[:half] + lax.ppermute(blocks[half:].astype(BF), "zp", [(0, 1), (1, 0)]).astype(F32)
 
 
 def two_parts(value):
@@ -522,13 +514,15 @@
     gamma_own = lax.dynamic_slice_in_dim(gamma_f, owner * cdev, cdev)
 
     member = lax.axis_index(("x", "c")).astype(jnp.int32)[None]
-    shards = lax.all_to_all(slices(part, nz, member, w_in, w_out, b_in), ZLO, 0, 0, tiled=True)
+    shards = lax.all_to_all(slices(part, nz // 2, member, w_in, w_out, b_in), "zq", 0, 0, tiled=True)
+    beside = lax.ppermute(shards, "zp", [(0, 1), (1, 0)])
 
     up, down = halos(block_input[:, :3], block_input[:, rows - 3 :])
     blocks = forward(kernel, conv_bias, block_input, up, down, metric, out_grad)
-    blocks, shards = lax.optimization_barrier((blocks, shards))
+    blocks, shards, beside = lax.optimization_barrier((blocks, shards, beside))
 
     recv = exchange(blocks)
+    shards = jnp.concatenate([shards, beside], 0)
     one, last = along_ring(shards, 1), along_ring(shards, -1)
     recv, one, last = lax.optimization_barrier((recv, one, last))
 
@@ -543,13 +537,15 @@
     dn, n, dy, acts = mlp(core, pair, other, wi, wo, bi, gamma_f)
     dn = lax.all_to_all(dn, ("c", "x"), 0, 0, tiled=True)
 
-    dws, gam_part, db_part = grads(part, ny, lax.axis_index("y").astype(jnp.int32)[None], n, dy, acts, wo, gamma_f)
+    place = jnp.stack([lax.axis_index("y"), lax.axis_index("zp")]).astype(jnp.int32)
+    dws, gam_part, db_part = grads(part, ny, place, n, dy, acts, wo, gamma_f)
     dws = to_ring(dws.reshape(ny, nz, 2 * part, chans))
     dws = to_neighbour(dws).astype(BF)
+
+    payload = exchange(norm_back(dn, nhat, rstd, ln_gain, gam_part, db_part, nchan))
+    payload, dws = lax.optimization_barrier((payload, dws))
     dws = lax.all_to_all(dws, "zq", 0, 0, tiled=True)
     dws = jnp.sum(dws.astype(F32), 0)
-
-    payload = exchange(norm_back(dn, nhat, rstd, ln_gain, gam_part, db_part, nchan))
     dconv, ends, taps, extra = tap_sums(payload, block_input, up, down, metric, out_grad)
     dup, ddown = halos(ends[0], ends[1])
 

time: 209 us -> 185 us (0.89)
  waiting for transfers between devices: 57.5 us -> 34.5 us
  starting transfers between devices: 122 us -> 116 us
  local copies, waits for them, and re-layouts: 4.73 us -> 7.44 us
    all_to_all x2, waiting for transfers between devices: 12.1 us -> 3.32 us  [exchange(): return lax.all_to_all(blocks, CHAN, 0, 0, tiled=True)]
    ppermute x3, waiting for transfers between devices: 6.83 us -> 0.01 us  [to_ring(): lax.ppermute(blocks[k], 'y', [(i, (i + k) % count) for i in range(count)])]
    ppermute x1 -> x2, starting transfers between devices: 2.96 us -> 8.24 us  [the longest x1 5.1 us: per_device(): beside = lax.ppermute(shards, 'zp', [(0, 1), (1, 0)])]
    all_to_all x1, starting transfers between devices: 12.8 us -> 8.08 us  [to_all(): lax.all_to_all(jnp.broadcast_to(block[None], (count,) + block.shape), axi...]
    all_to_all x1, waiting for transfers between devices: 7.64 us -> 2.96 us  [per_device(): dws = lax.all_to_all(dws, 'zq', 0, 0, tiled=True)]
    all_to_all x1, waiting for transfers between devices: 5.3 us -> 1.33 us  [per_device(): lax.all_to_all(slices(part, nz // 2, member, w_in, w_out, b_in), 'zq', 0,...]
    ppermute x1, starting transfers between devices: 1.91 us -> 5.25 us  [per_device(): other = lax.ppermute(pair, 'c', [(0, 1), (1, 0)])]
    unnamed x24 -> x27, local copies, waits for them, and re-layouts: 2.54 us -> 4.58 us
  transfers between devices with their start and end apart: 21 -> 22, of which waited for: 15 -> 12; matrix products, arithmetic and copies ran while one was open for 1% -> 2% of each run, Pallas kernels for 5% -> 7%
where the time goes in v8:
time: 185 us; the launch traced here: 183 us
  starting transfers between devices  116 us (63%)
  waiting for transfers between devices  34.5 us (19%)
  Pallas kernels  20.3 us (11%)
  local copies, waits for them, and re-layouts  7.44 us (4%)
  other arithmetic  3.65 us (2%)
    all_to_all x2, starting transfers between devices, exchange(): return lax.all_to_all(blocks, CHAN, 0, 0, tiled=True)  22 us
    ppermute x4, waiting for transfers between devices, along_ring(): lax.ppermute(block, 'y', [((i + ahead) % count, i) for i in range(count)])  14.1 us
    all_to_all x1, starting transfers between devices, per_device(): lax.all_to_all(slices(part, nz // 2, member, w_in, w_out, b_in), 'zq', 0,...  11.8 us
    ppermute x4, starting transfers between devices, along_ring(): lax.ppermute(block, 'y', [((i + ahead) % count, i) for i in range(count)])  11.6 us
    all_to_all x1, starting transfers between devices, per_device(): pair = lax.all_to_all(pair, 'x', 0, 0, tiled=True)  9.6 us
    ppermute x1, starting transfers between devices, per_device(): other = lax.ppermute(mine, 'zh', [(0, 1), (1, 0)]).astype(F32)  9.18 us
    ppermute x2, starting transfers between devices, halos(): lax.ppermute(jnp.where(even, first, last), LAT, pairs + [(j, i) for i, j...  8.69 us
    all_to_all x1, starting transfers between devices, to_all(): lax.all_to_all(jnp.broadcast_to(block[None], (count,) + block.shape), axi...  8.08 us
  transfers between devices with their start and end apart: 22, of which 12 were waited for; matrix products, arithmetic and copies ran while one was open for 2% of the time, Pallas kernels for 7%

profile of v8, /device:TPU:1, one launch (start us, length us, event | category | flops | bytes accessed | tf_op | source)
XLA Modules:
  0.0 183.3 jit_solution(5016366173251273084)
XLA Ops:
  4.0 11.8 %all-to-all-start = ((bf16[4,24,896]{2,1,0:T(8,128)(2,1)}), bf16[4,24,896]{2,1,0:T(8,128)(2,1)S(1)}, u32[]{:S(2)}, u32[]{:S(2)}) async-start(bf16[4,24,896]{2,1,0:T(8,128)(2,1)} %shard_map.196), calls=%async_computation | async-start | bytes 344064 | tf_op jit(solution)/shard_map/all_to_all | solution.py:517
  16.9 4.0 %collective-permute-start = (bf16[24,3,256]{2,1,0:T(4,128)(2,1)S(1)}, bf16[24,3,256]{2,1,0:T(4,128)(2,1)S(1)}, u32[]{:S(2)}, u32[]{:S(2)}) collective-permute-start(bf16[24,3,256]{2,1,0:T(4,128)(2,1)S(1)} %get-tuple-element.97), channel_id=1, source_target_pairs={{32,64},{96,128},{160,192},{224,256},{288,320},{352,384},{416,448}... | collective-permute-start | bytes 110600 | tf_op jit(solution)/shard_map/ppermute | solution.py:473
  24.9 5.1 %collective-permute-start.2 = (bf16[4,24,896]{2,1,0:T(8,128)(2,1)S(1)}, bf16[4,24,896]{2,1,0:T(8,128)(2,1)S(1)}, u32[]{:S(2)}, u32[]{:S(2)}) collective-permute-start(bf16[4,24,896]{2,1,0:T(8,128)(2,1)S(1)} %all-to-all-done), channel_id=1, source_target_pairs={{0,4},{4,0},{1,5},{5,1},{2,6},{6,2},{3,7},{7,3},{8,12},{12,8},{9,1... | collective-permute-start | bytes 516104 | tf_op jit(solution)/shard_map/ppermute | solution.py:518
  30.1 3.6 %shard_map.195 = bf16[32,24,128]{2,1,0:T(8,128)(2,1)} custom-call(f32[24,49]{1,0:T(8,128)S(1)} %copy-done.6, f32[24]{0:T(128)S(1)} %copy-done.8, bf16[24,8,256]{2,1,0:T(8,128)(2,1)S(1)} %copy-done.1, bf16[24,3,256]{2,1,0:T(4,128)(2,1)S(1)} %get-tuple-element.95.up_ref, bf16[24,3,256]{2,1,0:T(4,128)(2,1)S(1)} %get-tuple-element.94.down_ref, ...), custom_call_target="tpu_custom_call" | custom-call | tf_op jit(solution)/shard_map/pallas_call | solution.py:100
  33.7 11.2 %all-to-all-start.1 = ((bf16[32,24,128]{2,1,0:T(8,128)(2,1)}), bf16[32,24,128]{2,1,0:T(8,128)(2,1)S(1)}, u32[]{:S(2)}, u32[]{:S(2)}) async-start(bf16[32,24,128]{2,1,0:T(8,128)(2,1)} %shard_map.195), calls=%async_computation.1 | async-start | bytes 393216 | tf_op jit(solution)/shard_map/all_to_all | solution.py:463
  44.9 4.3 %collective-permute-start.3 = (bf16[8,24,896]{2,1,0:T(8,128)(2,1)S(1)}, bf16[8,24,896]{2,1,0:T(8,128)(2,1)S(1)}, u32[]{:S(2)}, u32[]{:S(2)}) collective-permute-start(bf16[8,24,896]{2,1,0:T(8,128)(2,1)S(1)} %constant_dynamic-update-slice_fusion.own_ref), channel_id=1, source_target_pairs={{1,0},{2,1},{3,2},{0,3},{5,4},{6,5},{7,6},{4,7},{9,8},{10,9},{11,1... | collective-permute-start | bytes 1032200 | tf_op jit(solution)/shard_map/ppermute | solution.py:479
  51.2 5.3 %collective-permute-done.3.one_ref = bf16[8,24,896]{2,1,0:T(8,128)(2,1)S(1)} collective-permute-done((bf16[8,24,896]{2,1,0:T(8,128)(2,1)S(1)}, bf16[8,24,896]{2,1,0:T(8,128)(2,1)S(1)}, u32[]{:S(2)}, u32[]{:S(2)}) %collective-permute-start.3) | collective-permute-done | bytes 344096 | tf_op jit(solution)/shard_map/ppermute | solution.py:479
  56.5 4.5 %collective-permute-done.4.last_ref = bf16[8,24,896]{2,1,0:T(8,128)(2,1)S(1)} collective-permute-done((bf16[8,24,896]{2,1,0:T(8,128)(2,1)S(1)}, bf16[8,24,896]{2,1,0:T(8,128)(2,1)S(1)}, u32[]{:S(2)}, u32[]{:S(2)}) %collective-permute-start.4) | collective-permute-done | bytes 344096 | tf_op jit(solution)/shard_map/ppermute | solution.py:479
  62.2 9.6 %all-to-all-start.2 = ((bf16[4,128,768]{2,1,0:T(8,128)(2,1)}), bf16[4,128,768]{2,1,0:T(8,128)(2,1)S(1)}, u32[]{:S(2)}, u32[]{:S(2)}) async-start(bf16[4,128,768]{2,1,0:T(8,128)(2,1)} %get-tuple-element.50), calls=%async_computation.2 | async-start | bytes 1572864 | tf_op jit(solution)/shard_map/all_to_all | solution.py:530
  73.8 3.4 %collective-permute-start.6 = (bf16[4,24,896]{2,1,0:T(8,128)(2,1)S(1)}, bf16[4,24,896]{2,1,0:T(8,128)(2,1)S(1)}, u32[]{:S(2)}, u32[]{:S(2)}) collective-permute-start(bf16[4,24,896]{2,1,0:T(8,128)(2,1)S(1)} %slice.71), channel_id=1, source_target_pairs={{3,0},{0,1},{1,2},{2,3},{7,4},{4,5},{5,6},{6,7},{11,8},{8,9},{9,10... | collective-permute-start | bytes 516104 | tf_op jit(solution)/shard_map/ppermute | solution.py:479
  78.3 3.2 %collective-permute-done.6.high_ref = bf16[4,24,896]{2,1,0:T(8,128)(2,1)S(1)} collective-permute-done((bf16[4,24,896]{2,1,0:T(8,128)(2,1)S(1)}, bf16[4,24,896]{2,1,0:T(8,128)(2,1)S(1)}, u32[]{:S(2)}, u32[]{:S(2)}) %collective-permute-start.6) | collective-permute-done | bytes 172064 | tf_op jit(solution)/shard_map/ppermute | solution.py:479
  81.7 5.2 %collective-permute-start.7 = (bf16[4,128,768]{2,1,0:T(8,128)(2,1)S(1)}, bf16[4,128,768]{2,1,0:T(8,128)(2,1)S(1)}, u32[]{:S(2)}, u32[]{:S(2)}) collective-permute-start(bf16[4,128,768]{2,1,0:T(8,128)(2,1)S(1)} %all-to-all-done.2.own_ref), channel_id=1, source_target_pairs={{0,32},{32,0},{1,33},{33,1},{2,34},{34,2},{3,35},{35,3},{4,36},{36... | collective-permute-start | bytes 2359304 | tf_op jit(solution)/shard_map/ppermute | solution.py:534
  92.2 4.6 %all-to-all-start.3 = ((bf16[8,64,768]{2,1,0:T(8,128)(2,1)}), bf16[8,64,768]{2,1,0:T(8,128)(2,1)S(1)}, u32[]{:S(2)}, u32[]{:S(2)}) async-start(bf16[8,64,768]{2,1,0:T(8,128)(2,1)} %get-tuple-element.59), calls=%async_computation.3 | async-start | bytes 1572864 | tf_op jit(solution)/shard_map/all_to_all | solution.py:538
  103.0 3.4 %collective-permute-start.8 = (bf16[8,24,768]{2,1,0:T(8,128)(2,1)S(1)}, bf16[8,24,768]{2,1,0:T(8,128)(2,1)S(1)}, u32[]{:S(2)}, u32[]{:S(2)}) collective-permute-start(bf16[8,24,768]{2,1,0:T(8,128)(2,1)S(1)} %bitcast.36), channel_id=1, source_target_pairs={{0,1},{1,2},{2,3},{3,0},{4,5},{5,6},{6,7},{7,4},{8,9},{9,10},{10,1... | collective-permute-start | bytes 884744 | tf_op jit(solution)/shard_map/ppermute | solution.py:486
  110.3 10.8 %all-to-all-start.4 = ((bf16[32,16,128]{2,1,0:T(8,128)(2,1)}), bf16[32,16,128]{2,1,0:T(8,128)(2,1)S(1)}, u32[]{:S(2)}, u32[]{:S(2)}) async-start(bf16[32,16,128]{2,1,0:T(8,128)(2,1)} %shard_map.201), calls=%async_computation.4 | async-start | bytes 262144 | tf_op jit(solution)/shard_map/all_to_all | solution.py:463
  125.4 3.8 %collective-permute-done.11 = bf16[4,24,768]{2,1,0:T(8,128)(2,1)S(1)} collective-permute-done((bf16[4,24,768]{2,1,0:T(8,128)(2,1)S(1)}, bf16[4,24,768]{2,1,0:T(8,128)(2,1)S(1)}, u32[]{:S(2)}, u32[]{:S(2)}) %collective-permute-start.11) | collective-permute-done | bytes 147488 | tf_op jit(solution)/shard_map/ppermute | solution.py:449
  129.9 3.3 %all-to-all-done.4.recv_ref = bf16[32,16,128]{2,1,0:T(8,128)(2,1)S(1)} async-done(((bf16[32,16,128]{2,1,0:T(8,128)(2,1)}), bf16[32,16,128]{2,1,0:T(8,128)(2,1)S(1)}, u32[]{:S(2)}, u32[]{:S(2)}) %all-to-all-start.4) | async-done | bytes 131104 | tf_op jit(solution)/shard_map/all_to_all | solution.py:463
  135.6 5.5 %all-to-all-start.5 = ((bf16[4,24,768]{2,1,0:T(8,128)(2,1)}), bf16[4,24,768]{2,1,0:T(8,128)(2,1)S(1)}, u32[]{:S(2)}, u32[]{:S(2)}) async-start(bf16[4,24,768]{2,1,0:T(8,128)(2,1)} %fusion.2), calls=%async_computation.5 | async-start | bytes 294912 | tf_op jit(solution)/shard_map/all_to_all | solution.py:547
  141.1 4.7 %collective-permute-start.13 = (bf16[24,3,256]{2,1,0:T(4,128)(2,1)S(1)}, bf16[24,3,256]{2,1,0:T(4,128)(2,1)S(1)}, u32[]{:S(2)}, u32[]{:S(2)}) collective-permute-start(bf16[24,3,256]{2,1,0:T(4,128)(2,1)S(1)} %get-tuple-element.91), channel_id=1, source_target_pairs={{32,64},{96,128},{160,192},{224,256},{288,320},{352,384},{416,448}... | collective-permute-start | bytes 110600 | tf_op jit(solution)/shard_map/ppermute | solution.py:473
  151.2 9.2 %collective-permute-start.12 = (bf16[24,896]{1,0:T(8,128)(2,1)S(1)}, bf16[24,896]{1,0:T(8,128)(2,1)S(1)}, u32[]{:S(2)}, u32[]{:S(2)}) collective-permute-start(bf16[24,896]{1,0:T(8,128)(2,1)S(1)} %pad_maximum_fusion), channel_id=1, source_target_pairs={{0,256},{256,0},{1,257},{257,1},{2,258},{258,2},{3,259},{259,3},{4... | collective-permute-start | bytes 129032 | tf_op jit(solution)/shard_map/ppermute | solution.py:554
  160.5 4.3 %collective-permute-done.12 = bf16[24,896]{1,0:T(8,128)(2,1)S(1)} collective-permute-done((bf16[24,896]{1,0:T(8,128)(2,1)S(1)}, bf16[24,896]{1,0:T(8,128)(2,1)S(1)}, u32[]{:S(2)}, u32[]{:S(2)}) %collective-permute-start.12) | collective-permute-done | bytes 43040 | tf_op jit(solution)/shard_map/ppermute | solution.py:554
  165.8 8.1 %all-to-all-start.6 = ((bf16[8,24,896]{2,1,0:T(8,128)(2,1)}), bf16[8,24,896]{2,1,0:T(8,128)(2,1)S(1)}, u32[]{:S(2)}, u32[]{:S(2)}) async-start(bf16[8,24,896]{2,1,0:T(8,128)(2,1)} %broadcast_in_dim.43), calls=%async_computation.6 | async-start | bytes 688128 | tf_op jit(solution)/shard_map/all_to_all | solution.py:459
  173.9 3.4 %shard_map.203 = f32[24,8,256]{2,1,0:T(8,128)} custom-call(f32[24,49]{1,0:T(8,128)S(1)} %copy-done.6, f32[24,8,256]{2,1,0:T(8,128)S(1)} %get-tuple-element.69.x_ref, bf16[24,3,256]{2,1,0:T(4,128)(2,1)S(1)} %get-tuple-element.74.up_ref, bf16[24,3,256]{2,1,0:T(4,128)(2,1)S(1)} %get-tuple-element.75.down_ref, bf16[24,8,256]{2,1,0:T(8,128)(2,1)S(1)} %copy-done), custom_call_target="tpu_custom_call" | custom-call | tf_op jit(solution)/shard_map/pallas_call | solution.py:253
  177.3 3.8 %all-to-all-done.6.gathered_ref = bf16[8,24,896]{2,1,0:T(8,128)(2,1)S(1)} async-done(((bf16[8,24,896]{2,1,0:T(8,128)(2,1)}), bf16[8,24,896]{2,1,0:T(8,128)(2,1)S(1)}, u32[]{:S(2)}, u32[]{:S(2)}) %all-to-all-start.6) | async-done | bytes 344096 | tf_op jit(solution)/shard_map/all_to_all | solution.py:459
  (88 shorter events, 46.1 us)
Async XLA Ops:
  4.0 47.2 %copy-start.11 = (f32[768]{0:T(1024)S(1)}, f32[768]{0:T(1024)}, u32[]{:S(2)}) copy-start(f32[768]{0:T(1024)} %param.17) | copy-start | bytes 9220
  4.0 47.2 %copy-start.12 = (f32[768]{0:T(1024)S(1)}, f32[768]{0:T(1024)}, u32[]{:S(2)}) copy-start(f32[768]{0:T(1024)} %param.18) | copy-start | bytes 9220
  4.0 20.8 %all-to-all-start = ((bf16[4,24,896]{2,1,0:T(8,128)(2,1)}), bf16[4,24,896]{2,1,0:T(8,128)(2,1)S(1)}, u32[]{:S(2)}, u32[]{:S(2)}) async-start(bf16[4,24,896]{2,1,0:T(8,128)(2,1)} %shard_map.196), calls=%async_computation | async-start | bytes 344064 | tf_op jit(solution)/shard_map/all_to_all | solution.py:517
  16.9 13.1 %collective-permute-start = (bf16[24,3,256]{2,1,0:T(4,128)(2,1)S(1)}, bf16[24,3,256]{2,1,0:T(4,128)(2,1)S(1)}, u32[]{:S(2)}, u32[]{:S(2)}) collective-permute-start(bf16[24,3,256]{2,1,0:T(4,128)(2,1)S(1)} %get-tuple-element.97), channel_id=1, source_target_pairs={{32,64},{96,128},{160,192},{224,256},{288,320},{352,384},{416,448}... | collective-permute-start | bytes 110600 | tf_op jit(solution)/shard_map/ppermute | solution.py:473
  20.9 9.1 %collective-permute-start.1 = (bf16[24,3,256]{2,1,0:T(4,128)(2,1)S(1)}, bf16[24,3,256]{2,1,0:T(4,128)(2,1)S(1)}, u32[]{:S(2)}, u32[]{:S(2)}) collective-permute-start(bf16[24,3,256]{2,1,0:T(4,128)(2,1)S(1)} %get-tuple-element.96), channel_id=1, source_target_pairs={{0,32},{64,96},{128,160},{192,224},{256,288},{320,352},{384,416},{... | collective-permute-start | bytes 110600 | tf_op jit(solution)/shard_map/ppermute | solution.py:471
  24.9 8.8 %collective-permute-start.2 = (bf16[4,24,896]{2,1,0:T(8,128)(2,1)S(1)}, bf16[4,24,896]{2,1,0:T(8,128)(2,1)S(1)}, u32[]{:S(2)}, u32[]{:S(2)}) collective-permute-start(bf16[4,24,896]{2,1,0:T(8,128)(2,1)S(1)} %all-to-all-done), channel_id=1, source_target_pairs={{0,4},{4,0},{1,5},{5,1},{2,6},{6,2},{3,7},{7,3},{8,12},{12,8},{9,1... | collective-permute-start | bytes 516104 | tf_op jit(solution)/shard_map/ppermute | solution.py:518
  33.7 27.4 %all-to-all-start.1 = ((bf16[32,24,128]{2,1,0:T(8,128)(2,1)}), bf16[32,24,128]{2,1,0:T(8,128)(2,1)S(1)}, u32[]{:S(2)}, u32[]{:S(2)}) async-start(bf16[32,24,128]{2,1,0:T(8,128)(2,1)} %shard_map.195), calls=%async_computation.1 | async-start | bytes 393216 | tf_op jit(solution)/shard_map/all_to_all | solution.py:463
  44.9 11.6 %collective-permute-start.3 = (bf16[8,24,896]{2,1,0:T(8,128)(2,1)S(1)}, bf16[8,24,896]{2,1,0:T(8,128)(2,1)S(1)}, u32[]{:S(2)}, u32[]{:S(2)}) collective-permute-start(bf16[8,24,896]{2,1,0:T(8,128)(2,1)S(1)} %constant_dynamic-update-slice_fusion.own_ref), channel_id=1, source_target_pairs={{1,0},{2,1},{3,2},{0,3},{5,4},{6,5},{7,6},{4,7},{9,8},{10,9},{11,1... | collective-permute-start | bytes 1032200 | tf_op jit(solution)/shard_map/ppermute | solution.py:479
  49.3 11.8 %collective-permute-start.4 = (bf16[8,24,896]{2,1,0:T(8,128)(2,1)S(1)}, bf16[8,24,896]{2,1,0:T(8,128)(2,1)S(1)}, u32[]{:S(2)}, u32[]{:S(2)}) collective-permute-start(bf16[8,24,896]{2,1,0:T(8,128)(2,1)S(1)} %constant_dynamic-update-slice_fusion.own_ref), channel_id=1, source_target_pairs={{3,0},{0,1},{1,2},{2,3},{7,4},{4,5},{5,6},{6,7},{11,8},{8,9},{9,10... | collective-permute-start | bytes 1032200 | tf_op jit(solution)/shard_map/ppermute | solution.py:479
  62.2 19.5 %all-to-all-start.2 = ((bf16[4,128,768]{2,1,0:T(8,128)(2,1)}), bf16[4,128,768]{2,1,0:T(8,128)(2,1)S(1)}, u32[]{:S(2)}, u32[]{:S(2)}) async-start(bf16[4,128,768]{2,1,0:T(8,128)(2,1)} %get-tuple-element.50), calls=%async_computation.2 | async-start | bytes 1572864 | tf_op jit(solution)/shard_map/all_to_all | solution.py:530
  71.9 6.4 %collective-permute-start.5 = (bf16[4,24,896]{2,1,0:T(8,128)(2,1)S(1)}, bf16[4,24,896]{2,1,0:T(8,128)(2,1)S(1)}, u32[]{:S(2)}, u32[]{:S(2)}) collective-permute-start(bf16[4,24,896]{2,1,0:T(8,128)(2,1)S(1)} %slice.70), channel_id=1, source_target_pairs={{1,0},{2,1},{3,2},{0,3},{5,4},{6,5},{7,6},{4,7},{9,8},{10,9},{11,1... | collective-permute-start | bytes 516104 | tf_op jit(solution)/shard_map/ppermute | solution.py:479
  73.8 7.7 %collective-permute-start.6 = (bf16[4,24,896]{2,1,0:T(8,128)(2,1)S(1)}, bf16[4,24,896]{2,1,0:T(8,128)(2,1)S(1)}, u32[]{:S(2)}, u32[]{:S(2)}) collective-permute-start(bf16[4,24,896]{2,1,0:T(8,128)(2,1)S(1)} %slice.71), channel_id=1, source_target_pairs={{3,0},{0,1},{1,2},{2,3},{7,4},{4,5},{5,6},{6,7},{11,8},{8,9},{9,10... | collective-permute-start | bytes 516104 | tf_op jit(solution)/shard_map/ppermute | solution.py:479
  81.7 7.1 %collective-permute-start.7 = (bf16[4,128,768]{2,1,0:T(8,128)(2,1)S(1)}, bf16[4,128,768]{2,1,0:T(8,128)(2,1)S(1)}, u32[]{:S(2)}, u32[]{:S(2)}) collective-permute-start(bf16[4,128,768]{2,1,0:T(8,128)(2,1)S(1)} %all-to-all-done.2.own_ref), channel_id=1, source_target_pairs={{0,32},{32,0},{1,33},{33,1},{2,34},{34,2},{3,35},{35,3},{4,36},{36... | collective-permute-start | bytes 2359304 | tf_op jit(solution)/shard_map/ppermute | solution.py:534
  92.2 16.9 %all-to-all-start.3 = ((bf16[8,64,768]{2,1,0:T(8,128)(2,1)}), bf16[8,64,768]{2,1,0:T(8,128)(2,1)S(1)}, u32[]{:S(2)}, u32[]{:S(2)}) async-start(bf16[8,64,768]{2,1,0:T(8,128)(2,1)} %get-tuple-element.59), calls=%async_computation.3 | async-start | bytes 1572864 | tf_op jit(solution)/shard_map/all_to_all | solution.py:538
  101.1 20.0 %collective-permute-start.10 = (bf16[8,24,768]{2,1,0:T(8,128)(2,1)S(1)}, bf16[8,24,768]{2,1,0:T(8,128)(2,1)S(1)}, u32[]{:S(2)}, u32[]{:S(2)}) collective-permute-start(bf16[8,24,768]{2,1,0:T(8,128)(2,1)S(1)} %bitcast.37), channel_id=1, source_target_pairs={{0,3},{1,0},{2,1},{3,2},{4,7},{5,4},{6,5},{7,6},{8,11},{9,8},{10,9... | collective-permute-start | bytes 884744 | tf_op jit(solution)/shard_map/ppermute | solution.py:486
  103.0 18.1 %collective-permute-start.8 = (bf16[8,24,768]{2,1,0:T(8,128)(2,1)S(1)}, bf16[8,24,768]{2,1,0:T(8,128)(2,1)S(1)}, u32[]{:S(2)}, u32[]{:S(2)}) collective-permute-start(bf16[8,24,768]{2,1,0:T(8,128)(2,1)S(1)} %bitcast.36), channel_id=1, source_target_pairs={{0,1},{1,2},{2,3},{3,0},{4,5},{5,6},{6,7},{7,4},{8,9},{9,10},{10,1... | collective-permute-start | bytes 884744 | tf_op jit(solution)/shard_map/ppermute | solution.py:486
  106.4 14.7 %collective-permute-start.9 = (bf16[8,24,768]{2,1,0:T(8,128)(2,1)S(1)}, bf16[8,24,768]{2,1,0:T(8,128)(2,1)}, u32[]{:S(2)}, u32[]{:S(2)}) collective-permute-start(bf16[8,24,768]{2,1,0:T(8,128)(2,1)S(1)} %bitcast.35), channel_id=1, source_target_pairs={{0,2},{1,3},{2,0},{3,1},{4,6},{5,7},{6,4},{7,5},{8,10},{9,11},{10,... | collective-permute-start | bytes 884744 | tf_op jit(solution)/shard_map/ppermute | solution.py:486
  110.3 22.9 %all-to-all-start.4 = ((bf16[32,16,128]{2,1,0:T(8,128)(2,1)}), bf16[32,16,128]{2,1,0:T(8,128)(2,1)S(1)}, u32[]{:S(2)}, u32[]{:S(2)}) async-start(bf16[32,16,128]{2,1,0:T(8,128)(2,1)} %shard_map.201), calls=%async_computation.4 | async-start | bytes 262144 | tf_op jit(solution)/shard_map/all_to_all | solution.py:463
  122.3 7.0 %collective-permute-start.11 = (bf16[4,24,768]{2,1,0:T(8,128)(2,1)S(1)}, bf16[4,24,768]{2,1,0:T(8,128)(2,1)S(1)}, u32[]{:S(2)}, u32[]{:S(2)}) collective-permute-start(bf16[4,24,768]{2,1,0:T(8,128)(2,1)S(1)} %slice.126), channel_id=1, source_target_pairs={{0,4},{4,0},{1,5},{5,1},{2,6},{6,2},{3,7},{7,3},{8,12},{12,8},{9,1... | collective-permute-start | bytes 442376 | tf_op jit(solution)/shard_map/ppermute | solution.py:449
  135.6 15.5 %all-to-all-start.5 = ((bf16[4,24,768]{2,1,0:T(8,128)(2,1)}), bf16[4,24,768]{2,1,0:T(8,128)(2,1)S(1)}, u32[]{:S(2)}, u32[]{:S(2)}) async-start(bf16[4,24,768]{2,1,0:T(8,128)(2,1)} %fusion.2), calls=%async_computation.5 | async-start | bytes 294912 | tf_op jit(solution)/shard_map/all_to_all | solution.py:547
  141.1 19.3 %collective-permute-start.13 = (bf16[24,3,256]{2,1,0:T(4,128)(2,1)S(1)}, bf16[24,3,256]{2,1,0:T(4,128)(2,1)S(1)}, u32[]{:S(2)}, u32[]{:S(2)}) collective-permute-start(bf16[24,3,256]{2,1,0:T(4,128)(2,1)S(1)} %get-tuple-element.91), channel_id=1, source_target_pairs={{32,64},{96,128},{160,192},{224,256},{288,320},{352,384},{416,448}... | collective-permute-start | bytes 110600 | tf_op jit(solution)/shard_map/ppermute | solution.py:473
  145.9 14.5 %collective-permute-start.14 = (bf16[24,3,256]{2,1,0:T(4,128)(2,1)S(1)}, bf16[24,3,256]{2,1,0:T(4,128)(2,1)S(1)}, u32[]{:S(2)}, u32[]{:S(2)}) collective-permute-start(bf16[24,3,256]{2,1,0:T(4,128)(2,1)S(1)} %get-tuple-element.90), channel_id=1, source_target_pairs={{0,32},{64,96},{128,160},{192,224},{256,288},{320,352},{384,416},{... | collective-permute-start | bytes 110600 | tf_op jit(solution)/shard_map/ppermute | solution.py:471
  151.2 13.6 %collective-permute-start.12 = (bf16[24,896]{1,0:T(8,128)(2,1)S(1)}, bf16[24,896]{1,0:T(8,128)(2,1)S(1)}, u32[]{:S(2)}, u32[]{:S(2)}) collective-permute-start(bf16[24,896]{1,0:T(8,128)(2,1)S(1)} %pad_maximum_fusion), channel_id=1, source_target_pairs={{0,256},{256,0},{1,257},{257,1},{2,258},{258,2},{3,259},{259,3},{4... | collective-permute-start | bytes 129032 | tf_op jit(solution)/shard_map/ppermute | solution.py:554
  165.8 15.4 %all-to-all-start.6 = ((bf16[8,24,896]{2,1,0:T(8,128)(2,1)}), bf16[8,24,896]{2,1,0:T(8,128)(2,1)S(1)}, u32[]{:S(2)}, u32[]{:S(2)}) async-start(bf16[8,24,896]{2,1,0:T(8,128)(2,1)} %broadcast_in_dim.43), calls=%async_computation.6 | async-start | bytes 688128 | tf_op jit(solution)/shard_map/all_to_all | solution.py:459
  (11 other events, 171.9 us)

commit v9 on v8

--- a/solution.py
+++ b/solution.py
@@ -303,13 +303,19 @@
     )(*parts)
 
 
-def mlp_body(core_ref, own_ref, other_ref, wi_ref, wo_ref, bi_ref, gamma_ref, dn_ref, n_ref, dy_ref, acts_ref):
+def fill_tokens(own_ref, other_ref, n_ref, dy_ref):
     members, lanes, _ = own_ref.shape
     piece = lanes // 2
     for at, ref in ((0, own_ref), (members, other_ref)):
         for k in range(members):
             n_ref[(at + k) * piece : (at + k + 1) * piece] = ref[k, :piece]
             dy_ref[(at + k) * piece : (at + k + 1) * piece] = ref[k, piece:]
+
+
+def mlp_body(core_ref, own_ref, other_ref, wi_ref, wo_ref, bi_ref, gamma_ref, dn_ref, acts_ref, n_ref, dy_ref):
+    members, lanes, _ = own_ref.shape
+    piece = lanes // 2
+    fill_tokens(own_ref, other_ref, n_ref, dy_ref)
     pre = dot(n_ref[...], wi_ref[...], 1, 1) + bi_ref[...]
     cdf = 0.5 + 0.5 * lax.erf(pre * (0.5**0.5))
     hid = pre.shape[1]
@@ -332,16 +338,16 @@
         mlp_body,
         [
             jax.ShapeDtypeStruct((2 * members, lanes // 2, chans), BF),
-            jax.ShapeDtypeStruct((toks, chans), BF),
-            jax.ShapeDtypeStruct((toks, chans), BF),
             jax.ShapeDtypeStruct((toks, 2 * hid), BF),
         ],
         [smem()] + [vmem()] * 6,
+        [pltpu.VMEM((toks, chans), BF)] * 2,
     )(core, own, other, wi, wo, bi, gamma[None])
 
 
-def grads_body(part, ny, place_ref, n_ref, dy_ref, acts_ref, wo_ref, gamma_ref, out_ref, gam_ref, db_ref):
+def grads_body(part, ny, place_ref, own_ref, other_ref, acts_ref, wo_ref, gamma_ref, out_ref, gam_ref, db_ref, n_ref, dy_ref):
     toks = n_ref.shape[0]
+    fill_tokens(own_ref, other_ref, n_ref, dy_ref)
     hid = acts_ref.shape[1] // 2
     first, second = picks(hid // part, part)
     dpre = acts_ref[:, hid:]
@@ -366,8 +372,8 @@
     db_ref[...] = dot(db, spot, 1, 1)[:1]
 
 
-def grads(part, ny, place, n, dy, acts, wo, gamma):
-    chans = n.shape[1]
+def grads(part, ny, place, own, other, acts, wo, gamma):
+    toks, chans = acts.shape[0], own.shape[2]
     hid = acts.shape[1] // 2
     return call(
         functools.partial(grads_body, part, ny),
@@ -377,7 +383,8 @@
             jax.ShapeDtypeStruct((1, 2 * hid), F32),
         ],
         [smem()] + [vmem()] * 5,
-    )(place, n, dy, acts, wo, gamma[None])
+        [pltpu.VMEM((toks, chans), BF)] * 2,
+    )(place, own, other, acts, wo, gamma[None])
 
 
 def slices_body(part, member_ref, w_in_ref, w_out_ref, b_ref, out_ref):
@@ -447,6 +454,11 @@
 def to_neighbour(blocks):
     half = blocks.shape[0] // 2
     return blocks[:half] + lax.ppermute(blocks[half:].astype(BF), "zp", [(0, 1), (1, 0)]).astype(F32)
+
+
+def to_both(blocks):
+    both = jnp.broadcast_to(blocks[None], (2,) + blocks.shape).reshape((-1,) + blocks.shape[1:])
+    return lax.all_to_all(both, ("zh", "zq"), 0, 0, tiled=True)
 
 
 def two_parts(value):
@@ -534,27 +546,26 @@
     other = lax.ppermute(pair, "c", [(0, 1), (1, 0)])
 
     core = lax.axis_index("c").astype(jnp.int32)[None]
-    dn, n, dy, acts = mlp(core, pair, other, wi, wo, bi, gamma_f)
+    dn, acts = mlp(core, pair, other, wi, wo, bi, gamma_f)
     dn = lax.all_to_all(dn, ("c", "x"), 0, 0, tiled=True)
 
     place = jnp.stack([lax.axis_index("y"), lax.axis_index("zp")]).astype(jnp.int32)
-    dws, gam_part, db_part = grads(part, ny, place, n, dy, acts, wo, gamma_f)
+    dws, gam_part, db_part = grads(part, ny, place, pair, other, acts, wo, gamma_f)
     dws = to_ring(dws.reshape(ny, nz, 2 * part, chans))
     dws = to_neighbour(dws).astype(BF)
 
     payload = exchange(norm_back(dn, nhat, rstd, ln_gain, gam_part, db_part, nchan))
-    payload, dws = lax.optimization_barrier((payload, dws))
-    dws = lax.all_to_all(dws, "zq", 0, 0, tiled=True)
-    dws = jnp.sum(dws.astype(F32), 0)
     dconv, ends, taps, extra = tap_sums(payload, block_input, up, down, metric, out_grad)
     dup, ddown = halos(ends[0], ends[1])
 
     small = jnp.concatenate([jnp.sum(taps, 2), extra[:, :8]], 1)
-    mine = jnp.concatenate([dws.astype(BF)] + list(two_parts(small)), 1)
-    other = lax.ppermute(mine, "zh", [(0, 1), (1, 0)]).astype(F32)
     count = small.shape[1]
-    dws = dws + other[:, :chans]
-    small = small + other[:, chans : chans + count] + other[:, chans + count :]
+    own = lax.broadcasted_iota(jnp.int32, (nz // 2, 1, 1), 0) == lax.axis_index("zq")
+    beside = jnp.where(own, jnp.concatenate(two_parts(small), 1)[None], jnp.zeros((), BF))
+    dws = to_both(jnp.concatenate([dws, beside], 2))
+    dws = jnp.sum(dws.astype(F32), 0)
+    small = dws[:, chans : chans + count] + dws[:, chans + count :]
+    dws = dws[:, :chans]
     mine = jnp.concatenate([dws.astype(BF)] + list(two_parts(small)), 1)
     mine, dup, ddown = lax.optimization_barrier((mine, dup, ddown))
     grad_input = spread_back(kernel, dconv, dup, ddown, out_grad)

time: 185 us -> 190 us (1.027)
  local copies, waits for them, and re-layouts: 7.44 us -> 13.7 us
    ppermute x1 -> x0, starting transfers between devices: 9.18 us -> none  [per_device(): other = lax.ppermute(mine, 'zh', [(0, 1), (1, 0)]).astype(F32)]
    all_to_all x1, starting transfers between devices: 5.52 us -> 11.3 us  [to_both(): return lax.all_to_all(both, ('zh', 'zq'), 0, 0, tiled=True)]
    unnamed x27 -> x59, local copies, waits for them, and re-layouts: 4.58 us -> 10.1 us
    all_to_all x1, waiting for transfers between devices: 2.96 us -> 8.45 us  [to_both(): return lax.all_to_all(both, ('zh', 'zq'), 0, 0, tiled=True)]
    ppermute x4, waiting for transfers between devices: 14.1 us -> 8.82 us  [along_ring(): lax.ppermute(block, 'y', [((i + ahead) % count, i) for i in range(count)])]
    ppermute x2, starting transfers between devices: 3.84 us -> 8.47 us  [halos(): lax.ppermute(jnp.where(even, last, first), LAT, pairs + [(j, i) for i, j...]
    ppermute x1 -> x0, waiting for transfers between devices: 4.34 us -> none  [per_device(): other = lax.ppermute(mine, 'zh', [(0, 1), (1, 0)]).astype(F32)]
    ppermute x1, starting transfers between devices: 5.25 us -> 1.91 us  [per_device(): other = lax.ppermute(pair, 'c', [(0, 1), (1, 0)])]
  transfers between devices with their start and end apart: 22 -> 21, of which waited for: 12 -> 12; matrix products, arithmetic and copies ran while one was open for 2% -> 2% of each run, Pallas kernels for 7% -> 7%
where the time goes in v9:
time: 190 us; the launch traced here: 189 us
  starting transfers between devices  117 us (62%)
  waiting for transfers between devices  34.2 us (18%)
  Pallas kernels  19.3 us (10%)
  local copies, waits for them, and re-layouts  13.7 us (7%)
  other arithmetic  3.11 us (2%)
    all_to_all x2, starting transfers between devices, exchange(): return lax.all_to_all(blocks, CHAN, 0, 0, tiled=True)  20.2 us
    ppermute x4, starting transfers between devices, along_ring(): lax.ppermute(block, 'y', [((i + ahead) % count, i) for i in range(count)])  13 us
    all_to_all x1, starting transfers between devices, per_device(): lax.all_to_all(slices(part, nz // 2, member, w_in, w_out, b_in), 'zq', 0,...  11.8 us
    all_to_all x1, starting transfers between devices, per_device(): pair = lax.all_to_all(pair, 'x', 0, 0, tiled=True)  11.8 us
    all_to_all x1, starting transfers between devices, to_both(): return lax.all_to_all(both, ('zh', 'zq'), 0, 0, tiled=True)  11.3 us
    all_to_all x1, starting transfers between devices, to_all(): lax.all_to_all(jnp.broadcast_to(block[None], (count,) + block.shape), axi...  10.4 us
    unnamed x59, local copies, waits for them, and re-layouts  10.1 us
    ppermute x3, starting transfers between devices, to_ring(): lax.ppermute(blocks[k], 'y', [(i, (i + k) % count) for i in range(count)])  10 us
  transfers between devices with their start and end apart: 21, of which 12 were waited for; matrix products, arithmetic and copies ran while one was open for 2% of the time, Pallas kernels for 7%

profile of v9, /device:TPU:1, one launch (start us, length us, event | category | flops | bytes accessed | tf_op | source)
XLA Modules:
  0.0 188.5 jit_solution(9309121292157041408)
XLA Ops:
  4.0 11.8 %all-to-all-start = ((bf16[4,24,896]{2,1,0:T(8,128)(2,1)}), bf16[4,24,896]{2,1,0:T(8,128)(2,1)S(1)}, u32[]{:S(2)}, u32[]{:S(2)}) async-start(bf16[4,24,896]{2,1,0:T(8,128)(2,1)} %shard_map.196), calls=%async_computation | async-start | bytes 344064 | tf_op jit(solution)/shard_map/all_to_all | solution.py:529
  16.9 2.9 %collective-permute-start.1 = (bf16[24,3,256]{2,1,0:T(4,128)(2,1)S(1)}, bf16[24,3,256]{2,1,0:T(4,128)(2,1)S(1)}, u32[]{:S(2)}, u32[]{:S(2)}) collective-permute-start(bf16[24,3,256]{2,1,0:T(4,128)(2,1)S(1)} %get-tuple-element.84), channel_id=1, source_target_pairs={{0,32},{64,96},{128,160},{192,224},{256,288},{320,352},{384,416},{... | collective-permute-start | bytes 110600 | tf_op jit(solution)/shard_map/ppermute | solution.py:483
  19.8 3.0 %collective-permute-start = (bf16[24,3,256]{2,1,0:T(4,128)(2,1)S(1)}, bf16[24,3,256]{2,1,0:T(4,128)(2,1)S(1)}, u32[]{:S(2)}, u32[]{:S(2)}) collective-permute-start(bf16[24,3,256]{2,1,0:T(4,128)(2,1)S(1)} %get-tuple-element.85), channel_id=1, source_target_pairs={{32,64},{96,128},{160,192},{224,256},{288,320},{352,384},{416,448}... | collective-permute-start | bytes 110600 | tf_op jit(solution)/shard_map/ppermute | solution.py:485
  24.9 5.1 %collective-permute-start.2 = (bf16[4,24,896]{2,1,0:T(8,128)(2,1)S(1)}, bf16[4,24,896]{2,1,0:T(8,128)(2,1)S(1)}, u32[]{:S(2)}, u32[]{:S(2)}) collective-permute-start(bf16[4,24,896]{2,1,0:T(8,128)(2,1)S(1)} %all-to-all-done), channel_id=1, source_target_pairs={{0,4},{4,0},{1,5},{5,1},{2,6},{6,2},{3,7},{7,3},{8,12},{12,8},{9,1... | collective-permute-start | bytes 516104 | tf_op jit(solution)/shard_map/ppermute | solution.py:530
  30.1 3.6 %shard_map.195 = bf16[32,24,128]{2,1,0:T(8,128)(2,1)} custom-call(f32[24,49]{1,0:T(8,128)S(1)} %copy-done.15, f32[24]{0:T(128)S(1)} %copy-done.23, bf16[24,8,256]{2,1,0:T(8,128)(2,1)S(1)} %copy-done.1, bf16[24,3,256]{2,1,0:T(4,128)(2,1)S(1)} %get-tuple-element.83.up_ref, bf16[24,3,256]{2,1,0:T(4,128)(2,1)S(1)} %get-tuple-element.82.down_ref, ...), custom_call_target="tpu_custom_call" | custom-call | tf_op jit(solution)/shard_map/pallas_call | solution.py:100
  34.3 10.3 %all-to-all-start.1 = ((bf16[32,24,128]{2,1,0:T(8,128)(2,1)}), bf16[32,24,128]{2,1,0:T(8,128)(2,1)S(1)}, u32[]{:S(2)}, u32[]{:S(2)}) async-start(bf16[32,24,128]{2,1,0:T(8,128)(2,1)} %shard_map.195), calls=%async_computation.1 | async-start | bytes 393216 | tf_op jit(solution)/shard_map/all_to_all | solution.py:475
  44.7 3.1 %collective-permute-start.4 = (bf16[8,24,896]{2,1,0:T(8,128)(2,1)S(1)}, bf16[8,24,896]{2,1,0:T(8,128)(2,1)S(1)}, u32[]{:S(2)}, u32[]{:S(2)}) collective-permute-start(bf16[8,24,896]{2,1,0:T(8,128)(2,1)S(1)} %constant_dynamic-update-slice_fusion.own_ref), channel_id=1, source_target_pairs={{3,0},{0,1},{1,2},{2,3},{7,4},{4,5},{5,6},{6,7},{11,8},{8,9},{9,10... | collective-permute-start | bytes 1032200 | tf_op jit(solution)/shard_map/ppermute | solution.py:491
  47.8 3.4 %collective-permute-start.3 = (bf16[8,24,896]{2,1,0:T(8,128)(2,1)S(1)}, bf16[8,24,896]{2,1,0:T(8,128)(2,1)S(1)}, u32[]{:S(2)}, u32[]{:S(2)}) collective-permute-start(bf16[8,24,896]{2,1,0:T(8,128)(2,1)S(1)} %constant_dynamic-update-slice_fusion.own_ref), channel_id=1, source_target_pairs={{1,0},{2,1},{3,2},{0,3},{5,4},{6,5},{7,6},{4,7},{9,8},{10,9},{11,1... | collective-permute-start | bytes 1032200 | tf_op jit(solution)/shard_map/ppermute | solution.py:491
  52.0 5.6 %collective-permute-done.4.last_ref = bf16[8,24,896]{2,1,0:T(8,128)(2,1)S(1)} collective-permute-done((bf16[8,24,896]{2,1,0:T(8,128)(2,1)S(1)}, bf16[8,24,896]{2,1,0:T(8,128)(2,1)S(1)}, u32[]{:S(2)}, u32[]{:S(2)}) %collective-permute-start.4) | collective-permute-done | bytes 344096 | tf_op jit(solution)/shard_map/ppermute | solution.py:491
  60.9 11.8 %all-to-all-start.2 = ((bf16[4,128,768]{2,1,0:T(8,128)(2,1)}), bf16[4,128,768]{2,1,0:T(8,128)(2,1)S(1)}, u32[]{:S(2)}, u32[]{:S(2)}) async-start(bf16[4,128,768]{2,1,0:T(8,128)(2,1)} %get-tuple-element.46), calls=%async_computation.2 | async-start | bytes 1572864 | tf_op jit(solution)/shard_map/all_to_all | solution.py:542
  74.9 4.3 %collective-permute-start.5 = (bf16[4,24,896]{2,1,0:T(8,128)(2,1)S(1)}, bf16[4,24,896]{2,1,0:T(8,128)(2,1)S(1)}, u32[]{:S(2)}, u32[]{:S(2)}) collective-permute-start(bf16[4,24,896]{2,1,0:T(8,128)(2,1)S(1)} %slice.71), channel_id=1, source_target_pairs={{1,0},{2,1},{3,2},{0,3},{5,4},{6,5},{7,6},{4,7},{9,8},{10,9},{11,1... | collective-permute-start | bytes 516104 | tf_op jit(solution)/shard_map/ppermute | solution.py:491
  90.9 4.5 %all-to-all-start.3 = ((bf16[8,64,768]{2,1,0:T(8,128)(2,1)}), bf16[8,64,768]{2,1,0:T(8,128)(2,1)S(1)}, u32[]{:S(2)}, u32[]{:S(2)}) async-start(bf16[8,64,768]{2,1,0:T(8,128)(2,1)} %copy-done.2), calls=%async_computation.3 | async-start | bytes 1572864 | tf_op jit(solution)/shard_map/all_to_all | solution.py:550
  96.6 3.0 %shard_map.200 = (bf16[768,768]{1,0:T(8,128)(2,1)S(1)}, f32[1,768]{1,0:T(1,128)S(1)}, f32[1,768]{1,0:T(1,128)S(1)}) custom-call(s32[2]{0:T(128)S(1)} %pad_add_fusion.place_ref, bf16[4,128,768]{2,1,0:T(8,128)(2,1)S(1)} %all-to-all-done.2.own_ref, bf16[4,128,768]{2,1,0:T(8,128)(2,1)S(1)} %collective-permute-done.7.other_ref, bf16[512,768]{1,0:T(8,128)(2,1)S(1)} %copy-done.4, ...), custom_call_target="tpu_custom_call" | custom-call | tf_op jit(solution)/shard_map/pallas_call | solution.py:378
  99.7 5.0 %collective-permute-start.10 = (bf16[8,24,768]{2,1,0:T(8,128)(2,1)S(1)}, bf16[8,24,768]{2,1,0:T(8,128)(2,1)S(1)}, u32[]{:S(2)}, u32[]{:S(2)}) collective-permute-start(bf16[8,24,768]{2,1,0:T(8,128)(2,1)S(1)} %bitcast.38), channel_id=1, source_target_pairs={{0,3},{1,0},{2,1},{3,2},{4,7},{5,4},{6,5},{7,6},{8,11},{9,8},{10,9... | collective-permute-start | bytes 884744 | tf_op jit(solution)/shard_map/ppermute | solution.py:498
  106.7 3.1 %collective-permute-start.9 = (bf16[8,24,768]{2,1,0:T(8,128)(2,1)S(1)}, bf16[8,24,768]{2,1,0:T(8,128)(2,1)}, u32[]{:S(2)}, u32[]{:S(2)}) collective-permute-start(bf16[8,24,768]{2,1,0:T(8,128)(2,1)S(1)} %bitcast.36), channel_id=1, source_target_pairs={{0,2},{1,3},{2,0},{3,1},{4,6},{5,7},{6,4},{7,5},{8,10},{9,11},{10,... | collective-permute-start | bytes 884744 | tf_op jit(solution)/shard_map/ppermute | solution.py:498
  111.0 9.9 %all-to-all-start.4 = ((bf16[32,16,128]{2,1,0:T(8,128)(2,1)}), bf16[32,16,128]{2,1,0:T(8,128)(2,1)S(1)}, u32[]{:S(2)}, u32[]{:S(2)}) async-start(bf16[32,16,128]{2,1,0:T(8,128)(2,1)} %shard_map.201), calls=%async_computation.4 | async-start | bytes 262144 | tf_op jit(solution)/shard_map/all_to_all | solution.py:475
  125.7 4.9 %collective-permute-done.11 = bf16[4,24,768]{2,1,0:T(8,128)(2,1)S(1)} collective-permute-done((bf16[4,24,768]{2,1,0:T(8,128)(2,1)S(1)}, bf16[4,24,768]{2,1,0:T(8,128)(2,1)S(1)}, u32[]{:S(2)}, u32[]{:S(2)}) %collective-permute-start.11) | collective-permute-done | bytes 147488 | tf_op jit(solution)/shard_map/ppermute | solution.py:456
  136.6 11.3 %all-to-all-start.5 = ((bf16[8,24,896]{2,1,0:T(8,128)(2,1)}), bf16[8,24,896]{2,1,0:T(8,128)(2,1)S(1)}, u32[]{:S(2)}, u32[]{:S(2)}) async-start(bf16[8,24,896]{2,1,0:T(8,128)(2,1)} %bitcast.11), calls=%async_computation.5 | async-start | bytes 688128 | tf_op jit(solution)/shard_map/all_to_all | solution.py:461
  147.9 5.6 %collective-permute-start.13 = (bf16[24,3,256]{2,1,0:T(4,128)(2,1)S(1)}, bf16[24,3,256]{2,1,0:T(4,128)(2,1)S(1)}, u32[]{:S(2)}, u32[]{:S(2)}) collective-permute-start(bf16[24,3,256]{2,1,0:T(4,128)(2,1)S(1)} %get-tuple-element.80), channel_id=1, source_target_pairs={{0,32},{64,96},{128,160},{192,224},{256,288},{320,352},{384,416},{... | collective-permute-start | bytes 110600 | tf_op jit(solution)/shard_map/ppermute | solution.py:483
  153.6 3.4 %collective-permute-start.12 = (bf16[24,3,256]{2,1,0:T(4,128)(2,1)S(1)}, bf16[24,3,256]{2,1,0:T(4,128)(2,1)S(1)}, u32[]{:S(2)}, u32[]{:S(2)}) collective-permute-start(bf16[24,3,256]{2,1,0:T(4,128)(2,1)S(1)} %get-tuple-element.81), channel_id=1, source_target_pairs={{32,64},{96,128},{160,192},{224,256},{288,320},{352,384},{416,448}... | collective-permute-start | bytes 110600 | tf_op jit(solution)/shard_map/ppermute | solution.py:485
  159.3 8.4 %all-to-all-done.5 = bf16[8,24,896]{2,1,0:T(8,128)(2,1)S(1)} async-done(((bf16[8,24,896]{2,1,0:T(8,128)(2,1)}), bf16[8,24,896]{2,1,0:T(8,128)(2,1)S(1)}, u32[]{:S(2)}, u32[]{:S(2)}) %all-to-all-start.5) | async-done | bytes 344096 | tf_op jit(solution)/shard_map/all_to_all | solution.py:461
  168.8 10.4 %all-to-all-start.6 = ((bf16[8,24,896]{2,1,0:T(8,128)(2,1)}), bf16[8,24,896]{2,1,0:T(8,128)(2,1)S(1)}, u32[]{:S(2)}, u32[]{:S(2)}) async-start(bf16[8,24,896]{2,1,0:T(8,128)(2,1)} %broadcast_in_dim.74), calls=%async_computation.6 | async-start | bytes 688128 | tf_op jit(solution)/shard_map/all_to_all | solution.py:471
  179.2 3.4 %shard_map.203 = f32[24,8,256]{2,1,0:T(8,128)} custom-call(f32[24,49]{1,0:T(8,128)S(1)} %copy-done.15, f32[24,8,256]{2,1,0:T(8,128)S(1)} %get-tuple-element.61.x_ref, bf16[24,3,256]{2,1,0:T(4,128)(2,1)S(1)} %get-tuple-element.66.up_ref, bf16[24,3,256]{2,1,0:T(4,128)(2,1)S(1)} %get-tuple-element.67.down_ref, bf16[24,8,256]{2,1,0:T(8,128)(2,1)S(1)} %copy-done), custom_call_target="tpu_custom_call" | custom-call | tf_op jit(solution)/shard_map/pallas_call | solution.py:253
  182.6 3.8 %all-to-all-done.6.gathered_ref = bf16[8,24,896]{2,1,0:T(8,128)(2,1)S(1)} async-done(((bf16[8,24,896]{2,1,0:T(8,128)(2,1)}), bf16[8,24,896]{2,1,0:T(8,128)(2,1)S(1)}, u32[]{:S(2)}, u32[]{:S(2)}) %all-to-all-start.6) | async-done | bytes 344096 | tf_op jit(solution)/shard_map/all_to_all | solution.py:471
  (119 shorter events, 45.7 us)
Async XLA Ops:
  4.0 47.9 %copy-start.27 = (f32[768]{0:T(1024)S(1)}, f32[768]{0:T(1024)}, u32[]{:S(2)}) copy-start(f32[768]{0:T(1024)} %param.17) | copy-start | bytes 9220
  4.0 47.9 %copy-start.28 = (f32[768]{0:T(1024)S(1)}, f32[768]{0:T(1024)}, u32[]{:S(2)}) copy-start(f32[768]{0:T(1024)} %param.18) | copy-start | bytes 9220
  4.0 20.8 %all-to-all-start = ((bf16[4,24,896]{2,1,0:T(8,128)(2,1)}), bf16[4,24,896]{2,1,0:T(8,128)(2,1)S(1)}, u32[]{:S(2)}, u32[]{:S(2)}) async-start(bf16[4,24,896]{2,1,0:T(8,128)(2,1)} %shard_map.196), calls=%async_computation | async-start | bytes 344064 | tf_op jit(solution)/shard_map/all_to_all | solution.py:529
  16.9 13.1 %collective-permute-start.1 = (bf16[24,3,256]{2,1,0:T(4,128)(2,1)S(1)}, bf16[24,3,256]{2,1,0:T(4,128)(2,1)S(1)}, u32[]{:S(2)}, u32[]{:S(2)}) collective-permute-start(bf16[24,3,256]{2,1,0:T(4,128)(2,1)S(1)} %get-tuple-element.84), channel_id=1, source_target_pairs={{0,32},{64,96},{128,160},{192,224},{256,288},{320,352},{384,416},{... | collective-permute-start | bytes 110600 | tf_op jit(solution)/shard_map/ppermute | solution.py:483
  19.8 10.2 %collective-permute-start = (bf16[24,3,256]{2,1,0:T(4,128)(2,1)S(1)}, bf16[24,3,256]{2,1,0:T(4,128)(2,1)S(1)}, u32[]{:S(2)}, u32[]{:S(2)}) collective-permute-start(bf16[24,3,256]{2,1,0:T(4,128)(2,1)S(1)} %get-tuple-element.85), channel_id=1, source_target_pairs={{32,64},{96,128},{160,192},{224,256},{288,320},{352,384},{416,448}... | collective-permute-start | bytes 110600 | tf_op jit(solution)/shard_map/ppermute | solution.py:485
  24.9 9.4 %collective-permute-start.2 = (bf16[4,24,896]{2,1,0:T(8,128)(2,1)S(1)}, bf16[4,24,896]{2,1,0:T(8,128)(2,1)S(1)}, u32[]{:S(2)}, u32[]{:S(2)}) collective-permute-start(bf16[4,24,896]{2,1,0:T(8,128)(2,1)S(1)} %all-to-all-done), channel_id=1, source_target_pairs={{0,4},{4,0},{1,5},{5,1},{2,6},{6,2},{3,7},{7,3},{8,12},{12,8},{9,1... | collective-permute-start | bytes 516104 | tf_op jit(solution)/shard_map/ppermute | solution.py:530
  34.3 24.2 %all-to-all-start.1 = ((bf16[32,24,128]{2,1,0:T(8,128)(2,1)}), bf16[32,24,128]{2,1,0:T(8,128)(2,1)S(1)}, u32[]{:S(2)}, u32[]{:S(2)}) async-start(bf16[32,24,128]{2,1,0:T(8,128)(2,1)} %shard_map.195), calls=%async_computation.1 | async-start | bytes 393216 | tf_op jit(solution)/shard_map/all_to_all | solution.py:475
  44.7 12.9 %collective-permute-start.4 = (bf16[8,24,896]{2,1,0:T(8,128)(2,1)S(1)}, bf16[8,24,896]{2,1,0:T(8,128)(2,1)S(1)}, u32[]{:S(2)}, u32[]{:S(2)}) collective-permute-start(bf16[8,24,896]{2,1,0:T(8,128)(2,1)S(1)} %constant_dynamic-update-slice_fusion.own_ref), channel_id=1, source_target_pairs={{3,0},{0,1},{1,2},{2,3},{7,4},{4,5},{5,6},{6,7},{11,8},{8,9},{9,10... | collective-permute-start | bytes 1032200 | tf_op jit(solution)/shard_map/ppermute | solution.py:491
  47.8 10.6 %collective-permute-start.3 = (bf16[8,24,896]{2,1,0:T(8,128)(2,1)S(1)}, bf16[8,24,896]{2,1,0:T(8,128)(2,1)S(1)}, u32[]{:S(2)}, u32[]{:S(2)}) collective-permute-start(bf16[8,24,896]{2,1,0:T(8,128)(2,1)S(1)} %constant_dynamic-update-slice_fusion.own_ref), channel_id=1, source_target_pairs={{1,0},{2,1},{3,2},{0,3},{5,4},{6,5},{7,6},{4,7},{9,8},{10,9},{11,1... | collective-permute-start | bytes 1032200 | tf_op jit(solution)/shard_map/ppermute | solution.py:491
  60.9 21.3 %all-to-all-start.2 = ((bf16[4,128,768]{2,1,0:T(8,128)(2,1)}), bf16[4,128,768]{2,1,0:T(8,128)(2,1)S(1)}, u32[]{:S(2)}, u32[]{:S(2)}) async-start(bf16[4,128,768]{2,1,0:T(8,128)(2,1)} %get-tuple-element.46), calls=%async_computation.2 | async-start | bytes 1572864 | tf_op jit(solution)/shard_map/all_to_all | solution.py:542
  72.8 7.4 %collective-permute-start.6 = (bf16[4,24,896]{2,1,0:T(8,128)(2,1)S(1)}, bf16[4,24,896]{2,1,0:T(8,128)(2,1)S(1)}, u32[]{:S(2)}, u32[]{:S(2)}) collective-permute-start(bf16[4,24,896]{2,1,0:T(8,128)(2,1)S(1)} %slice.72), channel_id=1, source_target_pairs={{3,0},{0,1},{1,2},{2,3},{7,4},{4,5},{5,6},{6,7},{11,8},{8,9},{9,10... | collective-permute-start | bytes 516104 | tf_op jit(solution)/shard_map/ppermute | solution.py:491
  74.9 6.7 %collective-permute-start.5 = (bf16[4,24,896]{2,1,0:T(8,128)(2,1)S(1)}, bf16[4,24,896]{2,1,0:T(8,128)(2,1)S(1)}, u32[]{:S(2)}, u32[]{:S(2)}) collective-permute-start(bf16[4,24,896]{2,1,0:T(8,128)(2,1)S(1)} %slice.71), channel_id=1, source_target_pairs={{1,0},{2,1},{3,2},{0,3},{5,4},{6,5},{7,6},{4,7},{9,8},{10,9},{11,1... | collective-permute-start | bytes 516104 | tf_op jit(solution)/shard_map/ppermute | solution.py:491
  82.2 5.3 %collective-permute-start.7 = (bf16[4,128,768]{2,1,0:T(8,128)(2,1)S(1)}, bf16[4,128,768]{2,1,0:T(8,128)(2,1)S(1)}, u32[]{:S(2)}, u32[]{:S(2)}) collective-permute-start(bf16[4,128,768]{2,1,0:T(8,128)(2,1)S(1)} %all-to-all-done.2.own_ref), channel_id=1, source_target_pairs={{0,32},{32,0},{1,33},{33,1},{2,34},{34,2},{3,35},{35,3},{4,36},{36... | collective-permute-start | bytes 2359304 | tf_op jit(solution)/shard_map/ppermute | solution.py:546
  90.9 18.9 %all-to-all-start.3 = ((bf16[8,64,768]{2,1,0:T(8,128)(2,1)}), bf16[8,64,768]{2,1,0:T(8,128)(2,1)S(1)}, u32[]{:S(2)}, u32[]{:S(2)}) async-start(bf16[8,64,768]{2,1,0:T(8,128)(2,1)} %copy-done.2), calls=%async_computation.3 | async-start | bytes 1572864 | tf_op jit(solution)/shard_map/all_to_all | solution.py:550
  99.7 21.1 %collective-permute-start.10 = (bf16[8,24,768]{2,1,0:T(8,128)(2,1)S(1)}, bf16[8,24,768]{2,1,0:T(8,128)(2,1)S(1)}, u32[]{:S(2)}, u32[]{:S(2)}) collective-permute-start(bf16[8,24,768]{2,1,0:T(8,128)(2,1)S(1)} %bitcast.38), channel_id=1, source_target_pairs={{0,3},{1,0},{2,1},{3,2},{4,7},{5,4},{6,5},{7,6},{8,11},{9,8},{10,9... | collective-permute-start | bytes 884744 | tf_op jit(solution)/shard_map/ppermute | solution.py:498
  104.7 17.8 %collective-permute-start.8 = (bf16[8,24,768]{2,1,0:T(8,128)(2,1)S(1)}, bf16[8,24,768]{2,1,0:T(8,128)(2,1)S(1)}, u32[]{:S(2)}, u32[]{:S(2)}) collective-permute-start(bf16[8,24,768]{2,1,0:T(8,128)(2,1)S(1)} %bitcast.37), channel_id=1, source_target_pairs={{0,1},{1,2},{2,3},{3,0},{4,5},{5,6},{6,7},{7,4},{8,9},{9,10},{10,1... | collective-permute-start | bytes 884744 | tf_op jit(solution)/shard_map/ppermute | solution.py:498
  106.7 15.8 %collective-permute-start.9 = (bf16[8,24,768]{2,1,0:T(8,128)(2,1)S(1)}, bf16[8,24,768]{2,1,0:T(8,128)(2,1)}, u32[]{:S(2)}, u32[]{:S(2)}) collective-permute-start(bf16[8,24,768]{2,1,0:T(8,128)(2,1)S(1)} %bitcast.36), channel_id=1, source_target_pairs={{0,2},{1,3},{2,0},{3,1},{4,6},{5,7},{6,4},{7,5},{8,10},{9,11},{10,... | collective-permute-start | bytes 884744 | tf_op jit(solution)/shard_map/ppermute | solution.py:498
  111.0 22.0 %all-to-all-start.4 = ((bf16[32,16,128]{2,1,0:T(8,128)(2,1)}), bf16[32,16,128]{2,1,0:T(8,128)(2,1)S(1)}, u32[]{:S(2)}, u32[]{:S(2)}) async-start(bf16[32,16,128]{2,1,0:T(8,128)(2,1)} %shard_map.201), calls=%async_computation.4 | async-start | bytes 262144 | tf_op jit(solution)/shard_map/all_to_all | solution.py:475
  123.7 7.0 %collective-permute-start.11 = (bf16[4,24,768]{2,1,0:T(8,128)(2,1)S(1)}, bf16[4,24,768]{2,1,0:T(8,128)(2,1)S(1)}, u32[]{:S(2)}, u32[]{:S(2)}) collective-permute-start(bf16[4,24,768]{2,1,0:T(8,128)(2,1)S(1)} %slice.123), channel_id=1, source_target_pairs={{0,4},{4,0},{1,5},{5,1},{2,6},{6,2},{3,7},{7,3},{8,12},{12,8},{9,1... | collective-permute-start | bytes 442376 | tf_op jit(solution)/shard_map/ppermute | solution.py:456
  136.6 31.2 %all-to-all-start.5 = ((bf16[8,24,896]{2,1,0:T(8,128)(2,1)}), bf16[8,24,896]{2,1,0:T(8,128)(2,1)S(1)}, u32[]{:S(2)}, u32[]{:S(2)}) async-start(bf16[8,24,896]{2,1,0:T(8,128)(2,1)} %bitcast.11), calls=%async_computation.5 | async-start | bytes 688128 | tf_op jit(solution)/shard_map/all_to_all | solution.py:461
  147.9 31.2 %copy-start.26 = (bf16[768]{0:T(1024)(128)(2,1)S(1)}, bf16[768]{0:T(1024)(128)(2,1)}, u32[]{:S(2)}) copy-start(bf16[768]{0:T(1024)(128)(2,1)} %param.23) | copy-start | bytes 4612
  147.9 9.0 %collective-permute-start.13 = (bf16[24,3,256]{2,1,0:T(4,128)(2,1)S(1)}, bf16[24,3,256]{2,1,0:T(4,128)(2,1)S(1)}, u32[]{:S(2)}, u32[]{:S(2)}) collective-permute-start(bf16[24,3,256]{2,1,0:T(4,128)(2,1)S(1)} %get-tuple-element.80), channel_id=1, source_target_pairs={{0,32},{64,96},{128,160},{192,224},{256,288},{320,352},{384,416},{... | collective-permute-start | bytes 110600 | tf_op jit(solution)/shard_map/ppermute | solution.py:483
  153.6 5.7 %collective-permute-start.12 = (bf16[24,3,256]{2,1,0:T(4,128)(2,1)S(1)}, bf16[24,3,256]{2,1,0:T(4,128)(2,1)S(1)}, u32[]{:S(2)}, u32[]{:S(2)}) collective-permute-start(bf16[24,3,256]{2,1,0:T(4,128)(2,1)S(1)} %get-tuple-element.81), channel_id=1, source_target_pairs={{32,64},{96,128},{160,192},{224,256},{288,320},{352,384},{416,448}... | collective-permute-start | bytes 110600 | tf_op jit(solution)/shard_map/ppermute | solution.py:485
  168.8 17.6 %all-to-all-start.6 = ((bf16[8,24,896]{2,1,0:T(8,128)(2,1)}), bf16[8,24,896]{2,1,0:T(8,128)(2,1)S(1)}, u32[]{:S(2)}, u32[]{:S(2)}) async-start(bf16[8,24,896]{2,1,0:T(8,128)(2,1)} %broadcast_in_dim.74), calls=%async_computation.6 | async-start | bytes 688128 | tf_op jit(solution)/shard_map/all_to_all | solution.py:471
  (26 other events, 244.9 us)

commit v10 on v8

--- a/solution.py
+++ b/solution.py
@@ -175,9 +175,8 @@
     )(recv, nhat, rstd, gain[None], gam, db)
 
 
-def taps_body(recv_ref, x_ref, up_ref, down_ref, metric_ref, dy_ref, dconv_ref, ends_ref, sums_ref, extra_ref, ext, dh_rows, prods):
-    cdev, rows, width = x_ref.shape
-    fill_rows(x_ref, up_ref, down_ref, ext)
+def dconv_body(recv_ref, metric_ref, dconv_ref, ends_ref, sums_ref, extra_ref, dh_rows):
+    cdev, rows, width = dconv_ref.shape
     low16 = lax.broadcasted_iota(jnp.int32, (16, 128), 1) < 64
     low8 = lax.broadcasted_iota(jnp.int32, (8, 128), 1) < 64
     extra = jnp.zeros((8, 128), F32)
@@ -190,15 +189,39 @@
             extra = extra + first[8:] + second[8:]
     for g in range(3):
         extra_ref[8 * g : 8 * g + 8] = pltpu.roll(extra, 64 - 8 * g, 1)
-    metric = jnp.broadcast_to(metric_ref[...], (rows, width))
+    metric = jnp.broadcast_to(metric_ref[...], (rows, 128))
+    for c in range(cdev):
+        for t in range(width // 128):
+            dh = dh_rows[t, c * rows : (c + 1) * rows, :]
+            dconv = metric * dh
+            lanes = slice(t * 128, t * 128 + 128)
+            dconv_ref[c, :, lanes] = dconv
+            ends_ref[0, c, :, lanes] = dconv[:3].astype(BF)
+            ends_ref[1, c, :, lanes] = dconv[rows - 3 :].astype(BF)
+            sums_ref[c] = dh if t == 0 else sums_ref[c] + dh
+
+
+def stencil_cotangent(recv, metric, cdev, width):
+    rows = metric.shape[0]
+    return call(
+        dconv_body,
+        [
+            jax.ShapeDtypeStruct((cdev, rows, width), F32),
+            jax.ShapeDtypeStruct((2, cdev, 3, width), BF),
+            jax.ShapeDtypeStruct((cdev, rows, 128), F32),
+            jax.ShapeDtypeStruct((cdev, 128), F32),
+        ],
+        [vmem()] * 2,
+        [pltpu.VMEM((width // 128, cdev * rows, 128), F32)],
+    )(recv, metric[:, None])
+
+
+def taps_body(dconv_ref, dh_sums_ref, x_ref, up_ref, down_ref, dy_ref, sums_ref, ext, prods):
+    cdev, rows, width = x_ref.shape
+    fill_rows(x_ref, up_ref, down_ref, ext)
 
     def channel(c, carry):
-        here = pl.ds(pl.multiple_of(c * rows, rows), rows)
-        dh = jnp.concatenate([dh_rows[t, here, :] for t in range(width // 128)], 1)
-        dconv = metric * dh
-        dconv_ref[c] = dconv
-        ends_ref[0, c] = dconv[:3].astype(BF)
-        ends_ref[1, c] = dconv[rows - 3 :].astype(BF)
+        dconv = dconv_ref[c]
         shifts = row_shifts(ext, c, rows)
         for b in range(7):
             moved = along(dconv, 3 - b)
@@ -206,7 +229,7 @@
                 product = shifts[a] * moved
                 prods[(a * 7 + b) * 8 : (a * 7 + b) * 8 + 8, :] = product[:, :128] + product[:, 128:]
         dy = dy_ref[c].astype(F32)
-        prods[392:400, :] = dh[:, :128] + dh[:, 128:]
+        prods[392:400, :] = dh_sums_ref[c]
         prods[400:408, :] = dy[:, :128] + dy[:, 128:]
         total = prods[pl.ds(0, 56, 8), :]
         for i in range(1, 8):
@@ -218,23 +241,14 @@
     lax.fori_loop(0, cdev, channel, 0, unroll=8)
 
 
-def tap_sums(recv, x, up, down, metric, dy):
+def tap_sums(dconv, dh_sums, x, up, down, dy):
     cdev, rows, width = x.shape
     return call(
         taps_body,
-        [
-            jax.ShapeDtypeStruct((cdev, rows, width), F32),
-            jax.ShapeDtypeStruct((2, cdev, 3, width), BF),
-            jax.ShapeDtypeStruct((cdev, 56, 128), F32),
-            jax.ShapeDtypeStruct((cdev, 128), F32),
-        ],
+        jax.ShapeDtypeStruct((cdev, 56, 128), F32),
         [vmem()] * 6,
-        [
-            pltpu.VMEM((cdev, EXT, width), F32),
-            pltpu.VMEM((width // 128, cdev * rows, 128), F32),
-            pltpu.VMEM((448, 128), F32),
-        ],
-    )(recv, x, up, down, metric[:, None], dy)
+        [pltpu.VMEM((cdev, EXT, width), F32), pltpu.VMEM((448, 128), F32)],
+    )(dconv, dh_sums, x, up, down, dy)
 
 
 def spread_body(taps_ref, x_ref, up_ref, down_ref, dy_ref, out_ref, ext):
@@ -380,31 +394,30 @@
     )(place, n, dy, acts, wo, gamma[None])
 
 
-def slices_body(part, member_ref, w_in_ref, w_out_ref, b_ref, out_ref):
-    hdev, chans = w_in_ref.shape
-    row = lax.broadcasted_iota(jnp.int32, (2 * part, hdev), 0)
-    place = lax.broadcasted_iota(jnp.int32, (2 * part, hdev), 1)
-    start = member_ref[0] * part
-    first = jnp.where((row < part) & (place == start + row), 1.0, 0.0).astype(BF)
-    second = jnp.where((row >= part) & (place == start + row - part), 1.0, 0.0).astype(BF)
+def slices_body(w_in_ref, w_out_ref, b_ref, out_ref):
+    part, chans = w_in_ref.shape
+    row = lax.broadcasted_iota(jnp.int32, (2 * part, part), 0)
+    place = lax.broadcasted_iota(jnp.int32, (2 * part, part), 1)
+    first = jnp.where(row == place, 1.0, 0.0).astype(BF)
+    second = jnp.where(row == place + part, 1.0, 0.0).astype(BF)
     rows = (dot(first, w_in_ref[...], 1, 0) + dot(second, w_out_ref[...], 1, 0)).astype(BF)
-    bias = jnp.broadcast_to(b_ref[...], (SIDE, hdev))
-    high = bias.astype(BF)
-    low = (bias - high.astype(F32)).astype(BF)
-    line = lax.broadcasted_iota(jnp.int32, (SIDE, hdev), 0)
-    high = jnp.where(line == 0, high.astype(F32), jnp.where(line == 1, low.astype(F32), 0.0)).astype(BF)
-    side = dot(first, high, 1, 1).astype(BF)
+    bias = jnp.broadcast_to(b_ref[...], (SIDE, part))
+    high = bias.astype(BF).astype(F32)
+    line = lax.broadcasted_iota(jnp.int32, (SIDE, part), 0)
+    both = jnp.where(line == 0, high, jnp.where(line == 1, bias - high, 0.0)).astype(BF)
+    side = dot(first, both, 1, 1).astype(BF)
     for k in range(out_ref.shape[0]):
         out_ref[k, :, :chans] = rows
         out_ref[k, :, chans:] = side
 
 
-def slices(part, copies, member, w_in, w_out, b_in):
-    return call(
-        functools.partial(slices_body, part),
-        jax.ShapeDtypeStruct((copies, 2 * part, w_in.shape[1] + SIDE), BF),
-        [smem()] + [vmem()] * 3,
-    )(member, w_in, w_out, b_in[None])
+def slices(copies, w_in, w_out, b_in):
+    part, chans = w_in.shape
+    return call(
+        slices_body,
+        jax.ShapeDtypeStruct((copies, 2 * part, chans + SIDE), BF),
+        [vmem()] * 3,
+    )(w_in, w_out, b_in[None])
 
 
 def results_body(part, n_taps, gathered_ref, gamma_ref, b_out_ref, dw_in_ref, dw_out_ref, taps_ref, db_ref, rest_ref):
@@ -513,8 +526,9 @@
     gamma_f = layer_scale.astype(F32)
     gamma_own = lax.dynamic_slice_in_dim(gamma_f, owner * cdev, cdev)
 
-    member = lax.axis_index(("x", "c")).astype(jnp.int32)[None]
-    shards = lax.all_to_all(slices(part, nz // 2, member, w_in, w_out, b_in), "zq", 0, 0, tiled=True)
+    start = lax.axis_index(("x", "c")) * part
+    cut = [lax.dynamic_slice_in_dim(w, start, part) for w in (w_in, w_out, b_in)]
+    shards = lax.all_to_all(slices(nz // 2, *cut), "zq", 0, 0, tiled=True)
     beside = lax.ppermute(shards, "zp", [(0, 1), (1, 0)])
 
     up, down = halos(block_input[:, :3], block_input[:, rows - 3 :])
@@ -546,7 +560,8 @@
     payload, dws = lax.optimization_barrier((payload, dws))
     dws = lax.all_to_all(dws, "zq", 0, 0, tiled=True)
     dws = jnp.sum(dws.astype(F32), 0)
-    dconv, ends, taps, extra = tap_sums(payload, block_input, up, down, metric, out_grad)
+    dconv, ends, dh_sums, extra = stencil_cotangent(payload, metric, cdev, width)
+    taps = tap_sums(dconv, dh_sums, block_input, up, down, out_grad)
     dup, ddown = halos(ends[0], ends[1])
 
     small = jnp.concatenate([jnp.sum(taps, 2), extra[:, :8]], 1)

time: 185 us -> 184 us (level)
  waiting for transfers between devices: 34.5 us -> 31.9 us
  starting transfers between devices: 116 us -> 118 us
    all_to_all x1, starting transfers between devices: 9.6 us -> 12.1 us  [per_device(): pair = lax.all_to_all(pair, 'x', 0, 0, tiled=True)]
    ppermute x1, starting transfers between devices: 9.18 us -> 11.5 us  [per_device(): other = lax.ppermute(mine, 'zh', [(0, 1), (1, 0)]).astype(F32)]
    all_to_all x1, waiting for transfers between devices: 2.96 us -> 0.69 us  [per_device(): dws = lax.all_to_all(dws, 'zq', 0, 0, tiled=True)]
    ppermute x1, waiting for transfers between devices: 4.34 us -> 2.3 us  [per_device(): other = lax.ppermute(mine, 'zh', [(0, 1), (1, 0)]).astype(F32)]
    unnamed x27 -> x25, local copies, waits for them, and re-layouts: 4.58 us -> 4.05 us
  transfers between devices with their start and end apart: 22 -> 22, of which waited for: 12 -> 13; matrix products, arithmetic and copies ran while one was open for 2% -> 2% of each run, Pallas kernels for 7% -> 8%
where the time goes in v10:
time: 184 us; the launch traced here: 183 us
  starting transfers between devices  118 us (64%)
  waiting for transfers between devices  31.9 us (17%)
  Pallas kernels  20.4 us (11%)
  local copies, waits for them, and re-layouts  7.78 us (4%)
  other arithmetic  3.65 us (2%)
    all_to_all x2, starting transfers between devices, exchange(): return lax.all_to_all(blocks, CHAN, 0, 0, tiled=True)  20.9 us
    ppermute x4, waiting for transfers between devices, along_ring(): lax.ppermute(block, 'y', [((i + ahead) % count, i) for i in range(count)])  14.5 us
    all_to_all x1, starting transfers between devices, per_device(): pair = lax.all_to_all(pair, 'x', 0, 0, tiled=True)  12.1 us
    all_to_all x1, starting transfers between devices, per_device(): shards = lax.all_to_all(slices(nz // 2, *cut), 'zq', 0, 0, tiled=True)  11.8 us
    ppermute x4, starting transfers between devices, along_ring(): lax.ppermute(block, 'y', [((i + ahead) % count, i) for i in range(count)])  11.6 us
    ppermute x1, starting transfers between devices, per_device(): other = lax.ppermute(mine, 'zh', [(0, 1), (1, 0)]).astype(F32)  11.5 us
    ppermute x2, starting transfers between devices, halos(): lax.ppermute(jnp.where(even, first, last), LAT, pairs + [(j, i) for i, j...  8.65 us
    all_to_all x1, starting transfers between devices, to_all(): lax.all_to_all(jnp.broadcast_to(block[None], (count,) + block.shape), axi...  8.53 us
  transfers between devices with their start and end apart: 22, of which 13 were waited for; matrix products, arithmetic and copies ran while one was open for 2% of the time, Pallas kernels for 8%

profile of v10, /device:TPU:1, one launch (start us, length us, event | category | flops | bytes accessed | tf_op | source)
XLA Modules:
  0.0 182.6 jit_solution(13283263135027618322)
XLA Ops:
  3.0 11.8 %all-to-all-start = ((bf16[4,24,896]{2,1,0:T(8,128)(2,1)}), bf16[4,24,896]{2,1,0:T(8,128)(2,1)S(1)}, u32[]{:S(2)}, u32[]{:S(2)}) async-start(bf16[4,24,896]{2,1,0:T(8,128)(2,1)} %shard_map.196), calls=%async_computation | async-start | bytes 344064 | tf_op jit(solution)/shard_map/all_to_all | solution.py:531
  15.9 4.0 %collective-permute-start = (bf16[24,3,256]{2,1,0:T(4,128)(2,1)S(1)}, bf16[24,3,256]{2,1,0:T(4,128)(2,1)S(1)}, u32[]{:S(2)}, u32[]{:S(2)}) collective-permute-start(bf16[24,3,256]{2,1,0:T(4,128)(2,1)S(1)} %get-tuple-element.97), channel_id=1, source_target_pairs={{32,64},{96,128},{160,192},{224,256},{288,320},{352,384},{416,448}... | collective-permute-start | bytes 110600 | tf_op jit(solution)/shard_map/ppermute | solution.py:486
  23.9 5.1 %collective-permute-start.2 = (bf16[4,24,896]{2,1,0:T(8,128)(2,1)S(1)}, bf16[4,24,896]{2,1,0:T(8,128)(2,1)S(1)}, u32[]{:S(2)}, u32[]{:S(2)}) collective-permute-start(bf16[4,24,896]{2,1,0:T(8,128)(2,1)S(1)} %all-to-all-done), channel_id=1, source_target_pairs={{0,4},{4,0},{1,5},{5,1},{2,6},{6,2},{3,7},{7,3},{8,12},{12,8},{9,1... | collective-permute-start | bytes 516104 | tf_op jit(solution)/shard_map/ppermute | solution.py:532
  30.4 3.6 %shard_map.195 = bf16[32,24,128]{2,1,0:T(8,128)(2,1)} custom-call(f32[24,49]{1,0:T(8,128)S(1)} %copy-done.5, f32[24]{0:T(128)S(1)} %copy-done.7, bf16[24,8,256]{2,1,0:T(8,128)(2,1)S(1)} %copy-done.2, bf16[24,3,256]{2,1,0:T(4,128)(2,1)S(1)} %get-tuple-element.95.up_ref, bf16[24,3,256]{2,1,0:T(4,128)(2,1)S(1)} %get-tuple-element.94.down_ref, ...), custom_call_target="tpu_custom_call" | custom-call | tf_op jit(solution)/shard_map/pallas_call | solution.py:100
  34.0 9.8 %all-to-all-start.1 = ((bf16[32,24,128]{2,1,0:T(8,128)(2,1)}), bf16[32,24,128]{2,1,0:T(8,128)(2,1)S(1)}, u32[]{:S(2)}, u32[]{:S(2)}) async-start(bf16[32,24,128]{2,1,0:T(8,128)(2,1)} %shard_map.195), calls=%async_computation.1 | async-start | bytes 393216 | tf_op jit(solution)/shard_map/all_to_all | solution.py:476
  43.9 4.3 %collective-permute-start.3 = (bf16[8,24,896]{2,1,0:T(8,128)(2,1)S(1)}, bf16[8,24,896]{2,1,0:T(8,128)(2,1)S(1)}, u32[]{:S(2)}, u32[]{:S(2)}) collective-permute-start(bf16[8,24,896]{2,1,0:T(8,128)(2,1)S(1)} %constant_dynamic-update-slice_fusion.own_ref), channel_id=1, source_target_pairs={{1,0},{2,1},{3,2},{0,3},{5,4},{6,5},{7,6},{4,7},{9,8},{10,9},{11,1... | collective-permute-start | bytes 1032200 | tf_op jit(solution)/shard_map/ppermute | solution.py:492
  50.2 5.3 %collective-permute-done.3.one_ref = bf16[8,24,896]{2,1,0:T(8,128)(2,1)S(1)} collective-permute-done((bf16[8,24,896]{2,1,0:T(8,128)(2,1)S(1)}, bf16[8,24,896]{2,1,0:T(8,128)(2,1)S(1)}, u32[]{:S(2)}, u32[]{:S(2)}) %collective-permute-start.3) | collective-permute-done | bytes 344096 | tf_op jit(solution)/shard_map/ppermute | solution.py:492
  55.5 4.5 %collective-permute-done.4.last_ref = bf16[8,24,896]{2,1,0:T(8,128)(2,1)S(1)} collective-permute-done((bf16[8,24,896]{2,1,0:T(8,128)(2,1)S(1)}, bf16[8,24,896]{2,1,0:T(8,128)(2,1)S(1)}, u32[]{:S(2)}, u32[]{:S(2)}) %collective-permute-start.4) | collective-permute-done | bytes 344096 | tf_op jit(solution)/shard_map/ppermute | solution.py:492
  61.2 12.1 %all-to-all-start.2 = ((bf16[4,128,768]{2,1,0:T(8,128)(2,1)}), bf16[4,128,768]{2,1,0:T(8,128)(2,1)S(1)}, u32[]{:S(2)}, u32[]{:S(2)}) async-start(bf16[4,128,768]{2,1,0:T(8,128)(2,1)} %get-tuple-element.50), calls=%async_computation.2 | async-start | bytes 1572864 | tf_op jit(solution)/shard_map/all_to_all | solution.py:544
  75.3 3.4 %collective-permute-start.6 = (bf16[4,24,896]{2,1,0:T(8,128)(2,1)S(1)}, bf16[4,24,896]{2,1,0:T(8,128)(2,1)S(1)}, u32[]{:S(2)}, u32[]{:S(2)}) collective-permute-start(bf16[4,24,896]{2,1,0:T(8,128)(2,1)S(1)} %slice.71), channel_id=1, source_target_pairs={{3,0},{0,1},{1,2},{2,3},{7,4},{4,5},{5,6},{6,7},{11,8},{8,9},{9,10... | collective-permute-start | bytes 516104 | tf_op jit(solution)/shard_map/ppermute | solution.py:492
  80.2 3.2 %collective-permute-done.6.high_ref = bf16[4,24,896]{2,1,0:T(8,128)(2,1)S(1)} collective-permute-done((bf16[4,24,896]{2,1,0:T(8,128)(2,1)S(1)}, bf16[4,24,896]{2,1,0:T(8,128)(2,1)S(1)}, u32[]{:S(2)}, u32[]{:S(2)}) %collective-permute-start.6) | collective-permute-done | bytes 172064 | tf_op jit(solution)/shard_map/ppermute | solution.py:492
  84.7 3.7 %collective-permute-start.7 = (bf16[4,128,768]{2,1,0:T(8,128)(2,1)S(1)}, bf16[4,128,768]{2,1,0:T(8,128)(2,1)S(1)}, u32[]{:S(2)}, u32[]{:S(2)}) collective-permute-start(bf16[4,128,768]{2,1,0:T(8,128)(2,1)S(1)} %all-to-all-done.2.own_ref), channel_id=1, source_target_pairs={{0,32},{32,0},{1,33},{33,1},{2,34},{34,2},{3,35},{35,3},{4,36},{36... | collective-permute-start | bytes 2359304 | tf_op jit(solution)/shard_map/ppermute | solution.py:548
  93.7 3.8 %all-to-all-start.3 = ((bf16[8,64,768]{2,1,0:T(8,128)(2,1)}), bf16[8,64,768]{2,1,0:T(8,128)(2,1)S(1)}, u32[]{:S(2)}, u32[]{:S(2)}) async-start(bf16[8,64,768]{2,1,0:T(8,128)(2,1)} %get-tuple-element.59), calls=%async_computation.3 | async-start | bytes 1572864 | tf_op jit(solution)/shard_map/all_to_all | solution.py:552
  103.8 3.4 %collective-permute-start.8 = (bf16[8,24,768]{2,1,0:T(8,128)(2,1)S(1)}, bf16[8,24,768]{2,1,0:T(8,128)(2,1)S(1)}, u32[]{:S(2)}, u32[]{:S(2)}) collective-permute-start(bf16[8,24,768]{2,1,0:T(8,128)(2,1)S(1)} %bitcast.35), channel_id=1, source_target_pairs={{0,1},{1,2},{2,3},{3,0},{4,5},{5,6},{6,7},{7,4},{8,9},{9,10},{10,1... | collective-permute-start | bytes 884744 | tf_op jit(solution)/shard_map/ppermute | solution.py:499
  110.9 11.0 %all-to-all-start.4 = ((bf16[32,16,128]{2,1,0:T(8,128)(2,1)}), bf16[32,16,128]{2,1,0:T(8,128)(2,1)S(1)}, u32[]{:S(2)}, u32[]{:S(2)}) async-start(bf16[32,16,128]{2,1,0:T(8,128)(2,1)} %shard_map.201), calls=%async_computation.4 | async-start | bytes 262144 | tf_op jit(solution)/shard_map/all_to_all | solution.py:476
  123.1 3.1 %collective-permute-start.11 = (bf16[4,24,768]{2,1,0:T(8,128)(2,1)S(1)}, bf16[4,24,768]{2,1,0:T(8,128)(2,1)S(1)}, u32[]{:S(2)}, u32[]{:S(2)}) collective-permute-start(bf16[4,24,768]{2,1,0:T(8,128)(2,1)S(1)} %slice.126), channel_id=1, source_target_pairs={{0,4},{4,0},{1,5},{5,1},{2,6},{6,2},{3,7},{7,3},{8,12},{12,8},{9,1... | collective-permute-start | bytes 442376 | tf_op jit(solution)/shard_map/ppermute | solution.py:462
  126.2 3.7 %collective-permute-done.11 = bf16[4,24,768]{2,1,0:T(8,128)(2,1)S(1)} collective-permute-done((bf16[4,24,768]{2,1,0:T(8,128)(2,1)S(1)}, bf16[4,24,768]{2,1,0:T(8,128)(2,1)S(1)}, u32[]{:S(2)}, u32[]{:S(2)}) %collective-permute-start.11) | collective-permute-done | bytes 147488 | tf_op jit(solution)/shard_map/ppermute | solution.py:462
  130.6 3.4 %all-to-all-done.4.recv_ref = bf16[32,16,128]{2,1,0:T(8,128)(2,1)S(1)} async-done(((bf16[32,16,128]{2,1,0:T(8,128)(2,1)}), bf16[32,16,128]{2,1,0:T(8,128)(2,1)S(1)}, u32[]{:S(2)}, u32[]{:S(2)}) %all-to-all-start.4) | async-done | bytes 131104 | tf_op jit(solution)/shard_map/all_to_all | solution.py:476
  134.2 5.5 %all-to-all-start.5 = ((bf16[4,24,768]{2,1,0:T(8,128)(2,1)}), bf16[4,24,768]{2,1,0:T(8,128)(2,1)S(1)}, u32[]{:S(2)}, u32[]{:S(2)}) async-start(bf16[4,24,768]{2,1,0:T(8,128)(2,1)} %fusion.2), calls=%async_computation.5 | async-start | bytes 294912 | tf_op jit(solution)/shard_map/all_to_all | solution.py:561
  139.8 4.7 %collective-permute-start.13 = (bf16[24,3,256]{2,1,0:T(4,128)(2,1)S(1)}, bf16[24,3,256]{2,1,0:T(4,128)(2,1)S(1)}, u32[]{:S(2)}, u32[]{:S(2)}) collective-permute-start(bf16[24,3,256]{2,1,0:T(4,128)(2,1)S(1)} %get-tuple-element.91), channel_id=1, source_target_pairs={{32,64},{96,128},{160,192},{224,256},{288,320},{352,384},{416,448}... | collective-permute-start | bytes 110600 | tf_op jit(solution)/shard_map/ppermute | solution.py:486
  149.8 11.5 %collective-permute-start.12 = (bf16[24,896]{1,0:T(8,128)(2,1)S(1)}, bf16[24,896]{1,0:T(8,128)(2,1)S(1)}, u32[]{:S(2)}, u32[]{:S(2)}) collective-permute-start(bf16[24,896]{1,0:T(8,128)(2,1)S(1)} %pad_maximum_fusion), channel_id=1, source_target_pairs={{0,256},{256,0},{1,257},{257,1},{2,258},{258,2},{3,259},{259,3},{4... | collective-permute-start | bytes 129032 | tf_op jit(solution)/shard_map/ppermute | solution.py:569
  164.6 8.5 %all-to-all-start.6 = ((bf16[8,24,896]{2,1,0:T(8,128)(2,1)}), bf16[8,24,896]{2,1,0:T(8,128)(2,1)S(1)}, u32[]{:S(2)}, u32[]{:S(2)}) async-start(bf16[8,24,896]{2,1,0:T(8,128)(2,1)} %broadcast_in_dim.39), calls=%async_computation.6 | async-start | bytes 688128 | tf_op jit(solution)/shard_map/all_to_all | solution.py:472
  173.3 3.4 %shard_map.204 = f32[24,8,256]{2,1,0:T(8,128)} custom-call(f32[24,49]{1,0:T(8,128)S(1)} %copy-done.6, f32[24,8,256]{2,1,0:T(8,128)S(1)} %get-tuple-element.69.dconv_ref.x_ref, bf16[24,3,256]{2,1,0:T(4,128)(2,1)S(1)} %get-tuple-element.74.up_ref, bf16[24,3,256]{2,1,0:T(4,128)(2,1)S(1)} %get-tuple-element.75.down_ref, bf16[24,8,256]{2,1,0:T(8,128)(2,1)S(1)} %copy-done.1), custom_call_target="tpu_custom_call" | custom-call | tf_op jit(solution)/shard_map/pallas_call | solution.py:267
  176.6 3.8 %all-to-all-done.6.gathered_ref = bf16[8,24,896]{2,1,0:T(8,128)(2,1)S(1)} async-done(((bf16[8,24,896]{2,1,0:T(8,128)(2,1)}), bf16[8,24,896]{2,1,0:T(8,128)(2,1)S(1)}, u32[]{:S(2)}, u32[]{:S(2)}) %all-to-all-start.6) | async-done | bytes 344096 | tf_op jit(solution)/shard_map/all_to_all | solution.py:472
  (89 shorter events, 44.7 us)
Async XLA Ops:
  3.0 47.2 %copy-start.10 = (f32[768]{0:T(1024)S(1)}, f32[768]{0:T(1024)}, u32[]{:S(2)}) copy-start(f32[768]{0:T(1024)} %param.17) | copy-start | bytes 9220
  3.0 47.2 %copy-start.11 = (f32[768]{0:T(1024)S(1)}, f32[768]{0:T(1024)}, u32[]{:S(2)}) copy-start(f32[768]{0:T(1024)} %param.18) | copy-start | bytes 9220
  3.0 20.8 %all-to-all-start = ((bf16[4,24,896]{2,1,0:T(8,128)(2,1)}), bf16[4,24,896]{2,1,0:T(8,128)(2,1)S(1)}, u32[]{:S(2)}, u32[]{:S(2)}) async-start(bf16[4,24,896]{2,1,0:T(8,128)(2,1)} %shard_map.196), calls=%async_computation | async-start | bytes 344064 | tf_op jit(solution)/shard_map/all_to_all | solution.py:531
  15.9 13.1 %collective-permute-start = (bf16[24,3,256]{2,1,0:T(4,128)(2,1)S(1)}, bf16[24,3,256]{2,1,0:T(4,128)(2,1)S(1)}, u32[]{:S(2)}, u32[]{:S(2)}) collective-permute-start(bf16[24,3,256]{2,1,0:T(4,128)(2,1)S(1)} %get-tuple-element.97), channel_id=1, source_target_pairs={{32,64},{96,128},{160,192},{224,256},{288,320},{352,384},{416,448}... | collective-permute-start | bytes 110600 | tf_op jit(solution)/shard_map/ppermute | solution.py:486
  19.9 9.1 %collective-permute-start.1 = (bf16[24,3,256]{2,1,0:T(4,128)(2,1)S(1)}, bf16[24,3,256]{2,1,0:T(4,128)(2,1)S(1)}, u32[]{:S(2)}, u32[]{:S(2)}) collective-permute-start(bf16[24,3,256]{2,1,0:T(4,128)(2,1)S(1)} %get-tuple-element.96), channel_id=1, source_target_pairs={{0,32},{64,96},{128,160},{192,224},{256,288},{320,352},{384,416},{... | collective-permute-start | bytes 110600 | tf_op jit(solution)/shard_map/ppermute | solution.py:484
  23.9 10.1 %collective-permute-start.2 = (bf16[4,24,896]{2,1,0:T(8,128)(2,1)S(1)}, bf16[4,24,896]{2,1,0:T(8,128)(2,1)S(1)}, u32[]{:S(2)}, u32[]{:S(2)}) collective-permute-start(bf16[4,24,896]{2,1,0:T(8,128)(2,1)S(1)} %all-to-all-done), channel_id=1, source_target_pairs={{0,4},{4,0},{1,5},{5,1},{2,6},{6,2},{3,7},{7,3},{8,12},{12,8},{9,1... | collective-permute-start | bytes 516104 | tf_op jit(solution)/shard_map/ppermute | solution.py:532
  34.0 26.1 %all-to-all-start.1 = ((bf16[32,24,128]{2,1,0:T(8,128)(2,1)}), bf16[32,24,128]{2,1,0:T(8,128)(2,1)S(1)}, u32[]{:S(2)}, u32[]{:S(2)}) async-start(bf16[32,24,128]{2,1,0:T(8,128)(2,1)} %shard_map.195), calls=%async_computation.1 | async-start | bytes 393216 | tf_op jit(solution)/shard_map/all_to_all | solution.py:476
  43.9 11.6 %collective-permute-start.3 = (bf16[8,24,896]{2,1,0:T(8,128)(2,1)S(1)}, bf16[8,24,896]{2,1,0:T(8,128)(2,1)S(1)}, u32[]{:S(2)}, u32[]{:S(2)}) collective-permute-start(bf16[8,24,896]{2,1,0:T(8,128)(2,1)S(1)} %constant_dynamic-update-slice_fusion.own_ref), channel_id=1, source_target_pairs={{1,0},{2,1},{3,2},{0,3},{5,4},{6,5},{7,6},{4,7},{9,8},{10,9},{11,1... | collective-permute-start | bytes 1032200 | tf_op jit(solution)/shard_map/ppermute | solution.py:492
  48.2 11.8 %collective-permute-start.4 = (bf16[8,24,896]{2,1,0:T(8,128)(2,1)S(1)}, bf16[8,24,896]{2,1,0:T(8,128)(2,1)S(1)}, u32[]{:S(2)}, u32[]{:S(2)}) collective-permute-start(bf16[8,24,896]{2,1,0:T(8,128)(2,1)S(1)} %constant_dynamic-update-slice_fusion.own_ref), channel_id=1, source_target_pairs={{3,0},{0,1},{1,2},{2,3},{7,4},{4,5},{5,6},{6,7},{11,8},{8,9},{9,10... | collective-permute-start | bytes 1032200 | tf_op jit(solution)/shard_map/ppermute | solution.py:492
  61.2 23.5 %all-to-all-start.2 = ((bf16[4,128,768]{2,1,0:T(8,128)(2,1)}), bf16[4,128,768]{2,1,0:T(8,128)(2,1)S(1)}, u32[]{:S(2)}, u32[]{:S(2)}) async-start(bf16[4,128,768]{2,1,0:T(8,128)(2,1)} %get-tuple-element.50), calls=%async_computation.2 | async-start | bytes 1572864 | tf_op jit(solution)/shard_map/all_to_all | solution.py:544
  73.3 6.9 %collective-permute-start.5 = (bf16[4,24,896]{2,1,0:T(8,128)(2,1)S(1)}, bf16[4,24,896]{2,1,0:T(8,128)(2,1)S(1)}, u32[]{:S(2)}, u32[]{:S(2)}) collective-permute-start(bf16[4,24,896]{2,1,0:T(8,128)(2,1)S(1)} %slice.70), channel_id=1, source_target_pairs={{1,0},{2,1},{3,2},{0,3},{5,4},{6,5},{7,6},{4,7},{9,8},{10,9},{11,1... | collective-permute-start | bytes 516104 | tf_op jit(solution)/shard_map/ppermute | solution.py:492
  75.3 8.1 %collective-permute-start.6 = (bf16[4,24,896]{2,1,0:T(8,128)(2,1)S(1)}, bf16[4,24,896]{2,1,0:T(8,128)(2,1)S(1)}, u32[]{:S(2)}, u32[]{:S(2)}) collective-permute-start(bf16[4,24,896]{2,1,0:T(8,128)(2,1)S(1)} %slice.71), channel_id=1, source_target_pairs={{3,0},{0,1},{1,2},{2,3},{7,4},{4,5},{5,6},{6,7},{11,8},{8,9},{9,10... | collective-permute-start | bytes 516104 | tf_op jit(solution)/shard_map/ppermute | solution.py:492
  84.7 5.6 %collective-permute-start.7 = (bf16[4,128,768]{2,1,0:T(8,128)(2,1)S(1)}, bf16[4,128,768]{2,1,0:T(8,128)(2,1)S(1)}, u32[]{:S(2)}, u32[]{:S(2)}) collective-permute-start(bf16[4,128,768]{2,1,0:T(8,128)(2,1)S(1)} %all-to-all-done.2.own_ref), channel_id=1, source_target_pairs={{0,32},{32,0},{1,33},{33,1},{2,34},{34,2},{3,35},{35,3},{4,36},{36... | collective-permute-start | bytes 2359304 | tf_op jit(solution)/shard_map/ppermute | solution.py:548
  93.7 16.0 %all-to-all-start.3 = ((bf16[8,64,768]{2,1,0:T(8,128)(2,1)}), bf16[8,64,768]{2,1,0:T(8,128)(2,1)S(1)}, u32[]{:S(2)}, u32[]{:S(2)}) async-start(bf16[8,64,768]{2,1,0:T(8,128)(2,1)} %get-tuple-element.59), calls=%async_computation.3 | async-start | bytes 1572864 | tf_op jit(solution)/shard_map/all_to_all | solution.py:552
  101.9 20.1 %collective-permute-start.10 = (bf16[8,24,768]{2,1,0:T(8,128)(2,1)S(1)}, bf16[8,24,768]{2,1,0:T(8,128)(2,1)S(1)}, u32[]{:S(2)}, u32[]{:S(2)}) collective-permute-start(bf16[8,24,768]{2,1,0:T(8,128)(2,1)S(1)} %bitcast.36), channel_id=1, source_target_pairs={{0,3},{1,0},{2,1},{3,2},{4,7},{5,4},{6,5},{7,6},{8,11},{9,8},{10,9... | collective-permute-start | bytes 884744 | tf_op jit(solution)/shard_map/ppermute | solution.py:499
  103.8 18.1 %collective-permute-start.8 = (bf16[8,24,768]{2,1,0:T(8,128)(2,1)S(1)}, bf16[8,24,768]{2,1,0:T(8,128)(2,1)S(1)}, u32[]{:S(2)}, u32[]{:S(2)}) collective-permute-start(bf16[8,24,768]{2,1,0:T(8,128)(2,1)S(1)} %bitcast.35), channel_id=1, source_target_pairs={{0,1},{1,2},{2,3},{3,0},{4,5},{5,6},{6,7},{7,4},{8,9},{9,10},{10,1... | collective-permute-start | bytes 884744 | tf_op jit(solution)/shard_map/ppermute | solution.py:499
  107.2 14.8 %collective-permute-start.9 = (bf16[8,24,768]{2,1,0:T(8,128)(2,1)S(1)}, bf16[8,24,768]{2,1,0:T(8,128)(2,1)}, u32[]{:S(2)}, u32[]{:S(2)}) collective-permute-start(bf16[8,24,768]{2,1,0:T(8,128)(2,1)S(1)} %bitcast.34), channel_id=1, source_target_pairs={{0,2},{1,3},{2,0},{3,1},{4,6},{5,7},{6,4},{7,5},{8,10},{9,11},{10,... | collective-permute-start | bytes 884744 | tf_op jit(solution)/shard_map/ppermute | solution.py:499
  110.9 23.2 %all-to-all-start.4 = ((bf16[32,16,128]{2,1,0:T(8,128)(2,1)}), bf16[32,16,128]{2,1,0:T(8,128)(2,1)S(1)}, u32[]{:S(2)}, u32[]{:S(2)}) async-start(bf16[32,16,128]{2,1,0:T(8,128)(2,1)} %shard_map.201), calls=%async_computation.4 | async-start | bytes 262144 | tf_op jit(solution)/shard_map/all_to_all | solution.py:476
  123.1 6.9 %collective-permute-start.11 = (bf16[4,24,768]{2,1,0:T(8,128)(2,1)S(1)}, bf16[4,24,768]{2,1,0:T(8,128)(2,1)S(1)}, u32[]{:S(2)}, u32[]{:S(2)}) collective-permute-start(bf16[4,24,768]{2,1,0:T(8,128)(2,1)S(1)} %slice.126), channel_id=1, source_target_pairs={{0,4},{4,0},{1,5},{5,1},{2,6},{6,2},{3,7},{7,3},{8,12},{12,8},{9,1... | collective-permute-start | bytes 442376 | tf_op jit(solution)/shard_map/ppermute | solution.py:462
  134.2 15.5 %all-to-all-start.5 = ((bf16[4,24,768]{2,1,0:T(8,128)(2,1)}), bf16[4,24,768]{2,1,0:T(8,128)(2,1)S(1)}, u32[]{:S(2)}, u32[]{:S(2)}) async-start(bf16[4,24,768]{2,1,0:T(8,128)(2,1)} %fusion.2), calls=%async_computation.5 | async-start | bytes 294912 | tf_op jit(solution)/shard_map/all_to_all | solution.py:561
  139.8 21.5 %collective-permute-start.13 = (bf16[24,3,256]{2,1,0:T(4,128)(2,1)S(1)}, bf16[24,3,256]{2,1,0:T(4,128)(2,1)S(1)}, u32[]{:S(2)}, u32[]{:S(2)}) collective-permute-start(bf16[24,3,256]{2,1,0:T(4,128)(2,1)S(1)} %get-tuple-element.91), channel_id=1, source_target_pairs={{32,64},{96,128},{160,192},{224,256},{288,320},{352,384},{416,448}... | collective-permute-start | bytes 110600 | tf_op jit(solution)/shard_map/ppermute | solution.py:486
  144.5 16.8 %collective-permute-start.14 = (bf16[24,3,256]{2,1,0:T(4,128)(2,1)S(1)}, bf16[24,3,256]{2,1,0:T(4,128)(2,1)S(1)}, u32[]{:S(2)}, u32[]{:S(2)}) collective-permute-start(bf16[24,3,256]{2,1,0:T(4,128)(2,1)S(1)} %get-tuple-element.90), channel_id=1, source_target_pairs={{0,32},{64,96},{128,160},{192,224},{256,288},{320,352},{384,416},{... | collective-permute-start | bytes 110600 | tf_op jit(solution)/shard_map/ppermute | solution.py:484
  149.8 13.9 %collective-permute-start.12 = (bf16[24,896]{1,0:T(8,128)(2,1)S(1)}, bf16[24,896]{1,0:T(8,128)(2,1)S(1)}, u32[]{:S(2)}, u32[]{:S(2)}) collective-permute-start(bf16[24,896]{1,0:T(8,128)(2,1)S(1)} %pad_maximum_fusion), channel_id=1, source_target_pairs={{0,256},{256,0},{1,257},{257,1},{2,258},{258,2},{3,259},{259,3},{4... | collective-permute-start | bytes 129032 | tf_op jit(solution)/shard_map/ppermute | solution.py:569
  164.6 15.8 %all-to-all-start.6 = ((bf16[8,24,896]{2,1,0:T(8,128)(2,1)}), bf16[8,24,896]{2,1,0:T(8,128)(2,1)S(1)}, u32[]{:S(2)}, u32[]{:S(2)}) async-start(bf16[8,24,896]{2,1,0:T(8,128)(2,1)} %broadcast_in_dim.39), calls=%async_computation.6 | async-start | bytes 688128 | tf_op jit(solution)/shard_map/all_to_all | solution.py:472
  (10 other events, 143.0 us)

commit v11 on v10

--- a/solution.py
+++ b/solution.py
@@ -14,7 +14,7 @@
 F32 = jnp.float32
 BF = jnp.bfloat16
 EXT = 16
-VMEM_BYTES = 20 * 1024 * 1024
+VMEM_BYTES = 12 * 1024 * 1024
 SIDE = 128
 
 
@@ -71,7 +71,7 @@
     return total
 
 
-def forward_body(taps_ref, bias_ref, x_ref, up_ref, down_ref, metric_ref, dy_ref, out_ref, ext, h_rows, dy_rows):
+def forward_body(taps_ref, x_ref, up_ref, down_ref, metric_ref, dy_ref, out_ref, ext, h_rows, dy_rows):
     cdev, rows, width = x_ref.shape
     fill_rows(x_ref, up_ref, down_ref, ext)
     dy_flat = dy_ref[...].astype(F32).reshape(cdev * rows, width)
@@ -80,7 +80,7 @@
     metric = jnp.broadcast_to(metric_ref[...], (rows, width))
 
     def channel(c, carry):
-        h = bias_ref[c] + metric * stencil(taps_ref, c, row_shifts(ext, c, rows), False)
+        h = taps_ref[c, 49] + metric * stencil(taps_ref, c, row_shifts(ext, c, rows), False)
         for t in range(width // 128):
             h_rows[t, pl.ds(pl.multiple_of(c * rows, rows), rows), :] = h[:, t * 128 : t * 128 + 128]
         return carry
@@ -95,18 +95,18 @@
             out_ref[at + 1] = jnp.where(low, pltpu.roll(h_tile, 64, 1), dy_tile).astype(BF)
 
 
-def forward(taps, bias, x, up, down, metric, dy):
+def forward(taps, x, up, down, metric, dy):
     cdev, rows, width = x.shape
     return call(
         forward_body,
         jax.ShapeDtypeStruct((rows * width // 64, cdev, 128), BF),
-        [smem(), smem()] + [vmem()] * 5,
+        [smem()] + [vmem()] * 5,
         [
             pltpu.VMEM((cdev, EXT, width), F32),
             pltpu.VMEM((width // 128, cdev * rows, 128), F32),
             pltpu.VMEM((width // 128, cdev * rows, 128), F32),
         ],
-    )(taps, bias, x, up, down, metric[:, None], dy)
+    )(taps, x, up, down, metric[:, None], dy)
 
 
 def norm_body(recv_ref, gain_ref, bias_ref, pair_ref, nhat_ref, rstd_ref):
@@ -420,9 +420,10 @@
     )(w_in, w_out, b_in[None])
 
 
-def results_body(part, n_taps, gathered_ref, gamma_ref, b_out_ref, dw_in_ref, dw_out_ref, taps_ref, db_ref, rest_ref):
+def results_body(part, n_taps, gathered_ref, gamma_ref, b_out_ref, dw_in_ref, dw_out_ref, taps_ref, db_ref, *rest):
     chans = dw_in_ref.shape[1]
-    total = None
+    lane = lax.broadcasted_iota(jnp.int32, (1, 128), 1)
+    total, db = None, None
     for k in range(gathered_ref.shape[0]):
         block = gathered_ref[k].astype(F32)
         dw_in_ref[k * part : (k + 1) * part] = block[:part, :chans]
@@ -430,16 +431,21 @@
         side = block[:, chans:]
         side = side + pltpu.roll(side, 64, 1)
         line = side.T
-        db_ref[k : k + 1] = (line[62:63] + line[63:64])[:, :part]
+        line = line[62:63] + line[63:64]
+        line = jnp.concatenate([line, jnp.zeros((1, 128 - line.shape[1]), F32)], 1)
+        line = jnp.where(lane < part, line, 0.0)
+        line = line if k == 0 else pltpu.roll(line, k * part, 1)
+        db = line if db is None else db + line
         total = side if total is None else total + side
+    db_ref[...] = db[0, : db_ref.shape[0]]
     taps_ref[...] = total[:, :n_taps]
     lines = total.T
-    dysum = lines[n_taps + 1 : n_taps + 2]
-    rest_ref[0:1] = lines[n_taps : n_taps + 1]
-    rest_ref[1:2] = lines[56:57] + lines[57:58]
-    rest_ref[2:3] = lines[58:59] + lines[59:60]
-    rest_ref[3:4] = gamma_ref[...] * dysum
-    rest_ref[4:5] = lines[60:61] + lines[61:62] + b_out_ref[...] * dysum
+    dysum = lines[n_taps + 1]
+    rest[0][...] = lines[n_taps]
+    rest[1][...] = lines[56] + lines[57]
+    rest[2][...] = lines[58] + lines[59]
+    rest[3][...] = gamma_ref[...] * dysum
+    rest[4][...] = lines[60] + lines[61] + b_out_ref[...] * dysum
 
 
 def results(part, n_taps, gathered, chans, gamma, b_out):
@@ -450,11 +456,11 @@
             jax.ShapeDtypeStruct((members * part, chans), F32),
             jax.ShapeDtypeStruct((members * part, chans), F32),
             jax.ShapeDtypeStruct((rows, n_taps), F32),
-            jax.ShapeDtypeStruct((members, part), F32),
-            jax.ShapeDtypeStruct((5, rows), F32),
-        ],
+            jax.ShapeDtypeStruct((members * part,), F32),
+        ]
+        + [jax.ShapeDtypeStruct((rows,), F32)] * 5,
         [vmem()] * 3,
-    )(gathered, gamma[None], b_out[None])
+    )(gathered, gamma, b_out)
 
 
 def to_neighbour(blocks):
@@ -532,7 +538,8 @@
     beside = lax.ppermute(shards, "zp", [(0, 1), (1, 0)])
 
     up, down = halos(block_input[:, :3], block_input[:, rows - 3 :])
-    blocks = forward(kernel, conv_bias, block_input, up, down, metric, out_grad)
+    taps_bias = jnp.concatenate([kernel, conv_bias[:, None]], 1)
+    blocks = forward(taps_bias, block_input, up, down, metric, out_grad)
     blocks, shards, beside = lax.optimization_barrier((blocks, shards, beside))
 
     recv = exchange(blocks)
@@ -572,8 +579,8 @@
     small = small + other[:, chans : chans + count] + other[:, chans + count :]
     mine = jnp.concatenate([dws.astype(BF)] + list(two_parts(small)), 1)
     mine, dup, ddown = lax.optimization_barrier((mine, dup, ddown))
-    grad_input = spread_back(kernel, dconv, dup, ddown, out_grad)
-    grad_w_in, grad_w_out, grad_kernel, db, rest = results(
+    grad_input = spread_back(taps_bias, dconv, dup, ddown, out_grad)
+    grad_w_in, grad_w_out, grad_kernel, db, *rest = results(
         part, kernel.shape[1], to_all(mine, ("x", "c")), chans, gamma_own, b_out
     )
     return (
@@ -583,7 +590,7 @@
         rest[1],
         rest[2],
         grad_w_in,
-        db.reshape(hdev),
+        db,
         grad_w_out,
         rest[3],
         rest[4],

time: 184 us -> 183 us (level)
  waiting for transfers between devices: 31.9 us -> 28.4 us
  starting transfers between devices: 118 us -> 121 us
    all_to_all x1, starting transfers between devices: 12.1 us -> 8.52 us  [per_device(): pair = lax.all_to_all(pair, 'x', 0, 0, tiled=True)]
    ppermute x1, starting transfers between devices: 3.72 us -> 5.87 us  [per_device(): other = lax.ppermute(pair, 'c', [(0, 1), (1, 0)])]
    unnamed x25 -> x19, local copies, waits for them, and re-layouts: 4.05 us -> 2.67 us
  transfers between devices with their start and end apart: 22 -> 22, of which waited for: 13 -> 10; matrix products, arithmetic and copies ran while one was open for 2% -> 3% of each run, Pallas kernels for 8% -> 8%
where the time goes in v11:
time: 183 us; the launch traced here: 182 us
  starting transfers between devices  121 us (66%)
  waiting for transfers between devices  28.4 us (16%)
  Pallas kernels  20.5 us (11%)
  local copies, waits for them, and re-layouts  6 us (3%)
  other arithmetic  4.43 us (2%)
    all_to_all x2, starting transfers between devices, exchange(): return lax.all_to_all(blocks, CHAN, 0, 0, tiled=True)  22.6 us
    ppermute x4, waiting for transfers between devices, along_ring(): lax.ppermute(block, 'y', [((i + ahead) % count, i) for i in range(count)])  14 us
    all_to_all x1, starting transfers between devices, per_device(): shards = lax.all_to_all(slices(nz // 2, *cut), 'zq', 0, 0, tiled=True)  11.8 us
    ppermute x4, starting transfers between devices, along_ring(): lax.ppermute(block, 'y', [((i + ahead) % count, i) for i in range(count)])  11.6 us
    ppermute x1, starting transfers between devices, per_device(): other = lax.ppermute(mine, 'zh', [(0, 1), (1, 0)]).astype(F32)  11.4 us
    all_to_all x1, starting transfers between devices, to_all(): lax.all_to_all(jnp.broadcast_to(block[None], (count,) + block.shape), axi...  10.1 us
    ppermute x2, starting transfers between devices, halos(): lax.ppermute(jnp.where(even, first, last), LAT, pairs + [(j, i) for i, j...  8.7 us
    all_to_all x1, starting transfers between devices, per_device(): pair = lax.all_to_all(pair, 'x', 0, 0, tiled=True)  8.52 us
  transfers between devices with their start and end apart: 22, of which 10 were waited for; matrix products, arithmetic and copies ran while one was open for 3% of the time, Pallas kernels for 8%

profile of v11, /device:TPU:1, one launch (start us, length us, event | category | flops | bytes accessed | tf_op | source)
XLA Modules:
  0.0 181.7 jit_solution(3806498746021268421)
XLA Ops:
  3.0 11.8 %all-to-all-start = ((bf16[4,24,896]{2,1,0:T(8,128)(2,1)}), bf16[4,24,896]{2,1,0:T(8,128)(2,1)S(1)}, u32[]{:S(2)}, u32[]{:S(2)}) async-start(bf16[4,24,896]{2,1,0:T(8,128)(2,1)} %shard_map.196), calls=%async_computation | async-start | bytes 344064 | tf_op jit(solution)/shard_map/all_to_all | solution.py:537
  15.9 4.0 %collective-permute-start = (bf16[24,3,256]{2,1,0:T(4,128)(2,1)S(1)}, bf16[24,3,256]{2,1,0:T(4,128)(2,1)S(1)}, u32[]{:S(2)}, u32[]{:S(2)}) collective-permute-start(bf16[24,3,256]{2,1,0:T(4,128)(2,1)S(1)} %get-tuple-element.105), channel_id=1, source_target_pairs={{32,64},{96,128},{160,192},{224,256},{288,320},{352,384},{416,448}... | collective-permute-start | bytes 110600 | tf_op jit(solution)/shard_map/ppermute | solution.py:492
  24.0 4.9 %collective-permute-start.2 = (bf16[4,24,896]{2,1,0:T(8,128)(2,1)S(1)}, bf16[4,24,896]{2,1,0:T(8,128)(2,1)S(1)}, u32[]{:S(2)}, u32[]{:S(2)}) collective-permute-start(bf16[4,24,896]{2,1,0:T(8,128)(2,1)S(1)} %all-to-all-done), channel_id=1, source_target_pairs={{0,4},{4,0},{1,5},{5,1},{2,6},{6,2},{3,7},{7,3},{8,12},{12,8},{9,1... | collective-permute-start | bytes 516104 | tf_op jit(solution)/shard_map/ppermute | solution.py:538
  29.1 3.6 %shard_map.195 = bf16[32,24,128]{2,1,0:T(8,128)(2,1)} custom-call(f32[24,50]{1,0:T(8,128)S(1)} %pad_maximum_fusion.2.taps_ref, bf16[24,8,256]{2,1,0:T(8,128)(2,1)S(1)} %copy-done.2, bf16[24,3,256]{2,1,0:T(4,128)(2,1)S(1)} %get-tuple-element.103.up_ref, bf16[24,3,256]{2,1,0:T(4,128)(2,1)S(1)} %get-tuple-element.102.down_ref, f32[8,1]{1,0:T(8,128)S(1)} %copy.23.metric_ref, ...), custom_call_target="tpu_custom_call" | custom-call | tf_op jit(solution)/shard_map/pallas_call | solution.py:100
  32.6 11.9 %all-to-all-start.1 = ((bf16[32,24,128]{2,1,0:T(8,128)(2,1)}), bf16[32,24,128]{2,1,0:T(8,128)(2,1)S(1)}, u32[]{:S(2)}, u32[]{:S(2)}) async-start(bf16[32,24,128]{2,1,0:T(8,128)(2,1)} %shard_map.195), calls=%async_computation.1 | async-start | bytes 393216 | tf_op jit(solution)/shard_map/all_to_all | solution.py:482
  44.6 4.3 %collective-permute-start.3 = (bf16[8,24,896]{2,1,0:T(8,128)(2,1)S(1)}, bf16[8,24,896]{2,1,0:T(8,128)(2,1)S(1)}, u32[]{:S(2)}, u32[]{:S(2)}) collective-permute-start(bf16[8,24,896]{2,1,0:T(8,128)(2,1)S(1)} %constant_dynamic-update-slice_fusion.own_ref), channel_id=1, source_target_pairs={{1,0},{2,1},{3,2},{0,3},{5,4},{6,5},{7,6},{4,7},{9,8},{10,9},{11,1... | collective-permute-start | bytes 1032200 | tf_op jit(solution)/shard_map/ppermute | solution.py:498
  50.9 5.2 %collective-permute-done.3.one_ref = bf16[8,24,896]{2,1,0:T(8,128)(2,1)S(1)} collective-permute-done((bf16[8,24,896]{2,1,0:T(8,128)(2,1)S(1)}, bf16[8,24,896]{2,1,0:T(8,128)(2,1)S(1)}, u32[]{:S(2)}, u32[]{:S(2)}) %collective-permute-start.3) | collective-permute-done | bytes 344096 | tf_op jit(solution)/shard_map/ppermute | solution.py:498
  56.2 4.5 %collective-permute-done.4.last_ref = bf16[8,24,896]{2,1,0:T(8,128)(2,1)S(1)} collective-permute-done((bf16[8,24,896]{2,1,0:T(8,128)(2,1)S(1)}, bf16[8,24,896]{2,1,0:T(8,128)(2,1)S(1)}, u32[]{:S(2)}, u32[]{:S(2)}) %collective-permute-start.4) | collective-permute-done | bytes 344096 | tf_op jit(solution)/shard_map/ppermute | solution.py:498
  61.8 8.5 %all-to-all-start.2 = ((bf16[4,128,768]{2,1,0:T(8,128)(2,1)}), bf16[4,128,768]{2,1,0:T(8,128)(2,1)S(1)}, u32[]{:S(2)}, u32[]{:S(2)}) async-start(bf16[4,128,768]{2,1,0:T(8,128)(2,1)} %get-tuple-element.54), calls=%async_computation.2 | async-start | bytes 1572864 | tf_op jit(solution)/shard_map/all_to_all | solution.py:551
  72.3 3.4 %collective-permute-start.6 = (bf16[4,24,896]{2,1,0:T(8,128)(2,1)S(1)}, bf16[4,24,896]{2,1,0:T(8,128)(2,1)S(1)}, u32[]{:S(2)}, u32[]{:S(2)}) collective-permute-start(bf16[4,24,896]{2,1,0:T(8,128)(2,1)S(1)} %slice.56), channel_id=1, source_target_pairs={{3,0},{0,1},{1,2},{2,3},{7,4},{4,5},{5,6},{6,7},{11,8},{8,9},{9,10... | collective-permute-start | bytes 516104 | tf_op jit(solution)/shard_map/ppermute | solution.py:498
  76.5 3.5 %collective-permute-done.6.high_ref = bf16[4,24,896]{2,1,0:T(8,128)(2,1)S(1)} collective-permute-done((bf16[4,24,896]{2,1,0:T(8,128)(2,1)S(1)}, bf16[4,24,896]{2,1,0:T(8,128)(2,1)S(1)}, u32[]{:S(2)}, u32[]{:S(2)}) %collective-permute-start.6) | collective-permute-done | bytes 172064 | tf_op jit(solution)/shard_map/ppermute | solution.py:498
  79.9 5.9 %collective-permute-start.7 = (bf16[4,128,768]{2,1,0:T(8,128)(2,1)S(1)}, bf16[4,128,768]{2,1,0:T(8,128)(2,1)S(1)}, u32[]{:S(2)}, u32[]{:S(2)}) collective-permute-start(bf16[4,128,768]{2,1,0:T(8,128)(2,1)S(1)} %all-to-all-done.2.own_ref), channel_id=1, source_target_pairs={{0,32},{32,0},{1,33},{33,1},{2,34},{34,2},{3,35},{35,3},{4,36},{36... | collective-permute-start | bytes 2359304 | tf_op jit(solution)/shard_map/ppermute | solution.py:555
  91.0 5.2 %all-to-all-start.3 = ((bf16[8,64,768]{2,1,0:T(8,128)(2,1)}), bf16[8,64,768]{2,1,0:T(8,128)(2,1)S(1)}, u32[]{:S(2)}, u32[]{:S(2)}) async-start(bf16[8,64,768]{2,1,0:T(8,128)(2,1)} %get-tuple-element.63), calls=%async_computation.3 | async-start | bytes 1572864 | tf_op jit(solution)/shard_map/all_to_all | solution.py:559
  102.5 3.4 %collective-permute-start.8 = (bf16[8,24,768]{2,1,0:T(8,128)(2,1)S(1)}, bf16[8,24,768]{2,1,0:T(8,128)(2,1)S(1)}, u32[]{:S(2)}, u32[]{:S(2)}) collective-permute-start(bf16[8,24,768]{2,1,0:T(8,128)(2,1)S(1)} %bitcast.22), channel_id=1, source_target_pairs={{0,1},{1,2},{2,3},{3,0},{4,5},{5,6},{6,7},{7,4},{8,9},{9,10},{10,1... | collective-permute-start | bytes 884744 | tf_op jit(solution)/shard_map/ppermute | solution.py:505
  109.8 10.7 %all-to-all-start.4 = ((bf16[32,16,128]{2,1,0:T(8,128)(2,1)}), bf16[32,16,128]{2,1,0:T(8,128)(2,1)S(1)}, u32[]{:S(2)}, u32[]{:S(2)}) async-start(bf16[32,16,128]{2,1,0:T(8,128)(2,1)} %shard_map.201), calls=%async_computation.4 | async-start | bytes 262144 | tf_op jit(solution)/shard_map/all_to_all | solution.py:482
  121.7 3.1 %collective-permute-start.11 = (bf16[4,24,768]{2,1,0:T(8,128)(2,1)S(1)}, bf16[4,24,768]{2,1,0:T(8,128)(2,1)S(1)}, u32[]{:S(2)}, u32[]{:S(2)}) collective-permute-start(bf16[4,24,768]{2,1,0:T(8,128)(2,1)S(1)} %slice.101), channel_id=1, source_target_pairs={{0,4},{4,0},{1,5},{5,1},{2,6},{6,2},{3,7},{7,3},{8,12},{12,8},{9,1... | collective-permute-start | bytes 442376 | tf_op jit(solution)/shard_map/ppermute | solution.py:468
  124.8 3.8 %collective-permute-done.11 = bf16[4,24,768]{2,1,0:T(8,128)(2,1)S(1)} collective-permute-done((bf16[4,24,768]{2,1,0:T(8,128)(2,1)S(1)}, bf16[4,24,768]{2,1,0:T(8,128)(2,1)S(1)}, u32[]{:S(2)}, u32[]{:S(2)}) %collective-permute-start.11) | collective-permute-done | bytes 147488 | tf_op jit(solution)/shard_map/ppermute | solution.py:468
  129.3 3.3 %all-to-all-done.4.recv_ref = bf16[32,16,128]{2,1,0:T(8,128)(2,1)S(1)} async-done(((bf16[32,16,128]{2,1,0:T(8,128)(2,1)}), bf16[32,16,128]{2,1,0:T(8,128)(2,1)S(1)}, u32[]{:S(2)}, u32[]{:S(2)}) %all-to-all-start.4) | async-done | bytes 131104 | tf_op jit(solution)/shard_map/all_to_all | solution.py:482
  132.8 5.5 %all-to-all-start.5 = ((bf16[4,24,768]{2,1,0:T(8,128)(2,1)}), bf16[4,24,768]{2,1,0:T(8,128)(2,1)S(1)}, u32[]{:S(2)}, u32[]{:S(2)}) async-start(bf16[4,24,768]{2,1,0:T(8,128)(2,1)} %fusion.2), calls=%async_computation.5 | async-start | bytes 294912 | tf_op jit(solution)/shard_map/all_to_all | solution.py:568
  138.4 4.7 %collective-permute-start.13 = (bf16[24,3,256]{2,1,0:T(4,128)(2,1)S(1)}, bf16[24,3,256]{2,1,0:T(4,128)(2,1)S(1)}, u32[]{:S(2)}, u32[]{:S(2)}) collective-permute-start(bf16[24,3,256]{2,1,0:T(4,128)(2,1)S(1)} %get-tuple-element.99), channel_id=1, source_target_pairs={{32,64},{96,128},{160,192},{224,256},{288,320},{352,384},{416,448}... | collective-permute-start | bytes 110600 | tf_op jit(solution)/shard_map/ppermute | solution.py:492
  148.5 11.4 %collective-permute-start.12 = (bf16[24,896]{1,0:T(8,128)(2,1)S(1)}, bf16[24,896]{1,0:T(8,128)(2,1)S(1)}, u32[]{:S(2)}, u32[]{:S(2)}) collective-permute-start(bf16[24,896]{1,0:T(8,128)(2,1)S(1)} %pad_maximum_fusion), channel_id=1, source_target_pairs={{0,256},{256,0},{1,257},{257,1},{2,258},{258,2},{3,259},{259,3},{4... | collective-permute-start | bytes 129032 | tf_op jit(solution)/shard_map/ppermute | solution.py:576
  163.2 10.1 %all-to-all-start.6 = ((bf16[8,24,896]{2,1,0:T(8,128)(2,1)}), bf16[8,24,896]{2,1,0:T(8,128)(2,1)S(1)}, u32[]{:S(2)}, u32[]{:S(2)}) async-start(bf16[8,24,896]{2,1,0:T(8,128)(2,1)} %broadcast_in_dim.37), calls=%async_computation.6 | async-start | bytes 688128 | tf_op jit(solution)/shard_map/all_to_all | solution.py:478
  173.3 3.4 %shard_map.204 = f32[24,8,256]{2,1,0:T(8,128)} custom-call(f32[24,50]{1,0:T(8,128)S(1)} %pad_maximum_fusion.2.taps_ref, f32[24,8,256]{2,1,0:T(8,128)S(1)} %get-tuple-element.73.dconv_ref.x_ref, bf16[24,3,256]{2,1,0:T(4,128)(2,1)S(1)} %get-tuple-element.78.up_ref, bf16[24,3,256]{2,1,0:T(4,128)(2,1)S(1)} %get-tuple-element.79.down_ref, ...), custom_call_target="tpu_custom_call" | custom-call | tf_op jit(solution)/shard_map/pallas_call | solution.py:267
  176.7 3.8 %all-to-all-done.6.gathered_ref = bf16[8,24,896]{2,1,0:T(8,128)(2,1)S(1)} async-done(((bf16[8,24,896]{2,1,0:T(8,128)(2,1)}), bf16[8,24,896]{2,1,0:T(8,128)(2,1)S(1)}, u32[]{:S(2)}, u32[]{:S(2)}) %all-to-all-start.6) | async-done | bytes 344096 | tf_op jit(solution)/shard_map/all_to_all | solution.py:478
  (82 shorter events, 40.7 us)
Async XLA Ops:
  3.0 47.9 %copy-start.6 = (f32[768]{0:T(1024)S(1)}, f32[768]{0:T(1024)}, u32[]{:S(2)}) copy-start(f32[768]{0:T(1024)} %param.17) | copy-start | bytes 9220
  3.0 47.9 %copy-start.7 = (f32[768]{0:T(1024)S(1)}, f32[768]{0:T(1024)}, u32[]{:S(2)}) copy-start(f32[768]{0:T(1024)} %param.18) | copy-start | bytes 9220
  3.0 21.0 %all-to-all-start = ((bf16[4,24,896]{2,1,0:T(8,128)(2,1)}), bf16[4,24,896]{2,1,0:T(8,128)(2,1)S(1)}, u32[]{:S(2)}, u32[]{:S(2)}) async-start(bf16[4,24,896]{2,1,0:T(8,128)(2,1)} %shard_map.196), calls=%async_computation | async-start | bytes 344064 | tf_op jit(solution)/shard_map/all_to_all | solution.py:537
  15.9 13.1 %collective-permute-start = (bf16[24,3,256]{2,1,0:T(4,128)(2,1)S(1)}, bf16[24,3,256]{2,1,0:T(4,128)(2,1)S(1)}, u32[]{:S(2)}, u32[]{:S(2)}) collective-permute-start(bf16[24,3,256]{2,1,0:T(4,128)(2,1)S(1)} %get-tuple-element.105), channel_id=1, source_target_pairs={{32,64},{96,128},{160,192},{224,256},{288,320},{352,384},{416,448}... | collective-permute-start | bytes 110600 | tf_op jit(solution)/shard_map/ppermute | solution.py:492
  19.9 9.1 %collective-permute-start.1 = (bf16[24,3,256]{2,1,0:T(4,128)(2,1)S(1)}, bf16[24,3,256]{2,1,0:T(4,128)(2,1)S(1)}, u32[]{:S(2)}, u32[]{:S(2)}) collective-permute-start(bf16[24,3,256]{2,1,0:T(4,128)(2,1)S(1)} %get-tuple-element.104), channel_id=1, source_target_pairs={{0,32},{64,96},{128,160},{192,224},{256,288},{320,352},{384,416},{... | collective-permute-start | bytes 110600 | tf_op jit(solution)/shard_map/ppermute | solution.py:490
  24.0 8.6 %collective-permute-start.2 = (bf16[4,24,896]{2,1,0:T(8,128)(2,1)S(1)}, bf16[4,24,896]{2,1,0:T(8,128)(2,1)S(1)}, u32[]{:S(2)}, u32[]{:S(2)}) collective-permute-start(bf16[4,24,896]{2,1,0:T(8,128)(2,1)S(1)} %all-to-all-done), channel_id=1, source_target_pairs={{0,4},{4,0},{1,5},{5,1},{2,6},{6,2},{3,7},{7,3},{8,12},{12,8},{9,1... | collective-permute-start | bytes 516104 | tf_op jit(solution)/shard_map/ppermute | solution.py:538
  32.6 28.0 %all-to-all-start.1 = ((bf16[32,24,128]{2,1,0:T(8,128)(2,1)}), bf16[32,24,128]{2,1,0:T(8,128)(2,1)S(1)}, u32[]{:S(2)}, u32[]{:S(2)}) async-start(bf16[32,24,128]{2,1,0:T(8,128)(2,1)} %shard_map.195), calls=%async_computation.1 | async-start | bytes 393216 | tf_op jit(solution)/shard_map/all_to_all | solution.py:482
  44.6 11.6 %collective-permute-start.3 = (bf16[8,24,896]{2,1,0:T(8,128)(2,1)S(1)}, bf16[8,24,896]{2,1,0:T(8,128)(2,1)S(1)}, u32[]{:S(2)}, u32[]{:S(2)}) collective-permute-start(bf16[8,24,896]{2,1,0:T(8,128)(2,1)S(1)} %constant_dynamic-update-slice_fusion.own_ref), channel_id=1, source_target_pairs={{1,0},{2,1},{3,2},{0,3},{5,4},{6,5},{7,6},{4,7},{9,8},{10,9},{11,1... | collective-permute-start | bytes 1032200 | tf_op jit(solution)/shard_map/ppermute | solution.py:498
  49.0 11.7 %collective-permute-start.4 = (bf16[8,24,896]{2,1,0:T(8,128)(2,1)S(1)}, bf16[8,24,896]{2,1,0:T(8,128)(2,1)S(1)}, u32[]{:S(2)}, u32[]{:S(2)}) collective-permute-start(bf16[8,24,896]{2,1,0:T(8,128)(2,1)S(1)} %constant_dynamic-update-slice_fusion.own_ref), channel_id=1, source_target_pairs={{3,0},{0,1},{1,2},{2,3},{7,4},{4,5},{5,6},{6,7},{11,8},{8,9},{9,10... | collective-permute-start | bytes 1032200 | tf_op jit(solution)/shard_map/ppermute | solution.py:498
  61.8 18.1 %all-to-all-start.2 = ((bf16[4,128,768]{2,1,0:T(8,128)(2,1)}), bf16[4,128,768]{2,1,0:T(8,128)(2,1)S(1)}, u32[]{:S(2)}, u32[]{:S(2)}) async-start(bf16[4,128,768]{2,1,0:T(8,128)(2,1)} %get-tuple-element.54), calls=%async_computation.2 | async-start | bytes 1572864 | tf_op jit(solution)/shard_map/all_to_all | solution.py:551
  70.3 6.2 %collective-permute-start.5 = (bf16[4,24,896]{2,1,0:T(8,128)(2,1)S(1)}, bf16[4,24,896]{2,1,0:T(8,128)(2,1)S(1)}, u32[]{:S(2)}, u32[]{:S(2)}) collective-permute-start(bf16[4,24,896]{2,1,0:T(8,128)(2,1)S(1)} %slice.55), channel_id=1, source_target_pairs={{1,0},{2,1},{3,2},{0,3},{5,4},{6,5},{7,6},{4,7},{9,8},{10,9},{11,1... | collective-permute-start | bytes 516104 | tf_op jit(solution)/shard_map/ppermute | solution.py:498
  72.3 7.7 %collective-permute-start.6 = (bf16[4,24,896]{2,1,0:T(8,128)(2,1)S(1)}, bf16[4,24,896]{2,1,0:T(8,128)(2,1)S(1)}, u32[]{:S(2)}, u32[]{:S(2)}) collective-permute-start(bf16[4,24,896]{2,1,0:T(8,128)(2,1)S(1)} %slice.56), channel_id=1, source_target_pairs={{3,0},{0,1},{1,2},{2,3},{7,4},{4,5},{5,6},{6,7},{11,8},{8,9},{9,10... | collective-permute-start | bytes 516104 | tf_op jit(solution)/shard_map/ppermute | solution.py:498
  79.9 7.8 %collective-permute-start.7 = (bf16[4,128,768]{2,1,0:T(8,128)(2,1)S(1)}, bf16[4,128,768]{2,1,0:T(8,128)(2,1)S(1)}, u32[]{:S(2)}, u32[]{:S(2)}) collective-permute-start(bf16[4,128,768]{2,1,0:T(8,128)(2,1)S(1)} %all-to-all-done.2.own_ref), channel_id=1, source_target_pairs={{0,32},{32,0},{1,33},{33,1},{2,34},{34,2},{3,35},{35,3},{4,36},{36... | collective-permute-start | bytes 2359304 | tf_op jit(solution)/shard_map/ppermute | solution.py:555
  91.0 17.6 %all-to-all-start.3 = ((bf16[8,64,768]{2,1,0:T(8,128)(2,1)}), bf16[8,64,768]{2,1,0:T(8,128)(2,1)S(1)}, u32[]{:S(2)}, u32[]{:S(2)}) async-start(bf16[8,64,768]{2,1,0:T(8,128)(2,1)} %get-tuple-element.63), calls=%async_computation.3 | async-start | bytes 1572864 | tf_op jit(solution)/shard_map/all_to_all | solution.py:559
  100.5 20.0 %collective-permute-start.10 = (bf16[8,24,768]{2,1,0:T(8,128)(2,1)S(1)}, bf16[8,24,768]{2,1,0:T(8,128)(2,1)S(1)}, u32[]{:S(2)}, u32[]{:S(2)}) collective-permute-start(bf16[8,24,768]{2,1,0:T(8,128)(2,1)S(1)} %bitcast.23), channel_id=1, source_target_pairs={{0,3},{1,0},{2,1},{3,2},{4,7},{5,4},{6,5},{7,6},{8,11},{9,8},{10,9... | collective-permute-start | bytes 884744 | tf_op jit(solution)/shard_map/ppermute | solution.py:505
  102.5 18.0 %collective-permute-start.8 = (bf16[8,24,768]{2,1,0:T(8,128)(2,1)S(1)}, bf16[8,24,768]{2,1,0:T(8,128)(2,1)S(1)}, u32[]{:S(2)}, u32[]{:S(2)}) collective-permute-start(bf16[8,24,768]{2,1,0:T(8,128)(2,1)S(1)} %bitcast.22), channel_id=1, source_target_pairs={{0,1},{1,2},{2,3},{3,0},{4,5},{5,6},{6,7},{7,4},{8,9},{9,10},{10,1... | collective-permute-start | bytes 884744 | tf_op jit(solution)/shard_map/ppermute | solution.py:505
  105.8 14.7 %collective-permute-start.9 = (bf16[8,24,768]{2,1,0:T(8,128)(2,1)S(1)}, bf16[8,24,768]{2,1,0:T(8,128)(2,1)}, u32[]{:S(2)}, u32[]{:S(2)}) collective-permute-start(bf16[8,24,768]{2,1,0:T(8,128)(2,1)S(1)} %bitcast.21), channel_id=1, source_target_pairs={{0,2},{1,3},{2,0},{3,1},{4,6},{5,7},{6,4},{7,5},{8,10},{9,11},{10,... | collective-permute-start | bytes 884744 | tf_op jit(solution)/shard_map/ppermute | solution.py:505
  109.8 22.8 %all-to-all-start.4 = ((bf16[32,16,128]{2,1,0:T(8,128)(2,1)}), bf16[32,16,128]{2,1,0:T(8,128)(2,1)S(1)}, u32[]{:S(2)}, u32[]{:S(2)}) async-start(bf16[32,16,128]{2,1,0:T(8,128)(2,1)} %shard_map.201), calls=%async_computation.4 | async-start | bytes 262144 | tf_op jit(solution)/shard_map/all_to_all | solution.py:482
  121.7 7.0 %collective-permute-start.11 = (bf16[4,24,768]{2,1,0:T(8,128)(2,1)S(1)}, bf16[4,24,768]{2,1,0:T(8,128)(2,1)S(1)}, u32[]{:S(2)}, u32[]{:S(2)}) collective-permute-start(bf16[4,24,768]{2,1,0:T(8,128)(2,1)S(1)} %slice.101), channel_id=1, source_target_pairs={{0,4},{4,0},{1,5},{5,1},{2,6},{6,2},{3,7},{7,3},{8,12},{12,8},{9,1... | collective-permute-start | bytes 442376 | tf_op jit(solution)/shard_map/ppermute | solution.py:468
  132.8 15.5 %all-to-all-start.5 = ((bf16[4,24,768]{2,1,0:T(8,128)(2,1)}), bf16[4,24,768]{2,1,0:T(8,128)(2,1)S(1)}, u32[]{:S(2)}, u32[]{:S(2)}) async-start(bf16[4,24,768]{2,1,0:T(8,128)(2,1)} %fusion.2), calls=%async_computation.5 | async-start | bytes 294912 | tf_op jit(solution)/shard_map/all_to_all | solution.py:568
  138.4 21.5 %collective-permute-start.13 = (bf16[24,3,256]{2,1,0:T(4,128)(2,1)S(1)}, bf16[24,3,256]{2,1,0:T(4,128)(2,1)S(1)}, u32[]{:S(2)}, u32[]{:S(2)}) collective-permute-start(bf16[24,3,256]{2,1,0:T(4,128)(2,1)S(1)} %get-tuple-element.99), channel_id=1, source_target_pairs={{32,64},{96,128},{160,192},{224,256},{288,320},{352,384},{416,448}... | collective-permute-start | bytes 110600 | tf_op jit(solution)/shard_map/ppermute | solution.py:492
  143.1 16.8 %collective-permute-start.14 = (bf16[24,3,256]{2,1,0:T(4,128)(2,1)S(1)}, bf16[24,3,256]{2,1,0:T(4,128)(2,1)S(1)}, u32[]{:S(2)}, u32[]{:S(2)}) collective-permute-start(bf16[24,3,256]{2,1,0:T(4,128)(2,1)S(1)} %get-tuple-element.98), channel_id=1, source_target_pairs={{0,32},{64,96},{128,160},{192,224},{256,288},{320,352},{384,416},{... | collective-permute-start | bytes 110600 | tf_op jit(solution)/shard_map/ppermute | solution.py:490
  148.5 13.8 %collective-permute-start.12 = (bf16[24,896]{1,0:T(8,128)(2,1)S(1)}, bf16[24,896]{1,0:T(8,128)(2,1)S(1)}, u32[]{:S(2)}, u32[]{:S(2)}) collective-permute-start(bf16[24,896]{1,0:T(8,128)(2,1)S(1)} %pad_maximum_fusion), channel_id=1, source_target_pairs={{0,256},{256,0},{1,257},{257,1},{2,258},{258,2},{3,259},{259,3},{4... | collective-permute-start | bytes 129032 | tf_op jit(solution)/shard_map/ppermute | solution.py:576
  163.2 17.3 %all-to-all-start.6 = ((bf16[8,24,896]{2,1,0:T(8,128)(2,1)}), bf16[8,24,896]{2,1,0:T(8,128)(2,1)S(1)}, u32[]{:S(2)}, u32[]{:S(2)}) async-start(bf16[8,24,896]{2,1,0:T(8,128)(2,1)} %broadcast_in_dim.37), calls=%async_computation.6 | async-start | bytes 688128 | tf_op jit(solution)/shard_map/all_to_all | solution.py:478
  (7 other events, 115.5 us)

commit v12 on v11

--- a/solution.py
+++ b/solution.py
@@ -482,6 +482,16 @@
     return lax.all_to_all(blocks, CHAN, 0, 0, tiled=True)
 
 
+def halo_swaps(first, last):
+    count = lax.axis_size(LAT)
+    even = lax.axis_index(LAT) % 2 == 0
+    pairs = [(i, i + 1) for i in range(0, count, 2)]
+    within = lax.ppermute(jnp.where(even, last, first), LAT, pairs + [(j, i) for i, j in pairs])
+    pairs = [(i, i + 1) for i in range(1, count - 1, 2)]
+    across = lax.ppermute(jnp.where(even, first, last), LAT, pairs + [(j, i) for i, j in pairs])
+    return within, across
+
+
 def halos(first, last):
     count = lax.axis_size(LAT)
     place = lax.axis_index(LAT)
@@ -569,16 +579,20 @@
     dws = jnp.sum(dws.astype(F32), 0)
     dconv, ends, dh_sums, extra = stencil_cotangent(payload, metric, cdev, width)
     taps = tap_sums(dconv, dh_sums, block_input, up, down, out_grad)
-    dup, ddown = halos(ends[0], ends[1])
 
     small = jnp.concatenate([jnp.sum(taps, 2), extra[:, :8]], 1)
     mine = jnp.concatenate([dws.astype(BF)] + list(two_parts(small)), 1)
-    other = lax.ppermute(mine, "zh", [(0, 1), (1, 0)]).astype(F32)
+    mine, ends = lax.optimization_barrier((mine, ends))
+    other = lax.ppermute(mine, "zh", [(0, 1), (1, 0)])
+    within, across = halo_swaps(ends[0], ends[1])
+    other, within, across = lax.optimization_barrier((other, within, across))
+    even = lax.axis_index(LAT) % 2 == 0
+    dup, ddown = jnp.where(even, across, within), jnp.where(even, within, across)
+    other = other.astype(F32)
     count = small.shape[1]
     dws = dws + other[:, :chans]
     small = small + other[:, chans : chans + count] + other[:, chans + count :]
     mine = jnp.concatenate([dws.astype(BF)] + list(two_parts(small)), 1)
-    mine, dup, ddown = lax.optimization_barrier((mine, dup, ddown))
     grad_input = spread_back(taps_bias, dconv, dup, ddown, out_grad)
     grad_w_in, grad_w_out, grad_kernel, db, *rest = results(
         part, kernel.shape[1], to_all(mine, ("x", "c")), chans, gamma_own, b_out

time: 183 us -> 192 us (1.049)
  waiting for transfers between devices: 28.4 us -> 34.8 us
  starting transfers between devices: 121 us -> 123 us
    all_to_all x1, waiting for transfers between devices: 0.7 us -> 7.22 us  [per_device(): dws = lax.all_to_all(dws, 'zq', 0, 0, tiled=True)]
    all_to_all x1, starting transfers between devices: 10.1 us -> 15.2 us  [to_all(): lax.all_to_all(jnp.broadcast_to(block[None], (count,) + block.shape), axi...]
    ppermute x2 -> x1, starting transfers between devices: 8.7 us -> 3.96 us  [halos(): lax.ppermute(jnp.where(even, first, last), LAT, pairs + [(j, i) for i, j...]
    ppermute x1 -> x3, starting transfers between devices: 11.4 us -> 14.8 us  [the longest x1 7.55 us: per_device(): other = lax.ppermute(mine, 'zh', [(0, 1), (1, 0)])]
    ppermute x2 -> x1, starting transfers between devices: 3.84 us -> 1.92 us  [halos(): lax.ppermute(jnp.where(even, last, first), LAT, pairs + [(j, i) for i, j...]
where the time goes in v12:
time: 192 us; the launch traced here: 190 us
  starting transfers between devices  123 us (64%)
  waiting for transfers between devices  34.8 us (18%)
  Pallas kernels  20.5 us (11%)
  local copies, waits for them, and re-layouts  6.01 us (3%)
  other arithmetic  4.43 us (2%)
    all_to_all x2, starting transfers between devices, exchange(): return lax.all_to_all(blocks, CHAN, 0, 0, tiled=True)  22.6 us
    all_to_all x1, starting transfers between devices, to_all(): lax.all_to_all(jnp.broadcast_to(block[None], (count,) + block.shape), axi...  15.2 us
    ppermute x4, waiting for transfers between devices, along_ring(): lax.ppermute(block, 'y', [((i + ahead) % count, i) for i in range(count)])  14 us
    all_to_all x1, starting transfers between devices, per_device(): shards = lax.all_to_all(slices(nz // 2, *cut), 'zq', 0, 0, tiled=True)  11.8 us
    ppermute x4, starting transfers between devices, along_ring(): lax.ppermute(block, 'y', [((i + ahead) % count, i) for i in range(count)])  11.6 us
    all_to_all x1, starting transfers between devices, per_device(): pair = lax.all_to_all(pair, 'x', 0, 0, tiled=True)  8.52 us
    ppermute x3, starting transfers between devices, to_ring(): lax.ppermute(blocks[k], 'y', [(i, (i + k) % count) for i in range(count)])  8.05 us
    ppermute x1, starting transfers between devices, per_device(): other = lax.ppermute(mine, 'zh', [(0, 1), (1, 0)])  7.55 us
  transfers between devices with their start and end apart: 22, of which 10 were waited for; matrix products, arithmetic and copies ran while one was open for 3% of the time, Pallas kernels for 8%

profile of v12, /device:TPU:1, one launch (start us, length us, event | category | flops | bytes accessed | tf_op | source)
XLA Modules:
  0.0 189.8 jit_solution(892286587764207893)
XLA Ops:
  3.0 11.8 %all-to-all-start = ((bf16[4,24,896]{2,1,0:T(8,128)(2,1)}), bf16[4,24,896]{2,1,0:T(8,128)(2,1)S(1)}, u32[]{:S(2)}, u32[]{:S(2)}) async-start(bf16[4,24,896]{2,1,0:T(8,128)(2,1)} %shard_map.196), calls=%async_computation | async-start | bytes 344064 | tf_op jit(solution)/shard_map/all_to_all | solution.py:547
  15.9 4.0 %collective-permute-start = (bf16[24,3,256]{2,1,0:T(4,128)(2,1)S(1)}, bf16[24,3,256]{2,1,0:T(4,128)(2,1)S(1)}, u32[]{:S(2)}, u32[]{:S(2)}) collective-permute-start(bf16[24,3,256]{2,1,0:T(4,128)(2,1)S(1)} %get-tuple-element.109), channel_id=1, source_target_pairs={{32,64},{96,128},{160,192},{224,256},{288,320},{352,384},{416,448}... | collective-permute-start | bytes 110600 | tf_op jit(solution)/shard_map/ppermute | solution.py:502
  24.0 4.9 %collective-permute-start.2 = (bf16[4,24,896]{2,1,0:T(8,128)(2,1)S(1)}, bf16[4,24,896]{2,1,0:T(8,128)(2,1)S(1)}, u32[]{:S(2)}, u32[]{:S(2)}) collective-permute-start(bf16[4,24,896]{2,1,0:T(8,128)(2,1)S(1)} %all-to-all-done), channel_id=1, source_target_pairs={{0,4},{4,0},{1,5},{5,1},{2,6},{6,2},{3,7},{7,3},{8,12},{12,8},{9,1... | collective-permute-start | bytes 516104 | tf_op jit(solution)/shard_map/ppermute | solution.py:548
  29.1 3.6 %shard_map.195 = bf16[32,24,128]{2,1,0:T(8,128)(2,1)} custom-call(f32[24,50]{1,0:T(8,128)S(1)} %pad_maximum_fusion.2.taps_ref, bf16[24,8,256]{2,1,0:T(8,128)(2,1)S(1)} %copy-done.2, bf16[24,3,256]{2,1,0:T(4,128)(2,1)S(1)} %get-tuple-element.107.up_ref, bf16[24,3,256]{2,1,0:T(4,128)(2,1)S(1)} %get-tuple-element.106.down_ref, f32[8,1]{1,0:T(8,128)S(1)} %copy.23.metric_ref, ...), custom_call_target="tpu_custom_call" | custom-call | tf_op jit(solution)/shard_map/pallas_call | solution.py:100
  32.6 11.9 %all-to-all-start.1 = ((bf16[32,24,128]{2,1,0:T(8,128)(2,1)}), bf16[32,24,128]{2,1,0:T(8,128)(2,1)S(1)}, u32[]{:S(2)}, u32[]{:S(2)}) async-start(bf16[32,24,128]{2,1,0:T(8,128)(2,1)} %shard_map.195), calls=%async_computation.1 | async-start | bytes 393216 | tf_op jit(solution)/shard_map/all_to_all | solution.py:482
  44.6 4.3 %collective-permute-start.3 = (bf16[8,24,896]{2,1,0:T(8,128)(2,1)S(1)}, bf16[8,24,896]{2,1,0:T(8,128)(2,1)S(1)}, u32[]{:S(2)}, u32[]{:S(2)}) collective-permute-start(bf16[8,24,896]{2,1,0:T(8,128)(2,1)S(1)} %constant_dynamic-update-slice_fusion.own_ref), channel_id=1, source_target_pairs={{1,0},{2,1},{3,2},{0,3},{5,4},{6,5},{7,6},{4,7},{9,8},{10,9},{11,1... | collective-permute-start | bytes 1032200 | tf_op jit(solution)/shard_map/ppermute | solution.py:508
  50.9 5.2 %collective-permute-done.3.one_ref = bf16[8,24,896]{2,1,0:T(8,128)(2,1)S(1)} collective-permute-done((bf16[8,24,896]{2,1,0:T(8,128)(2,1)S(1)}, bf16[8,24,896]{2,1,0:T(8,128)(2,1)S(1)}, u32[]{:S(2)}, u32[]{:S(2)}) %collective-permute-start.3) | collective-permute-done | bytes 344096 | tf_op jit(solution)/shard_map/ppermute | solution.py:508
  56.2 4.5 %collective-permute-done.4.last_ref = bf16[8,24,896]{2,1,0:T(8,128)(2,1)S(1)} collective-permute-done((bf16[8,24,896]{2,1,0:T(8,128)(2,1)S(1)}, bf16[8,24,896]{2,1,0:T(8,128)(2,1)S(1)}, u32[]{:S(2)}, u32[]{:S(2)}) %collective-permute-start.4) | collective-permute-done | bytes 344096 | tf_op jit(solution)/shard_map/ppermute | solution.py:508
  61.8 8.5 %all-to-all-start.2 = ((bf16[4,128,768]{2,1,0:T(8,128)(2,1)}), bf16[4,128,768]{2,1,0:T(8,128)(2,1)S(1)}, u32[]{:S(2)}, u32[]{:S(2)}) async-start(bf16[4,128,768]{2,1,0:T(8,128)(2,1)} %get-tuple-element.56), calls=%async_computation.2 | async-start | bytes 1572864 | tf_op jit(solution)/shard_map/all_to_all | solution.py:561
  72.3 3.4 %collective-permute-start.6 = (bf16[4,24,896]{2,1,0:T(8,128)(2,1)S(1)}, bf16[4,24,896]{2,1,0:T(8,128)(2,1)S(1)}, u32[]{:S(2)}, u32[]{:S(2)}) collective-permute-start(bf16[4,24,896]{2,1,0:T(8,128)(2,1)S(1)} %slice.56), channel_id=1, source_target_pairs={{3,0},{0,1},{1,2},{2,3},{7,4},{4,5},{5,6},{6,7},{11,8},{8,9},{9,10... | collective-permute-start | bytes 516104 | tf_op jit(solution)/shard_map/ppermute | solution.py:508
  76.5 3.5 %collective-permute-done.6.high_ref = bf16[4,24,896]{2,1,0:T(8,128)(2,1)S(1)} collective-permute-done((bf16[4,24,896]{2,1,0:T(8,128)(2,1)S(1)}, bf16[4,24,896]{2,1,0:T(8,128)(2,1)S(1)}, u32[]{:S(2)}, u32[]{:S(2)}) %collective-permute-start.6) | collective-permute-done | bytes 172064 | tf_op jit(solution)/shard_map/ppermute | solution.py:508
  79.9 5.9 %collective-permute-start.7 = (bf16[4,128,768]{2,1,0:T(8,128)(2,1)S(1)}, bf16[4,128,768]{2,1,0:T(8,128)(2,1)S(1)}, u32[]{:S(2)}, u32[]{:S(2)}) collective-permute-start(bf16[4,128,768]{2,1,0:T(8,128)(2,1)S(1)} %all-to-all-done.2.own_ref), channel_id=1, source_target_pairs={{0,32},{32,0},{1,33},{33,1},{2,34},{34,2},{3,35},{35,3},{4,36},{36... | collective-permute-start | bytes 2359304 | tf_op jit(solution)/shard_map/ppermute | solution.py:565
  91.0 5.2 %all-to-all-start.3 = ((bf16[8,64,768]{2,1,0:T(8,128)(2,1)}), bf16[8,64,768]{2,1,0:T(8,128)(2,1)S(1)}, u32[]{:S(2)}, u32[]{:S(2)}) async-start(bf16[8,64,768]{2,1,0:T(8,128)(2,1)} %get-tuple-element.65), calls=%async_computation.3 | async-start | bytes 1572864 | tf_op jit(solution)/shard_map/all_to_all | solution.py:569
  102.5 3.4 %collective-permute-start.8 = (bf16[8,24,768]{2,1,0:T(8,128)(2,1)S(1)}, bf16[8,24,768]{2,1,0:T(8,128)(2,1)S(1)}, u32[]{:S(2)}, u32[]{:S(2)}) collective-permute-start(bf16[8,24,768]{2,1,0:T(8,128)(2,1)S(1)} %bitcast.22), channel_id=1, source_target_pairs={{0,1},{1,2},{2,3},{3,0},{4,5},{5,6},{6,7},{7,4},{8,9},{9,10},{10,1... | collective-permute-start | bytes 884744 | tf_op jit(solution)/shard_map/ppermute | solution.py:515
  109.8 10.7 %all-to-all-start.4 = ((bf16[32,16,128]{2,1,0:T(8,128)(2,1)}), bf16[32,16,128]{2,1,0:T(8,128)(2,1)S(1)}, u32[]{:S(2)}, u32[]{:S(2)}) async-start(bf16[32,16,128]{2,1,0:T(8,128)(2,1)} %shard_map.201), calls=%async_computation.4 | async-start | bytes 262144 | tf_op jit(solution)/shard_map/all_to_all | solution.py:482
  124.8 3.8 %collective-permute-done.11 = bf16[4,24,768]{2,1,0:T(8,128)(2,1)S(1)} collective-permute-done((bf16[4,24,768]{2,1,0:T(8,128)(2,1)S(1)}, bf16[4,24,768]{2,1,0:T(8,128)(2,1)S(1)}, u32[]{:S(2)}, u32[]{:S(2)}) %collective-permute-start.11) | collective-permute-done | bytes 147488 | tf_op jit(solution)/shard_map/ppermute | solution.py:468
  129.3 3.3 %all-to-all-done.4.recv_ref = bf16[32,16,128]{2,1,0:T(8,128)(2,1)S(1)} async-done(((bf16[32,16,128]{2,1,0:T(8,128)(2,1)}), bf16[32,16,128]{2,1,0:T(8,128)(2,1)S(1)}, u32[]{:S(2)}, u32[]{:S(2)}) %all-to-all-start.4) | async-done | bytes 131104 | tf_op jit(solution)/shard_map/all_to_all | solution.py:482
  132.6 5.5 %all-to-all-start.5 = ((bf16[4,24,768]{2,1,0:T(8,128)(2,1)}), bf16[4,24,768]{2,1,0:T(8,128)(2,1)S(1)}, u32[]{:S(2)}, u32[]{:S(2)}) async-start(bf16[4,24,768]{2,1,0:T(8,128)(2,1)} %fusion.2), calls=%async_computation.5 | async-start | bytes 294912 | tf_op jit(solution)/shard_map/all_to_all | solution.py:578
  140.9 7.2 %all-to-all-done.5 = bf16[4,24,768]{2,1,0:T(8,128)(2,1)S(1)} async-done(((bf16[4,24,768]{2,1,0:T(8,128)(2,1)}), bf16[4,24,768]{2,1,0:T(8,128)(2,1)S(1)}, u32[]{:S(2)}, u32[]{:S(2)}) %all-to-all-start.5) | async-done | bytes 147488 | tf_op jit(solution)/shard_map/all_to_all | solution.py:578
  148.3 7.6 %collective-permute-start.12 = (bf16[24,896]{1,0:T(8,128)(2,1)S(1)}, bf16[24,896]{1,0:T(8,128)(2,1)S(1)}, u32[]{:S(2)}, u32[]{:S(2)}) collective-permute-start(bf16[24,896]{1,0:T(8,128)(2,1)S(1)} %pad_maximum_fusion), channel_id=1, source_target_pairs={{0,256},{256,0},{1,257},{257,1},{2,258},{258,2},{3,259},{259,3},{4... | collective-permute-start | bytes 129032 | tf_op jit(solution)/shard_map/ppermute | solution.py:586
  155.9 4.0 %collective-permute-start.13 = (bf16[24,3,256]{2,1,0:T(4,128)(2,1)S(1)}, bf16[24,3,256]{2,1,0:T(4,128)(2,1)S(1)}, u32[]{:S(2)}, u32[]{:S(2)}) collective-permute-start(bf16[24,3,256]{2,1,0:T(4,128)(2,1)S(1)} %get-tuple-element.105), channel_id=1, source_target_pairs={{0,32},{64,96},{128,160},{192,224},{256,288},{320,352},{384,416},{... | collective-permute-start | bytes 110600 | tf_op jit(solution)/shard_map/ppermute | solution.py:489
  166.2 15.2 %all-to-all-start.6 = ((bf16[8,24,896]{2,1,0:T(8,128)(2,1)}), bf16[8,24,896]{2,1,0:T(8,128)(2,1)S(1)}, u32[]{:S(2)}, u32[]{:S(2)}) async-start(bf16[8,24,896]{2,1,0:T(8,128)(2,1)} %broadcast_in_dim.37), calls=%async_computation.6 | async-start | bytes 688128 | tf_op jit(solution)/shard_map/all_to_all | solution.py:478
  181.5 3.4 %shard_map.204 = f32[24,8,256]{2,1,0:T(8,128)} custom-call(f32[24,50]{1,0:T(8,128)S(1)} %pad_maximum_fusion.2.taps_ref, f32[24,8,256]{2,1,0:T(8,128)S(1)} %get-tuple-element.75.dconv_ref.x_ref, bf16[24,3,256]{2,1,0:T(4,128)(2,1)S(1)} %get-tuple-element.103.up_ref, bf16[24,3,256]{2,1,0:T(4,128)(2,1)S(1)} %get-tuple-element.102.down_ref, ...), custom_call_target="tpu_custom_call" | custom-call | tf_op jit(solution)/shard_map/pallas_call | solution.py:267
  184.9 3.8 %all-to-all-done.6.gathered_ref = bf16[8,24,896]{2,1,0:T(8,128)(2,1)S(1)} async-done(((bf16[8,24,896]{2,1,0:T(8,128)(2,1)}), bf16[8,24,896]{2,1,0:T(8,128)(2,1)S(1)}, u32[]{:S(2)}, u32[]{:S(2)}) %all-to-all-start.6) | async-done | bytes 344096 | tf_op jit(solution)/shard_map/all_to_all | solution.py:478
  (82 shorter events, 44.3 us)
Async XLA Ops:
  3.0 47.9 %copy-start.6 = (f32[768]{0:T(1024)S(1)}, f32[768]{0:T(1024)}, u32[]{:S(2)}) copy-start(f32[768]{0:T(1024)} %param.17) | copy-start | bytes 9220
  3.0 47.9 %copy-start.7 = (f32[768]{0:T(1024)S(1)}, f32[768]{0:T(1024)}, u32[]{:S(2)}) copy-start(f32[768]{0:T(1024)} %param.18) | copy-start | bytes 9220
  3.0 21.0 %all-to-all-start = ((bf16[4,24,896]{2,1,0:T(8,128)(2,1)}), bf16[4,24,896]{2,1,0:T(8,128)(2,1)S(1)}, u32[]{:S(2)}, u32[]{:S(2)}) async-start(bf16[4,24,896]{2,1,0:T(8,128)(2,1)} %shard_map.196), calls=%async_computation | async-start | bytes 344064 | tf_op jit(solution)/shard_map/all_to_all | solution.py:547
  15.9 13.1 %collective-permute-start = (bf16[24,3,256]{2,1,0:T(4,128)(2,1)S(1)}, bf16[24,3,256]{2,1,0:T(4,128)(2,1)S(1)}, u32[]{:S(2)}, u32[]{:S(2)}) collective-permute-start(bf16[24,3,256]{2,1,0:T(4,128)(2,1)S(1)} %get-tuple-element.109), channel_id=1, source_target_pairs={{32,64},{96,128},{160,192},{224,256},{288,320},{352,384},{416,448}... | collective-permute-start | bytes 110600 | tf_op jit(solution)/shard_map/ppermute | solution.py:502
  19.9 9.1 %collective-permute-start.1 = (bf16[24,3,256]{2,1,0:T(4,128)(2,1)S(1)}, bf16[24,3,256]{2,1,0:T(4,128)(2,1)S(1)}, u32[]{:S(2)}, u32[]{:S(2)}) collective-permute-start(bf16[24,3,256]{2,1,0:T(4,128)(2,1)S(1)} %get-tuple-element.108), channel_id=1, source_target_pairs={{0,32},{64,96},{128,160},{192,224},{256,288},{320,352},{384,416},{... | collective-permute-start | bytes 110600 | tf_op jit(solution)/shard_map/ppermute | solution.py:500
  24.0 8.6 %collective-permute-start.2 = (bf16[4,24,896]{2,1,0:T(8,128)(2,1)S(1)}, bf16[4,24,896]{2,1,0:T(8,128)(2,1)S(1)}, u32[]{:S(2)}, u32[]{:S(2)}) collective-permute-start(bf16[4,24,896]{2,1,0:T(8,128)(2,1)S(1)} %all-to-all-done), channel_id=1, source_target_pairs={{0,4},{4,0},{1,5},{5,1},{2,6},{6,2},{3,7},{7,3},{8,12},{12,8},{9,1... | collective-permute-start | bytes 516104 | tf_op jit(solution)/shard_map/ppermute | solution.py:548
  32.6 28.0 %all-to-all-start.1 = ((bf16[32,24,128]{2,1,0:T(8,128)(2,1)}), bf16[32,24,128]{2,1,0:T(8,128)(2,1)S(1)}, u32[]{:S(2)}, u32[]{:S(2)}) async-start(bf16[32,24,128]{2,1,0:T(8,128)(2,1)} %shard_map.195), calls=%async_computation.1 | async-start | bytes 393216 | tf_op jit(solution)/shard_map/all_to_all | solution.py:482
  44.6 11.6 %collective-permute-start.3 = (bf16[8,24,896]{2,1,0:T(8,128)(2,1)S(1)}, bf16[8,24,896]{2,1,0:T(8,128)(2,1)S(1)}, u32[]{:S(2)}, u32[]{:S(2)}) collective-permute-start(bf16[8,24,896]{2,1,0:T(8,128)(2,1)S(1)} %constant_dynamic-update-slice_fusion.own_ref), channel_id=1, source_target_pairs={{1,0},{2,1},{3,2},{0,3},{5,4},{6,5},{7,6},{4,7},{9,8},{10,9},{11,1... | collective-permute-start | bytes 1032200 | tf_op jit(solution)/shard_map/ppermute | solution.py:508
  49.0 11.7 %collective-permute-start.4 = (bf16[8,24,896]{2,1,0:T(8,128)(2,1)S(1)}, bf16[8,24,896]{2,1,0:T(8,128)(2,1)S(1)}, u32[]{:S(2)}, u32[]{:S(2)}) collective-permute-start(bf16[8,24,896]{2,1,0:T(8,128)(2,1)S(1)} %constant_dynamic-update-slice_fusion.own_ref), channel_id=1, source_target_pairs={{3,0},{0,1},{1,2},{2,3},{7,4},{4,5},{5,6},{6,7},{11,8},{8,9},{9,10... | collective-permute-start | bytes 1032200 | tf_op jit(solution)/shard_map/ppermute | solution.py:508
  61.8 18.1 %all-to-all-start.2 = ((bf16[4,128,768]{2,1,0:T(8,128)(2,1)}), bf16[4,128,768]{2,1,0:T(8,128)(2,1)S(1)}, u32[]{:S(2)}, u32[]{:S(2)}) async-start(bf16[4,128,768]{2,1,0:T(8,128)(2,1)} %get-tuple-element.56), calls=%async_computation.2 | async-start | bytes 1572864 | tf_op jit(solution)/shard_map/all_to_all | solution.py:561
  70.3 6.2 %collective-permute-start.5 = (bf16[4,24,896]{2,1,0:T(8,128)(2,1)S(1)}, bf16[4,24,896]{2,1,0:T(8,128)(2,1)S(1)}, u32[]{:S(2)}, u32[]{:S(2)}) collective-permute-start(bf16[4,24,896]{2,1,0:T(8,128)(2,1)S(1)} %slice.55), channel_id=1, source_target_pairs={{1,0},{2,1},{3,2},{0,3},{5,4},{6,5},{7,6},{4,7},{9,8},{10,9},{11,1... | collective-permute-start | bytes 516104 | tf_op jit(solution)/shard_map/ppermute | solution.py:508
  72.3 7.7 %collective-permute-start.6 = (bf16[4,24,896]{2,1,0:T(8,128)(2,1)S(1)}, bf16[4,24,896]{2,1,0:T(8,128)(2,1)S(1)}, u32[]{:S(2)}, u32[]{:S(2)}) collective-permute-start(bf16[4,24,896]{2,1,0:T(8,128)(2,1)S(1)} %slice.56), channel_id=1, source_target_pairs={{3,0},{0,1},{1,2},{2,3},{7,4},{4,5},{5,6},{6,7},{11,8},{8,9},{9,10... | collective-permute-start | bytes 516104 | tf_op jit(solution)/shard_map/ppermute | solution.py:508
  79.9 7.8 %collective-permute-start.7 = (bf16[4,128,768]{2,1,0:T(8,128)(2,1)S(1)}, bf16[4,128,768]{2,1,0:T(8,128)(2,1)S(1)}, u32[]{:S(2)}, u32[]{:S(2)}) collective-permute-start(bf16[4,128,768]{2,1,0:T(8,128)(2,1)S(1)} %all-to-all-done.2.own_ref), channel_id=1, source_target_pairs={{0,32},{32,0},{1,33},{33,1},{2,34},{34,2},{3,35},{35,3},{4,36},{36... | collective-permute-start | bytes 2359304 | tf_op jit(solution)/shard_map/ppermute | solution.py:565
  91.0 17.6 %all-to-all-start.3 = ((bf16[8,64,768]{2,1,0:T(8,128)(2,1)}), bf16[8,64,768]{2,1,0:T(8,128)(2,1)S(1)}, u32[]{:S(2)}, u32[]{:S(2)}) async-start(bf16[8,64,768]{2,1,0:T(8,128)(2,1)} %get-tuple-element.65), calls=%async_computation.3 | async-start | bytes 1572864 | tf_op jit(solution)/shard_map/all_to_all | solution.py:569
  100.5 20.0 %collective-permute-start.10 = (bf16[8,24,768]{2,1,0:T(8,128)(2,1)S(1)}, bf16[8,24,768]{2,1,0:T(8,128)(2,1)S(1)}, u32[]{:S(2)}, u32[]{:S(2)}) collective-permute-start(bf16[8,24,768]{2,1,0:T(8,128)(2,1)S(1)} %bitcast.23), channel_id=1, source_target_pairs={{0,3},{1,0},{2,1},{3,2},{4,7},{5,4},{6,5},{7,6},{8,11},{9,8},{10,9... | collective-permute-start | bytes 884744 | tf_op jit(solution)/shard_map/ppermute | solution.py:515
  102.5 18.0 %collective-permute-start.8 = (bf16[8,24,768]{2,1,0:T(8,128)(2,1)S(1)}, bf16[8,24,768]{2,1,0:T(8,128)(2,1)S(1)}, u32[]{:S(2)}, u32[]{:S(2)}) collective-permute-start(bf16[8,24,768]{2,1,0:T(8,128)(2,1)S(1)} %bitcast.22), channel_id=1, source_target_pairs={{0,1},{1,2},{2,3},{3,0},{4,5},{5,6},{6,7},{7,4},{8,9},{9,10},{10,1... | collective-permute-start | bytes 884744 | tf_op jit(solution)/shard_map/ppermute | solution.py:515
  105.8 14.7 %collective-permute-start.9 = (bf16[8,24,768]{2,1,0:T(8,128)(2,1)S(1)}, bf16[8,24,768]{2,1,0:T(8,128)(2,1)}, u32[]{:S(2)}, u32[]{:S(2)}) collective-permute-start(bf16[8,24,768]{2,1,0:T(8,128)(2,1)S(1)} %bitcast.21), channel_id=1, source_target_pairs={{0,2},{1,3},{2,0},{3,1},{4,6},{5,7},{6,4},{7,5},{8,10},{9,11},{10,... | collective-permute-start | bytes 884744 | tf_op jit(solution)/shard_map/ppermute | solution.py:515
  109.8 22.8 %all-to-all-start.4 = ((bf16[32,16,128]{2,1,0:T(8,128)(2,1)}), bf16[32,16,128]{2,1,0:T(8,128)(2,1)S(1)}, u32[]{:S(2)}, u32[]{:S(2)}) async-start(bf16[32,16,128]{2,1,0:T(8,128)(2,1)} %shard_map.201), calls=%async_computation.4 | async-start | bytes 262144 | tf_op jit(solution)/shard_map/all_to_all | solution.py:482
  121.7 7.0 %collective-permute-start.11 = (bf16[4,24,768]{2,1,0:T(8,128)(2,1)S(1)}, bf16[4,24,768]{2,1,0:T(8,128)(2,1)S(1)}, u32[]{:S(2)}, u32[]{:S(2)}) collective-permute-start(bf16[4,24,768]{2,1,0:T(8,128)(2,1)S(1)} %slice.101), channel_id=1, source_target_pairs={{0,4},{4,0},{1,5},{5,1},{2,6},{6,2},{3,7},{7,3},{8,12},{12,8},{9,1... | collective-permute-start | bytes 442376 | tf_op jit(solution)/shard_map/ppermute | solution.py:468
  132.6 15.5 %all-to-all-start.5 = ((bf16[4,24,768]{2,1,0:T(8,128)(2,1)}), bf16[4,24,768]{2,1,0:T(8,128)(2,1)S(1)}, u32[]{:S(2)}, u32[]{:S(2)}) async-start(bf16[4,24,768]{2,1,0:T(8,128)(2,1)} %fusion.2), calls=%async_computation.5 | async-start | bytes 294912 | tf_op jit(solution)/shard_map/all_to_all | solution.py:578
  148.3 17.0 %collective-permute-start.12 = (bf16[24,896]{1,0:T(8,128)(2,1)S(1)}, bf16[24,896]{1,0:T(8,128)(2,1)S(1)}, u32[]{:S(2)}, u32[]{:S(2)}) collective-permute-start(bf16[24,896]{1,0:T(8,128)(2,1)S(1)} %pad_maximum_fusion), channel_id=1, source_target_pairs={{0,256},{256,0},{1,257},{257,1},{2,258},{258,2},{3,259},{259,3},{4... | collective-permute-start | bytes 129032 | tf_op jit(solution)/shard_map/ppermute | solution.py:586
  155.9 7.3 %collective-permute-start.13 = (bf16[24,3,256]{2,1,0:T(4,128)(2,1)S(1)}, bf16[24,3,256]{2,1,0:T(4,128)(2,1)S(1)}, u32[]{:S(2)}, u32[]{:S(2)}) collective-permute-start(bf16[24,3,256]{2,1,0:T(4,128)(2,1)S(1)} %get-tuple-element.105), channel_id=1, source_target_pairs={{0,32},{64,96},{128,160},{192,224},{256,288},{320,352},{384,416},{... | collective-permute-start | bytes 110600 | tf_op jit(solution)/shard_map/ppermute | solution.py:489
  159.9 5.4 %collective-permute-start.14 = (bf16[24,3,256]{2,1,0:T(4,128)(2,1)S(1)}, bf16[24,3,256]{2,1,0:T(4,128)(2,1)S(1)}, u32[]{:S(2)}, u32[]{:S(2)}) collective-permute-start(bf16[24,3,256]{2,1,0:T(4,128)(2,1)S(1)} %get-tuple-element.104), channel_id=1, source_target_pairs={{32,64},{96,128},{160,192},{224,256},{288,320},{352,384},{416,448}... | collective-permute-start | bytes 110600 | tf_op jit(solution)/shard_map/ppermute | solution.py:491
  166.2 22.5 %all-to-all-start.6 = ((bf16[8,24,896]{2,1,0:T(8,128)(2,1)}), bf16[8,24,896]{2,1,0:T(8,128)(2,1)S(1)}, u32[]{:S(2)}, u32[]{:S(2)}) async-start(bf16[8,24,896]{2,1,0:T(8,128)(2,1)} %broadcast_in_dim.37), calls=%async_computation.6 | async-start | bytes 688128 | tf_op jit(solution)/shard_map/all_to_all | solution.py:478
  (7 other events, 112.3 us)

commit v13 on v11

--- a/solution.py
+++ b/solution.py
@@ -482,14 +482,20 @@
     return lax.all_to_all(blocks, CHAN, 0, 0, tiled=True)
 
 
-def halos(first, last):
-    count = lax.axis_size(LAT)
-    place = lax.axis_index(LAT)
-    even = place % 2 == 0
-    pairs = [(i, i + 1) for i in range(0, count, 2)]
-    within = lax.ppermute(jnp.where(even, last, first), LAT, pairs + [(j, i) for i, j in pairs])
-    pairs = [(i, i + 1) for i in range(1, count - 1, 2)]
-    across = lax.ppermute(jnp.where(even, first, last), LAT, pairs + [(j, i) for i, j in pairs])
+def swap_even(first, last):
+    even = lax.axis_index(LAT) % 2 == 0
+    pairs = [(i, i + 1) for i in range(0, lax.axis_size(LAT), 2)]
+    return lax.ppermute(jnp.where(even, last, first), LAT, pairs + [(j, i) for i, j in pairs])
+
+
+def swap_odd(first, last):
+    even = lax.axis_index(LAT) % 2 == 0
+    pairs = [(i, i + 1) for i in range(1, lax.axis_size(LAT) - 1, 2)]
+    return lax.ppermute(jnp.where(even, first, last), LAT, pairs + [(j, i) for i, j in pairs])
+
+
+def up_down(within, across):
+    even = lax.axis_index(LAT) % 2 == 0
     return jnp.where(even, across, within), jnp.where(even, within, across)
 
 
@@ -537,7 +543,8 @@
     shards = lax.all_to_all(slices(nz // 2, *cut), "zq", 0, 0, tiled=True)
     beside = lax.ppermute(shards, "zp", [(0, 1), (1, 0)])
 
-    up, down = halos(block_input[:, :3], block_input[:, rows - 3 :])
+    across = swap_odd(block_input[:, :3], block_input[:, rows - 3 :])
+    up, down = up_down(swap_even(block_input[:, :3], block_input[:, rows - 3 :]), across)
     taps_bias = jnp.concatenate([kernel, conv_bias[:, None]], 1)
     blocks = forward(taps_bias, block_input, up, down, metric, out_grad)
     blocks, shards, beside = lax.optimization_barrier((blocks, shards, beside))
@@ -569,16 +576,20 @@
     dws = jnp.sum(dws.astype(F32), 0)
     dconv, ends, dh_sums, extra = stencil_cotangent(payload, metric, cdev, width)
     taps = tap_sums(dconv, dh_sums, block_input, up, down, out_grad)
-    dup, ddown = halos(ends[0], ends[1])
+    across = swap_odd(ends[0], ends[1])
 
     small = jnp.concatenate([jnp.sum(taps, 2), extra[:, :8]], 1)
     mine = jnp.concatenate([dws.astype(BF)] + list(two_parts(small)), 1)
-    other = lax.ppermute(mine, "zh", [(0, 1), (1, 0)]).astype(F32)
+    mine, ends = lax.optimization_barrier((mine, ends))
+    other = lax.ppermute(mine, "zh", [(0, 1), (1, 0)])
+    within = swap_even(ends[0], ends[1])
+    other, within, across = lax.optimization_barrier((other, within, across))
+    other = other.astype(F32)
     count = small.shape[1]
     dws = dws + other[:, :chans]
     small = small + other[:, chans : chans + count] + other[:, chans + count :]
     mine = jnp.concatenate([dws.astype(BF)] + list(two_parts(small)), 1)
-    mine, dup, ddown = lax.optimization_barrier((mine, dup, ddown))
+    dup, ddown = up_down(within, across)
     grad_input = spread_back(taps_bias, dconv, dup, ddown, out_grad)
     grad_w_in, grad_w_out, grad_kernel, db, *rest = results(
         part, kernel.shape[1], to_all(mine, ("x", "c")), chans, gamma_own, b_out

time: 183 us -> 182 us (level)
  starting transfers between devices: 121 us -> 117 us
    all_to_all x1, starting transfers between devices: 10.1 us -> 8.03 us  [to_all(): lax.all_to_all(jnp.broadcast_to(block[None], (count,) + block.shape), axi...]
    all_to_all x1, waiting for transfers between devices: 0.7 us -> 2.65 us  [per_device(): dws = lax.all_to_all(dws, 'zq', 0, 0, tiled=True)]
  transfers between devices with their start and end apart: 22 -> 22, of which waited for: 10 -> 11; matrix products, arithmetic and copies ran while one was open for 3% -> 3% of each run, Pallas kernels for 8% -> 8%
where the time goes in v13:
time: 182 us; the launch traced here: 179 us
  starting transfers between devices  117 us (64%)
  waiting for transfers between devices  29.9 us (16%)
  Pallas kernels  20.5 us (11%)
  local copies, waits for them, and re-layouts  6.02 us (3%)
  other arithmetic  4.44 us (2%)
    all_to_all x2, starting transfers between devices, exchange(): return lax.all_to_all(blocks, CHAN, 0, 0, tiled=True)  22.6 us
    ppermute x4, waiting for transfers between devices, along_ring(): lax.ppermute(block, 'y', [((i + ahead) % count, i) for i in range(count)])  14 us
    all_to_all x1, starting transfers between devices, per_device(): shards = lax.all_to_all(slices(nz // 2, *cut), 'zq', 0, 0, tiled=True)  11.8 us
    ppermute x4, starting transfers between devices, along_ring(): lax.ppermute(block, 'y', [((i + ahead) % count, i) for i in range(count)])  11.6 us
    ppermute x2, starting transfers between devices, swap_odd(): lax.ppermute(jnp.where(even, first, last), LAT, pairs + [(j, i) for i, j...  8.7 us
    all_to_all x1, starting transfers between devices, per_device(): pair = lax.all_to_all(pair, 'x', 0, 0, tiled=True)  8.52 us
    ppermute x3, starting transfers between devices, to_ring(): lax.ppermute(blocks[k], 'y', [(i, (i + k) % count) for i in range(count)])  8.04 us
    all_to_all x1, starting transfers between devices, to_all(): lax.all_to_all(jnp.broadcast_to(block[None], (count,) + block.shape), axi...  8.03 us
  transfers between devices with their start and end apart: 22, of which 11 were waited for; matrix products, arithmetic and copies ran while one was open for 3% of the time, Pallas kernels for 8%

profile of v13, /device:TPU:1, one launch (start us, length us, event | category | flops | bytes accessed | tf_op | source)
XLA Modules:
  0.0 179.4 jit_solution(4455870880063024146)
XLA Ops:
  3.0 11.8 %all-to-all-start = ((bf16[4,24,896]{2,1,0:T(8,128)(2,1)}), bf16[4,24,896]{2,1,0:T(8,128)(2,1)S(1)}, u32[]{:S(2)}, u32[]{:S(2)}) async-start(bf16[4,24,896]{2,1,0:T(8,128)(2,1)} %shard_map.196), calls=%async_computation | async-start | bytes 344064 | tf_op jit(solution)/shard_map/all_to_all | solution.py:543
  15.9 4.0 %collective-permute-start = (bf16[24,3,256]{2,1,0:T(4,128)(2,1)S(1)}, bf16[24,3,256]{2,1,0:T(4,128)(2,1)S(1)}, u32[]{:S(2)}, u32[]{:S(2)}) collective-permute-start(bf16[24,3,256]{2,1,0:T(4,128)(2,1)S(1)} %get-tuple-element.107), channel_id=1, source_target_pairs={{32,64},{96,128},{160,192},{224,256},{288,320},{352,384},{416,448}... | collective-permute-start | bytes 110600 | tf_op jit(solution)/shard_map/ppermute | solution.py:494
  24.0 4.9 %collective-permute-start.2 = (bf16[4,24,896]{2,1,0:T(8,128)(2,1)S(1)}, bf16[4,24,896]{2,1,0:T(8,128)(2,1)S(1)}, u32[]{:S(2)}, u32[]{:S(2)}) collective-permute-start(bf16[4,24,896]{2,1,0:T(8,128)(2,1)S(1)} %all-to-all-done), channel_id=1, source_target_pairs={{0,4},{4,0},{1,5},{5,1},{2,6},{6,2},{3,7},{7,3},{8,12},{12,8},{9,1... | collective-permute-start | bytes 516104 | tf_op jit(solution)/shard_map/ppermute | solution.py:544
  29.1 3.6 %shard_map.195 = bf16[32,24,128]{2,1,0:T(8,128)(2,1)} custom-call(f32[24,50]{1,0:T(8,128)S(1)} %pad_maximum_fusion.2.taps_ref, bf16[24,8,256]{2,1,0:T(8,128)(2,1)S(1)} %copy-done.2, bf16[24,3,256]{2,1,0:T(4,128)(2,1)S(1)} %get-tuple-element.105.up_ref, bf16[24,3,256]{2,1,0:T(4,128)(2,1)S(1)} %get-tuple-element.104.down_ref, f32[8,1]{1,0:T(8,128)S(1)} %copy.23.metric_ref, ...), custom_call_target="tpu_custom_call" | custom-call | tf_op jit(solution)/shard_map/pallas_call | solution.py:100
  32.6 11.9 %all-to-all-start.1 = ((bf16[32,24,128]{2,1,0:T(8,128)(2,1)}), bf16[32,24,128]{2,1,0:T(8,128)(2,1)S(1)}, u32[]{:S(2)}, u32[]{:S(2)}) async-start(bf16[32,24,128]{2,1,0:T(8,128)(2,1)} %shard_map.195), calls=%async_computation.1 | async-start | bytes 393216 | tf_op jit(solution)/shard_map/all_to_all | solution.py:482
  44.6 4.3 %collective-permute-start.3 = (bf16[8,24,896]{2,1,0:T(8,128)(2,1)S(1)}, bf16[8,24,896]{2,1,0:T(8,128)(2,1)S(1)}, u32[]{:S(2)}, u32[]{:S(2)}) collective-permute-start(bf16[8,24,896]{2,1,0:T(8,128)(2,1)S(1)} %constant_dynamic-update-slice_fusion.own_ref), channel_id=1, source_target_pairs={{1,0},{2,1},{3,2},{0,3},{5,4},{6,5},{7,6},{4,7},{9,8},{10,9},{11,1... | collective-permute-start | bytes 1032200 | tf_op jit(solution)/shard_map/ppermute | solution.py:504
  50.9 5.2 %collective-permute-done.3.one_ref = bf16[8,24,896]{2,1,0:T(8,128)(2,1)S(1)} collective-permute-done((bf16[8,24,896]{2,1,0:T(8,128)(2,1)S(1)}, bf16[8,24,896]{2,1,0:T(8,128)(2,1)S(1)}, u32[]{:S(2)}, u32[]{:S(2)}) %collective-permute-start.3) | collective-permute-done | bytes 344096 | tf_op jit(solution)/shard_map/ppermute | solution.py:504
  56.2 4.5 %collective-permute-done.4.last_ref = bf16[8,24,896]{2,1,0:T(8,128)(2,1)S(1)} collective-permute-done((bf16[8,24,896]{2,1,0:T(8,128)(2,1)S(1)}, bf16[8,24,896]{2,1,0:T(8,128)(2,1)S(1)}, u32[]{:S(2)}, u32[]{:S(2)}) %collective-permute-start.4) | collective-permute-done | bytes 344096 | tf_op jit(solution)/shard_map/ppermute | solution.py:504
  61.8 8.5 %all-to-all-start.2 = ((bf16[4,128,768]{2,1,0:T(8,128)(2,1)}), bf16[4,128,768]{2,1,0:T(8,128)(2,1)S(1)}, u32[]{:S(2)}, u32[]{:S(2)}) async-start(bf16[4,128,768]{2,1,0:T(8,128)(2,1)} %get-tuple-element.56), calls=%async_computation.2 | async-start | bytes 1572864 | tf_op jit(solution)/shard_map/all_to_all | solution.py:558
  72.3 3.4 %collective-permute-start.6 = (bf16[4,24,896]{2,1,0:T(8,128)(2,1)S(1)}, bf16[4,24,896]{2,1,0:T(8,128)(2,1)S(1)}, u32[]{:S(2)}, u32[]{:S(2)}) collective-permute-start(bf16[4,24,896]{2,1,0:T(8,128)(2,1)S(1)} %slice.64), channel_id=1, source_target_pairs={{3,0},{0,1},{1,2},{2,3},{7,4},{4,5},{5,6},{6,7},{11,8},{8,9},{9,10... | collective-permute-start | bytes 516104 | tf_op jit(solution)/shard_map/ppermute | solution.py:504
  76.5 3.5 %collective-permute-done.6.high_ref = bf16[4,24,896]{2,1,0:T(8,128)(2,1)S(1)} collective-permute-done((bf16[4,24,896]{2,1,0:T(8,128)(2,1)S(1)}, bf16[4,24,896]{2,1,0:T(8,128)(2,1)S(1)}, u32[]{:S(2)}, u32[]{:S(2)}) %collective-permute-start.6) | collective-permute-done | bytes 172064 | tf_op jit(solution)/shard_map/ppermute | solution.py:504
  79.9 5.9 %collective-permute-start.7 = (bf16[4,128,768]{2,1,0:T(8,128)(2,1)S(1)}, bf16[4,128,768]{2,1,0:T(8,128)(2,1)S(1)}, u32[]{:S(2)}, u32[]{:S(2)}) collective-permute-start(bf16[4,128,768]{2,1,0:T(8,128)(2,1)S(1)} %all-to-all-done.2.own_ref), channel_id=1, source_target_pairs={{0,32},{32,0},{1,33},{33,1},{2,34},{34,2},{3,35},{35,3},{4,36},{36... | collective-permute-start | bytes 2359304 | tf_op jit(solution)/shard_map/ppermute | solution.py:562
  91.0 5.2 %all-to-all-start.3 = ((bf16[8,64,768]{2,1,0:T(8,128)(2,1)}), bf16[8,64,768]{2,1,0:T(8,128)(2,1)S(1)}, u32[]{:S(2)}, u32[]{:S(2)}) async-start(bf16[8,64,768]{2,1,0:T(8,128)(2,1)} %get-tuple-element.65), calls=%async_computation.3 | async-start | bytes 1572864 | tf_op jit(solution)/shard_map/all_to_all | solution.py:566
  102.5 3.4 %collective-permute-start.8 = (bf16[8,24,768]{2,1,0:T(8,128)(2,1)S(1)}, bf16[8,24,768]{2,1,0:T(8,128)(2,1)S(1)}, u32[]{:S(2)}, u32[]{:S(2)}) collective-permute-start(bf16[8,24,768]{2,1,0:T(8,128)(2,1)S(1)} %bitcast.22), channel_id=1, source_target_pairs={{0,1},{1,2},{2,3},{3,0},{4,5},{5,6},{6,7},{7,4},{8,9},{9,10},{10,1... | collective-permute-start | bytes 884744 | tf_op jit(solution)/shard_map/ppermute | solution.py:511
  109.8 10.7 %all-to-all-start.4 = ((bf16[32,16,128]{2,1,0:T(8,128)(2,1)}), bf16[32,16,128]{2,1,0:T(8,128)(2,1)S(1)}, u32[]{:S(2)}, u32[]{:S(2)}) async-start(bf16[32,16,128]{2,1,0:T(8,128)(2,1)} %shard_map.201), calls=%async_computation.4 | async-start | bytes 262144 | tf_op jit(solution)/shard_map/all_to_all | solution.py:482
  124.8 3.8 %collective-permute-done.11 = bf16[4,24,768]{2,1,0:T(8,128)(2,1)S(1)} collective-permute-done((bf16[4,24,768]{2,1,0:T(8,128)(2,1)S(1)}, bf16[4,24,768]{2,1,0:T(8,128)(2,1)S(1)}, u32[]{:S(2)}, u32[]{:S(2)}) %collective-permute-start.11) | collective-permute-done | bytes 147488 | tf_op jit(solution)/shard_map/ppermute | solution.py:468
  129.3 3.3 %all-to-all-done.4.recv_ref = bf16[32,16,128]{2,1,0:T(8,128)(2,1)S(1)} async-done(((bf16[32,16,128]{2,1,0:T(8,128)(2,1)}), bf16[32,16,128]{2,1,0:T(8,128)(2,1)S(1)}, u32[]{:S(2)}, u32[]{:S(2)}) %all-to-all-start.4) | async-done | bytes 131104 | tf_op jit(solution)/shard_map/all_to_all | solution.py:482
  132.8 5.5 %all-to-all-start.5 = ((bf16[4,24,768]{2,1,0:T(8,128)(2,1)}), bf16[4,24,768]{2,1,0:T(8,128)(2,1)S(1)}, u32[]{:S(2)}, u32[]{:S(2)}) async-start(bf16[4,24,768]{2,1,0:T(8,128)(2,1)} %fusion.2), calls=%async_computation.5 | async-start | bytes 294912 | tf_op jit(solution)/shard_map/all_to_all | solution.py:575
  138.4 4.7 %collective-permute-start.14 = (bf16[24,3,256]{2,1,0:T(4,128)(2,1)S(1)}, bf16[24,3,256]{2,1,0:T(4,128)(2,1)S(1)}, u32[]{:S(2)}, u32[]{:S(2)}) collective-permute-start(bf16[24,3,256]{2,1,0:T(4,128)(2,1)S(1)} %select_bitcast_fusion), channel_id=1, source_target_pairs={{32,64},{96,128},{160,192},{224,256},{288,320},{352,384},{416,448}... | collective-permute-start | bytes 110600 | tf_op jit(solution)/shard_map/ppermute | solution.py:494
  148.5 7.6 %collective-permute-start.12 = (bf16[24,896]{1,0:T(8,128)(2,1)S(1)}, bf16[24,896]{1,0:T(8,128)(2,1)S(1)}, u32[]{:S(2)}, u32[]{:S(2)}) collective-permute-start(bf16[24,896]{1,0:T(8,128)(2,1)S(1)} %pad_maximum_fusion), channel_id=1, source_target_pairs={{0,256},{256,0},{1,257},{257,1},{2,258},{258,2},{3,259},{259,3},{4... | collective-permute-start | bytes 129032 | tf_op jit(solution)/shard_map/ppermute | solution.py:584
  156.1 4.0 %collective-permute-start.13 = (bf16[24,3,256]{2,1,0:T(4,128)(2,1)S(1)}, bf16[24,3,256]{2,1,0:T(4,128)(2,1)S(1)}, u32[]{:S(2)}, u32[]{:S(2)}) collective-permute-start(bf16[24,3,256]{2,1,0:T(4,128)(2,1)S(1)} %select_bitcast_fusion.1), channel_id=1, source_target_pairs={{0,32},{64,96},{128,160},{192,224},{256,288},{320,352},{384,416},{... | collective-permute-start | bytes 110600 | tf_op jit(solution)/shard_map/ppermute | solution.py:488
  162.9 8.0 %all-to-all-start.6 = ((bf16[8,24,896]{2,1,0:T(8,128)(2,1)}), bf16[8,24,896]{2,1,0:T(8,128)(2,1)S(1)}, u32[]{:S(2)}, u32[]{:S(2)}) async-start(bf16[8,24,896]{2,1,0:T(8,128)(2,1)} %broadcast_in_dim.37), calls=%async_computation.6 | async-start | bytes 688128 | tf_op jit(solution)/shard_map/all_to_all | solution.py:478
  171.1 3.4 %shard_map.204 = f32[24,8,256]{2,1,0:T(8,128)} custom-call(f32[24,50]{1,0:T(8,128)S(1)} %pad_maximum_fusion.2.taps_ref, f32[24,8,256]{2,1,0:T(8,128)S(1)} %get-tuple-element.75.dconv_ref.x_ref, bf16[24,3,256]{2,1,0:T(4,128)(2,1)S(1)} %get-tuple-element.103.up_ref, bf16[24,3,256]{2,1,0:T(4,128)(2,1)S(1)} %get-tuple-element.102.down_ref, ...), custom_call_target="tpu_custom_call" | custom-call | tf_op jit(solution)/shard_map/pallas_call | solution.py:267
  174.5 3.8 %all-to-all-done.6.gathered_ref = bf16[8,24,896]{2,1,0:T(8,128)(2,1)S(1)} async-done(((bf16[8,24,896]{2,1,0:T(8,128)(2,1)}), bf16[8,24,896]{2,1,0:T(8,128)(2,1)S(1)}, u32[]{:S(2)}, u32[]{:S(2)}) %all-to-all-start.6) | async-done | bytes 344096 | tf_op jit(solution)/shard_map/all_to_all | solution.py:478
  (83 shorter events, 43.5 us)
Async XLA Ops:
  3.0 47.9 %copy-start.6 = (f32[768]{0:T(1024)S(1)}, f32[768]{0:T(1024)}, u32[]{:S(2)}) copy-start(f32[768]{0:T(1024)} %param.17) | copy-start | bytes 9220
  3.0 47.9 %copy-start.7 = (f32[768]{0:T(1024)S(1)}, f32[768]{0:T(1024)}, u32[]{:S(2)}) copy-start(f32[768]{0:T(1024)} %param.18) | copy-start | bytes 9220
  3.0 21.0 %all-to-all-start = ((bf16[4,24,896]{2,1,0:T(8,128)(2,1)}), bf16[4,24,896]{2,1,0:T(8,128)(2,1)S(1)}, u32[]{:S(2)}, u32[]{:S(2)}) async-start(bf16[4,24,896]{2,1,0:T(8,128)(2,1)} %shard_map.196), calls=%async_computation | async-start | bytes 344064 | tf_op jit(solution)/shard_map/all_to_all | solution.py:543
  15.9 13.1 %collective-permute-start = (bf16[24,3,256]{2,1,0:T(4,128)(2,1)S(1)}, bf16[24,3,256]{2,1,0:T(4,128)(2,1)S(1)}, u32[]{:S(2)}, u32[]{:S(2)}) collective-permute-start(bf16[24,3,256]{2,1,0:T(4,128)(2,1)S(1)} %get-tuple-element.107), channel_id=1, source_target_pairs={{32,64},{96,128},{160,192},{224,256},{288,320},{352,384},{416,448}... | collective-permute-start | bytes 110600 | tf_op jit(solution)/shard_map/ppermute | solution.py:494
  19.9 9.1 %collective-permute-start.1 = (bf16[24,3,256]{2,1,0:T(4,128)(2,1)S(1)}, bf16[24,3,256]{2,1,0:T(4,128)(2,1)S(1)}, u32[]{:S(2)}, u32[]{:S(2)}) collective-permute-start(bf16[24,3,256]{2,1,0:T(4,128)(2,1)S(1)} %get-tuple-element.106), channel_id=1, source_target_pairs={{0,32},{64,96},{128,160},{192,224},{256,288},{320,352},{384,416},{... | collective-permute-start | bytes 110600 | tf_op jit(solution)/shard_map/ppermute | solution.py:488
  24.0 8.6 %collective-permute-start.2 = (bf16[4,24,896]{2,1,0:T(8,128)(2,1)S(1)}, bf16[4,24,896]{2,1,0:T(8,128)(2,1)S(1)}, u32[]{:S(2)}, u32[]{:S(2)}) collective-permute-start(bf16[4,24,896]{2,1,0:T(8,128)(2,1)S(1)} %all-to-all-done), channel_id=1, source_target_pairs={{0,4},{4,0},{1,5},{5,1},{2,6},{6,2},{3,7},{7,3},{8,12},{12,8},{9,1... | collective-permute-start | bytes 516104 | tf_op jit(solution)/shard_map/ppermute | solution.py:544
  32.6 28.0 %all-to-all-start.1 = ((bf16[32,24,128]{2,1,0:T(8,128)(2,1)}), bf16[32,24,128]{2,1,0:T(8,128)(2,1)S(1)}, u32[]{:S(2)}, u32[]{:S(2)}) async-start(bf16[32,24,128]{2,1,0:T(8,128)(2,1)} %shard_map.195), calls=%async_computation.1 | async-start | bytes 393216 | tf_op jit(solution)/shard_map/all_to_all | solution.py:482
  44.6 11.6 %collective-permute-start.3 = (bf16[8,24,896]{2,1,0:T(8,128)(2,1)S(1)}, bf16[8,24,896]{2,1,0:T(8,128)(2,1)S(1)}, u32[]{:S(2)}, u32[]{:S(2)}) collective-permute-start(bf16[8,24,896]{2,1,0:T(8,128)(2,1)S(1)} %constant_dynamic-update-slice_fusion.own_ref), channel_id=1, source_target_pairs={{1,0},{2,1},{3,2},{0,3},{5,4},{6,5},{7,6},{4,7},{9,8},{10,9},{11,1... | collective-permute-start | bytes 1032200 | tf_op jit(solution)/shard_map/ppermute | solution.py:504
  49.0 11.7 %collective-permute-start.4 = (bf16[8,24,896]{2,1,0:T(8,128)(2,1)S(1)}, bf16[8,24,896]{2,1,0:T(8,128)(2,1)S(1)}, u32[]{:S(2)}, u32[]{:S(2)}) collective-permute-start(bf16[8,24,896]{2,1,0:T(8,128)(2,1)S(1)} %constant_dynamic-update-slice_fusion.own_ref), channel_id=1, source_target_pairs={{3,0},{0,1},{1,2},{2,3},{7,4},{4,5},{5,6},{6,7},{11,8},{8,9},{9,10... | collective-permute-start | bytes 1032200 | tf_op jit(solution)/shard_map/ppermute | solution.py:504
  61.8 18.1 %all-to-all-start.2 = ((bf16[4,128,768]{2,1,0:T(8,128)(2,1)}), bf16[4,128,768]{2,1,0:T(8,128)(2,1)S(1)}, u32[]{:S(2)}, u32[]{:S(2)}) async-start(bf16[4,128,768]{2,1,0:T(8,128)(2,1)} %get-tuple-element.56), calls=%async_computation.2 | async-start | bytes 1572864 | tf_op jit(solution)/shard_map/all_to_all | solution.py:558
  70.3 6.2 %collective-permute-start.5 = (bf16[4,24,896]{2,1,0:T(8,128)(2,1)S(1)}, bf16[4,24,896]{2,1,0:T(8,128)(2,1)S(1)}, u32[]{:S(2)}, u32[]{:S(2)}) collective-permute-start(bf16[4,24,896]{2,1,0:T(8,128)(2,1)S(1)} %slice.63), channel_id=1, source_target_pairs={{1,0},{2,1},{3,2},{0,3},{5,4},{6,5},{7,6},{4,7},{9,8},{10,9},{11,1... | collective-permute-start | bytes 516104 | tf_op jit(solution)/shard_map/ppermute | solution.py:504
  72.3 7.7 %collective-permute-start.6 = (bf16[4,24,896]{2,1,0:T(8,128)(2,1)S(1)}, bf16[4,24,896]{2,1,0:T(8,128)(2,1)S(1)}, u32[]{:S(2)}, u32[]{:S(2)}) collective-permute-start(bf16[4,24,896]{2,1,0:T(8,128)(2,1)S(1)} %slice.64), channel_id=1, source_target_pairs={{3,0},{0,1},{1,2},{2,3},{7,4},{4,5},{5,6},{6,7},{11,8},{8,9},{9,10... | collective-permute-start | bytes 516104 | tf_op jit(solution)/shard_map/ppermute | solution.py:504
  79.9 7.8 %collective-permute-start.7 = (bf16[4,128,768]{2,1,0:T(8,128)(2,1)S(1)}, bf16[4,128,768]{2,1,0:T(8,128)(2,1)S(1)}, u32[]{:S(2)}, u32[]{:S(2)}) collective-permute-start(bf16[4,128,768]{2,1,0:T(8,128)(2,1)S(1)} %all-to-all-done.2.own_ref), channel_id=1, source_target_pairs={{0,32},{32,0},{1,33},{33,1},{2,34},{34,2},{3,35},{35,3},{4,36},{36... | collective-permute-start | bytes 2359304 | tf_op jit(solution)/shard_map/ppermute | solution.py:562
  91.0 17.6 %all-to-all-start.3 = ((bf16[8,64,768]{2,1,0:T(8,128)(2,1)}), bf16[8,64,768]{2,1,0:T(8,128)(2,1)S(1)}, u32[]{:S(2)}, u32[]{:S(2)}) async-start(bf16[8,64,768]{2,1,0:T(8,128)(2,1)} %get-tuple-element.65), calls=%async_computation.3 | async-start | bytes 1572864 | tf_op jit(solution)/shard_map/all_to_all | solution.py:566
  100.6 20.0 %collective-permute-start.10 = (bf16[8,24,768]{2,1,0:T(8,128)(2,1)S(1)}, bf16[8,24,768]{2,1,0:T(8,128)(2,1)S(1)}, u32[]{:S(2)}, u32[]{:S(2)}) collective-permute-start(bf16[8,24,768]{2,1,0:T(8,128)(2,1)S(1)} %bitcast.23), channel_id=1, source_target_pairs={{0,3},{1,0},{2,1},{3,2},{4,7},{5,4},{6,5},{7,6},{8,11},{9,8},{10,9... | collective-permute-start | bytes 884744 | tf_op jit(solution)/shard_map/ppermute | solution.py:511
  102.5 18.0 %collective-permute-start.8 = (bf16[8,24,768]{2,1,0:T(8,128)(2,1)S(1)}, bf16[8,24,768]{2,1,0:T(8,128)(2,1)S(1)}, u32[]{:S(2)}, u32[]{:S(2)}) collective-permute-start(bf16[8,24,768]{2,1,0:T(8,128)(2,1)S(1)} %bitcast.22), channel_id=1, source_target_pairs={{0,1},{1,2},{2,3},{3,0},{4,5},{5,6},{6,7},{7,4},{8,9},{9,10},{10,1... | collective-permute-start | bytes 884744 | tf_op jit(solution)/shard_map/ppermute | solution.py:511
  105.9 14.7 %collective-permute-start.9 = (bf16[8,24,768]{2,1,0:T(8,128)(2,1)S(1)}, bf16[8,24,768]{2,1,0:T(8,128)(2,1)}, u32[]{:S(2)}, u32[]{:S(2)}) collective-permute-start(bf16[8,24,768]{2,1,0:T(8,128)(2,1)S(1)} %bitcast.21), channel_id=1, source_target_pairs={{0,2},{1,3},{2,0},{3,1},{4,6},{5,7},{6,4},{7,5},{8,10},{9,11},{10,... | collective-permute-start | bytes 884744 | tf_op jit(solution)/shard_map/ppermute | solution.py:511
  109.8 22.8 %all-to-all-start.4 = ((bf16[32,16,128]{2,1,0:T(8,128)(2,1)}), bf16[32,16,128]{2,1,0:T(8,128)(2,1)S(1)}, u32[]{:S(2)}, u32[]{:S(2)}) async-start(bf16[32,16,128]{2,1,0:T(8,128)(2,1)} %shard_map.201), calls=%async_computation.4 | async-start | bytes 262144 | tf_op jit(solution)/shard_map/all_to_all | solution.py:482
  121.7 7.0 %collective-permute-start.11 = (bf16[4,24,768]{2,1,0:T(8,128)(2,1)S(1)}, bf16[4,24,768]{2,1,0:T(8,128)(2,1)S(1)}, u32[]{:S(2)}, u32[]{:S(2)}) collective-permute-start(bf16[4,24,768]{2,1,0:T(8,128)(2,1)S(1)} %slice.111), channel_id=1, source_target_pairs={{0,4},{4,0},{1,5},{5,1},{2,6},{6,2},{3,7},{7,3},{8,12},{12,8},{9,1... | collective-permute-start | bytes 442376 | tf_op jit(solution)/shard_map/ppermute | solution.py:468
  132.8 15.5 %all-to-all-start.5 = ((bf16[4,24,768]{2,1,0:T(8,128)(2,1)}), bf16[4,24,768]{2,1,0:T(8,128)(2,1)S(1)}, u32[]{:S(2)}, u32[]{:S(2)}) async-start(bf16[4,24,768]{2,1,0:T(8,128)(2,1)} %fusion.2), calls=%async_computation.5 | async-start | bytes 294912 | tf_op jit(solution)/shard_map/all_to_all | solution.py:575
  138.4 21.7 %collective-permute-start.14 = (bf16[24,3,256]{2,1,0:T(4,128)(2,1)S(1)}, bf16[24,3,256]{2,1,0:T(4,128)(2,1)S(1)}, u32[]{:S(2)}, u32[]{:S(2)}) collective-permute-start(bf16[24,3,256]{2,1,0:T(4,128)(2,1)S(1)} %select_bitcast_fusion), channel_id=1, source_target_pairs={{32,64},{96,128},{160,192},{224,256},{288,320},{352,384},{416,448}... | collective-permute-start | bytes 110600 | tf_op jit(solution)/shard_map/ppermute | solution.py:494
  148.5 13.5 %collective-permute-start.12 = (bf16[24,896]{1,0:T(8,128)(2,1)S(1)}, bf16[24,896]{1,0:T(8,128)(2,1)S(1)}, u32[]{:S(2)}, u32[]{:S(2)}) collective-permute-start(bf16[24,896]{1,0:T(8,128)(2,1)S(1)} %pad_maximum_fusion), channel_id=1, source_target_pairs={{0,256},{256,0},{1,257},{257,1},{2,258},{258,2},{3,259},{259,3},{4... | collective-permute-start | bytes 129032 | tf_op jit(solution)/shard_map/ppermute | solution.py:584
  156.1 4.9 %collective-permute-start.13 = (bf16[24,3,256]{2,1,0:T(4,128)(2,1)S(1)}, bf16[24,3,256]{2,1,0:T(4,128)(2,1)S(1)}, u32[]{:S(2)}, u32[]{:S(2)}) collective-permute-start(bf16[24,3,256]{2,1,0:T(4,128)(2,1)S(1)} %select_bitcast_fusion.1), channel_id=1, source_target_pairs={{0,32},{64,96},{128,160},{192,224},{256,288},{320,352},{384,416},{... | collective-permute-start | bytes 110600 | tf_op jit(solution)/shard_map/ppermute | solution.py:488
  162.9 15.3 %all-to-all-start.6 = ((bf16[8,24,896]{2,1,0:T(8,128)(2,1)}), bf16[8,24,896]{2,1,0:T(8,128)(2,1)S(1)}, u32[]{:S(2)}, u32[]{:S(2)}) async-start(bf16[8,24,896]{2,1,0:T(8,128)(2,1)} %broadcast_in_dim.37), calls=%async_computation.6 | async-start | bytes 688128 | tf_op jit(solution)/shard_map/all_to_all | solution.py:478
  (7 other events, 105.6 us)

commit v14 on v13

--- a/solution.py
+++ b/solution.py
@@ -317,7 +317,7 @@
     )(*parts)
 
 
-def mlp_body(core_ref, own_ref, other_ref, wi_ref, wo_ref, bi_ref, gamma_ref, dn_ref, n_ref, dy_ref, acts_ref):
+def mlp_body(core_ref, own_ref, other_ref, wi_ref, wo_ref, bi_ref, gamma_ref, dn_ref, n_ref, dy_ref, acts_ref, gam_ref):
     members, lanes, _ = own_ref.shape
     piece = lanes // 2
     for at, ref in ((0, own_ref), (members, other_ref)):
@@ -337,6 +337,8 @@
     for k in range(members):
         dn_ref[core * members + k] = dn[k * piece : (k + 1) * piece]
         dn_ref[(1 - core) * members + k] = dn[(members + k) * piece : (members + k + 1) * piece]
+    back = dot(acts_ref[:, :hid], wo_ref[...], 1, 0)
+    gam_ref[...] = jnp.sum(dy_ref[...].astype(F32) * back, 0, keepdims=True)
 
 
 def mlp(core, own, other, wi, wo, bi, gamma):
@@ -349,19 +351,19 @@
             jax.ShapeDtypeStruct((toks, chans), BF),
             jax.ShapeDtypeStruct((toks, chans), BF),
             jax.ShapeDtypeStruct((toks, 2 * hid), BF),
+            jax.ShapeDtypeStruct((1, chans), F32),
         ],
         [smem()] + [vmem()] * 6,
     )(core, own, other, wi, wo, bi, gamma[None])
 
 
-def grads_body(part, ny, place_ref, n_ref, dy_ref, acts_ref, wo_ref, gamma_ref, out_ref, gam_ref, db_ref):
+def grads_body(part, ny, place_ref, n_ref, dy_ref, acts_ref, gamma_ref, out_ref, db_ref):
     toks = n_ref.shape[0]
     hid = acts_ref.shape[1] // 2
     first, second = picks(hid // part, part)
     dpre = acts_ref[:, hid:]
     dw_in = dot(dpre, n_ref[...], 0, 0).astype(BF)
     proj = dot(acts_ref[:, :hid], dy_ref[...], 0, 0)
-    gam_ref[...] = jnp.sum(wo_ref[...].astype(F32) * proj, 0, keepdims=True)
     dw_out = (proj * gamma_ref[...]).astype(BF)
     out_ref[...] = (dot(first, dw_in, 1, 0) + dot(second, dw_out, 1, 0)).astype(BF)
     nz = hid // part // ny
@@ -380,18 +382,17 @@
     db_ref[...] = dot(db, spot, 1, 1)[:1]
 
 
-def grads(part, ny, place, n, dy, acts, wo, gamma):
+def grads(part, ny, place, n, dy, acts, gamma):
     chans = n.shape[1]
     hid = acts.shape[1] // 2
     return call(
         functools.partial(grads_body, part, ny),
         [
             jax.ShapeDtypeStruct((2 * hid, chans), BF),
-            jax.ShapeDtypeStruct((1, chans), F32),
             jax.ShapeDtypeStruct((1, 2 * hid), F32),
         ],
-        [smem()] + [vmem()] * 5,
-    )(place, n, dy, acts, wo, gamma[None])
+        [smem()] + [vmem()] * 4,
+    )(place, n, dy, acts, gamma[None])
 
 
 def slices_body(w_in_ref, w_out_ref, b_ref, out_ref):
@@ -562,11 +563,11 @@
     other = lax.ppermute(pair, "c", [(0, 1), (1, 0)])
 
     core = lax.axis_index("c").astype(jnp.int32)[None]
-    dn, n, dy, acts = mlp(core, pair, other, wi, wo, bi, gamma_f)
+    dn, n, dy, acts, gam_part = mlp(core, pair, other, wi, wo, bi, gamma_f)
     dn = lax.all_to_all(dn, ("c", "x"), 0, 0, tiled=True)
 
     place = jnp.stack([lax.axis_index("y"), lax.axis_index("zp")]).astype(jnp.int32)
-    dws, gam_part, db_part = grads(part, ny, place, n, dy, acts, wo, gamma_f)
+    dws, db_part = grads(part, ny, place, n, dy, acts, gamma_f)
     dws = to_ring(dws.reshape(ny, nz, 2 * part, chans))
     dws = to_neighbour(dws).astype(BF)
 

time: 182 us -> 181 us (level)
  starting transfers between devices: 117 us -> 119 us
where the time goes in v14:
time: 181 us; the launch traced here: 180 us
  starting transfers between devices  119 us (66%)
  waiting for transfers between devices  30.9 us (17%)
  Pallas kernels  20.5 us (11%)
  local copies, waits for them, and re-layouts  4.68 us (3%)
  other arithmetic  3.48 us (2%)
    all_to_all x2, starting transfers between devices, exchange(): return lax.all_to_all(blocks, CHAN, 0, 0, tiled=True)  21.3 us
    ppermute x4, waiting for transfers between devices, along_ring(): lax.ppermute(block, 'y', [((i + ahead) % count, i) for i in range(count)])  14 us
    all_to_all x1, starting transfers between devices, per_device(): shards = lax.all_to_all(slices(nz // 2, *cut), 'zq', 0, 0, tiled=True)  11.8 us
    ppermute x4, starting transfers between devices, along_ring(): lax.ppermute(block, 'y', [((i + ahead) % count, i) for i in range(count)])  11.6 us
    all_to_all x1, starting transfers between devices, to_all(): lax.all_to_all(jnp.broadcast_to(block[None], (count,) + block.shape), axi...  9.32 us
    ppermute x2, starting transfers between devices, swap_odd(): lax.ppermute(jnp.where(even, first, last), LAT, pairs + [(j, i) for i, j...  8.8 us
    all_to_all x1, starting transfers between devices, per_device(): pair = lax.all_to_all(pair, 'x', 0, 0, tiled=True)  8.52 us
    ppermute x3, starting transfers between devices, to_ring(): lax.ppermute(blocks[k], 'y', [(i, (i + k) % count) for i in range(count)])  8.05 us
  transfers between devices with their start and end apart: 22, of which 11 were waited for; matrix products, arithmetic and copies ran while one was open for 3% of the time, Pallas kernels for 8%

profile of v14, /device:TPU:1, one launch (start us, length us, event | category | flops | bytes accessed | tf_op | source)
XLA Modules:
  0.0 179.7 jit_solution(13646774384655073167)
XLA Ops:
  3.0 11.8 %all-to-all-start = ((bf16[4,24,896]{2,1,0:T(8,128)(2,1)}), bf16[4,24,896]{2,1,0:T(8,128)(2,1)S(1)}, u32[]{:S(2)}, u32[]{:S(2)}) async-start(bf16[4,24,896]{2,1,0:T(8,128)(2,1)} %shard_map.196), calls=%async_computation | async-start | bytes 344064 | tf_op jit(solution)/shard_map/all_to_all | solution.py:544
  15.9 4.0 %collective-permute-start = (bf16[24,3,256]{2,1,0:T(4,128)(2,1)S(1)}, bf16[24,3,256]{2,1,0:T(4,128)(2,1)S(1)}, u32[]{:S(2)}, u32[]{:S(2)}) collective-permute-start(bf16[24,3,256]{2,1,0:T(4,128)(2,1)S(1)} %get-tuple-element.107), channel_id=1, source_target_pairs={{32,64},{96,128},{160,192},{224,256},{288,320},{352,384},{416,448}... | collective-permute-start | bytes 110600 | tf_op jit(solution)/shard_map/ppermute | solution.py:495
  24.0 4.9 %collective-permute-start.2 = (bf16[4,24,896]{2,1,0:T(8,128)(2,1)S(1)}, bf16[4,24,896]{2,1,0:T(8,128)(2,1)S(1)}, u32[]{:S(2)}, u32[]{:S(2)}) collective-permute-start(bf16[4,24,896]{2,1,0:T(8,128)(2,1)S(1)} %all-to-all-done), channel_id=1, source_target_pairs={{0,4},{4,0},{1,5},{5,1},{2,6},{6,2},{3,7},{7,3},{8,12},{12,8},{9,1... | collective-permute-start | bytes 516104 | tf_op jit(solution)/shard_map/ppermute | solution.py:545
  29.1 3.6 %shard_map.195 = bf16[32,24,128]{2,1,0:T(8,128)(2,1)} custom-call(f32[24,50]{1,0:T(8,128)S(1)} %pad_maximum_fusion.2.taps_ref, bf16[24,8,256]{2,1,0:T(8,128)(2,1)S(1)} %copy-done.2, bf16[24,3,256]{2,1,0:T(4,128)(2,1)S(1)} %get-tuple-element.105.up_ref, bf16[24,3,256]{2,1,0:T(4,128)(2,1)S(1)} %get-tuple-element.104.down_ref, f32[8,1]{1,0:T(8,128)S(1)} %copy.23.metric_ref, ...), custom_call_target="tpu_custom_call" | custom-call | tf_op jit(solution)/shard_map/pallas_call | solution.py:100
  32.6 11.9 %all-to-all-start.1 = ((bf16[32,24,128]{2,1,0:T(8,128)(2,1)}), bf16[32,24,128]{2,1,0:T(8,128)(2,1)S(1)}, u32[]{:S(2)}, u32[]{:S(2)}) async-start(bf16[32,24,128]{2,1,0:T(8,128)(2,1)} %shard_map.195), calls=%async_computation.1 | async-start | bytes 393216 | tf_op jit(solution)/shard_map/all_to_all | solution.py:483
  44.6 4.3 %collective-permute-start.3 = (bf16[8,24,896]{2,1,0:T(8,128)(2,1)S(1)}, bf16[8,24,896]{2,1,0:T(8,128)(2,1)S(1)}, u32[]{:S(2)}, u32[]{:S(2)}) collective-permute-start(bf16[8,24,896]{2,1,0:T(8,128)(2,1)S(1)} %constant_dynamic-update-slice_fusion.own_ref), channel_id=1, source_target_pairs={{1,0},{2,1},{3,2},{0,3},{5,4},{6,5},{7,6},{4,7},{9,8},{10,9},{11,1... | collective-permute-start | bytes 1032200 | tf_op jit(solution)/shard_map/ppermute | solution.py:505
  50.9 5.2 %collective-permute-done.3.one_ref = bf16[8,24,896]{2,1,0:T(8,128)(2,1)S(1)} collective-permute-done((bf16[8,24,896]{2,1,0:T(8,128)(2,1)S(1)}, bf16[8,24,896]{2,1,0:T(8,128)(2,1)S(1)}, u32[]{:S(2)}, u32[]{:S(2)}) %collective-permute-start.3) | collective-permute-done | bytes 344096 | tf_op jit(solution)/shard_map/ppermute | solution.py:505
  56.2 4.5 %collective-permute-done.4.last_ref = bf16[8,24,896]{2,1,0:T(8,128)(2,1)S(1)} collective-permute-done((bf16[8,24,896]{2,1,0:T(8,128)(2,1)S(1)}, bf16[8,24,896]{2,1,0:T(8,128)(2,1)S(1)}, u32[]{:S(2)}, u32[]{:S(2)}) %collective-permute-start.4) | collective-permute-done | bytes 344096 | tf_op jit(solution)/shard_map/ppermute | solution.py:505
  62.5 8.5 %all-to-all-start.2 = ((bf16[4,128,768]{2,1,0:T(8,128)(2,1)}), bf16[4,128,768]{2,1,0:T(8,128)(2,1)S(1)}, u32[]{:S(2)}, u32[]{:S(2)}) async-start(bf16[4,128,768]{2,1,0:T(8,128)(2,1)} %get-tuple-element.56), calls=%async_computation.2 | async-start | bytes 1572864 | tf_op jit(solution)/shard_map/all_to_all | solution.py:559
  73.0 3.4 %collective-permute-start.6 = (bf16[4,24,896]{2,1,0:T(8,128)(2,1)S(1)}, bf16[4,24,896]{2,1,0:T(8,128)(2,1)S(1)}, u32[]{:S(2)}, u32[]{:S(2)}) collective-permute-start(bf16[4,24,896]{2,1,0:T(8,128)(2,1)S(1)} %slice.64), channel_id=1, source_target_pairs={{3,0},{0,1},{1,2},{2,3},{7,4},{4,5},{5,6},{6,7},{11,8},{8,9},{9,10... | collective-permute-start | bytes 516104 | tf_op jit(solution)/shard_map/ppermute | solution.py:505
  77.2 3.5 %collective-permute-done.6.high_ref = bf16[4,24,896]{2,1,0:T(8,128)(2,1)S(1)} collective-permute-done((bf16[4,24,896]{2,1,0:T(8,128)(2,1)S(1)}, bf16[4,24,896]{2,1,0:T(8,128)(2,1)S(1)}, u32[]{:S(2)}, u32[]{:S(2)}) %collective-permute-start.6) | collective-permute-done | bytes 172064 | tf_op jit(solution)/shard_map/ppermute | solution.py:505
  80.6 5.9 %collective-permute-start.7 = (bf16[4,128,768]{2,1,0:T(8,128)(2,1)S(1)}, bf16[4,128,768]{2,1,0:T(8,128)(2,1)S(1)}, u32[]{:S(2)}, u32[]{:S(2)}) collective-permute-start(bf16[4,128,768]{2,1,0:T(8,128)(2,1)S(1)} %all-to-all-done.2.own_ref), channel_id=1, source_target_pairs={{0,32},{32,0},{1,33},{33,1},{2,34},{34,2},{3,35},{35,3},{4,36},{36... | collective-permute-start | bytes 2359304 | tf_op jit(solution)/shard_map/ppermute | solution.py:563
  90.9 5.2 %all-to-all-start.3 = ((bf16[8,64,768]{2,1,0:T(8,128)(2,1)}), bf16[8,64,768]{2,1,0:T(8,128)(2,1)S(1)}, u32[]{:S(2)}, u32[]{:S(2)}) async-start(bf16[8,64,768]{2,1,0:T(8,128)(2,1)} %get-tuple-element.65), calls=%async_computation.3 | async-start | bytes 1572864 | tf_op jit(solution)/shard_map/all_to_all | solution.py:567
  101.1 3.4 %collective-permute-start.8 = (bf16[8,24,768]{2,1,0:T(8,128)(2,1)S(1)}, bf16[8,24,768]{2,1,0:T(8,128)(2,1)S(1)}, u32[]{:S(2)}, u32[]{:S(2)}) collective-permute-start(bf16[8,24,768]{2,1,0:T(8,128)(2,1)S(1)} %bitcast.22), channel_id=1, source_target_pairs={{0,1},{1,2},{2,3},{3,0},{4,5},{5,6},{6,7},{7,4},{8,9},{9,10},{10,1... | collective-permute-start | bytes 884744 | tf_op jit(solution)/shard_map/ppermute | solution.py:512
  109.7 9.4 %all-to-all-start.4 = ((bf16[32,16,128]{2,1,0:T(8,128)(2,1)}), bf16[32,16,128]{2,1,0:T(8,128)(2,1)S(1)}, u32[]{:S(2)}, u32[]{:S(2)}) async-start(bf16[32,16,128]{2,1,0:T(8,128)(2,1)} %shard_map.201), calls=%async_computation.4 | async-start | bytes 262144 | tf_op jit(solution)/shard_map/all_to_all | solution.py:483
  122.5 3.9 %collective-permute-done.11 = bf16[4,24,768]{2,1,0:T(8,128)(2,1)S(1)} collective-permute-done((bf16[4,24,768]{2,1,0:T(8,128)(2,1)S(1)}, bf16[4,24,768]{2,1,0:T(8,128)(2,1)S(1)}, u32[]{:S(2)}, u32[]{:S(2)}) %collective-permute-start.11) | collective-permute-done | bytes 147488 | tf_op jit(solution)/shard_map/ppermute | solution.py:469
  127.0 4.2 %all-to-all-done.4.recv_ref = bf16[32,16,128]{2,1,0:T(8,128)(2,1)S(1)} async-done(((bf16[32,16,128]{2,1,0:T(8,128)(2,1)}), bf16[32,16,128]{2,1,0:T(8,128)(2,1)S(1)}, u32[]{:S(2)}, u32[]{:S(2)}) %all-to-all-start.4) | async-done | bytes 131104 | tf_op jit(solution)/shard_map/all_to_all | solution.py:483
  131.4 5.4 %all-to-all-start.5 = ((bf16[4,24,768]{2,1,0:T(8,128)(2,1)}), bf16[4,24,768]{2,1,0:T(8,128)(2,1)S(1)}, u32[]{:S(2)}, u32[]{:S(2)}) async-start(bf16[4,24,768]{2,1,0:T(8,128)(2,1)} %fusion.2), calls=%async_computation.5 | async-start | bytes 294912 | tf_op jit(solution)/shard_map/all_to_all | solution.py:576
  136.9 4.8 %collective-permute-start.14 = (bf16[24,3,256]{2,1,0:T(4,128)(2,1)S(1)}, bf16[24,3,256]{2,1,0:T(4,128)(2,1)S(1)}, u32[]{:S(2)}, u32[]{:S(2)}) collective-permute-start(bf16[24,3,256]{2,1,0:T(4,128)(2,1)S(1)} %select_bitcast_fusion), channel_id=1, source_target_pairs={{32,64},{96,128},{160,192},{224,256},{288,320},{352,384},{416,448}... | collective-permute-start | bytes 110600 | tf_op jit(solution)/shard_map/ppermute | solution.py:495
  146.8 7.6 %collective-permute-start.12 = (bf16[24,896]{1,0:T(8,128)(2,1)S(1)}, bf16[24,896]{1,0:T(8,128)(2,1)S(1)}, u32[]{:S(2)}, u32[]{:S(2)}) collective-permute-start(bf16[24,896]{1,0:T(8,128)(2,1)S(1)} %pad_maximum_fusion), channel_id=1, source_target_pairs={{0,256},{256,0},{1,257},{257,1},{2,258},{258,2},{3,259},{259,3},{4... | collective-permute-start | bytes 129032 | tf_op jit(solution)/shard_map/ppermute | solution.py:585
  154.5 5.6 %collective-permute-start.13 = (bf16[24,3,256]{2,1,0:T(4,128)(2,1)S(1)}, bf16[24,3,256]{2,1,0:T(4,128)(2,1)S(1)}, u32[]{:S(2)}, u32[]{:S(2)}) collective-permute-start(bf16[24,3,256]{2,1,0:T(4,128)(2,1)S(1)} %select_bitcast_fusion.1), channel_id=1, source_target_pairs={{0,32},{64,96},{128,160},{192,224},{256,288},{320,352},{384,416},{... | collective-permute-start | bytes 110600 | tf_op jit(solution)/shard_map/ppermute | solution.py:489
  161.9 9.3 %all-to-all-start.6 = ((bf16[8,24,896]{2,1,0:T(8,128)(2,1)}), bf16[8,24,896]{2,1,0:T(8,128)(2,1)S(1)}, u32[]{:S(2)}, u32[]{:S(2)}) async-start(bf16[8,24,896]{2,1,0:T(8,128)(2,1)} %broadcast_in_dim.37), calls=%async_computation.6 | async-start | bytes 688128 | tf_op jit(solution)/shard_map/all_to_all | solution.py:479
  171.4 3.4 %shard_map.204 = f32[24,8,256]{2,1,0:T(8,128)} custom-call(f32[24,50]{1,0:T(8,128)S(1)} %pad_maximum_fusion.2.taps_ref, f32[24,8,256]{2,1,0:T(8,128)S(1)} %get-tuple-element.75.dconv_ref.x_ref, bf16[24,3,256]{2,1,0:T(4,128)(2,1)S(1)} %get-tuple-element.103.up_ref, bf16[24,3,256]{2,1,0:T(4,128)(2,1)S(1)} %get-tuple-element.102.down_ref, ...), custom_call_target="tpu_custom_call" | custom-call | tf_op jit(solution)/shard_map/pallas_call | solution.py:267
  174.8 3.8 %all-to-all-done.6.gathered_ref = bf16[8,24,896]{2,1,0:T(8,128)(2,1)S(1)} async-done(((bf16[8,24,896]{2,1,0:T(8,128)(2,1)}), bf16[8,24,896]{2,1,0:T(8,128)(2,1)S(1)}, u32[]{:S(2)}, u32[]{:S(2)}) %all-to-all-start.6) | async-done | bytes 344096 | tf_op jit(solution)/shard_map/all_to_all | solution.py:479
  (83 shorter events, 41.2 us)
Async XLA Ops:
  3.0 47.9 %copy-start.6 = (f32[768]{0:T(1024)S(1)}, f32[768]{0:T(1024)}, u32[]{:S(2)}) copy-start(f32[768]{0:T(1024)} %param.17) | copy-start | bytes 9220
  3.0 47.9 %copy-start.7 = (f32[768]{0:T(1024)S(1)}, f32[768]{0:T(1024)}, u32[]{:S(2)}) copy-start(f32[768]{0:T(1024)} %param.18) | copy-start | bytes 9220
  3.0 21.0 %all-to-all-start = ((bf16[4,24,896]{2,1,0:T(8,128)(2,1)}), bf16[4,24,896]{2,1,0:T(8,128)(2,1)S(1)}, u32[]{:S(2)}, u32[]{:S(2)}) async-start(bf16[4,24,896]{2,1,0:T(8,128)(2,1)} %shard_map.196), calls=%async_computation | async-start | bytes 344064 | tf_op jit(solution)/shard_map/all_to_all | solution.py:544
  15.9 13.1 %collective-permute-start = (bf16[24,3,256]{2,1,0:T(4,128)(2,1)S(1)}, bf16[24,3,256]{2,1,0:T(4,128)(2,1)S(1)}, u32[]{:S(2)}, u32[]{:S(2)}) collective-permute-start(bf16[24,3,256]{2,1,0:T(4,128)(2,1)S(1)} %get-tuple-element.107), channel_id=1, source_target_pairs={{32,64},{96,128},{160,192},{224,256},{288,320},{352,384},{416,448}... | collective-permute-start | bytes 110600 | tf_op jit(solution)/shard_map/ppermute | solution.py:495
  19.9 9.1 %collective-permute-start.1 = (bf16[24,3,256]{2,1,0:T(4,128)(2,1)S(1)}, bf16[24,3,256]{2,1,0:T(4,128)(2,1)S(1)}, u32[]{:S(2)}, u32[]{:S(2)}) collective-permute-start(bf16[24,3,256]{2,1,0:T(4,128)(2,1)S(1)} %get-tuple-element.106), channel_id=1, source_target_pairs={{0,32},{64,96},{128,160},{192,224},{256,288},{320,352},{384,416},{... | collective-permute-start | bytes 110600 | tf_op jit(solution)/shard_map/ppermute | solution.py:489
  24.0 8.6 %collective-permute-start.2 = (bf16[4,24,896]{2,1,0:T(8,128)(2,1)S(1)}, bf16[4,24,896]{2,1,0:T(8,128)(2,1)S(1)}, u32[]{:S(2)}, u32[]{:S(2)}) collective-permute-start(bf16[4,24,896]{2,1,0:T(8,128)(2,1)S(1)} %all-to-all-done), channel_id=1, source_target_pairs={{0,4},{4,0},{1,5},{5,1},{2,6},{6,2},{3,7},{7,3},{8,12},{12,8},{9,1... | collective-permute-start | bytes 516104 | tf_op jit(solution)/shard_map/ppermute | solution.py:545
  32.6 28.0 %all-to-all-start.1 = ((bf16[32,24,128]{2,1,0:T(8,128)(2,1)}), bf16[32,24,128]{2,1,0:T(8,128)(2,1)S(1)}, u32[]{:S(2)}, u32[]{:S(2)}) async-start(bf16[32,24,128]{2,1,0:T(8,128)(2,1)} %shard_map.195), calls=%async_computation.1 | async-start | bytes 393216 | tf_op jit(solution)/shard_map/all_to_all | solution.py:483
  44.6 11.6 %collective-permute-start.3 = (bf16[8,24,896]{2,1,0:T(8,128)(2,1)S(1)}, bf16[8,24,896]{2,1,0:T(8,128)(2,1)S(1)}, u32[]{:S(2)}, u32[]{:S(2)}) collective-permute-start(bf16[8,24,896]{2,1,0:T(8,128)(2,1)S(1)} %constant_dynamic-update-slice_fusion.own_ref), channel_id=1, source_target_pairs={{1,0},{2,1},{3,2},{0,3},{5,4},{6,5},{7,6},{4,7},{9,8},{10,9},{11,1... | collective-permute-start | bytes 1032200 | tf_op jit(solution)/shard_map/ppermute | solution.py:505
  49.0 11.7 %collective-permute-start.4 = (bf16[8,24,896]{2,1,0:T(8,128)(2,1)S(1)}, bf16[8,24,896]{2,1,0:T(8,128)(2,1)S(1)}, u32[]{:S(2)}, u32[]{:S(2)}) collective-permute-start(bf16[8,24,896]{2,1,0:T(8,128)(2,1)S(1)} %constant_dynamic-update-slice_fusion.own_ref), channel_id=1, source_target_pairs={{3,0},{0,1},{1,2},{2,3},{7,4},{4,5},{5,6},{6,7},{11,8},{8,9},{9,10... | collective-permute-start | bytes 1032200 | tf_op jit(solution)/shard_map/ppermute | solution.py:505
  62.5 18.1 %all-to-all-start.2 = ((bf16[4,128,768]{2,1,0:T(8,128)(2,1)}), bf16[4,128,768]{2,1,0:T(8,128)(2,1)S(1)}, u32[]{:S(2)}, u32[]{:S(2)}) async-start(bf16[4,128,768]{2,1,0:T(8,128)(2,1)} %get-tuple-element.56), calls=%async_computation.2 | async-start | bytes 1572864 | tf_op jit(solution)/shard_map/all_to_all | solution.py:559
  71.0 6.2 %collective-permute-start.5 = (bf16[4,24,896]{2,1,0:T(8,128)(2,1)S(1)}, bf16[4,24,896]{2,1,0:T(8,128)(2,1)S(1)}, u32[]{:S(2)}, u32[]{:S(2)}) collective-permute-start(bf16[4,24,896]{2,1,0:T(8,128)(2,1)S(1)} %slice.63), channel_id=1, source_target_pairs={{1,0},{2,1},{3,2},{0,3},{5,4},{6,5},{7,6},{4,7},{9,8},{10,9},{11,1... | collective-permute-start | bytes 516104 | tf_op jit(solution)/shard_map/ppermute | solution.py:505
  73.0 7.7 %collective-permute-start.6 = (bf16[4,24,896]{2,1,0:T(8,128)(2,1)S(1)}, bf16[4,24,896]{2,1,0:T(8,128)(2,1)S(1)}, u32[]{:S(2)}, u32[]{:S(2)}) collective-permute-start(bf16[4,24,896]{2,1,0:T(8,128)(2,1)S(1)} %slice.64), channel_id=1, source_target_pairs={{3,0},{0,1},{1,2},{2,3},{7,4},{4,5},{5,6},{6,7},{11,8},{8,9},{9,10... | collective-permute-start | bytes 516104 | tf_op jit(solution)/shard_map/ppermute | solution.py:505
  80.6 7.8 %collective-permute-start.7 = (bf16[4,128,768]{2,1,0:T(8,128)(2,1)S(1)}, bf16[4,128,768]{2,1,0:T(8,128)(2,1)S(1)}, u32[]{:S(2)}, u32[]{:S(2)}) collective-permute-start(bf16[4,128,768]{2,1,0:T(8,128)(2,1)S(1)} %all-to-all-done.2.own_ref), channel_id=1, source_target_pairs={{0,32},{32,0},{1,33},{33,1},{2,34},{34,2},{3,35},{35,3},{4,36},{36... | collective-permute-start | bytes 2359304 | tf_op jit(solution)/shard_map/ppermute | solution.py:563
  90.9 17.6 %all-to-all-start.3 = ((bf16[8,64,768]{2,1,0:T(8,128)(2,1)}), bf16[8,64,768]{2,1,0:T(8,128)(2,1)S(1)}, u32[]{:S(2)}, u32[]{:S(2)}) async-start(bf16[8,64,768]{2,1,0:T(8,128)(2,1)} %get-tuple-element.65), calls=%async_computation.3 | async-start | bytes 1572864 | tf_op jit(solution)/shard_map/all_to_all | solution.py:567
  99.2 20.0 %collective-permute-start.10 = (bf16[8,24,768]{2,1,0:T(8,128)(2,1)S(1)}, bf16[8,24,768]{2,1,0:T(8,128)(2,1)S(1)}, u32[]{:S(2)}, u32[]{:S(2)}) collective-permute-start(bf16[8,24,768]{2,1,0:T(8,128)(2,1)S(1)} %bitcast.23), channel_id=1, source_target_pairs={{0,3},{1,0},{2,1},{3,2},{4,7},{5,4},{6,5},{7,6},{8,11},{9,8},{10,9... | collective-permute-start | bytes 884744 | tf_op jit(solution)/shard_map/ppermute | solution.py:512
  101.1 18.0 %collective-permute-start.8 = (bf16[8,24,768]{2,1,0:T(8,128)(2,1)S(1)}, bf16[8,24,768]{2,1,0:T(8,128)(2,1)S(1)}, u32[]{:S(2)}, u32[]{:S(2)}) collective-permute-start(bf16[8,24,768]{2,1,0:T(8,128)(2,1)S(1)} %bitcast.22), channel_id=1, source_target_pairs={{0,1},{1,2},{2,3},{3,0},{4,5},{5,6},{6,7},{7,4},{8,9},{9,10},{10,1... | collective-permute-start | bytes 884744 | tf_op jit(solution)/shard_map/ppermute | solution.py:512
  104.5 14.7 %collective-permute-start.9 = (bf16[8,24,768]{2,1,0:T(8,128)(2,1)S(1)}, bf16[8,24,768]{2,1,0:T(8,128)(2,1)S(1)}, u32[]{:S(2)}, u32[]{:S(2)}) collective-permute-start(bf16[8,24,768]{2,1,0:T(8,128)(2,1)S(1)} %bitcast.21), channel_id=1, source_target_pairs={{0,2},{1,3},{2,0},{3,1},{4,6},{5,7},{6,4},{7,5},{8,10},{9,11},{10,... | collective-permute-start | bytes 884744 | tf_op jit(solution)/shard_map/ppermute | solution.py:512
  109.7 21.5 %all-to-all-start.4 = ((bf16[32,16,128]{2,1,0:T(8,128)(2,1)}), bf16[32,16,128]{2,1,0:T(8,128)(2,1)S(1)}, u32[]{:S(2)}, u32[]{:S(2)}) async-start(bf16[32,16,128]{2,1,0:T(8,128)(2,1)} %shard_map.201), calls=%async_computation.4 | async-start | bytes 262144 | tf_op jit(solution)/shard_map/all_to_all | solution.py:483
  119.3 7.0 %collective-permute-start.11 = (bf16[4,24,768]{2,1,0:T(8,128)(2,1)S(1)}, bf16[4,24,768]{2,1,0:T(8,128)(2,1)S(1)}, u32[]{:S(2)}, u32[]{:S(2)}) collective-permute-start(bf16[4,24,768]{2,1,0:T(8,128)(2,1)S(1)} %slice.111), channel_id=1, source_target_pairs={{0,4},{4,0},{1,5},{5,1},{2,6},{6,2},{3,7},{7,3},{8,12},{12,8},{9,1... | collective-permute-start | bytes 442376 | tf_op jit(solution)/shard_map/ppermute | solution.py:469
  131.4 15.3 %all-to-all-start.5 = ((bf16[4,24,768]{2,1,0:T(8,128)(2,1)}), bf16[4,24,768]{2,1,0:T(8,128)(2,1)S(1)}, u32[]{:S(2)}, u32[]{:S(2)}) async-start(bf16[4,24,768]{2,1,0:T(8,128)(2,1)} %fusion.2), calls=%async_computation.5 | async-start | bytes 294912 | tf_op jit(solution)/shard_map/all_to_all | solution.py:576
  136.9 23.3 %collective-permute-start.14 = (bf16[24,3,256]{2,1,0:T(4,128)(2,1)S(1)}, bf16[24,3,256]{2,1,0:T(4,128)(2,1)S(1)}, u32[]{:S(2)}, u32[]{:S(2)}) collective-permute-start(bf16[24,3,256]{2,1,0:T(4,128)(2,1)S(1)} %select_bitcast_fusion), channel_id=1, source_target_pairs={{32,64},{96,128},{160,192},{224,256},{288,320},{352,384},{416,448}... | collective-permute-start | bytes 110600 | tf_op jit(solution)/shard_map/ppermute | solution.py:495
  146.8 14.1 %collective-permute-start.12 = (bf16[24,896]{1,0:T(8,128)(2,1)S(1)}, bf16[24,896]{1,0:T(8,128)(2,1)S(1)}, u32[]{:S(2)}, u32[]{:S(2)}) collective-permute-start(bf16[24,896]{1,0:T(8,128)(2,1)S(1)} %pad_maximum_fusion), channel_id=1, source_target_pairs={{0,256},{256,0},{1,257},{257,1},{2,258},{258,2},{3,259},{259,3},{4... | collective-permute-start | bytes 129032 | tf_op jit(solution)/shard_map/ppermute | solution.py:585
  154.5 6.5 %collective-permute-start.13 = (bf16[24,3,256]{2,1,0:T(4,128)(2,1)S(1)}, bf16[24,3,256]{2,1,0:T(4,128)(2,1)S(1)}, u32[]{:S(2)}, u32[]{:S(2)}) collective-permute-start(bf16[24,3,256]{2,1,0:T(4,128)(2,1)S(1)} %select_bitcast_fusion.1), channel_id=1, source_target_pairs={{0,32},{64,96},{128,160},{192,224},{256,288},{320,352},{384,416},{... | collective-permute-start | bytes 110600 | tf_op jit(solution)/shard_map/ppermute | solution.py:489
  161.9 16.6 %all-to-all-start.6 = ((bf16[8,24,896]{2,1,0:T(8,128)(2,1)}), bf16[8,24,896]{2,1,0:T(8,128)(2,1)S(1)}, u32[]{:S(2)}, u32[]{:S(2)}) async-start(bf16[8,24,896]{2,1,0:T(8,128)(2,1)} %broadcast_in_dim.37), calls=%async_computation.6 | async-start | bytes 688128 | tf_op jit(solution)/shard_map/all_to_all | solution.py:479
  (7 other events, 115.7 us)
